TPU v7x, 32 devices: a whole 2x2x4 slice. The times are simulated.
32 devices in a mesh: seq: 8 (over z, x), ffn: 4 (over y, core).
Axes of the slice: x: 2, y: 2, z: 4, core: 2. Of those that a mesh axis runs over, the one named last changes fastest.
Arguments:
- block_in: bfloat16 [32768, 768], P(('seq', 'ffn')), may hold values from -6 to 6
- block_cot: bfloat16 [32768, 768], P(('seq', 'ffn')), may hold values from -6 to 6
- cluster_perm: int32 [8, 12, 4096], P('seq', 'ffn'), may hold values from 0 to 4095, each once within a row
- w_qkv: float32 [3, 768, 12, 64], P(None, None, 'ffn', 'seq'), may hold values from -0.21875 to 0.21875
- w_out: float32 [12, 64, 768], P('ffn', 'seq'), may hold values from -1.5 to 1.5
- w_up: float32 [768, 3072], P(None, ('seq', 'ffn')), may hold values from -0.21875 to 0.21875
- w_down: float32 [3072, 768], P(('seq', 'ffn')), may hold values from -0.109375 to 0.109375
- mom_qkv: float32 [3, 768, 12, 64], P(None, None, 'ffn', 'seq'), may hold values from -512 to 512
- mom_out: float32 [12, 64, 768], P('ffn', 'seq'), may hold values from -160 to 160
- mom_up: float32 [768, 3072], P(None, ('seq', 'ffn')), may hold values from -256 to 256
- mom_down: float32 [3072, 768], P(('seq', 'ffn')), may hold values from -512 to 512
- norm_params: float32 [4, 768], replicated, may hold values from -0.9 to 1.45, as said below
- norm_first: float32 [4, 768], replicated, may hold values from -112 to 112
- norm_second: float32 [4, 768], replicated, may hold values from 16.384 to 131.072
Outputs:
- block_out: bfloat16 [32768, 768], P(('seq', 'ffn'))
- input_grad: float32 [32768, 768], P(('seq', 'ffn'))
- grad_qkv: float32 [3, 768, 12, 64], P(None, None, 'ffn', 'seq')
- grad_out: float32 [12, 64, 768], P('ffn', 'seq')
- grad_up: float32 [768, 3072], P(None, ('seq', 'ffn'))
- grad_down: float32 [3072, 768], P(('seq', 'ffn'))
- grad_norm: float32 [4, 768], replicated
- moment_qkv: float32 [3, 768, 12, 64], P(None, None, 'ffn', 'seq')
- moment_out: float32 [12, 64, 768], P('ffn', 'seq')
- moment_up: float32 [768, 3072], P(None, ('seq', 'ffn'))
- moment_down: float32 [3072, 768], P(('seq', 'ffn'))
- master_qkv: float32 [3, 768, 12, 64], P(None, None, 'ffn', 'seq')
- master_out: float32 [12, 64, 768], P('ffn', 'seq')
- master_up: float32 [768, 3072], P(None, ('seq', 'ffn'))
- master_down: float32 [3072, 768], P(('seq', 'ffn'))
- first_new: float32 [4, 768], replicated
- second_new: float32 [4, 768], replicated
- norm_new: float32 [4, 768], replicated
- occupancy: float32 [12, 32], replicated
Inputs may be any that keep to these rules, and one draw needn't show every extreme that they name: `cluster_perm`: each head's row is an order of the 4096 positions of its sequence; its aligned runs of 128 are the clusters. `norm_params`: rows 0 and 2 are gains, rows 1 and 3 biases.
All inputs are finite; a program needn't handle non-finite values.
Results may differ from a plain program's by a relative error of at most 0.02.
Values may be sent and summed in bfloat16 or wider, within the bound.
No kernel may reach another device: no remote copies, remote signals or barrier semaphores. Data moves between devices by JAX's collectives and lax.ppermute only.
A program may use at most 192 MiB of HBM per device.

v0:
```python
import math

import jax
import jax.numpy as jnp
from jax import lax
from jax.sharding import PartitionSpec as P

D = 768
HD = 64
FF = 3072
CLUSTER = 128
NS_STEPS = 3
ADAM_STEP = 10


highest = lax.Precision.HIGHEST
schulz_coeffs = (3.4445, -4.775, 2.0315)
norm_epsilon = 1e-05


def contract(left, right, left_axis, right_axis):
    return lax.dot_general(
        left, right, (((left_axis,), (right_axis,)), ((), ())), preferred_element_type=jnp.float32
    )


def norm_forward(inputs, gains, biases):
    center = inputs - jnp.mean(inputs, axis=-1, keepdims=True)
    spread = jnp.mean(center * center, axis=-1, keepdims=True)
    inv_std = lax.rsqrt(spread + norm_epsilon)
    normed = center * inv_std
    return (normed * gains + biases, normed, inv_std)


def norm_backward(upstream, normed, inv_std, gains):
    scaled = upstream * gains
    inside = (
        scaled
        - jnp.mean(scaled, axis=-1, keepdims=True)
        - normed * jnp.mean(scaled * normed, axis=-1, keepdims=True)
    )
    return (inside * inv_std, jnp.sum(upstream * normed, axis=0), jnp.sum(upstream, axis=0))


def gelu_value(preact):
    return preact * 0.5 * (1.0 + jax.scipy.special.erf(preact * 0.7071067811865476))


def gelu_slope(preact):
    cumulative = 0.5 * (1.0 + jax.scipy.special.erf(preact * 0.7071067811865476))
    density = jnp.exp(-0.5 * preact * preact) * 0.3989422804014327
    return cumulative + preact * density


def by_rows(lookup, indices):
    return lookup[indices]


def gram_qkv(matrix):
    return jnp.einsum("kdhe,kfhe->df", matrix, matrix, precision=highest)


def gram_out(matrix):
    return jnp.einsum("hed,hef->df", matrix, matrix, precision=highest)


def gram_up(matrix):
    return jnp.einsum("dn,fn->df", matrix, matrix, precision=highest)


def gram_down(matrix):
    return jnp.einsum("nd,nf->df", matrix, matrix, precision=highest)


def apply_qkv(mixing, matrix):
    return jnp.einsum("df,kfhe->kdhe", mixing, matrix, precision=highest)


def apply_out(mixing, matrix):
    return jnp.einsum("hef,fd->hed", matrix, mixing, precision=highest)


def apply_up(mixing, matrix):
    return jnp.dot(mixing, matrix, precision=highest)


def apply_down(mixing, matrix):
    return jnp.dot(matrix, mixing, precision=highest)


def fresh_grams(iterates):
    return lax.psum(
        (
            gram_qkv(iterates[0]),
            gram_out(iterates[1]),
            gram_up(iterates[2]),
            gram_down(iterates[3]),
        ),
        ("seq", "ffn"),
    )


def on_device(
    block_in,
    block_cot,
    cluster_perm,
    w_qkv,
    w_out,
    w_up,
    w_down,
    mom_qkv,
    mom_out,
    mom_up,
    mom_down,
    norm_params,
    norm_first,
    norm_second,
):
    weight_qkv, weight_out, weight_up, weight_down = (
        lax.all_gather(w_qkv.astype(jnp.bfloat16), "seq", axis=3, tiled=True),
        lax.all_gather(w_out.astype(jnp.bfloat16), "seq", axis=1, tiled=True),
        lax.all_gather(w_up.astype(jnp.bfloat16), "seq", axis=1, tiled=True),
        lax.all_gather(w_down.astype(jnp.bfloat16), "seq", axis=0, tiled=True),
    )
    heads_here = weight_out.shape[0]
    out_flat = weight_out.reshape(heads_here * HD, D)
    score_scale = 1.0 / math.sqrt(HD)
    tokens_all = lax.all_gather(block_in, "ffn", axis=0, tiled=True)
    seq_len = tokens_all.shape[0]
    clusters = seq_len // CLUSTER
    projected = jnp.einsum(
        "td,kdhe->tkhe", tokens_all, weight_qkv, preferred_element_type=jnp.float32
    ).astype(jnp.bfloat16)
    cluster_order = cluster_perm[0]
    positions = jnp.broadcast_to(jnp.arange(seq_len, dtype=jnp.int32)[None, :], cluster_order.shape)
    inverse = (
        jnp.zeros_like(cluster_order)
        .at[jnp.arange(heads_here)[:, None], cluster_order]
        .set(positions)
    )
    grouped = jax.vmap(by_rows)(jnp.moveaxis(projected, 2, 0), cluster_order)
    grouped = grouped.reshape(heads_here, clusters, CLUSTER, 3, HD)
    query_blocks = grouped[:, :, :, 0]
    key_blocks = grouped[:, :, :, 1]
    value_blocks = grouped[:, :, :, 2]

    def cluster_scores():
        return (
            jnp.einsum(
                "hcqd,hckd->hcqk", query_blocks, key_blocks, preferred_element_type=jnp.float32
            )
            * score_scale
        )

    scores = cluster_scores()
    peak_score = jnp.max(scores, axis=-1, keepdims=True)
    log_total = peak_score + jnp.log(jnp.sum(jnp.exp(scores - peak_score), axis=-1, keepdims=True))
    attn_probs = jnp.exp(scores - log_total).astype(jnp.bfloat16)
    attended = jnp.einsum(
        "hcqk,hckd->hcqd", attn_probs, value_blocks, preferred_element_type=jnp.float32
    ).astype(jnp.bfloat16)
    restored = jax.vmap(by_rows)(attended.reshape(heads_here, seq_len, HD), inverse)
    heads_tok = jnp.moveaxis(restored, 0, 1).reshape(seq_len, heads_here * HD)
    attn_rows = lax.psum_scatter(
        jnp.dot(heads_tok, out_flat, preferred_element_type=jnp.float32),
        "ffn",
        scatter_dimension=0,
        tiled=True,
    )
    residual = block_in.astype(jnp.float32) + attn_rows
    hidden_rows, normed_one, inv_one = norm_forward(residual, norm_params[0], norm_params[1])
    hidden_low = hidden_rows.astype(jnp.bfloat16)
    hidden_all = lax.all_gather(hidden_low, "ffn", axis=0, tiled=True)
    inner_pre = jnp.dot(hidden_all, weight_up, preferred_element_type=jnp.float32)
    gelu_low = gelu_value(inner_pre).astype(jnp.bfloat16)
    branch = lax.psum_scatter(
        jnp.dot(gelu_low, weight_down, preferred_element_type=jnp.float32).astype(jnp.bfloat16),
        "ffn",
        scatter_dimension=0,
        tiled=True,
    ).astype(jnp.float32)
    output_rows, normed_two, inv_two = norm_forward(
        hidden_rows + branch, norm_params[2], norm_params[3]
    )
    block_out = output_rows.astype(jnp.bfloat16)
    upstream = block_cot.astype(jnp.float32)
    dsum_two, gain_two, bias_two = norm_backward(upstream, normed_two, inv_two, norm_params[2])
    dbranch = dsum_two.astype(jnp.bfloat16)
    dbranch_all = lax.all_gather(dbranch, "ffn", axis=0, tiled=True)
    dgelu_rows = contract(dbranch_all, weight_down, 1, 1)
    dinner = (dgelu_rows * gelu_slope(inner_pre)).astype(jnp.bfloat16)
    grad_up_part = contract(hidden_all, dinner, 0, 0)
    grad_down_part = contract(gelu_low, dbranch_all, 0, 0)
    dhidden_ffn = lax.psum_scatter(
        contract(dinner, weight_up, 1, 1).astype(jnp.bfloat16),
        "ffn",
        scatter_dimension=0,
        tiled=True,
    ).astype(jnp.float32)
    dresidual, gain_one, bias_one = norm_backward(
        dsum_two + dhidden_ffn, normed_one, inv_one, norm_params[0]
    )
    dattn_all = lax.all_gather(dresidual.astype(jnp.bfloat16), "ffn", axis=0, tiled=True)
    grad_out_part = contract(heads_tok, dattn_all, 0, 0).reshape(heads_here, HD, D)
    dheads = contract(dattn_all, out_flat, 1, 1).astype(jnp.bfloat16)
    dattended = jax.vmap(by_rows)(
        jnp.moveaxis(dheads.reshape(seq_len, heads_here, HD), 1, 0), cluster_order
    )
    dattended = dattended.reshape(heads_here, clusters, CLUSTER, HD)
    probs_again = jnp.exp(cluster_scores() - log_total)
    probs_low = probs_again.astype(jnp.bfloat16)
    dprobs = jnp.einsum(
        "hcqd,hckd->hcqk", dattended, value_blocks, preferred_element_type=jnp.float32
    )
    dscores = (
        probs_again * (dprobs - jnp.sum(probs_again * dprobs, axis=-1, keepdims=True))
    ).astype(jnp.bfloat16)
    dquery = (
        jnp.einsum("hcqk,hckd->hcqd", dscores, key_blocks, preferred_element_type=jnp.float32)
        * score_scale
    )
    dkey_blocks = (
        jnp.einsum("hcqk,hcqd->hckd", dscores, query_blocks, preferred_element_type=jnp.float32)
        * score_scale
    )
    dvalue = jnp.einsum("hcqk,hcqd->hckd", probs_low, dattended, preferred_element_type=jnp.float32)
    dgrouped = (
        jnp.stack([dquery, dkey_blocks, dvalue], axis=3)
        .astype(jnp.bfloat16)
        .reshape(heads_here, seq_len, 3, HD)
    )
    dprojected = jnp.moveaxis(jax.vmap(by_rows)(dgrouped, inverse), 0, 2)
    grad_qkv_part = jnp.einsum(
        "td,tkhe->kdhe", tokens_all, dprojected, preferred_element_type=jnp.float32
    )
    input_grad = dresidual + lax.psum_scatter(
        jnp.einsum(
            "tkhe,kdhe->td", dprojected, weight_qkv, preferred_element_type=jnp.float32
        ).astype(jnp.bfloat16),
        "ffn",
        scatter_dimension=0,
        tiled=True,
    ).astype(jnp.float32)
    grad_qkv, grad_out, grad_up, grad_down = (
        lax.psum_scatter(
            grad_qkv_part.astype(jnp.bfloat16), "seq", scatter_dimension=3, tiled=True
        ).astype(jnp.float32),
        lax.psum_scatter(
            grad_out_part.astype(jnp.bfloat16), "seq", scatter_dimension=1, tiled=True
        ).astype(jnp.float32),
        lax.psum_scatter(
            grad_up_part.astype(jnp.bfloat16), "seq", scatter_dimension=1, tiled=True
        ).astype(jnp.float32),
        lax.psum_scatter(
            grad_down_part.astype(jnp.bfloat16), "seq", scatter_dimension=0, tiled=True
        ).astype(jnp.float32),
    )
    norm_part = jnp.stack([gain_one, bias_one, gain_two, bias_two])
    early_half = (
        (cluster_order < seq_len // 2).astype(jnp.float32).reshape(heads_here, clusters, CLUSTER)
    )
    cluster_share = jnp.sum(early_half, axis=2) / CLUSTER
    share_full = lax.dynamic_update_slice(
        jnp.zeros((heads_here * lax.axis_size("ffn"), clusters), jnp.float32),
        cluster_share,
        (lax.axis_index("ffn") * heads_here, 0),
    )
    moment_qkv = 0.5 * mom_qkv + grad_qkv
    moment_out = 0.5 * mom_out + grad_out
    moment_up = 0.5 * mom_up + grad_up
    moment_down = 0.5 * mom_down + grad_down
    gram_q, gram_o, gram_u, gram_d, grad_norm, occupancy = lax.psum(
        (
            gram_qkv(moment_qkv),
            gram_out(moment_out),
            gram_up(moment_up),
            gram_down(moment_down),
            norm_part,
            share_full,
        ),
        ("seq", "ffn"),
    )
    iterates = [moment_qkv, moment_out, moment_up, moment_down]
    gram_list = [gram_q, gram_o, gram_u, gram_d]
    for member in range(4):
        shrink = 1.0 / (jnp.sqrt(jnp.trace(gram_list[member])) + 1e-07)
        iterates[member] = iterates[member] * shrink
        gram_list[member] = gram_list[member] * (shrink * shrink)
    appliers = (apply_qkv, apply_out, apply_up, apply_down)
    for iteration in range(NS_STEPS):
        if iteration > 0:
            gram_list = list(fresh_grams(iterates))
        for member in range(4):
            once = appliers[member](gram_list[member], iterates[member])
            twice = appliers[member](gram_list[member], once)
            iterates[member] = schulz_coeffs[0] * iterates[member] + (
                schulz_coeffs[1] * once + schulz_coeffs[2] * twice
            )
    step_rates = (
        0.5 * math.sqrt(3.0),
        0.5 * math.sqrt(CLUSTER / 3.0),
        0.5 * math.sqrt(FF / D),
        0.5,
    )
    master_qkv = w_qkv - step_rates[0] * iterates[0]
    master_out = w_out - step_rates[1] * iterates[1]
    master_up = w_up - step_rates[2] * iterates[2]
    master_down = w_down - step_rates[3] * iterates[3]
    first_fix = 1.0 - 0.9**ADAM_STEP
    second_fix = 1.0 - 0.999**ADAM_STEP
    first_new = 0.9 * norm_first + 0.1 * grad_norm
    second_new = 0.999 * norm_second + 0.001 * grad_norm * grad_norm
    first_hat = first_new / first_fix
    second_hat = second_new / second_fix
    norm_new = norm_params - 0.5 * (first_hat / (jnp.sqrt(second_hat) + 1e-08) + 0.01 * norm_params)
    return (
        block_out,
        input_grad,
        grad_qkv,
        grad_out,
        grad_up,
        grad_down,
        grad_norm,
        moment_qkv,
        moment_out,
        moment_up,
        moment_down,
        master_qkv,
        master_out,
        master_up,
        master_down,
        first_new,
        second_new,
        norm_new,
        occupancy,
    )


def solution(mesh):
    placed = (
        P(("seq", "ffn"), None),
        P(("seq", "ffn"), None),
        P("seq", "ffn", None),
        P(None, None, "ffn", "seq"),
        P("ffn", "seq", None),
        P(None, ("seq", "ffn")),
        P(("seq", "ffn"), None),
        P(None, None, "ffn", "seq"),
        P("ffn", "seq", None),
        P(None, ("seq", "ffn")),
        P(("seq", "ffn"), None),
        P(),
        P(),
        P(),
    )
    return jax.shard_map(
        on_device,
        mesh=mesh,
        in_specs=placed,
        out_specs=(
            P(("seq", "ffn"), None),
            P(("seq", "ffn"), None),
            P(None, None, "ffn", "seq"),
            P("ffn", "seq", None),
            P(None, ("seq", "ffn")),
            P(("seq", "ffn"), None),
            P(),
            P(None, None, "ffn", "seq"),
            P("ffn", "seq", None),
            P(None, ("seq", "ffn")),
            P(("seq", "ffn"), None),
            P(None, None, "ffn", "seq"),
            P("ffn", "seq", None),
            P(None, ("seq", "ffn")),
            P(("seq", "ffn"), None),
            P(),
            P(),
            P(),
            P(),
        ),
        check_vma=False,
    )
```

profile of v0, /device:TPU:0, one launch (start us, length us, event | category | flops | bytes accessed | tf_op | source)
XLA Modules:
  0.0 2054.3 jit_solution(17826261720105817848)
XLA Ops:
  12.7 45.4 %scatter_custom_fusion = s32[12288]{0:T(1024)S(1)} fusion(s32[12288]{0:T(1024)S(1)} %reshape.189, s32[12288]{0:T(1024)S(1)} %reshape.191, s32[]{:T(128)} %constant.31.clone.1), kind=kCustom, calls=%fused_computation.214 | custom fusion | bytes 49156
  59.0 34.8 %all_gather.26 = bf16[3,64,768]{2,1,0:T(8,128)(2,1)} all-gather(bf16[3,8,768]{2,1,0:T(8,128)(2,1)S(1)} %convert_element_type.120), channel_id=1, replica_groups=mesh['seq'=8,'ffn'=4] {'seq'}, dimensions={1}, use_global_device_ids=true | all-gather | bytes 331776 | tf_op jit(solution)/shard_map/all_gather | solution.py:121
  93.8 31.8 %all_gather.25 = bf16[3,768,3,64]{1,3,2,0:T(8,128)(2,1)S(1)} all-gather(bf16[3,768,3,8]{1,3,2,0:T(8,128)(2,1)S(1)} %convert_element_type.115), channel_id=1, replica_groups=mesh['seq'=8,'ffn'=4] {'seq'}, dimensions={3}, use_global_device_ids=true | all-gather | bytes 995328 | tf_op jit(solution)/shard_map/all_gather | solution.py:120
  125.7 6.2 fusion.235
  134.8 16.9 copy.138
  151.6 106.6 %gather_fusion = bf16[12288,3,64]{2,1,0:T(4,128)(2,1)} fusion(bf16[3,4096,3,64]{3,2,1,0:T(4,128)(2,1)} %copy.138, s32[12288]{0:T(1024)S(1)} %bitcast.302), kind=kCustom, calls=%fused_computation | custom fusion | bytes 9535488 | tf_op jit(solution)/shard_map/vmap()/gather | solution.py:56
  258.2 29.8 %fusion.234 = (bf16[3,32,128,1,64]{4,3,2,1,0:T(2,128)(2,1)}, bf16[3,32,128,1,64]{4,3,2,1,0:T(2,128)(2,1)}, bf16[3,32,128,1,64]{4,3,2,1,0:T(2,128)(2,1)}) fusion(bf16[3,32,128,3,64]{4,3,2,1,0:T(4,128)(2,1)} %bitcast.308), kind=kLoop, calls=%fused_computation.241 | loop fusion | bytes 9437184 | tf_op jit(solution)/shard_map/slice | solution.py:143
  288.0 12.8 copy.203
  300.9 13.2 copy.204
  317.9 12.9 copy.202
  332.0 5.0 convolution_convert_fusion.4
  337.0 3.1 copy.187
  340.1 120.6 %gather_fusion.1 = bf16[12288,64]{1,0:T(8,128)(2,1)} fusion(bf16[3,4096,64]{2,1,0:T(8,128)(2,1)S(1)} %bitcast.305, s32[12288]{0:T(1024)S(1)} %bitcast.300), kind=kCustom, calls=%fused_computation.1 | custom fusion | bytes 3244032 | tf_op jit(solution)/shard_map/vmap()/gather | solution.py:56
  460.7 3.2 copy.146
  463.9 6.4 convolution_bitcast_fusion
  472.0 98.8 %reduce-scatter.13.cloned.1.call-done = f32[1024,768]{1,0:T(8,128)} async-done(((f32[4096,768]{1,0:T(8,128)}), f32[1024,768]{1,0:T(8,128)}) %reduce-scatter.13.cloned.1.call-update) | async-done | bytes 3145744 | tf_op jit(solution)/shard_map/reduce_scatter | solution.py:164
  577.6 44.6 %all-gather.9.cloned.1.call-done = bf16[4096,768]{1,0:T(8,128)(2,1)} async-done(((bf16[1024,768]{1,0:T(8,128)(2,1)}), bf16[4096,768]{1,0:T(8,128)(2,1)}) %all-gather.9.cloned.1.call-update) | async-done | bytes 6291472 | tf_op jit(solution)/shard_map/all_gather | solution.py:173
  622.2 11.9 multiply_convert_fusion
  634.1 32.3 %all-gather.13.cloned.1.call-done = bf16[768,768]{1,0:T(8,128)(2,1)} async-done(((bf16[96,768]{1,0:T(8,128)(2,1)}), bf16[768,768]{1,0:T(8,128)(2,1)}) %all-gather.13.cloned.1.call-update) | async-done | bytes 1179664 | tf_op jit(solution)/shard_map/all_gather | solution.py:123
  666.4 9.2 convolution_convert_fusion.1
  675.6 56.8 %reduce-scatter.15.cloned.1.call-done = bf16[1024,768]{1,0:T(8,128)(2,1)} async-done(((bf16[4096,768]{1,0:T(8,128)(2,1)}), bf16[1024,768]{1,0:T(8,128)(2,1)}) %reduce-scatter.15.cloned.1.call-update) | async-done | bytes 1572880 | tf_op jit(solution)/shard_map/reduce_scatter | solution.py:176
  738.5 3.6 fusion.230
  742.4 46.1 %all-gather.15.cloned.1.call-done = bf16[4096,768]{1,0:T(8,128)(2,1)} async-done(((bf16[1024,768]{1,0:T(8,128)(2,1)}), bf16[4096,768]{1,0:T(8,128)(2,1)}) %all-gather.15.cloned.1.call-update) | async-done | bytes 6291472 | tf_op jit(solution)/shard_map/all_gather | solution.py:189
  788.5 11.6 fusion.5
  802.6 7.0 convolution_convert_fusion
  809.8 58.5 %reduce-scatter.17.cloned.1.call-done = bf16[1024,768]{1,0:T(8,128)(2,1)} async-done(((bf16[4096,768]{1,0:T(8,128)(2,1)}), bf16[1024,768]{1,0:T(8,128)(2,1)}) %reduce-scatter.17.cloned.1.call-update) | async-done | bytes 1572880 | tf_op jit(solution)/shard_map/reduce_scatter | solution.py:194
  868.2 4.1 multiply_reduce_fusion.2
  875.3 9.9 convolution_convert_fusion.5
  885.3 10.2 convolution_convert_fusion.6
  895.7 25.9 %all-gather.17.cloned.1.call-done = bf16[4096,768]{1,0:T(8,128)(2,1)} async-done(((bf16[1024,768]{1,0:T(8,128)(2,1)}), bf16[4096,768]{1,0:T(8,128)(2,1)}) %all-gather.17.cloned.1.call-update) | async-done | bytes 6291472 | tf_op jit(solution)/shard_map/all_gather | solution.py:203
  921.6 6.1 convolution_convert_fusion.2
  930.8 119.4 %gather_fusion.2 = bf16[12288,64]{1,0:T(8,128)(2,1)} fusion(bf16[3,4096,64]{2,1,0:T(8,128)(2,1)S(1)} %bitcast.304, s32[12288]{0:T(1024)S(1)} %bitcast.303), kind=kCustom, calls=%fused_computation.2 | custom fusion | bytes 3244032 | tf_op jit(solution)/shard_map/vmap()/gather | solution.py:56
  1050.2 6.9 multiply_reduce_fusion
  1061.3 3.4 multiply_convert_fusion.2
  1064.7 3.4 convolution_convert_fusion.3
  1073.7 9.2 reshape.220
  1086.0 9.3 reshape.221
  1098.3 9.2 reshape.222
  1107.5 29.1 %pad_maximum_fusion = bf16[3,4096,3,64]{3,2,1,0:T(4,128)(2,1)} fusion(bf16[3,4096,1,64]{3,2,1,0:T(2,128)(2,1)} %reshape.222, bf16[3,4096,1,64]{3,2,1,0:T(2,128)(2,1)} %reshape.221, bf16[3,4096,1,64]{3,2,1,0:T(2,128)(2,1)} %reshape.220), kind=kLoop, calls=%fused_computation.12 | loop fusion | flops 14155776 | bytes 9437184 | tf_op jit(solution)/shard_map/stack | solution.py:228
  1136.6 106.6 %gather_fusion.3 = bf16[12288,3,64]{2,1,0:T(4,128)(2,1)} fusion(bf16[3,4096,3,64]{3,2,1,0:T(4,128)(2,1)} %pad_maximum_fusion, s32[12288]{0:T(1024)S(1)} %bitcast.301), kind=kCustom, calls=%fused_computation.3 | custom fusion | bytes 9535488 | tf_op jit(solution)/shard_map/vmap()/gather | solution.py:56
  1243.3 10.5 fusion.75
  1260.1 3.4 fusion.241
  1263.6 3.4 fusion.236
  1267.0 35.2 %reduce-scatter.27.cloned.1.call-done = bf16[8,2304]{1,0:T(8,128)(2,1)} async-done(((bf16[64,2304]{1,0:T(8,128)(2,1)}), bf16[8,2304]{1,0:T(8,128)(2,1)}) %reduce-scatter.27.cloned.1.call-update) | async-done | bytes 36880
  1303.7 3.5 convolution_bitcast_fusion.6
  1307.2 58.7 %reduce-scatter.25.cloned.1.call-done = bf16[8,6912]{1,0:T(8,128)(2,1)} async-done(((bf16[64,6912]{1,0:T(8,128)(2,1)}), bf16[8,6912]{1,0:T(8,128)(2,1)}) %reduce-scatter.25.cloned.1.call-update) | async-done | bytes 110608
  1367.6 3.5 convolution_bitcast_fusion.3
  1371.3 190.9 %all-reduce.12.cloned.1.call-done = (f32[768,768]{1,0:T(8,128)}, f32[768,768]{1,0:T(8,128)}, f32[768,768]{1,0:T(8,128)}, f32[768,768]{1,0:T(8,128)}) async-done(((f32[768,768]{1,0:T(8,128)}, f32[768,768]{1,0:T(8,128)}, f32[768,768]{1,0:T(8,128)}, f32[768,768]{1,0:T(8,128)}), (f32[768,768]{1,0:T(8,128)}, f32[768,768]{1,0:T(8,128)}, f32[768,768]{1,0:T(8,128)}, ...) | async-done | bytes 9437200 | tf_op jit(solution)/shard_map/psum | solution.py:272
  1568.7 3.5 fusion.242
  1578.5 3.5 fusion.237
  1586.6 3.5 convolution_bitcast_fusion.5
  1596.2 3.5 convolution_bitcast_fusion.2
  1600.8 12.8 bitcast_convert_fusion
  1613.9 187.9 %all-reduce.10.cloned.1.call-done = (f32[768,768]{1,0:T(8,128)}, f32[768,768]{1,0:T(8,128)}, f32[768,768]{1,0:T(8,128)}, f32[768,768]{1,0:T(8,128)}) async-done(((f32[768,768]{1,0:T(8,128)}, f32[768,768]{1,0:T(8,128)}, f32[768,768]{1,0:T(8,128)}, f32[768,768]{1,0:T(8,128)}), (f32[768,768]{1,0:T(8,128)}, f32[768,768]{1,0:T(8,128)}, f32[768,768]{1,0:T(8,128)}, ...) | async-done | bytes 9437200 | tf_op jit(solution)/shard_map/psum | solution.py:92
  1806.0 3.5 convolution_bitcast_fusion.4
  1814.9 3.5 fusion.244
  1823.3 3.5 fusion.239
  1830.0 3.5 convolution_bitcast_fusion.1
  1836.3 42.7 %all-reduce = (f32[4,768]{1,0:T(4,128)}, f32[12,32]{1,0:T(8,128)}) all-reduce(f32[4,768]{1,0:T(4,128)S(1)} %pad_maximum_fusion.1, f32[12,32]{1,0:T(8,128)S(1)} %dynamic_update_slice.3), channel_id=1, replica_groups=mesh['seq'=8,'ffn'=4] {'seq','ffn'}, use_global_device_ids=true, to_apply=%region_24.0 | all-reduce | flops 3456 | bytes 27648 | tf_op jit(solution)/shard_map/psum | solution.py:272
  1880.4 3.4 convert_add_fusion
  1883.8 142.9 %all-reduce.8.cloned.1.call-done = (f32[768,768]{1,0:T(8,128)}, f32[768,768]{1,0:T(8,128)}, f32[768,768]{1,0:T(8,128)}, f32[768,768]{1,0:T(8,128)}) async-done(((f32[768,768]{1,0:T(8,128)}, f32[768,768]{1,0:T(8,128)}, f32[768,768]{1,0:T(8,128)}, f32[768,768]{1,0:T(8,128)}), (f32[768,768]{1,0:T(8,128)}, f32[768,768]{1,0:T(8,128)}, f32[768,768]{1,0:T(8,128)}, ...) | async-done | bytes 9437200 | tf_op jit(solution)/shard_map/psum | solution.py:92
  2026.7 3.3 fusion.245
  2034.6 3.1 fusion.120
  2043.2 3.1 fusion.170
  (258 shorter events, 116.4 us)
Async XLA Ops:
  8.0 117.7 %all-gather.7.cloned.1.call-start = ((), (), s32[]{:S(2)}) async-start(), calls=%async_computation.8 | async-start | bytes 7864320 | tf_op jit(solution)/shard_map/all_gather | solution.py:128
  8.8 562.1 %reduce-scatter.13.cloned.1.call-start = ((), (), s32[]{:S(2)}) async-start(), calls=%async_computation.9 | async-start | bytes 15728640 | tf_op jit(solution)/shard_map/reduce_scatter | solution.py:164
  125.6 6.3 copy-start.46
  125.7 214.4 %copy-start = (s32[3,4096,1]{1,2,0:T(1,128)}, s32[3,4096,1]{1,2,0:T(1,128)S(1)}, u32[]{:S(2)}) copy-start(s32[3,4096,1]{1,2,0:T(1,128)S(1)} %reshape_or_fusion) | copy-start | bytes 147460
  300.9 13.2 copy-start.15
  460.7 3.2 copy-start.43
  463.9 6.4 copy-start.26
  470.3 107.3 %all-gather.11.cloned.1.call-start = ((), (), s32[]{:S(2)}) async-start(), calls=%async_computation.11 | async-start | bytes 1327104 | tf_op jit(solution)/shard_map/all_gather | solution.py:122
  471.9 150.3 %all-gather.9.cloned.1.call-start = ((), (), s32[]{:S(2)}) async-start(), calls=%async_computation.10 | async-start | bytes 7864320 | tf_op jit(solution)/shard_map/all_gather | solution.py:173
  575.8 90.5 %all-gather.13.cloned.1.call-start = ((), (), s32[]{:S(2)}) async-start(), calls=%async_computation.12 | async-start | bytes 1327104 | tf_op jit(solution)/shard_map/all_gather | solution.py:123
  577.6 154.8 %reduce-scatter.15.cloned.1.call-start = ((), (), s32[]{:S(2)}) async-start(), calls=%async_computation.13 | async-start | bytes 7864320 | tf_op jit(solution)/shard_map/reduce_scatter | solution.py:176
  675.6 112.9 %all-gather.15.cloned.1.call-start = ((), (), s32[]{:S(2)}) async-start(), calls=%async_computation.14 | async-start | bytes 7864320 | tf_op jit(solution)/shard_map/all_gather | solution.py:189
  742.1 126.1 %reduce-scatter.17.cloned.1.call-start = ((), (), s32[]{:S(2)}) async-start(), calls=%async_computation.15 | async-start | bytes 7864320 | tf_op jit(solution)/shard_map/reduce_scatter | solution.py:194
  788.5 14.2 copy-start.59
  809.7 111.9 %all-gather.17.cloned.1.call-start = ((), (), s32[]{:S(2)}) async-start(), calls=%async_computation.16 | async-start | bytes 7864320 | tf_op jit(solution)/shard_map/all_gather | solution.py:203
  868.2 4.1 copy-start.3
  868.2 4.1 copy-start.33
  875.3 381.4 %reduce-scatter.23.cloned.1.call-start = ((), (), s32[]{:S(2)}) async-start(), calls=%async_computation.19 | async-start | bytes 1327104 | tf_op jit(solution)/shard_map/reduce_scatter | solution.py:254
  885.2 36.4 %copy-start.44 = (bf16[3,64,768]{2,1,0:T(8,128)(2,1)S(1)}, bf16[3,64,768]{2,1,0:T(8,128)(2,1)}, u32[]{:S(2)}) copy-start(bf16[3,64,768]{2,1,0:T(8,128)(2,1)} %all_gather.26) | copy-start | bytes 884740
  885.2 373.1 %reduce-scatter.21.cloned.1.call-start = ((), (), s32[]{:S(2)}) async-start(), calls=%async_computation.18 | async-start | bytes 1327104 | tf_op jit(solution)/shard_map/reduce_scatter | solution.py:251
  895.5 406.8 %reduce-scatter.27.cloned.1.call-start = ((), (), s32[]{:S(2)}) async-start(), calls=%async_computation.21 | async-start | bytes 331776
  1050.2 6.9 slice-start
  1050.2 6.9 slice-start.1
  1061.3 3.4 copy-start.4
  1061.3 6.9 slice-start.2
  1064.7 3.4 copy-start.27
  1064.7 3.4 slice-start.3
  1107.5 29.1 %copy-start.1 = (s32[3,4096,1]{1,2,0:T(1,128)S(1)}, s32[3,4096,1]{1,2,0:T(1,128)}, u32[]{:S(2)}) copy-start(s32[3,4096,1]{1,2,0:T(1,128)} %copy-done) | copy-start | bytes 147460
  1243.2 122.7 %reduce-scatter.25.cloned.1.call-start = ((), (), s32[]{:S(2)}) async-start(), calls=%async_computation.20 | async-start | bytes 995328
  1253.8 2.9 copy-start.48
  1253.8 4.6 copy-start.49
  1256.4 305.8 %all-reduce.12.cloned.1.call-start = ((), (), s32[]{:S(2)}) async-start(), calls=%async_computation.24 | async-start | bytes 18874368 | tf_op jit(solution)/shard_map/psum | solution.py:272
  1258.3 308.7 %copy-start.30 = (f32[96,768]{1,0:T(8,128)}, f32[96,768]{1,0:T(8,128)S(1)}, u32[]{:S(2)}) copy-start(f32[96,768]{1,0:T(8,128)S(1)} %get-tuple-element.48) | copy-start | bytes 884740
  1260.1 315.9 %copy-start.31 = (f32[768,96]{0,1:T(8,128)}, f32[768,96]{0,1:T(8,128)S(1)}, u32[]{:S(2)}) copy-start(f32[768,96]{0,1:T(8,128)S(1)} %get-tuple-element.50) | copy-start | bytes 884740
  1260.1 42.9 %copy-start.52 = (f32[3,8,768]{2,1,0:T(8,128)S(1)}, f32[3,8,768]{2,1,0:T(8,128)}, u32[]{:S(2)}) copy-start(f32[3,8,768]{2,1,0:T(8,128)} %param.22) | copy-start | bytes 221188
  1263.6 103.3 %copy-start.51 = (f32[3,768,3,8]{1,3,2,0:T(8,128)S(1)}, f32[3,768,3,8]{1,3,2,0:T(8,128)}, u32[]{:S(2)}) copy-start(f32[3,768,3,8]{1,3,2,0:T(8,128)} %param.21) | copy-start | bytes 663556
  1303.7 281.7 %copy-start.39 = (f32[3,8,768]{2,1,0:T(8,128)}, f32[3,8,768]{2,1,0:T(8,128)S(1)}, u32[]{:S(2)}) copy-start(f32[3,8,768]{2,1,0:T(8,128)S(1)} %get-tuple-element.52) | copy-start | bytes 221188
  1367.6 226.3 %copy-start.36 = (f32[3,768,3,8]{1,3,2,0:T(8,128)}, f32[3,768,3,8]{1,3,2,0:T(8,128)S(1)}, u32[]{:S(2)}) copy-start(f32[3,768,3,8]{1,3,2,0:T(8,128)S(1)} %get-tuple-element.54) | copy-start | bytes 663556
  1371.1 430.7 %all-reduce.10.cloned.1.call-start = ((), (), s32[]{:S(2)}) async-start(), calls=%async_computation.23 | async-start | bytes 18874368 | tf_op jit(solution)/shard_map/psum | solution.py:92
  1562.2 3.3 copy-start.10
  1567.2 5.0 copy-start.8
  1576.1 6.0 copy-start.6
  1585.3 4.8 copy-start.5
  1596.1 213.4 %copy-start.37 = (f32[3,768,3,8]{1,3,2,0:T(8,128)}, f32[3,768,3,8]{1,3,2,0:T(8,128)S(1)}, u32[]{:S(2)}) copy-start(f32[3,768,3,8]{1,3,2,0:T(8,128)S(1)} %fusion.164) | copy-start | bytes 663556
  1599.7 280.7 %reduce-scatter.19.cloned.1.call-start = ((), (), s32[]{:S(2)}) async-start(), calls=%async_computation.17 | async-start | bytes 7864320 | tf_op jit(solution)/shard_map/reduce_scatter | solution.py:236
  1613.6 413.0 %all-reduce.8.cloned.1.call-start = ((), (), s32[]{:S(2)}) async-start(), calls=%async_computation.22 | async-start | bytes 18874368 | tf_op jit(solution)/shard_map/psum | solution.py:92
  1801.7 3.0 copy-start.25
  1804.8 4.7 copy-start.22
  1806.0 5.8 copy-start.24
  1813.4 5.0 copy-start.23
  1820.9 6.0 copy-start.38
  1823.3 5.9 copy-start.28
  1833.5 45.6 %copy-start.54 = (f32[4,768]{1,0:T(4,128)S(1)}, f32[4,768]{1,0:T(4,128)}, u32[]{:S(2)}) copy-start(f32[4,768]{1,0:T(4,128)} %param.25) | copy-start | bytes 36868
  1833.5 46.9 %copy-start.17 = (f32[1024,768]{1,0:T(8,128)S(1)}, f32[1024,768]{1,0:T(8,128)}, u32[]{:S(2)}) copy-start(f32[1024,768]{1,0:T(8,128)} %get-tuple-element.57) | copy-start | bytes 9437188
  1883.8 146.2 %copy-start.40 = (f32[96,768]{1,0:T(8,128)S(1)}, f32[96,768]{1,0:T(8,128)}, u32[]{:S(2)}) copy-start(f32[96,768]{1,0:T(8,128)} %param.20) | copy-start | bytes 884740
  2026.7 3.3 copy-start.21
  2026.7 5.6 copy-start.20
  2026.7 5.6 copy-start.29
  2030.0 4.6 copy-start.42
  2032.2 5.5 copy-start.19
  2034.6 4.4 copy-start.50
  2037.7 3.1 copy-start.18
  2037.7 3.1 copy-start.35
  2039.0 4.2 copy-start.45
  (18 other events, 34.7 us)
Sparse Core Ops, SparseCore 0:
  10.4 49.0 all-gather.6
  470.4 100.4 reduce-scatter.12
  809.8 58.3 reduce-scatter.16
  1371.2 190.9 all-reduce.11
  1599.8 201.8 all-reduce.9
  1833.6 192.9 all-reduce.7
Sparse Core Ops, SparseCore 1:
  473.5 42.6 all-gather.10
  575.9 46.2 all-gather.8
  624.8 41.5 all-gather.12
  675.6 56.7 reduce-scatter.14
  742.2 46.2 all-gather.14
  875.3 46.2 all-gather.16
  924.8 64.2 reduce-scatter.22
  992.4 63.2 reduce-scatter.20
  1243.3 58.8 reduce-scatter.26
  1305.6 60.2 reduce-scatter.24
  1613.7 58.6 reduce-scatter.18
where the time goes:
time: 2060 us; the launch traced here: 2050 us
  waiting for transfers between devices  980 us (48%)
  local copies, waits for them, and re-layouts  644 us (31%)
  matrix products  219 us (11%)
  blocking collectives  109 us (5%)
  other arithmetic  80.1 us (4%)
    gather x6, local copies, waits for them, and re-layouts, by_rows(): return lookup[indices]  456 us
    psum x2, waiting for transfers between devices, fresh_grams(): lax.psum((gram_qkv(iterates[0]), gram_out(iterates[1]), gram_up(iterates[...  331 us
    psum x1, waiting for transfers between devices, on_device(): lax.psum((gram_qkv(moment_qkv), gram_out(moment_out), gram_up(moment_up),...  191 us
    reduce_scatter x1, waiting for transfers between devices, on_device(): lax.psum_scatter(jnp.dot(heads_tok, out_flat, preferred_element_type=jnp....  98.8 us
    unnamed x141, local copies, waits for them, and re-layouts  97.8 us
    unnamed x19, waiting for transfers between devices  94.9 us
    reduce_scatter x1, waiting for transfers between devices, on_device(): lax.psum_scatter(contract(dinner, weight_up, 1, 1).astype(jnp.bfloat16),...  58.5 us
    reduce_scatter x1, waiting for transfers between devices, on_device(): lax.psum_scatter(jnp.dot(gelu_low, weight_down, preferred_element_type=jn...  56.8 us
  transfers between devices with their start and end apart: 17, of which 12 were waited for; matrix products, arithmetic and copies ran while one was open for 24% of the time, Pallas kernels for 0%

commit v1 on v0

v1 whole, which is shorter than its diff:
```python
import math

import jax
import jax.numpy as jnp
from jax import lax
from jax.experimental import pallas as pl
from jax.experimental.pallas import tpu as pltpu
from jax.sharding import PartitionSpec as P

D = 768
HD = 64
FF = 3072
CLUSTER = 128
NS_STEPS = 3
ADAM_STEP = 10

schulz_coeffs = (3.4445, -4.775, 2.0315)
norm_epsilon = 1e-05
low = jnp.bfloat16
full = jnp.float32
LANES = 128
GROUP = 8
UNROLL = 32
score_scale = 1.0 / math.sqrt(HD)


def contract(left, right, left_axis, right_axis):
    return lax.dot_general(
        left, right, (((left_axis,), (right_axis,)), ((), ())), preferred_element_type=full
    )


def swap(value, axis, bit):
    size = lax.axis_size(axis)
    return lax.ppermute(value, axis, [(place, place ^ bit) for place in range(size)])


def seq_bits():
    bits = []
    bit = lax.axis_size("seq") // 2
    while bit >= 1:
        bits.append(bit)
        bit //= 2
    return bits


def seq_stages():
    return [("seq", bit) for bit in seq_bits()]


def all_stages():
    far = [("seq", bit) for bit in seq_bits() if bit > 1]
    return far + [("ffn", 2), ("seq", 1), ("ffn", 1)]


def spread(shard, stages):
    for axis, bit in stages:
        shard = jnp.concatenate([shard, swap(shard, axis, bit)], axis=0)
    return shard


def fold(partial, stages):
    for axis, bit in reversed(stages):
        half = partial.shape[0] // 2
        kept = partial[:half]
        other = swap(partial[half:].astype(low), axis, bit)
        partial = kept.astype(full) + other.astype(full)
    return partial


def total(value, stages):
    for axis, bit in stages:
        value = value + swap(value, axis, bit)
    return value


def total_halves(value, stages):
    sides = [(lax.axis_index(axis) & bit) != 0 for axis, bit in stages]
    for (axis, bit), side in reversed(list(zip(stages, sides))):
        half = value.shape[0] // 2
        kept = jnp.where(side, value[half:], value[:half])
        sent = jnp.where(side, value[:half], value[half:]).astype(low)
        value = kept.astype(full) + swap(sent, axis, bit).astype(full)
    value = value.astype(low)
    for (axis, bit), side in zip(stages, sides):
        other = swap(value, axis, bit)
        value = jnp.concatenate([jnp.where(side, other, value), jnp.where(side, value, other)], axis=0)
    return value.astype(full)


def move_rows(perm_ref, base, count, move):
    def step(turn, carry):
        for inner in range(UNROLL):
            row = turn * UNROLL + inner
            move(perm_ref[0, 0, base + row], row)
        return carry

    lax.fori_loop(0, count // UNROLL, step, 0)


def softmax_rows(scores):
    peak = jnp.max(scores, axis=1, keepdims=True)
    powers = jnp.exp((scores - peak) * score_scale)
    return powers * (1.0 / jnp.sum(powers, axis=1, keepdims=True))


def left_half(rows):
    return lax.broadcasted_iota(jnp.int32, (rows, LANES), 1) < HD


def attend_kernel(
    perm_ref, x0, x1, x2, x3, w_ref, out_ref, qv_ref, key_ref, qv_rows, key_rows, qv_got, key_got, o_got, o_rows
):
    head = pl.program_id(0)
    here = x0.shape[0]
    seq_len = 4 * here
    half = here // 2
    for block, x_ref in enumerate((x0, x1, x2, x3)):
        for cut in range(2):
            both = contract(x_ref[pl.ds(cut * half, half), :], w_ref[...], 1, 1)
            rows = pl.ds(block * here + cut * half, half)
            qv_rows[rows, :] = both[:, :LANES]
            key_rows[rows, :] = both[:, LANES:]
    count = GROUP * CLUSTER

    def group(turn, carry):
        base = turn * count

        def fetch(index, row):
            qv_got[pl.ds(row, 1), :] = qv_rows[pl.ds(index, 1), :]
            key_got[pl.ds(row, 1), :] = key_rows[pl.ds(index, 1), :]

        move_rows(perm_ref, base, count, fetch)
        spans = [slice(part * CLUSTER, (part + 1) * CLUSTER) for part in range(GROUP)]
        qvs = [qv_got[span].astype(low) for span in spans]
        keys = [key_got[span].astype(low) for span in spans]
        for part in range(GROUP):
            rows = pl.ds(base + part * CLUSTER, CLUSTER)
            qv_ref[0, rows, :] = qvs[part]
            key_ref[0, rows, :] = keys[part]
        scores = [contract(qv, key, 1, 1) for qv, key in zip(qvs, keys)]
        probs = [softmax_rows(score).astype(low) for score in scores]
        for part in range(GROUP):
            o_got[spans[part]] = contract(probs[part], qvs[part], 1, 0)

        def place(index, row):
            o_rows[pl.ds(index, 1), :] = o_got[pl.ds(row, 1), :]

        move_rows(perm_ref, base, count, place)
        return carry

    lax.fori_loop(0, seq_len // count, group, 0)

    @pl.when(head == 0)
    def _():
        for block in range(4):
            out_ref[block, pl.ds(0, here), :] = o_rows[pl.ds(block * here, here), :].astype(low)

    @pl.when(head == 1)
    def _():
        for block in range(4):
            turned = pltpu.roll(o_rows[pl.ds(block * here, here), :], HD, 1).astype(low)
            before = out_ref[block, pl.ds(0, here), :]
            out_ref[block, pl.ds(0, here), :] = jnp.where(left_half(here), turned, before)

    @pl.when(head == 2)
    def _():
        for block in range(4):
            top = pltpu.roll(o_rows[pl.ds(block * here, half), :], HD, 1)
            bottom = o_rows[pl.ds(block * here + half, half), :]
            out_ref[block, pl.ds(here, half), :] = jnp.where(left_half(half), top, bottom).astype(low)


def attend(perm, tokens, weights):
    heads, seq_len = perm.shape
    here = tokens[0].shape[0]
    whole = pl.BlockSpec((here, D), lambda head: (0, 0), pipeline_mode=pl.Buffered(1))
    per_head = pl.BlockSpec((1, seq_len, LANES), lambda head: (head, 0, 0))
    return pl.pallas_call(
        attend_kernel,
        grid=(heads,),
        in_specs=[
            pl.BlockSpec((1, 1, seq_len), lambda head: (head, 0, 0), memory_space=pltpu.SMEM),
            whole,
            whole,
            whole,
            whole,
            pl.BlockSpec((2 * LANES, D), lambda head: (head, 0)),
        ],
        out_specs=[
            pl.BlockSpec((4, here + here // 2, LANES), lambda head: (0, 0, 0), pipeline_mode=pl.Buffered(1)),
            per_head,
            per_head,
        ],
        out_shape=[
            jax.ShapeDtypeStruct((4, here + here // 2, LANES), low),
            jax.ShapeDtypeStruct((heads, seq_len, LANES), low),
            jax.ShapeDtypeStruct((heads, seq_len, LANES), low),
        ],
        scratch_shapes=[
            pltpu.VMEM((seq_len, LANES), full),
            pltpu.VMEM((seq_len, LANES), full),
            pltpu.VMEM((GROUP * CLUSTER, LANES), full),
            pltpu.VMEM((GROUP * CLUSTER, LANES), full),
            pltpu.VMEM((GROUP * CLUSTER, LANES), full),
            pltpu.VMEM((seq_len, LANES), full),
        ],
        compiler_params=pltpu.CompilerParams(vmem_limit_bytes=52 * 2**20),
        cost_estimate=pl.CostEstimate(
            flops=2 * heads * seq_len * (2 * LANES * D + 2 * LANES * LANES),
            bytes_accessed=30 * 2**20,
            transcendentals=heads * seq_len * CLUSTER,
        ),
        name="attend",
    )(perm.reshape(heads, 1, seq_len), *tokens, weights)


def attend_back_kernel(
    perm_ref, qv_ref, key_ref, do_ref, x0, x1, x2, x3, w_ref, gw_ref, gx_ref, d_rows, d_got, dqv_got, dkey_got, dqv_rows, dkey_rows, gx_sum
):
    head = pl.program_id(0)
    here = x0.shape[0]
    seq_len = 4 * here
    half = here // 2

    @pl.when(head == 0)
    def _():
        for block in range(4):
            rows = do_ref[block, pl.ds(0, here), :].astype(full)
            d_rows[pl.ds(block * here, here), :] = jnp.where(left_half(here), 0.0, rows)

    @pl.when(head == 1)
    def _():
        for block in range(4):
            rows = pltpu.roll(do_ref[block, pl.ds(0, here), :].astype(full), HD, 1)
            d_rows[pl.ds(block * here, here), :] = jnp.where(left_half(here), 0.0, rows)

    @pl.when(head == 2)
    def _():
        for block in range(4):
            rows = do_ref[block, pl.ds(here, half), :].astype(full)
            top = pltpu.roll(rows, HD, 1)
            d_rows[pl.ds(block * here, half), :] = jnp.where(left_half(half), 0.0, top)
            d_rows[pl.ds(block * here + half, half), :] = jnp.where(left_half(half), 0.0, rows)

    count = GROUP * CLUSTER

    def group(turn, carry):
        base = turn * count

        def fetch(index, row):
            d_got[pl.ds(row, 1), :] = d_rows[pl.ds(index, 1), :]

        move_rows(perm_ref, base, count, fetch)
        spans = [slice(part * CLUSTER, (part + 1) * CLUSTER) for part in range(GROUP)]
        rows = [pl.ds(base + part * CLUSTER, CLUSTER) for part in range(GROUP)]
        qvs = [qv_ref[0, span, :] for span in rows]
        keys = [key_ref[0, span, :] for span in rows]
        dos = [d_got[span].astype(low) for span in spans]
        scores = [contract(qv, key, 1, 1) for qv, key in zip(qvs, keys)]
        dprobs = [contract(do, qv, 1, 1) for do, qv in zip(dos, qvs)]
        probs = [softmax_rows(score) for score in scores]
        probs_low = [prob.astype(low) for prob in probs]
        dscores = [
            (prob * (dprob - jnp.sum(prob * dprob, axis=1, keepdims=True))).astype(low)
            for prob, dprob in zip(probs, dprobs)
        ]
        for part in range(GROUP):
            dqv_got[spans[part]] = score_scale * contract(dscores[part], keys[part], 1, 0) + contract(
                probs_low[part], dos[part], 0, 0
            )
            dkey_got[spans[part]] = score_scale * contract(dscores[part], qvs[part], 0, 0)

        def place(index, row):
            dqv_rows[pl.ds(index, 1), :] = dqv_got[pl.ds(row, 1), :]
            dkey_rows[pl.ds(index, 1), :] = dkey_got[pl.ds(row, 1), :]

        move_rows(perm_ref, base, count, place)
        return carry

    lax.fori_loop(0, seq_len // count, group, 0)

    gw = jnp.zeros((2 * LANES, D), full)
    for block, x_ref in enumerate((x0, x1, x2, x3)):
        slot = (0, 2, 1, 3)[block]
        rows = pl.ds(block * here, here)
        dboth = jnp.concatenate([dqv_rows[rows, :].astype(low), dkey_rows[rows, :].astype(low)], axis=1)
        gw = gw + contract(dboth, x_ref[...], 0, 0)
        for cut in range(4):
            part = here // 4
            piece = contract(dboth[cut * part : (cut + 1) * part], w_ref[...], 1, 0)
            at = pl.ds(cut * part, part)

            @pl.when(head == 0)
            def _():
                gx_sum[slot, at, :] = piece

            @pl.when(head == 1)
            def _():
                gx_sum[slot, at, :] += piece

            @pl.when(head == 2)
            def _():
                gx_ref[slot, at, :] = (gx_sum[slot, at, :] + piece).astype(low)

    gw_ref[...] = gw.astype(low)


def attend_back(perm, qv, key, do, tokens, weights):
    heads, seq_len = perm.shape
    here = tokens[0].shape[0]
    whole = pl.BlockSpec((here, D), lambda head: (0, 0), pipeline_mode=pl.Buffered(1))
    per_head = pl.BlockSpec((1, seq_len, LANES), lambda head: (head, 0, 0))
    rows_got = pltpu.VMEM((GROUP * CLUSTER, LANES), full)
    rows_all = pltpu.VMEM((seq_len, LANES), full)
    return pl.pallas_call(
        attend_back_kernel,
        grid=(heads,),
        in_specs=[
            pl.BlockSpec((1, 1, seq_len), lambda head: (head, 0, 0), memory_space=pltpu.SMEM),
            per_head,
            per_head,
            pl.BlockSpec((4, here + here // 2, LANES), lambda head: (0, 0, 0), pipeline_mode=pl.Buffered(1)),
            whole,
            whole,
            whole,
            whole,
            pl.BlockSpec((2 * LANES, D), lambda head: (head, 0)),
        ],
        out_specs=[
            pl.BlockSpec((2 * LANES, D), lambda head: (head, 0)),
            pl.BlockSpec((4, here, D), lambda head: (0, 0, 0), pipeline_mode=pl.Buffered(1)),
        ],
        out_shape=[
            jax.ShapeDtypeStruct((heads * 2 * LANES, D), low),
            jax.ShapeDtypeStruct((4, here, D), low),
        ],
        scratch_shapes=[rows_all, rows_got, rows_got, rows_got, rows_all, rows_all, pltpu.VMEM((4, here, D), full)],
        compiler_params=pltpu.CompilerParams(vmem_limit_bytes=60 * 2**20),
        cost_estimate=pl.CostEstimate(
            flops=2 * heads * seq_len * (4 * LANES * D + 5 * LANES * LANES),
            bytes_accessed=30 * 2**20,
            transcendentals=heads * seq_len * CLUSTER,
        ),
        name="attend_back",
    )(perm.reshape(heads, 1, seq_len), qv, key, do, *tokens, weights)


def norm_forward(inputs, gains, biases):
    center = inputs - jnp.mean(inputs, axis=-1, keepdims=True)
    spread_of = jnp.mean(center * center, axis=-1, keepdims=True)
    inv_std = lax.rsqrt(spread_of + norm_epsilon)
    normed = center * inv_std
    return (normed * gains + biases, normed, inv_std)


def norm_backward(upstream, normed, inv_std, gains):
    scaled = upstream * gains
    inside = (
        scaled
        - jnp.mean(scaled, axis=-1, keepdims=True)
        - normed * jnp.mean(scaled * normed, axis=-1, keepdims=True)
    )
    return (inside * inv_std, jnp.sum(upstream * normed, axis=0), jnp.sum(upstream, axis=0))


def gelu_value(preact):
    return preact * 0.5 * (1.0 + jax.scipy.special.erf(preact * 0.7071067811865476))


def gelu_slope(preact):
    cumulative = 0.5 * (1.0 + jax.scipy.special.erf(preact * 0.7071067811865476))
    density = jnp.exp(-0.5 * preact * preact) * 0.3989422804014327
    return cumulative + preact * density


def rows_qkv(value):
    kinds, depth, heads, cut = value.shape
    return value.transpose(0, 2, 3, 1).reshape(kinds * heads * cut, depth)


def unrows_qkv(rows, shape):
    kinds, depth, heads, cut = shape
    return rows.reshape(kinds, heads, cut, depth).transpose(0, 3, 1, 2)


def on_device(
    block_in,
    block_cot,
    cluster_perm,
    w_qkv,
    w_out,
    w_up,
    w_down,
    mom_qkv,
    mom_out,
    mom_up,
    mom_down,
    norm_params,
    norm_first,
    norm_second,
):
    ffn_here = lax.axis_index("ffn")
    seqs = lax.axis_size("seq")
    n_bits = len(seq_bits())
    here = block_in.shape[0]
    half = here // 2
    heads = w_out.shape[0]
    cut = w_out.shape[1]
    seq_len = cluster_perm.shape[2]
    clusters = seq_len // CLUSTER

    weights = [rows_qkv(w_qkv), w_out.reshape(heads * cut, D), w_up.T, w_down]
    momenta = [rows_qkv(mom_qkv), mom_out.reshape(heads * cut, D), mom_up.T, mom_down]

    tokens = [block_in, swap(block_in, "ffn", 1), swap(block_in, "ffn", 2)]
    tokens.append(swap(tokens[2], "ffn", 1))
    wide_qkv = spread(weights[0].astype(low), seq_stages())
    wide_qkv = wide_qkv.reshape(seqs, 3, heads, cut, D).transpose(1, 2, 0, 3, 4).reshape(3, heads, HD, D)
    head_rows = jnp.stack(
        [wide_qkv[0], wide_qkv[2], wide_qkv[1], jnp.zeros_like(wide_qkv[1])], axis=1
    ).reshape(heads * 2 * LANES, D)

    stages = all_stages()
    up_rows = spread(weights[2].astype(low), stages)
    down_rows = spread(weights[3].astype(low), stages)
    out_wide = spread(weights[1].astype(low), stages)

    digits = (2, 2, 2) + (2,) * (n_bits - 1)
    order = (2, 0, 2 + n_bits, 1) + tuple(range(3, 2 + n_bits)) + (3 + n_bits, 4 + n_bits)
    back = tuple(sorted(range(len(order)), key=lambda at: order[at]))
    sizes = digits + (heads, cut, D)
    out_rows = out_wide.reshape(sizes).transpose(order).reshape(4 * heads * HD, D)

    perm = jnp.bitwise_xor(cluster_perm[0], ffn_here * here)
    o_blocks, kept_qv, kept_key = attend(perm, tokens, head_rows)
    got = [o_blocks[0]] + [swap(o_blocks[turn], "ffn", turn) for turn in (1, 2, 3)]
    pieces = []
    for block in got:
        third = jnp.concatenate([block[here:, :HD], block[here:, HD:]], axis=0)
        pieces += [block[:here, HD:], block[:here, :HD], third]
    o_rows = jnp.concatenate(pieces, axis=1)

    residual = block_in.astype(full) + contract(o_rows, out_rows, 1, 0)
    hidden, normed_one, inv_one = norm_forward(residual, norm_params[0], norm_params[1])
    hidden_low = hidden.astype(low)
    inner_pre = contract(hidden_low, up_rows, 1, 1)
    gelu_low = gelu_value(inner_pre).astype(low)
    branch = contract(gelu_low, down_rows, 1, 0)
    output_rows, normed_two, inv_two = norm_forward(hidden + branch, norm_params[2], norm_params[3])
    block_out = output_rows.astype(low)
    upstream = block_cot.astype(full)
    dsum_two, gain_two, bias_two = norm_backward(upstream, normed_two, inv_two, norm_params[2])
    dbranch = dsum_two.astype(low)
    dinner = (contract(dbranch, down_rows, 1, 1) * gelu_slope(inner_pre)).astype(low)
    dhidden = dsum_two + contract(dinner, up_rows, 1, 0)
    dresidual, gain_one, bias_one = norm_backward(dhidden, normed_one, inv_one, norm_params[0])
    dattn = dresidual.astype(low)
    do_rows = contract(dattn, out_rows, 1, 1).astype(low)
    do_blocks = []
    for block in range(4):
        part = do_rows[:, block * heads * HD : (block + 1) * heads * HD]
        pair = jnp.concatenate([part[:, HD : 2 * HD], part[:, :HD]], axis=1)
        third = jnp.concatenate([part[:half, 2 * HD :], part[half:, 2 * HD :]], axis=1)
        do_blocks.append(jnp.concatenate([pair, third], axis=0))
    do_got = jnp.stack([do_blocks[0]] + [swap(do_blocks[turn], "ffn", turn) for turn in (1, 2, 3)])

    part_down = contract(gelu_low, dbranch, 0, 0).astype(low)
    part_up = contract(dinner, hidden_low, 0, 0).astype(low)
    part_out = contract(o_rows, dattn, 0, 0).astype(low)
    part_out = part_out.reshape(tuple(sizes[at] for at in order)).transpose(back)
    part_out = part_out.reshape(4 * heads * HD, D)
    grad_down = fold(part_down, stages)
    grad_up = fold(part_up, stages)
    grad_out = fold(part_out, stages)

    part_qkv, gx_blocks = attend_back(perm, kept_qv, kept_key, do_got, tokens, head_rows)
    part_qkv = part_qkv.reshape(heads, 4, HD, D)
    part_qkv = jnp.stack([part_qkv[:, 0], part_qkv[:, 2], part_qkv[:, 1]])
    part_qkv = part_qkv.reshape(3, heads, seqs, cut, D).transpose(2, 0, 1, 3, 4)
    grad_qkv = fold(part_qkv.reshape(seqs * 3 * heads * cut, D), seq_stages())
    gx = fold(gx_blocks.reshape(4 * here, D), [("ffn", 2), ("ffn", 1)])
    input_grad = dresidual + gx

    early_half = (cluster_perm[0] < seq_len // 2).astype(full).reshape(heads, clusters, CLUSTER)
    share = lax.dynamic_update_slice(
        jnp.zeros((4 * heads, clusters), full), jnp.sum(early_half, axis=2) / CLUSTER, (ffn_here * heads, 0)
    ).reshape(1, 4 * heads * clusters)
    small = jnp.concatenate(
        [jnp.stack([gain_one, bias_one, gain_two, bias_two]), jnp.pad(share, ((0, 0), (0, D - share.shape[1])))]
    )
    small = total(small, seq_stages() + [("ffn", 2), ("ffn", 1)])
    grad_norm = small[:4]
    occupancy = small[4, : 4 * heads * clusters].reshape(4 * heads, clusters)

    grads = [grad_qkv, grad_out, grad_up, grad_down]
    moments = [0.5 * mom + grad for mom, grad in zip(momenta, grads)]
    most = max(moment.shape[0] for moment in moments)
    stack = jnp.stack(
        [jnp.pad(moment.astype(low), ((0, most - moment.shape[0]), (0, 0))) for moment in moments]
    )

    def pick(turn):
        return lax.dynamic_index_in_dim(stack, jnp.bitwise_xor(ffn_here, turn), keepdims=False)

    matrix = jnp.concatenate([pick(0)] + [swap(pick(turn), "ffn", turn) for turn in (1, 2, 3)], axis=0)
    gram = total_halves(contract(matrix, matrix, 0, 0), seq_stages())
    diag = jnp.where(jnp.eye(D, dtype=bool), gram, 0.0)
    shrink = 1.0 / (jnp.sqrt(jnp.sum(diag)) + 1e-07)
    gram = gram * (shrink * shrink)
    iterate = matrix.astype(full) * shrink
    one, two, three = schulz_coeffs
    for step in range(NS_STEPS):
        gram_low = gram.astype(low)
        mixing = two * gram + three * contract(gram_low, gram_low, 1, 0)
        mixing_low = mixing.astype(low)
        iterate = one * iterate + contract(iterate.astype(low), mixing_low, 1, 0)
        if step < NS_STEPS - 1:
            once = contract(mixing_low, gram_low, 1, 0)
            gram = one * one * gram + 2.0 * one * once + contract(once.astype(low), mixing_low, 1, 0)
    steps = iterate.astype(low).reshape(4, most, D)
    home = jnp.stack([steps[0]] + [swap(steps[turn], "ffn", turn) for turn in (1, 2, 3)])
    step_rates = (
        0.5 * math.sqrt(3.0),
        0.5 * math.sqrt(CLUSTER / 3.0),
        0.5 * math.sqrt(FF / D),
        0.5,
    )
    masters = []
    for member in range(4):
        own = lax.dynamic_index_in_dim(home, jnp.bitwise_xor(ffn_here, member), keepdims=False)
        own = own[: moments[member].shape[0]].astype(full)
        masters.append(weights[member] - step_rates[member] * own)

    first_fix = 1.0 - 0.9**ADAM_STEP
    second_fix = 1.0 - 0.999**ADAM_STEP
    first_new = 0.9 * norm_first + 0.1 * grad_norm
    second_new = 0.999 * norm_second + 0.001 * grad_norm * grad_norm
    first_hat = first_new / first_fix
    second_hat = second_new / second_fix
    norm_new = norm_params - 0.5 * (first_hat / (jnp.sqrt(second_hat) + 1e-08) + 0.01 * norm_params)

    def shaped(four):
        return (unrows_qkv(four[0], w_qkv.shape), four[1].reshape(w_out.shape), four[2].T, four[3])

    return (
        (block_out, input_grad)
        + shaped(grads)
        + (grad_norm,)
        + shaped(moments)
        + shaped(masters)
        + (first_new, second_new, norm_new, occupancy)
    )


def solution(mesh):
    rows = P(("seq", "ffn"), None)
    placed = (
        rows,
        rows,
        P("seq", "ffn", None),
        P(None, None, "ffn", "seq"),
        P("ffn", "seq", None),
        P(None, ("seq", "ffn")),
        rows,
        P(None, None, "ffn", "seq"),
        P("ffn", "seq", None),
        P(None, ("seq", "ffn")),
        rows,
        P(),
        P(),
        P(),
    )
    four = placed[3:7]
    return jax.shard_map(
        on_device,
        mesh=mesh,
        in_specs=placed,
        out_specs=(rows, rows) + four + (P(),) + four + four + (P(), P(), P(), P()),
        check_vma=False,
    )
```

time: 2060 us -> 644 us (0.31)
  waiting for transfers between devices: 980 us -> 240 us
  local copies, waits for them, and re-layouts: 644 us -> 65.2 us
  matrix products: 219 us -> 76.3 us
  Pallas kernels: 0 us -> 130 us
  blocking collectives: 109 us -> 0 us
  starting transfers between devices: 2.08 us -> 60 us
    psum x3 -> x0, waiting for transfers between devices: 522 us -> none  [the longest x2 331 us: fresh_grams(): lax.psum((gram_qkv(iterates[0]), gram_out(iterates[1]), gram_up(iterates[...]
    gather x6 -> x0, local copies, waits for them, and re-layouts: 456 us -> none  [by_rows(): return lookup[indices]]
    ppermute x0 -> x64, waiting for transfers between devices: none -> 240 us  [swap(): lax.ppermute(value, axis, [(place, place ^ bit) for place in range(size)])]
    reduce_scatter x6 -> x0, waiting for transfers between devices: 214 us -> none  [the longest x1 98.8 us: on_device(): lax.psum_scatter(jnp.dot(heads_tok, out_flat, preferred_element_type=jnp....]
    dot_general x47 -> x0, matrix products: 167 us -> none  [the longest x6 15.3 us: apply_up(): return jnp.dot(mixing, matrix, precision=highest)]
    all_gather x6 -> x0, waiting for transfers between devices: 149 us -> none  [the longest x1 46.1 us: on_device(): dbranch_all = lax.all_gather(dbranch, 'ffn', axis=0, tiled=True)]
    pallas_call x0 -> x2, Pallas kernels: none -> 130 us  [the longest x1 78 us: attend_back(): pl.pallas_call(attend_back_kernel, grid=(heads,), in_specs=[pl.BlockSpec(...]
    unnamed x19 -> x0, waiting for transfers between devices: 94.9 us -> none
  transfers between devices with their start and end apart: 17 -> 64, of which waited for: 12 -> 32; matrix products, arithmetic and copies ran while one was open for 24% -> 19% of each run, Pallas kernels for 0% -> 20%
where the time goes in v1:
time: 644 us; the launch traced here: 635 us
  waiting for transfers between devices  240 us (37%)
  Pallas kernels  130 us (20%)
  matrix products  76.3 us (12%)
  local copies, waits for them, and re-layouts  65.2 us (10%)
  other arithmetic  60.8 us (9%)
  starting transfers between devices  60 us (9%)
    ppermute x64, waiting for transfers between devices, swap(): lax.ppermute(value, axis, [(place, place ^ bit) for place in range(size)])  240 us
    pallas_call x1, Pallas kernels, attend_back(): pl.pallas_call(attend_back_kernel, grid=(heads,), in_specs=[pl.BlockSpec(...  78 us
    dot_general x19, matrix products, contract(): lax.dot_general(left, right, (((left_axis,), (right_axis,)), ((), ())), p...  76.3 us
    ppermute x64, starting transfers between devices, swap(): lax.ppermute(value, axis, [(place, place ^ bit) for place in range(size)])  60 us
    pallas_call x1, Pallas kernels, attend(): pl.pallas_call(attend_kernel, grid=(heads,), in_specs=[pl.BlockSpec((1, 1...  51.6 us
    unnamed x126, local copies, waits for them, and re-layouts  27.2 us
  transfers between devices with their start and end apart: 64, of which 32 were waited for; matrix products, arithmetic and copies ran while one was open for 19% of the time, Pallas kernels for 20%

profile of v1, /device:TPU:0, one launch (start us, length us, event | category | flops | bytes accessed | tf_op | source)
XLA Modules:
  0.0 635.1 jit_solution(15307966209699481081)
XLA Ops:
  2.5 4.0 collective-permute-start.19
  9.0 3.0 collective-permute-start.3
  35.8 14.8 %collective-permute-done.11 = bf16[96,768]{1,0:T(8,128)(2,1)S(1)} collective-permute-done((bf16[96,768]{1,0:T(8,128)(2,1)S(1)}, bf16[96,768]{1,0:T(8,128)(2,1)S(1)}, u32[]{:S(2)}, u32[]{:S(2)}) %collective-permute-start.11) | collective-permute-done | bytes 147488 | tf_op jit(solution)/shard_map/ppermute | solution.py:35
  58.6 2.3 collective-permute-done.12
  60.9 8.4 %collective-permute-done.21 = bf16[384,768]{1,0:T(8,128)(2,1)S(1)} collective-permute-done((bf16[384,768]{1,0:T(8,128)(2,1)S(1)}, bf16[384,768]{1,0:T(8,128)(2,1)S(1)}, u32[]{:S(2)}, u32[]{:S(2)}) %collective-permute-start.21) | collective-permute-done | bytes 589856 | tf_op jit(solution)/shard_map/ppermute | solution.py:35
  70.0 8.9 %collective-permute-done.16 = bf16[384,768]{1,0:T(8,128)(2,1)S(1)} collective-permute-done((bf16[384,768]{1,0:T(8,128)(2,1)S(1)}, bf16[384,768]{1,0:T(8,128)(2,1)S(1)}, u32[]{:S(2)}, u32[]{:S(2)}) %collective-permute-start.16) | collective-permute-done | bytes 589856 | tf_op jit(solution)/shard_map/ppermute | solution.py:35
  85.9 21.9 %collective-permute-done.22 = bf16[768,768]{1,0:T(8,128)(2,1)S(1)} collective-permute-done((bf16[768,768]{1,0:T(8,128)(2,1)S(1)}, bf16[768,768]{1,0:T(8,128)(2,1)S(1)}, u32[]{:S(2)}, u32[]{:S(2)}) %collective-permute-start.22) | collective-permute-done | bytes 1179680 | tf_op jit(solution)/shard_map/ppermute | solution.py:35
  109.4 19.6 %collective-permute-done.17 = bf16[768,768]{1,0:T(8,128)(2,1)S(1)} collective-permute-done((bf16[768,768]{1,0:T(8,128)(2,1)S(1)}, bf16[768,768]{1,0:T(8,128)(2,1)S(1)}, u32[]{:S(2)}, u32[]{:S(2)}) %collective-permute-start.17) | collective-permute-done | bytes 1179680 | tf_op jit(solution)/shard_map/ppermute | solution.py:35
  132.9 51.6 %attend.1 = (bf16[4,1536,128]{2,1,0:T(8,128)(2,1)}, bf16[3,4096,128]{2,1,0:T(8,128)(2,1)}, bf16[3,4096,128]{2,1,0:T(8,128)(2,1)}) custom-call(s32[3,1,4096]{2,1,0:T(1,128)S(1)} %xor_bitcast_fusion.perm_ref, bf16[1024,768]{1,0:T(8,128)(2,1)} %x0.3, bf16[1024,768]{1,0:T(8,128)(2,1)} %copy-done.36, bf16[1024,768]{1,0:T(8,128)(2,1)} %collective-permute-done.1.x2, ...), custom_call_target="tpu_custom_call" | custom-call | flops 5637144576 | bytes 31457280 | tf_op jit(solution)/shard_map/attend/pallas_call | solution.py:179
  189.2 7.9 %collective-permute-done.8 = bf16[1536,128]{1,0:T(8,128)(2,1)S(1)} collective-permute-done((bf16[1536,128]{1,0:T(8,128)(2,1)S(1)}, bf16[1536,128]{1,0:T(8,128)(2,1)S(1)}, u32[]{:S(2)}, u32[]{:S(2)}) %collective-permute-start.8) | collective-permute-done | bytes 393248 | tf_op jit(solution)/shard_map/ppermute | solution.py:35
  197.3 8.6 %collective-permute-done.7 = bf16[1536,128]{1,0:T(8,128)(2,1)S(1)} collective-permute-done((bf16[1536,128]{1,0:T(8,128)(2,1)S(1)}, bf16[1536,128]{1,0:T(8,128)(2,1)S(1)}, u32[]{:S(2)}, u32[]{:S(2)}) %collective-permute-start.7) | collective-permute-done | bytes 393248 | tf_op jit(solution)/shard_map/ppermute | solution.py:35
  209.1 4.9 concatenate.142
  214.0 3.4 fusion.81
  217.9 2.0 constant_dynamic-update-slice_fusion.16
  219.9 10.4 %multiply_convert_fusion = (bf16[1024,3072]{1,0:T(8,128)(2,1)}, f32[1024,3072]{1,0:T(8,128)}) fusion(bf16[3072,768]{1,0:T(8,128)(2,1)S(1)} %constant_dynamic-update-slice_fusion.16, f32[1024,768]{0,1:T(8,128)S(1)} %get-tuple-element.210, f32[768]{0:T(1024)S(1)} %get-tuple-element.95, f32[768]{0:T(1024)S(1)} %get-tuple-element.96, ...), kind=kOutput, calls=%fused_computation.7 | convolution fusion | flops 4851499008 | bytes 26753024 | tf_op jit(solution)/shard_map/dot_general | solution.py:28
  230.3 2.0 constant_dynamic-update-slice_fusion.27
  232.3 7.8 %fusion.82 = (f32[1024]{0:T(1024)S(1)}, f32[1024,768]{0,1:T(8,128)S(1)}) fusion(bf16[1024,3072]{1,0:T(8,128)(2,1)} %get-tuple-element.211, bf16[3072,768]{1,0:T(8,128)(2,1)S(1)} %constant_dynamic-update-slice_fusion.27, f32[768]{0:T(1024)S(1)} %get-tuple-element.95, f32[768]{0:T(1024)S(1)} %get-tuple-element.96, f32[1024]{0:T(1024)S(1)} %add_rsqrt_fusion.1, ...), kind=kOutput, calls=%fused_computation.267 | convolution fusion | flops 4836555776 | bytes 17319936 | tf_op jit(solution)/shard_map/dot_general | solution.py:28
  240.5 3.4 fusion.12
  244.0 7.8 %convolution_convert_fusion = bf16[3072,768]{1,0:T(8,128)(2,1)} fusion(bf16[1024,3072]{1,0:T(8,128)(2,1)S(1)} %bitcast.182, bf16[1024,768]{0,1:T(8,128)(2,1)S(1)} %copy.64, f32[1024,768]{0,1:T(8,128)S(1)} %get-tuple-element.214, f32[1024]{0:T(1024)S(1)} %broadcast_multiply_fusion.3, f32[1024]{0:T(1024)S(1)} %broadcast_multiply_fusion.4, ...), kind=kOutput, calls=%fused_computation.10 | convolution fusion | flops 4841275392 | bytes 15748096 | tf_op jit(solution)/shard_map/dot_general | solution.py:28
  251.7 10.1 %fusion.5 = bf16[1024,3072]{1,0:T(8,128)(2,1)S(1)} fusion(f32[1024,3072]{1,0:T(8,128)} %get-tuple-element.212, bf16[3072,768]{1,0:T(8,128)(2,1)S(1)} %constant_dynamic-update-slice_fusion.27, bf16[1024,768]{0,1:T(8,128)(2,1)S(1)} %copy.64, f32[1024,768]{0,1:T(8,128)S(1)} %get-tuple-element.214, f32[1024]{0:T(1024)S(1)} %broadcast_multiply_fusion.3, ...), kind=kOutput, calls=%fused_computation.6 | convolution fusion | flops 4870373376 | bytes 28331008 | tf_op jit(solution)/shard_map/dot_general | solution.py:28
  261.9 2.6 copy-done.44
  264.4 6.2 convolution_convert_fusion.1
  270.6 14.2 %multiply_reduce_fusion = (f32[768]{0:T(1024)}, f32[1024]{0:T(1024)S(1)}, f32[1024]{0:T(1024)S(1)}, f32[768]{0:T(1024)}, f32[1024,768]{0,1:T(8,128)}) fusion(f32[1024,768]{0,1:T(8,128)S(1)} %get-tuple-element.210, f32[1024]{0:T(1024)S(1)} %add_rsqrt_fusion.1, f32[1024]{0:T(1024)S(1)} %broadcast_multiply_fusion.6, f32[768]{0:T(1024)S(1)} %get-tuple-element.96, ...), kind=kOutput, calls=%fused_computation.28 | convolution fusion | flops 4845989888 | bytes 22065152 | tf_op jit(solution)/shard_map/dot_general | solution.py:28
  284.8 2.8 subtract_multiply_fusion
  297.7 2.7 collective-permute-done.24
  300.5 6.4 %collective-permute-done.25 = bf16[1536,128]{1,0:T(8,128)(2,1)S(1)} collective-permute-done((bf16[1536,128]{1,0:T(8,128)(2,1)S(1)}, bf16[1536,128]{1,0:T(8,128)(2,1)S(1)}, u32[]{:S(2)}, u32[]{:S(2)}) %collective-permute-start.25) | collective-permute-done | bytes 393248 | tf_op jit(solution)/shard_map/ppermute | solution.py:35
  306.9 7.6 %collective-permute-done.26 = bf16[1536,128]{1,0:T(8,128)(2,1)S(1)} collective-permute-done((bf16[1536,128]{1,0:T(8,128)(2,1)S(1)}, bf16[1536,128]{1,0:T(8,128)(2,1)S(1)}, u32[]{:S(2)}, u32[]{:S(2)}) %collective-permute-start.26) | collective-permute-done | bytes 393248 | tf_op jit(solution)/shard_map/ppermute | solution.py:35
  315.9 78.0 %attend_back.1 = (bf16[768,768]{1,0:T(8,128)(2,1)}, bf16[4,1024,768]{2,1,0:T(8,128)(2,1)}) custom-call(s32[3,1,4096]{2,1,0:T(1,128)} %copy-done.1, bf16[3,4096,128]{2,1,0:T(8,128)(2,1)} %get-tuple-element.25.qv_ref, bf16[3,4096,128]{2,1,0:T(8,128)(2,1)} %get-tuple-element.26.key_ref, bf16[4,1536,128]{2,1,0:T(8,128)(2,1)} %pad_maximum_fusion.do_ref, ...), custom_call_target="tpu_custom_call" | custom-call | flops 11676942336 | bytes 31457280 | tf_op jit(solution)/shard_map/attend_back/pallas_call | solution.py:316
  396.1 8.5 %collective-permute-done.33 = bf16[192,768]{1,0:T(8,128)(2,1)S(1)} collective-permute-done((bf16[192,768]{1,0:T(8,128)(2,1)S(1)}, bf16[192,768]{1,0:T(8,128)(2,1)S(1)}, u32[]{:S(2)}, u32[]{:S(2)}) %collective-permute-start.33) | collective-permute-done | bytes 294944 | tf_op jit(solution)/shard_map/ppermute | solution.py:35
  406.9 3.0 collective-permute-done.34
  411.6 2.9 convert_add_fusion.1
  415.3 2.2 convert_add_fusion.2
  421.7 4.2 collective-permute-done.30
  428.7 16.0 %collective-permute-done.43 = bf16[768,768]{1,0:T(8,128)(2,1)S(1)} collective-permute-done((bf16[768,768]{1,0:T(8,128)(2,1)S(1)}, bf16[768,768]{1,0:T(8,128)(2,1)S(1)}, u32[]{:S(2)}, u32[]{:S(2)}) %collective-permute-start.43) | collective-permute-done | bytes 1179680 | tf_op jit(solution)/shard_map/ppermute | solution.py:35
  445.5 22.6 %collective-permute-done.38 = bf16[768,768]{1,0:T(8,128)(2,1)S(1)} collective-permute-done((bf16[768,768]{1,0:T(8,128)(2,1)S(1)}, bf16[768,768]{1,0:T(8,128)(2,1)S(1)}, u32[]{:S(2)}, u32[]{:S(2)}) %collective-permute-start.38) | collective-permute-done | bytes 1179680 | tf_op jit(solution)/shard_map/ppermute | solution.py:35
  471.7 10.3 %collective-permute-done.39 = bf16[384,768]{1,0:T(8,128)(2,1)S(1)} collective-permute-done((bf16[384,768]{1,0:T(8,128)(2,1)S(1)}, bf16[384,768]{1,0:T(8,128)(2,1)S(1)}, u32[]{:S(2)}, u32[]{:S(2)}) %collective-permute-start.39) | collective-permute-done | bytes 589856 | tf_op jit(solution)/shard_map/ppermute | solution.py:35
  484.3 6.9 %collective-permute-done.40 = bf16[192,768]{1,0:T(8,128)(2,1)S(1)} collective-permute-done((bf16[192,768]{1,0:T(8,128)(2,1)S(1)}, bf16[192,768]{1,0:T(8,128)(2,1)S(1)}, u32[]{:S(2)}, u32[]{:S(2)}) %collective-permute-start.40) | collective-permute-done | bytes 294944 | tf_op jit(solution)/shard_map/ppermute | solution.py:35
  491.4 2.9 collective-permute-done.46
  495.2 3.9 collective-permute-done.41
  502.0 4.8 collective-permute-done.53
  506.8 2.3 collective-permute-done.54
  513.0 4.9 fusion.68
  518.0 3.0 copy.67
  521.0 7.1 %collective-permute-done.55 = bf16[384,768]{1,0:T(8,128)(2,1)} collective-permute-done((bf16[384,768]{1,0:T(8,128)(2,1)}, bf16[384,768]{1,0:T(8,128)(2,1)}, u32[]{:S(2)}, u32[]{:S(2)}) %collective-permute-start.55) | collective-permute-done | bytes 589856 | tf_op jit(solution)/shard_map/ppermute | solution.py:35
  528.2 2.0 convert_add_fusion.4
  531.1 1.8 collective-permute-start.47
  533.0 4.1 collective-permute-done.47
  537.0 2.5 collective-permute-start.48
  539.5 1.8 collective-permute-done.48
  542.2 3.0 collective-permute-start.57
  546.1 3.0 collective-permute-done.50
  549.1 2.7 copy.74
  553.6 2.9 collective-permute-start.58
  557.2 7.0 %collective-permute-done.58 = bf16[96,768]{1,0:T(8,128)(2,1)S(1)} collective-permute-done((bf16[96,768]{1,0:T(8,128)(2,1)S(1)}, bf16[96,768]{1,0:T(8,128)(2,1)S(1)}, u32[]{:S(2)}, u32[]{:S(2)}) %collective-permute-start.58) | collective-permute-done | bytes 147488 | tf_op jit(solution)/shard_map/ppermute | solution.py:35
  565.0 3.4 bitcast_convert_fusion
  568.3 6.8 %copy.68 = f32[2048,768]{0,1:T(8,128)} copy(f32[2048,768]{1,0:T(8,128)} %bitcast_convert_fusion) | data formatting | bytes 12582912 | tf_op jit(solution)/shard_map/convert_element_type | solution.py:67
  577.5 4.6 convert_add_fusion
  582.2 2.6 copy-done.2
  587.2 4.2 collective-permute-done.60
  602.6 3.3 fusion.24
  608.6 15.2 %collective-permute-done.28 = bf16[1024,768]{0,1:T(8,128)(2,1)} collective-permute-done((bf16[1024,768]{0,1:T(8,128)(2,1)}, bf16[1024,768]{0,1:T(8,128)(2,1)}, u32[]{:S(2)}, u32[]{:S(2)}) %collective-permute-start.28) | collective-permute-done | bytes 1572896 | tf_op jit(solution)/shard_map/ppermute | solution.py:35
  623.8 4.3 fusion.13
  628.1 2.4 copy.75
  631.7 1.8 bitcast_subtract_fusion
  (364 shorter events, 123.9 us)
Async XLA Ops:
  2.5 29.6 %collective-permute-start.19 = (bf16[96,768]{1,0:T(8,128)(2,1)S(1)}, bf16[96,768]{1,0:T(8,128)(2,1)S(1)}, u32[]{:S(2)}, u32[]{:S(2)}) collective-permute-start(bf16[96,768]{1,0:T(8,128)(2,1)S(1)} %get-tuple-element.109), channel_id=1, source_target_pairs={{0,16},{4,20},{8,24},{12,28},{16,0},{20,4},{24,8},{28,12},{1,17},{... | collective-permute-start | bytes 442376 | tf_op jit(solution)/shard_map/ppermute | solution.py:35
  8.0 14.4 %collective-permute-start.9 = (bf16[24,768]{1,0:T(8,128)(2,1)S(1)}, bf16[24,768]{1,0:T(8,128)(2,1)}, u32[]{:S(2)}, u32[]{:S(2)}) collective-permute-start(bf16[24,768]{1,0:T(8,128)(2,1)S(1)} %get-tuple-element.111), channel_id=1, source_target_pairs={{0,16},{4,20},{8,24},{12,28},{16,0},{20,4},{24,8},{28,12},{1,17},{... | collective-permute-start | bytes 110600 | tf_op jit(solution)/shard_map/ppermute | solution.py:35
  9.0 21.2 %collective-permute-start.3 = (bf16[72,768]{1,0:T(8,128)(2,1)S(1)}, bf16[72,768]{1,0:T(8,128)(2,1)}, u32[]{:S(2)}, u32[]{:S(2)}) collective-permute-start(bf16[72,768]{1,0:T(8,128)(2,1)S(1)} %bitcast.159), channel_id=1, source_target_pairs={{0,16},{4,20},{8,24},{12,28},{16,0},{20,4},{24,8},{28,12},{1,17},{... | collective-permute-start | bytes 331784 | tf_op jit(solution)/shard_map/ppermute | solution.py:35
  11.9 57.4 %collective-permute-start.1 = (bf16[1024,768]{1,0:T(8,128)(2,1)}, bf16[1024,768]{1,0:T(8,128)(2,1)}, u32[]{:S(2)}, u32[]{:S(2)}) collective-permute-start(bf16[1024,768]{1,0:T(8,128)(2,1)} %x0.3), channel_id=1, source_target_pairs={{0,2},{1,3},{2,0},{3,1},{4,6},{5,7},{6,4},{7,5},{8,10},{9,11},{10,... | collective-permute-start | bytes 4718600 | tf_op jit(solution)/shard_map/ppermute | solution.py:35
  15.1 18.8 %collective-permute-start.14 = (bf16[96,768]{1,0:T(8,128)(2,1)S(1)}, bf16[96,768]{1,0:T(8,128)(2,1)S(1)}, u32[]{:S(2)}, u32[]{:S(2)}) collective-permute-start(bf16[96,768]{1,0:T(8,128)(2,1)S(1)} %get-tuple-element.113), channel_id=1, source_target_pairs={{0,16},{4,20},{8,24},{12,28},{16,0},{20,4},{24,8},{28,12},{1,17},{... | collective-permute-start | bytes 442376 | tf_op jit(solution)/shard_map/ppermute | solution.py:35
  23.2 4.5 collective-permute-start.10
  28.5 22.1 %collective-permute-start.11 = (bf16[96,768]{1,0:T(8,128)(2,1)S(1)}, bf16[96,768]{1,0:T(8,128)(2,1)S(1)}, u32[]{:S(2)}, u32[]{:S(2)}) collective-permute-start(bf16[96,768]{1,0:T(8,128)(2,1)S(1)} %pad_maximum_fusion.22), channel_id=1, source_target_pairs={{0,2},{1,3},{2,0},{3,1},{4,6},{5,7},{6,4},{7,5},{8,10},{9,11},{10,... | collective-permute-start | bytes 442376 | tf_op jit(solution)/shard_map/ppermute | solution.py:35
  31.1 24.2 %collective-permute-start.4 = (bf16[144,768]{1,0:T(8,128)(2,1)S(1)}, bf16[144,768]{1,0:T(8,128)(2,1)S(1)}, u32[]{:S(2)}, u32[]{:S(2)}) collective-permute-start(bf16[144,768]{1,0:T(8,128)(2,1)S(1)} %pad_maximum_fusion.21), channel_id=1, source_target_pairs={{0,8},{4,12},{8,0},{12,4},{16,24},{20,28},{24,16},{28,20},{1,9},{5... | collective-permute-start | bytes 663560 | tf_op jit(solution)/shard_map/ppermute | solution.py:35
  32.1 20.9 %collective-permute-start.20 = (bf16[192,768]{1,0:T(8,128)(2,1)S(1)}, bf16[192,768]{1,0:T(8,128)(2,1)S(1)}, u32[]{:S(2)}, u32[]{:S(2)}) collective-permute-start(bf16[192,768]{1,0:T(8,128)(2,1)S(1)} %pad_maximum_fusion.15), channel_id=1, source_target_pairs={{0,8},{4,12},{8,0},{12,4},{16,24},{20,28},{24,16},{28,20},{1,9},{5... | collective-permute-start | bytes 884744 | tf_op jit(solution)/shard_map/ppermute | solution.py:35
  33.9 20.7 %collective-permute-start.15 = (bf16[192,768]{1,0:T(8,128)(2,1)S(1)}, bf16[192,768]{1,0:T(8,128)(2,1)S(1)}, u32[]{:S(2)}, u32[]{:S(2)}) collective-permute-start(bf16[192,768]{1,0:T(8,128)(2,1)S(1)} %pad_maximum_fusion.14), channel_id=1, source_target_pairs={{0,8},{4,12},{8,0},{12,4},{16,24},{20,28},{24,16},{28,20},{1,9},{5... | collective-permute-start | bytes 884744 | tf_op jit(solution)/shard_map/ppermute | solution.py:35
  51.4 9.5 %collective-permute-start.12 = (bf16[192,768]{1,0:T(8,128)(2,1)S(1)}, bf16[192,768]{1,0:T(8,128)(2,1)S(1)}, u32[]{:S(2)}, u32[]{:S(2)}) collective-permute-start(bf16[192,768]{1,0:T(8,128)(2,1)S(1)} %pad_maximum_fusion.13), channel_id=1, source_target_pairs={{0,4},{4,0},{8,12},{12,8},{16,20},{20,16},{24,28},{28,24},{1,5},{5... | collective-permute-start | bytes 884744 | tf_op jit(solution)/shard_map/ppermute | solution.py:35
  53.1 16.3 %collective-permute-start.21 = (bf16[384,768]{1,0:T(8,128)(2,1)S(1)}, bf16[384,768]{1,0:T(8,128)(2,1)S(1)}, u32[]{:S(2)}, u32[]{:S(2)}) collective-permute-start(bf16[384,768]{1,0:T(8,128)(2,1)S(1)} %pad_maximum_fusion.7), channel_id=1, source_target_pairs={{0,2},{1,3},{2,0},{3,1},{4,6},{5,7},{6,4},{7,5},{8,10},{9,11},{10,... | collective-permute-start | bytes 1769480 | tf_op jit(solution)/shard_map/ppermute | solution.py:35
  54.7 24.2 %collective-permute-start.16 = (bf16[384,768]{1,0:T(8,128)(2,1)S(1)}, bf16[384,768]{1,0:T(8,128)(2,1)S(1)}, u32[]{:S(2)}, u32[]{:S(2)}) collective-permute-start(bf16[384,768]{1,0:T(8,128)(2,1)S(1)} %pad_maximum_fusion.6), channel_id=1, source_target_pairs={{0,2},{1,3},{2,0},{3,1},{4,6},{5,7},{6,4},{7,5},{8,10},{9,11},{10,... | collective-permute-start | bytes 1769480 | tf_op jit(solution)/shard_map/ppermute | solution.py:35
  56.2 23.3 %collective-permute-start.5 = (bf16[288,768]{1,0:T(8,128)(2,1)S(1)}, bf16[288,768]{1,0:T(8,128)(2,1)S(1)}, u32[]{:S(2)}, u32[]{:S(2)}) collective-permute-start(bf16[288,768]{1,0:T(8,128)(2,1)S(1)} %pad_maximum_fusion.12), channel_id=1, source_target_pairs={{0,4},{4,0},{8,12},{12,8},{16,20},{20,16},{24,28},{28,24},{1,5},{5... | collective-permute-start | bytes 1327112 | tf_op jit(solution)/shard_map/ppermute | solution.py:35
  60.9 69.7 %collective-permute-start = (bf16[1024,768]{1,0:T(8,128)(2,1)S(1)}, bf16[1024,768]{1,0:T(8,128)(2,1)S(1)}, u32[]{:S(2)}, u32[]{:S(2)}) collective-permute-start(bf16[1024,768]{1,0:T(8,128)(2,1)S(1)} %copy-done.9), channel_id=1, source_target_pairs={{0,1},{1,0},{2,3},{3,2},{4,5},{5,4},{6,7},{7,6},{8,9},{9,8},{10,11... | collective-permute-start | bytes 4718600 | tf_op jit(solution)/shard_map/ppermute | solution.py:35
  69.4 15.3 %collective-permute-start.13 = (bf16[384,768]{1,0:T(8,128)(2,1)S(1)}, bf16[384,768]{1,0:T(8,128)(2,1)S(1)}, u32[]{:S(2)}, u32[]{:S(2)}) collective-permute-start(bf16[384,768]{1,0:T(8,128)(2,1)S(1)} %get-tuple-element.192), channel_id=1, source_target_pairs={{0,1},{1,0},{2,3},{3,2},{4,5},{5,4},{6,7},{7,6},{8,9},{9,8},{10,11... | collective-permute-start | bytes 1769480 | tf_op jit(solution)/shard_map/ppermute | solution.py:35
  69.4 62.4 %collective-permute-start.2 = (bf16[1024,768]{1,0:T(8,128)(2,1)}, bf16[1024,768]{1,0:T(8,128)(2,1)S(1)}, u32[]{:S(2)}, u32[]{:S(2)}) collective-permute-start(bf16[1024,768]{1,0:T(8,128)(2,1)} %collective-permute-done.1.x2), channel_id=1, source_target_pairs={{0,1},{1,0},{2,3},{3,2},{4,5},{5,4},{6,7},{7,6},{8,9},{9,8},{10,11... | collective-permute-start | bytes 4718600 | tf_op jit(solution)/shard_map/ppermute | solution.py:35
  78.9 28.9 %collective-permute-start.22 = (bf16[768,768]{1,0:T(8,128)(2,1)S(1)}, bf16[768,768]{1,0:T(8,128)(2,1)S(1)}, u32[]{:S(2)}, u32[]{:S(2)}) collective-permute-start(bf16[768,768]{1,0:T(8,128)(2,1)S(1)} %pad_maximum_fusion.2), channel_id=1, source_target_pairs={{0,4},{4,0},{8,12},{12,8},{16,20},{20,16},{24,28},{28,24},{1,5},{5... | collective-permute-start | bytes 3538952 | tf_op jit(solution)/shard_map/ppermute | solution.py:35
  79.5 49.5 %collective-permute-start.17 = (bf16[768,768]{1,0:T(8,128)(2,1)S(1)}, bf16[768,768]{1,0:T(8,128)(2,1)S(1)}, u32[]{:S(2)}, u32[]{:S(2)}) collective-permute-start(bf16[768,768]{1,0:T(8,128)(2,1)S(1)} %pad_maximum_fusion.1), channel_id=1, source_target_pairs={{0,4},{4,0},{8,12},{12,8},{16,20},{20,16},{24,28},{28,24},{1,5},{5... | collective-permute-start | bytes 3538952 | tf_op jit(solution)/shard_map/ppermute | solution.py:35
  109.4 120.9 %collective-permute-start.23 = (bf16[1536,768]{1,0:T(8,128)(2,1)}, bf16[1536,768]{1,0:T(8,128)(2,1)}, u32[]{:S(2)}, u32[]{:S(2)}) collective-permute-start(bf16[1536,768]{1,0:T(8,128)(2,1)} %get-tuple-element.144), channel_id=1, source_target_pairs={{0,1},{1,0},{2,3},{3,2},{4,5},{5,4},{6,7},{7,6},{8,9},{9,8},{10,11... | collective-permute-start | bytes 7077896 | tf_op jit(solution)/shard_map/ppermute | solution.py:35
  130.6 87.3 %collective-permute-start.18 = (bf16[1536,768]{1,0:T(8,128)(2,1)}, bf16[1536,768]{1,0:T(8,128)(2,1)}, u32[]{:S(2)}, u32[]{:S(2)}) collective-permute-start(bf16[1536,768]{1,0:T(8,128)(2,1)} %get-tuple-element.146), channel_id=1, source_target_pairs={{0,1},{1,0},{2,3},{3,2},{4,5},{5,4},{6,7},{7,6},{8,9},{9,8},{10,11... | collective-permute-start | bytes 7077896 | tf_op jit(solution)/shard_map/ppermute | solution.py:35
  186.0 11.2 %collective-permute-start.8 = (bf16[1536,128]{1,0:T(8,128)(2,1)S(1)}, bf16[1536,128]{1,0:T(8,128)(2,1)S(1)}, u32[]{:S(2)}, u32[]{:S(2)}) collective-permute-start(bf16[1536,128]{1,0:T(8,128)(2,1)S(1)} %get-tuple-element.133), channel_id=1, source_target_pairs={{0,3},{1,2},{2,1},{3,0},{4,7},{5,6},{6,5},{7,4},{8,11},{9,10},{10,... | collective-permute-start | bytes 1179656 | tf_op jit(solution)/shard_map/ppermute | solution.py:35
  187.7 18.2 %collective-permute-start.7 = (bf16[1536,128]{1,0:T(8,128)(2,1)S(1)}, bf16[1536,128]{1,0:T(8,128)(2,1)S(1)}, u32[]{:S(2)}, u32[]{:S(2)}) collective-permute-start(bf16[1536,128]{1,0:T(8,128)(2,1)S(1)} %get-tuple-element.134), channel_id=1, source_target_pairs={{0,2},{1,3},{2,0},{3,1},{4,6},{5,7},{6,4},{7,5},{8,10},{9,11},{10,... | collective-permute-start | bytes 1179656 | tf_op jit(solution)/shard_map/ppermute | solution.py:35
  188.2 17.8 %collective-permute-start.6 = (bf16[1536,128]{1,0:T(8,128)(2,1)S(1)}, bf16[1536,128]{1,0:T(8,128)(2,1)S(1)}, u32[]{:S(2)}, u32[]{:S(2)}) collective-permute-start(bf16[1536,128]{1,0:T(8,128)(2,1)S(1)} %get-tuple-element.135), channel_id=1, source_target_pairs={{0,1},{1,0},{2,3},{3,2},{4,5},{5,4},{6,7},{7,6},{8,9},{9,8},{10,11... | collective-permute-start | bytes 1179656 | tf_op jit(solution)/shard_map/ppermute | solution.py:35
  293.7 117.9 %collective-permute-start.42 = (bf16[1536,768]{1,0:T(8,128)(2,1)}, bf16[1536,768]{1,0:T(8,128)(2,1)}, u32[]{:S(2)}, u32[]{:S(2)}) collective-permute-start(bf16[1536,768]{1,0:T(8,128)(2,1)} %slice.537), channel_id=1, source_target_pairs={{0,1},{1,0},{2,3},{3,2},{4,5},{5,4},{6,7},{7,6},{8,9},{9,8},{10,11... | collective-permute-start | bytes 7077896 | tf_op jit(solution)/shard_map/ppermute | solution.py:35
  293.8 121.5 %collective-permute-start.37 = (bf16[1536,768]{1,0:T(8,128)(2,1)S(1)}, bf16[1536,768]{1,0:T(8,128)(2,1)}, u32[]{:S(2)}, u32[]{:S(2)}) collective-permute-start(bf16[1536,768]{1,0:T(8,128)(2,1)S(1)} %slice.527), channel_id=1, source_target_pairs={{0,1},{1,0},{2,3},{3,2},{4,5},{5,4},{6,7},{7,6},{8,9},{9,8},{10,11... | collective-permute-start | bytes 7077896 | tf_op jit(solution)/shard_map/ppermute | solution.py:35
  294.6 5.8 collective-permute-start.24
  294.9 12.0 %collective-permute-start.25 = (bf16[1536,128]{1,0:T(8,128)(2,1)S(1)}, bf16[1536,128]{1,0:T(8,128)(2,1)S(1)}, u32[]{:S(2)}, u32[]{:S(2)}) collective-permute-start(bf16[1536,128]{1,0:T(8,128)(2,1)S(1)} %maximum_maximum_fusion.2), channel_id=1, source_target_pairs={{0,2},{1,3},{2,0},{3,1},{4,6},{5,7},{6,4},{7,5},{8,10},{9,11},{10,... | collective-permute-start | bytes 1179656 | tf_op jit(solution)/shard_map/ppermute | solution.py:35
  296.7 17.8 %collective-permute-start.26 = (bf16[1536,128]{1,0:T(8,128)(2,1)S(1)}, bf16[1536,128]{1,0:T(8,128)(2,1)S(1)}, u32[]{:S(2)}, u32[]{:S(2)}) collective-permute-start(bf16[1536,128]{1,0:T(8,128)(2,1)S(1)} %maximum_maximum_fusion.3), channel_id=1, source_target_pairs={{0,3},{1,2},{2,1},{3,0},{4,7},{5,6},{6,5},{7,4},{8,11},{9,10},{10,... | collective-permute-start | bytes 1179656 | tf_op jit(solution)/shard_map/ppermute | solution.py:35
  300.4 93.6 %collective-permute-start.32 = (bf16[384,768]{1,0:T(8,128)(2,1)S(1)}, bf16[384,768]{1,0:T(8,128)(2,1)}, u32[]{:S(2)}, u32[]{:S(2)}) collective-permute-start(bf16[384,768]{1,0:T(8,128)(2,1)S(1)} %bitcast.169), channel_id=1, source_target_pairs={{0,1},{1,0},{2,3},{3,2},{4,5},{5,4},{6,7},{7,6},{8,9},{9,8},{10,11... | collective-permute-start | bytes 1769480 | tf_op jit(solution)/shard_map/ppermute | solution.py:35
  395.3 9.2 %collective-permute-start.33 = (bf16[192,768]{1,0:T(8,128)(2,1)S(1)}, bf16[192,768]{1,0:T(8,128)(2,1)S(1)}, u32[]{:S(2)}, u32[]{:S(2)}) collective-permute-start(bf16[192,768]{1,0:T(8,128)(2,1)S(1)} %slice.644), channel_id=1, source_target_pairs={{0,4},{4,0},{8,12},{12,8},{16,20},{20,16},{24,28},{28,24},{1,5},{5... | collective-permute-start | bytes 884744 | tf_op jit(solution)/shard_map/ppermute | solution.py:35
  404.6 5.3 collective-permute-start.34
  406.3 13.2 %collective-permute-start.29 = (bf16[288,768]{1,0:T(8,128)(2,1)S(1)}, bf16[288,768]{1,0:T(8,128)(2,1)S(1)}, u32[]{:S(2)}, u32[]{:S(2)}) collective-permute-start(bf16[288,768]{1,0:T(8,128)(2,1)S(1)} %bitcast.170), channel_id=1, source_target_pairs={{0,4},{4,0},{8,12},{12,8},{16,20},{20,16},{24,28},{28,24},{1,5},{5... | collective-permute-start | bytes 1327112 | tf_op jit(solution)/shard_map/ppermute | solution.py:35
  410.0 11.3 %collective-permute-start.35 = (bf16[48,768]{1,0:T(8,128)(2,1)S(1)}, bf16[48,768]{1,0:T(8,128)(2,1)S(1)}, u32[]{:S(2)}, u32[]{:S(2)}) collective-permute-start(bf16[48,768]{1,0:T(8,128)(2,1)S(1)} %slice.650), channel_id=1, source_target_pairs={{0,8},{4,12},{8,0},{12,4},{16,24},{20,28},{24,16},{28,20},{1,9},{5... | collective-permute-start | bytes 221192 | tf_op jit(solution)/shard_map/ppermute | solution.py:35
  414.6 30.1 %collective-permute-start.43 = (bf16[768,768]{1,0:T(8,128)(2,1)S(1)}, bf16[768,768]{1,0:T(8,128)(2,1)S(1)}, u32[]{:S(2)}, u32[]{:S(2)}) collective-permute-start(bf16[768,768]{1,0:T(8,128)(2,1)S(1)} %slice.638), channel_id=1, source_target_pairs={{0,4},{4,0},{8,12},{12,8},{16,20},{20,16},{24,28},{28,24},{1,5},{5... | collective-permute-start | bytes 3538952 | tf_op jit(solution)/shard_map/ppermute | solution.py:35
  417.6 50.5 %collective-permute-start.38 = (bf16[768,768]{1,0:T(8,128)(2,1)S(1)}, bf16[768,768]{1,0:T(8,128)(2,1)S(1)}, u32[]{:S(2)}, u32[]{:S(2)}) collective-permute-start(bf16[768,768]{1,0:T(8,128)(2,1)S(1)} %slice.639), channel_id=1, source_target_pairs={{0,4},{4,0},{8,12},{12,8},{16,20},{20,16},{24,28},{28,24},{1,5},{5... | collective-permute-start | bytes 3538952 | tf_op jit(solution)/shard_map/ppermute | solution.py:35
  419.6 6.3 collective-permute-start.30
  421.3 6.7 %collective-permute-start.36 = (bf16[24,768]{1,0:T(8,128)(2,1)S(1)}, bf16[24,768]{1,0:T(8,128)(2,1)S(1)}, u32[]{:S(2)}, u32[]{:S(2)}) collective-permute-start(bf16[24,768]{1,0:T(8,128)(2,1)S(1)} %slice.651), channel_id=1, source_target_pairs={{0,16},{4,20},{8,24},{12,28},{16,0},{20,4},{24,8},{28,12},{1,17},{... | collective-permute-start | bytes 110600 | tf_op jit(solution)/shard_map/ppermute | solution.py:35
  426.0 43.1 %collective-permute-start.31 = (bf16[72,768]{1,0:T(8,128)(2,1)S(1)}, bf16[72,768]{1,0:T(8,128)(2,1)S(1)}, u32[]{:S(2)}, u32[]{:S(2)}) collective-permute-start(bf16[72,768]{1,0:T(8,128)(2,1)S(1)} %slice.649), channel_id=1, source_target_pairs={{0,16},{4,20},{8,24},{12,28},{16,0},{20,4},{24,8},{28,12},{1,17},{... | collective-permute-start | bytes 331784 | tf_op jit(solution)/shard_map/ppermute | solution.py:35
  445.0 24.8 %collective-permute-start.44 = (bf16[384,768]{1,0:T(8,128)(2,1)S(1)}, bf16[384,768]{1,0:T(8,128)(2,1)S(1)}, u32[]{:S(2)}, u32[]{:S(2)}) collective-permute-start(bf16[384,768]{1,0:T(8,128)(2,1)S(1)} %slice.640), channel_id=1, source_target_pairs={{0,2},{1,3},{2,0},{3,1},{4,6},{5,7},{6,4},{7,5},{8,10},{9,11},{10,... | collective-permute-start | bytes 1769480 | tf_op jit(solution)/shard_map/ppermute | solution.py:35
  468.4 13.5 %collective-permute-start.39 = (bf16[384,768]{1,0:T(8,128)(2,1)S(1)}, bf16[384,768]{1,0:T(8,128)(2,1)S(1)}, u32[]{:S(2)}, u32[]{:S(2)}) collective-permute-start(bf16[384,768]{1,0:T(8,128)(2,1)S(1)} %slice.641), channel_id=1, source_target_pairs={{0,2},{1,3},{2,0},{3,1},{4,6},{5,7},{6,4},{7,5},{8,10},{9,11},{10,... | collective-permute-start | bytes 1769480 | tf_op jit(solution)/shard_map/ppermute | solution.py:35
  470.0 13.9 %collective-permute-start.45 = (bf16[192,768]{1,0:T(8,128)(2,1)S(1)}, bf16[192,768]{1,0:T(8,128)(2,1)S(1)}, u32[]{:S(2)}, u32[]{:S(2)}) collective-permute-start(bf16[192,768]{1,0:T(8,128)(2,1)S(1)} %slice.642), channel_id=1, source_target_pairs={{0,8},{4,12},{8,0},{12,4},{16,24},{20,28},{24,16},{28,20},{1,9},{5... | collective-permute-start | bytes 884744 | tf_op jit(solution)/shard_map/ppermute | solution.py:35
  482.1 9.2 %collective-permute-start.40 = (bf16[192,768]{1,0:T(8,128)(2,1)S(1)}, bf16[192,768]{1,0:T(8,128)(2,1)S(1)}, u32[]{:S(2)}, u32[]{:S(2)}) collective-permute-start(bf16[192,768]{1,0:T(8,128)(2,1)S(1)} %slice.643), channel_id=1, source_target_pairs={{0,8},{4,12},{8,0},{12,4},{16,24},{20,28},{24,16},{28,20},{1,9},{5... | collective-permute-start | bytes 884744 | tf_op jit(solution)/shard_map/ppermute | solution.py:35
  484.0 10.3 %collective-permute-start.46 = (bf16[96,768]{1,0:T(8,128)(2,1)S(1)}, bf16[96,768]{1,0:T(8,128)(2,1)S(1)}, u32[]{:S(2)}, u32[]{:S(2)}) collective-permute-start(bf16[96,768]{1,0:T(8,128)(2,1)S(1)} %slice.646), channel_id=1, source_target_pairs={{0,16},{4,20},{8,24},{12,28},{16,0},{20,4},{24,8},{28,12},{1,17},{... | collective-permute-start | bytes 442376 | tf_op jit(solution)/shard_map/ppermute | solution.py:35
  491.4 7.7 %collective-permute-start.41 = (bf16[96,768]{1,0:T(8,128)(2,1)S(1)}, bf16[96,768]{1,0:T(8,128)(2,1)S(1)}, u32[]{:S(2)}, u32[]{:S(2)}) collective-permute-start(bf16[96,768]{1,0:T(8,128)(2,1)S(1)} %slice.647), channel_id=1, source_target_pairs={{0,16},{4,20},{8,24},{12,28},{16,0},{20,4},{24,8},{28,12},{1,17},{... | collective-permute-start | bytes 442376 | tf_op jit(solution)/shard_map/ppermute | solution.py:35
  500.1 1.9 collective-permute-start.52
  500.1 6.7 %collective-permute-start.53 = (bf16[96,768]{1,0:T(8,128)(2,1)S(1)}, bf16[96,768]{1,0:T(8,128)(2,1)S(1)}, u32[]{:S(2)}, u32[]{:S(2)}) collective-permute-start(bf16[96,768]{1,0:T(8,128)(2,1)S(1)} %get-tuple-element.166), channel_id=1, source_target_pairs={{0,2},{1,3},{2,0},{3,1},{4,6},{5,7},{6,4},{7,5},{8,10},{9,11},{10,... | collective-permute-start | bytes 442376 | tf_op jit(solution)/shard_map/ppermute | solution.py:35
  501.3 7.8 %collective-permute-start.54 = (bf16[96,768]{1,0:T(8,128)(2,1)S(1)}, bf16[96,768]{1,0:T(8,128)(2,1)S(1)}, u32[]{:S(2)}, u32[]{:S(2)}) collective-permute-start(bf16[96,768]{1,0:T(8,128)(2,1)S(1)} %get-tuple-element.165), channel_id=1, source_target_pairs={{0,3},{1,2},{2,1},{3,0},{4,7},{5,6},{6,5},{7,4},{8,11},{9,10},{10,... | collective-permute-start | bytes 442376 | tf_op jit(solution)/shard_map/ppermute | solution.py:35
  512.3 15.8 %collective-permute-start.55 = (bf16[384,768]{1,0:T(8,128)(2,1)}, bf16[384,768]{1,0:T(8,128)(2,1)}, u32[]{:S(2)}, u32[]{:S(2)}) collective-permute-start(bf16[384,768]{1,0:T(8,128)(2,1)} %select_convert_fusion), channel_id=1, source_target_pairs={{0,4},{4,0},{8,12},{12,8},{16,20},{20,16},{24,28},{28,24},{1,5},{5... | collective-permute-start | bytes 1769480 | tf_op jit(solution)/shard_map/ppermute | solution.py:35
  521.0 56.5 %collective-permute-start.27 = (bf16[2048,768]{0,1:T(8,128)(2,1)}, bf16[2048,768]{0,1:T(8,128)(2,1)}, u32[]{:S(2)}, u32[]{:S(2)}) collective-permute-start(bf16[2048,768]{0,1:T(8,128)(2,1)} %copy.67), channel_id=1, source_target_pairs={{0,1},{1,0},{2,3},{3,2},{4,5},{5,4},{6,7},{7,6},{8,9},{9,8},{10,11... | collective-permute-start | bytes 9437192 | tf_op jit(solution)/shard_map/ppermute | solution.py:35
  530.2 11.8 %collective-permute-start.56 = (bf16[192,768]{1,0:T(8,128)(2,1)S(1)}, bf16[192,768]{1,0:T(8,128)(2,1)S(1)}, u32[]{:S(2)}, u32[]{:S(2)}) collective-permute-start(bf16[192,768]{1,0:T(8,128)(2,1)S(1)} %select_convert_fusion.1), channel_id=1, source_target_pairs={{0,8},{4,12},{8,0},{12,4},{16,24},{20,28},{24,16},{28,20},{1,9},{5... | collective-permute-start | bytes 884744 | tf_op jit(solution)/shard_map/ppermute | solution.py:35
  531.1 5.9 collective-permute-start.47
  537.0 4.3 collective-permute-start.48
  541.4 3.8 collective-permute-start.49
  542.2 10.3 %collective-permute-start.57 = (bf16[96,768]{1,0:T(8,128)(2,1)S(1)}, bf16[96,768]{1,0:T(8,128)(2,1)S(1)}, u32[]{:S(2)}, u32[]{:S(2)}) collective-permute-start(bf16[96,768]{1,0:T(8,128)(2,1)S(1)} %select_convert_fusion.2), channel_id=1, source_target_pairs={{0,16},{4,20},{8,24},{12,28},{16,0},{20,4},{24,8},{28,12},{1,17},{... | collective-permute-start | bytes 442376 | tf_op jit(solution)/shard_map/ppermute | solution.py:35
  545.2 3.9 collective-permute-start.50
  549.1 2.8 collective-permute-start.51
  553.6 10.6 %collective-permute-start.58 = (bf16[96,768]{1,0:T(8,128)(2,1)S(1)}, bf16[96,768]{1,0:T(8,128)(2,1)S(1)}, u32[]{:S(2)}, u32[]{:S(2)}) collective-permute-start(bf16[96,768]{1,0:T(8,128)(2,1)S(1)} %add_convert_fusion.3), channel_id=1, source_target_pairs={{0,16},{4,20},{8,24},{12,28},{16,0},{20,4},{24,8},{28,12},{1,17},{... | collective-permute-start | bytes 442376 | tf_op jit(solution)/shard_map/ppermute | solution.py:35
  565.0 10.2 %collective-permute-start.59 = (bf16[192,768]{1,0:T(8,128)(2,1)}, bf16[192,768]{1,0:T(8,128)(2,1)}, u32[]{:S(2)}, u32[]{:S(2)}) collective-permute-start(bf16[192,768]{1,0:T(8,128)(2,1)} %pad_maximum_fusion.16), channel_id=1, source_target_pairs={{0,8},{4,12},{8,0},{12,4},{16,24},{20,28},{24,16},{28,20},{1,9},{5... | collective-permute-start | bytes 884744 | tf_op jit(solution)/shard_map/ppermute | solution.py:35
  576.3 15.1 %collective-permute-start.60 = (bf16[384,768]{1,0:T(8,128)(2,1)S(1)}, bf16[384,768]{1,0:T(8,128)(2,1)S(1)}, u32[]{:S(2)}, u32[]{:S(2)}) collective-permute-start(bf16[384,768]{1,0:T(8,128)(2,1)S(1)} %pad_maximum_fusion.10), channel_id=1, source_target_pairs={{0,4},{4,0},{8,12},{12,8},{16,20},{20,16},{24,28},{28,24},{1,5},{5... | collective-permute-start | bytes 1769480 | tf_op jit(solution)/shard_map/ppermute | solution.py:35
  586.1 37.6 %collective-permute-start.28 = (bf16[1024,768]{0,1:T(8,128)(2,1)}, bf16[1024,768]{0,1:T(8,128)(2,1)}, u32[]{:S(2)}, u32[]{:S(2)}) collective-permute-start(bf16[1024,768]{0,1:T(8,128)(2,1)} %slice.637), channel_id=1, source_target_pairs={{0,2},{1,3},{2,0},{3,1},{4,6},{5,7},{6,4},{7,5},{8,10},{9,11},{10,... | collective-permute-start | bytes 4718600 | tf_op jit(solution)/shard_map/ppermute | solution.py:35
  606.7 23.7 %collective-permute-start.61 = (bf16[96,768]{1,0:T(8,128)(2,1)}, bf16[96,768]{1,0:T(8,128)(2,1)}, u32[]{:S(2)}, u32[]{:S(2)}) collective-permute-start(bf16[96,768]{1,0:T(8,128)(2,1)} %get-tuple-element.161), channel_id=1, source_target_pairs={{0,1},{1,0},{2,3},{3,2},{4,5},{5,4},{6,7},{7,6},{8,9},{9,8},{10,11... | collective-permute-start | bytes 442376 | tf_op jit(solution)/shard_map/ppermute | solution.py:35
  606.7 23.7 %collective-permute-start.62 = (bf16[96,768]{1,0:T(8,128)(2,1)}, bf16[96,768]{1,0:T(8,128)(2,1)}, u32[]{:S(2)}, u32[]{:S(2)}) collective-permute-start(bf16[96,768]{1,0:T(8,128)(2,1)} %get-tuple-element.160), channel_id=1, source_target_pairs={{0,2},{1,3},{2,0},{3,1},{4,6},{5,7},{6,4},{7,5},{8,10},{9,11},{10,... | collective-permute-start | bytes 442376 | tf_op jit(solution)/shard_map/ppermute | solution.py:35
  607.9 22.6 %collective-permute-start.63 = (bf16[96,768]{1,0:T(8,128)(2,1)}, bf16[96,768]{1,0:T(8,128)(2,1)}, u32[]{:S(2)}, u32[]{:S(2)}) collective-permute-start(bf16[96,768]{1,0:T(8,128)(2,1)} %get-tuple-element.159), channel_id=1, source_target_pairs={{0,3},{1,2},{2,1},{3,0},{4,7},{5,6},{6,5},{7,4},{8,11},{9,10},{10,... | collective-permute-start | bytes 442376 | tf_op jit(solution)/shard_map/ppermute | solution.py:35
  (55 other events, 593.0 us)

commit v2 on v1

v2 whole, which is shorter than its diff:
```python
import math

import jax
import jax.numpy as jnp
from jax import lax
from jax.experimental import pallas as pl
from jax.experimental.pallas import tpu as pltpu
from jax.sharding import PartitionSpec as P

D = 768
HD = 64
FF = 3072
CLUSTER = 128
NS_STEPS = 3
ADAM_STEP = 10

schulz_coeffs = (3.4445, -4.775, 2.0315)
norm_epsilon = 1e-05
low = jnp.bfloat16
full = jnp.float32
LANES = 128
GROUP = 8
UNROLL = 32
score_scale = 1.0 / math.sqrt(HD)


def contract(left, right, left_axis, right_axis):
    return lax.dot_general(
        left, right, (((left_axis,), (right_axis,)), ((), ())), preferred_element_type=full
    )


def swap(value, axis, bit):
    size = lax.axis_size(axis)
    return lax.ppermute(value, axis, [(place, place ^ bit) for place in range(size)])


def seq_bits():
    bits = []
    bit = lax.axis_size("seq") // 2
    while bit >= 1:
        bits.append(bit)
        bit //= 2
    return bits


def seq_stages():
    return [("seq", bit) for bit in seq_bits()]


def far_stages():
    return [("seq", bit) for bit in seq_bits() if bit > 1]


def spread(shard, stages):
    for axis, bit in stages:
        shard = jnp.concatenate([shard, swap(shard, axis, bit)], axis=0)
    return shard


def fold(partial, stages):
    for axis, bit in reversed(stages):
        half = partial.shape[0] // 2
        kept = partial[:half]
        other = swap(partial[half:].astype(low), axis, bit)
        partial = kept.astype(full) + other.astype(full)
    return partial


def after(values, *tokens):
    return lax.optimization_barrier((values, tokens))[0]


def join_inner(near, other):
    rows = near.shape[0] // 2
    return jnp.concatenate([near[:rows], other[:rows], near[rows:], other[rows:]], axis=0)


def cut_outer(value):
    half = value.shape[0] // 2
    return value[:half], value[half:]


def cut_inner(value):
    rows = value.shape[0] // 4
    quarters = [value[part * rows : (part + 1) * rows] for part in range(4)]
    return tuple(jnp.concatenate(quarters[side::2], axis=0) for side in range(2))


def add_low(kept, other):
    return (kept.astype(full) + other.astype(full)).astype(low)


def fold_step(value, cut, axis, bit):
    kept, sent = cut(value)
    return add_low(kept, swap(sent, axis, bit))


def send_on(near, far_got):
    return swap(jnp.concatenate([near, far_got], axis=0), "ffn", 1)


def sides_of(stages):
    return [(axis, bit, (lax.axis_index(axis) & bit) != 0) for axis, bit in stages]


def sum_halves(value, stages):
    for axis, bit, side in reversed(sides_of(stages)):
        half = value.shape[0] // 2
        kept = jnp.where(side, value[half:], value[:half])
        sent = jnp.where(side, value[:half], value[half:]).astype(low)
        value = kept.astype(full) + swap(sent, axis, bit).astype(full)
    return value.astype(low)


def spread_halves(value, stages):
    for axis, bit, side in sides_of(stages):
        other = swap(value, axis, bit)
        value = jnp.concatenate([jnp.where(side, other, value), jnp.where(side, value, other)], axis=0)
    return value


def move_rows(perm_ref, head, base, count, move):
    def step(turn, carry):
        for inner in range(UNROLL):
            row = turn * UNROLL + inner
            move(perm_ref[head, base + row], row)
        return carry

    lax.fori_loop(0, count // UNROLL, step, 0)


def softmax_rows(scores):
    peak = jnp.max(scores, axis=1, keepdims=True)
    powers = jnp.exp((scores - peak) * score_scale)
    return powers * (1.0 / jnp.sum(powers, axis=1, keepdims=True))


def left_half(rows):
    return lax.broadcasted_iota(jnp.int32, (rows, LANES), 1) < HD


def attend_kernel(
    perm_ref, x0, x1, x2, x3, w_ref, own_ref, near_ref, far_ref, qv_ref, key_ref, qv_rows, key_rows, qv_got, key_got, o_got, o_rows
):
    here = x0.shape[0]
    seq_len = 4 * here
    half = here // 2
    for block, x_ref in enumerate((x0, x1, x2, x3)):
        for cut in range(2):
            both = contract(x_ref[pl.ds(cut * half, half), :], w_ref[...], 1, 1)
            rows = pl.ds(block * here + cut * half, half)
            qv_rows[rows, :] = both[:, :LANES]
            key_rows[rows, :] = both[:, LANES:]
    count = GROUP * CLUSTER

    def group(turn, carry):
        base = turn * count

        def fetch(index, row):
            qv_got[pl.ds(row, 1), :] = qv_rows[pl.ds(index, 1), :]
            key_got[pl.ds(row, 1), :] = key_rows[pl.ds(index, 1), :]

        move_rows(perm_ref, 0, base, count, fetch)
        spans = [slice(part * CLUSTER, (part + 1) * CLUSTER) for part in range(GROUP)]
        qvs = [qv_got[span].astype(low) for span in spans]
        keys = [key_got[span].astype(low) for span in spans]
        for part in range(GROUP):
            rows = pl.ds(base + part * CLUSTER, CLUSTER)
            qv_ref[rows, :] = qvs[part]
            key_ref[rows, :] = keys[part]
        scores = [contract(qv, key, 1, 1) for qv, key in zip(qvs, keys)]
        probs = [softmax_rows(score).astype(low) for score in scores]
        for part in range(GROUP):
            o_got[spans[part]] = contract(probs[part], qvs[part], 1, 0)

        def place(index, row):
            o_rows[pl.ds(index, 1), :] = o_got[pl.ds(row, 1), :]

        move_rows(perm_ref, 0, base, count, place)
        return carry

    lax.fori_loop(0, seq_len // count, group, 0)
    outs = (own_ref, near_ref, far_ref.at[pl.ds(0, half), :], far_ref.at[pl.ds(half, half), :])
    for block, out_ref in enumerate(outs):
        top = pltpu.roll(o_rows[pl.ds(block * here, half), :], HD, 1)
        bottom = o_rows[pl.ds(block * here + half, half), :]
        out_ref[...] = jnp.where(left_half(half), top, bottom).astype(low)


def vmem(*shape):
    return pl.BlockSpec(shape, memory_space=pltpu.VMEM)


def attend(perm, tokens, weights, name):
    seq_len = perm.shape[1]
    here = tokens[0].shape[0]
    rows_got = pltpu.VMEM((GROUP * CLUSTER, LANES), full)
    rows_all = pltpu.VMEM((seq_len, LANES), full)
    in_vmem = pl.BlockSpec(memory_space=pltpu.VMEM)
    return pl.pallas_call(
        attend_kernel,
        in_specs=[pl.BlockSpec(memory_space=pltpu.SMEM)] + [in_vmem] * 5,
        out_specs=[in_vmem] * 5,
        out_shape=[
            jax.ShapeDtypeStruct((here // 2, LANES), low),
            jax.ShapeDtypeStruct((here // 2, LANES), low),
            jax.ShapeDtypeStruct((here, LANES), low),
            jax.ShapeDtypeStruct((seq_len, LANES), low),
            jax.ShapeDtypeStruct((seq_len, LANES), low),
        ],
        scratch_shapes=[rows_all, rows_all, rows_got, rows_got, rows_got, rows_all],
        compiler_params=pltpu.CompilerParams(vmem_limit_bytes=40 * 2**20),
        cost_estimate=pl.CostEstimate(flops=18 * 10**9, bytes_accessed=1000, transcendentals=0),
        name=name,
    )(perm, *tokens, weights)


def attend_back_kernel(heads, *refs):
    perm_ref = refs[0]
    per_head = [refs[1 + 6 * head : 7 + 6 * head] for head in range(heads)]
    x_refs = refs[1 + 6 * heads : 5 + 6 * heads]
    outs = refs[5 + 6 * heads : 5 + 8 * heads]
    d_rows, d_got, dqv_got, dkey_got, dqv_rows, dkey_rows = refs[5 + 8 * heads :]
    here = x_refs[0].shape[0]
    seq_len = 4 * here
    half = here // 2
    count = GROUP * CLUSTER
    for head in range(heads):
        qv_ref, key_ref, *do_refs = per_head[head]
        gw_ref, dboth_ref = outs[2 * head : 2 * head + 2]
        for block, do_ref in enumerate(do_refs):
            rows = do_ref[...].astype(full)
            top = pltpu.roll(rows, HD, 1)
            d_rows[pl.ds(block * here, half), :] = jnp.where(left_half(half), 0.0, top)
            d_rows[pl.ds(block * here + half, half), :] = jnp.where(left_half(half), 0.0, rows)

        def group(turn, carry):
            base = turn * count

            def fetch(index, row):
                d_got[pl.ds(row, 1), :] = d_rows[pl.ds(index, 1), :]

            move_rows(perm_ref, head, base, count, fetch)
            spans = [slice(part * CLUSTER, (part + 1) * CLUSTER) for part in range(GROUP)]
            rows = [pl.ds(base + part * CLUSTER, CLUSTER) for part in range(GROUP)]
            qvs = [qv_ref[span, :] for span in rows]
            keys = [key_ref[span, :] for span in rows]
            dos = [d_got[span].astype(low) for span in spans]
            scores = [contract(qv, key, 1, 1) for qv, key in zip(qvs, keys)]
            dprobs = [contract(do, qv, 1, 1) for do, qv in zip(dos, qvs)]
            probs = [softmax_rows(score) for score in scores]
            probs_low = [prob.astype(low) for prob in probs]
            dscores = [
                (prob * (dprob - jnp.sum(prob * dprob, axis=1, keepdims=True))).astype(low)
                for prob, dprob in zip(probs, dprobs)
            ]
            for part in range(GROUP):
                dqv_got[spans[part]] = score_scale * contract(dscores[part], keys[part], 1, 0) + contract(
                    probs_low[part], dos[part], 0, 0
                )
                dkey_got[spans[part]] = score_scale * contract(dscores[part], qvs[part], 0, 0)

            def place(index, row):
                dqv_rows[pl.ds(index, 1), :] = dqv_got[pl.ds(row, 1), :]
                dkey_rows[pl.ds(index, 1), :] = dkey_got[pl.ds(row, 1), :]

            move_rows(perm_ref, head, base, count, place)
            return carry

        lax.fori_loop(0, seq_len // count, group, 0)

        gw = jnp.zeros((2 * LANES, D), full)
        for block, x_ref in enumerate(x_refs):
            rows = pl.ds(block * here, here)
            dboth_ref[rows, :LANES] = dqv_rows[rows, :].astype(low)
            dboth_ref[rows, LANES:] = dkey_rows[rows, :].astype(low)
            gw = gw + contract(dboth_ref[rows, :], x_ref[...], 0, 0)
        gw_ref[...] = gw.astype(low)


def attend_back(perm, head, kept, do, tokens):
    seq_len = perm.shape[1]
    here = tokens[0].shape[0]
    half = here // 2
    rows_got = pltpu.VMEM((GROUP * CLUSTER, LANES), full)
    rows_all = pltpu.VMEM((seq_len, LANES), full)
    in_vmem = pl.BlockSpec(memory_space=pltpu.VMEM)
    own, near, far = do

    def part(turn):
        return pl.BlockSpec((None, None, half, LANES), lambda step: (turn, head, 0, 0))

    return pl.pallas_call(
        lambda *refs: attend_back_kernel(1, *refs),
        grid=(1,),
        in_specs=[pl.BlockSpec(memory_space=pltpu.SMEM)]
        + [in_vmem] * 2
        + [part(0), part(0), part(0), part(1)]
        + [in_vmem] * 4,
        out_specs=[in_vmem] * 2,
        out_shape=[
            jax.ShapeDtypeStruct((2 * LANES, D), low),
            jax.ShapeDtypeStruct((seq_len, 2 * LANES), low),
        ],
        scratch_shapes=[rows_all, rows_got, rows_got, rows_got, rows_all, rows_all],
        compiler_params=pltpu.CompilerParams(vmem_limit_bytes=40 * 2**20),
        cost_estimate=pl.CostEstimate(flops=22 * 10**9, bytes_accessed=1000, transcendentals=0),
        name="attend_back",
    )(perm, *kept, own, near, far, near, *tokens)


def token_grad_kernel(d0, d1, d2, w_ref, kept_ref, sent_ref):
    sums = None
    for head, d_ref in enumerate((d0, d1, d2)):
        piece = contract(d_ref[...], w_ref[pl.ds(head * 2 * LANES, 2 * LANES), :], 1, 0)
        sums = piece if sums is None else sums + piece

    @pl.when(pl.program_id(0) < 2)
    def _():
        sent_ref[...] = sums.astype(low)

    @pl.when(pl.program_id(0) >= 2)
    def _():
        kept_ref[...] = sums.astype(low)


def token_grad(dboth, weights, here):
    split = 2
    rows = here // split

    def from_block(slot, part):
        return ((2 * (slot % 2) + 1 - slot // 2) * split + part, 0)

    def to_sent(slot, part):
        return (jnp.minimum(slot * split + part, 2 * split - 1), 0)

    def to_kept(slot, part):
        return (jnp.maximum(slot * split + part - 2 * split, 0), 0)

    return pl.pallas_call(
        token_grad_kernel,
        grid=(4, split),
        in_specs=[pl.BlockSpec((rows, 2 * LANES), from_block)] * 3
        + [pl.BlockSpec((6 * LANES, D), lambda slot, part: (0, 0))],
        out_specs=[pl.BlockSpec((rows, D), to_kept), pl.BlockSpec((rows, D), to_sent)],
        out_shape=[jax.ShapeDtypeStruct((2 * here, D), low)] * 2,
        compiler_params=pltpu.CompilerParams(vmem_limit_bytes=32 * 2**20),
        cost_estimate=pl.CostEstimate(flops=8 * 10**9, bytes_accessed=1000, transcendentals=0),
        name="token_grad",
    )(*dboth, weights)


def row_mean(value):
    return jnp.mean(value, axis=-1, keepdims=True)


def norm_forward(inputs, gains, biases):
    center = inputs - row_mean(inputs)
    inv_std = lax.rsqrt(row_mean(center * center) + norm_epsilon)
    normed = center * inv_std
    return (normed * gains + biases, normed, inv_std)


def norm_backward(upstream, normed, inv_std, gains):
    scaled = upstream * gains
    inside = scaled - row_mean(scaled) - normed * row_mean(scaled * normed)
    sums = [jnp.sum(upstream * normed, axis=0, keepdims=True), jnp.sum(upstream, axis=0, keepdims=True)]
    return (inside * inv_std, sums)


def layer_kernel(heads, *refs):
    o_refs = refs[: 4 * heads]
    (x_ref, cot_ref, wo_ref, norm_ref) = refs[4 * heads : 4 * heads + 4]
    up_refs = refs[4 * heads + 4 : 4 * heads + 8]
    down_refs = refs[4 * heads + 8 : 4 * heads + 12]
    outs = refs[4 * heads + 12 :]
    (do_own, do_near, do_far, block_ref, da_ref) = outs[:5]
    do_refs = (do_own.at[0], do_near.at[0], do_far.at[0], do_far.at[1])
    g_refs = outs[5:7]
    du_refs = outs[7:9]
    (df_ref, hb_ref, dattn_ref, o_ref, sums_ref, slope_ref) = outs[9:]
    part = x_ref.shape[1]
    rows = 2 * part
    left = left_half(part)

    def load(ref):
        return jnp.concatenate([ref[0], ref[1]], axis=0)

    def store(ref, value):
        ref[0] = value[:part]
        ref[1] = value[part:]

    packed = []
    for turn in range(4):
        for head in range(heads):
            packed.append(o_refs[4 * head + turn][...].astype(full))
    for pair in range(len(packed) // 2):
        first, second = packed[2 * pair], packed[2 * pair + 1]
        lanes = slice(pair * LANES, (pair + 1) * LANES)
        o_ref[0, :, lanes] = jnp.where(left, first, pltpu.roll(second, HD, 1)).astype(low)
        o_ref[1, :, lanes] = jnp.where(left, pltpu.roll(first, HD, 1), second).astype(low)

    gain_a, bias_a = norm_ref[0:1, :], norm_ref[1:2, :]
    gain_b, bias_b = norm_ref[2:3, :], norm_ref[3:4, :]
    residual = load(x_ref).astype(full) + contract(load(o_ref), wo_ref[...], 1, 0)
    hidden, normed_a, inv_a = norm_forward(residual, gain_a, bias_a)
    hidden_low = hidden.astype(low)
    store(hb_ref, hidden_low)
    branch = jnp.zeros((rows, D), full)
    quarter = FF // 4
    cuts = [slice(at, at + quarter) for at in range(0, FF, quarter)]
    for turn, cut in enumerate(cuts):
        side = turn // 2
        columns = slice(turn % 2 * quarter, (turn % 2 + 1) * quarter)
        preact = contract(hidden_low, up_refs[turn][...], 1, 1)
        cumulative = 0.5 * (1.0 + lax.erf(preact * 0.7071067811865476))
        gelu_low = (preact * cumulative).astype(low)
        slope_ref[:, cut] = cumulative + preact * (jnp.exp(-0.5 * preact * preact) * 0.3989422804014327)
        g_refs[side][0, :, columns] = gelu_low[:part]
        g_refs[side][1, :, columns] = gelu_low[part:]
        branch = branch + contract(gelu_low, down_refs[turn][...], 1, 0)
    outputs, normed_b, inv_b = norm_forward(hidden + branch, gain_b, bias_b)
    store(block_ref, outputs.astype(low))
    dsum, sums_b = norm_backward(load(cot_ref).astype(full), normed_b, inv_b, gain_b)
    dsum_low = dsum.astype(low)
    store(df_ref, dsum_low)
    dhidden = dsum
    for turn, cut in enumerate(cuts):
        side = turn // 2
        columns = slice(turn % 2 * quarter, (turn % 2 + 1) * quarter)
        dinner = (contract(dsum_low, down_refs[turn][...], 1, 1) * slope_ref[:, cut]).astype(low)
        du_refs[side][0, :, columns] = dinner[:part]
        du_refs[side][1, :, columns] = dinner[part:]
        dhidden = dhidden + contract(dinner, up_refs[turn][...], 1, 0)
    dresidual, sums_a = norm_backward(dhidden, normed_a, inv_a, gain_a)
    store(da_ref, dresidual)
    dattn = dresidual.astype(low)
    store(dattn_ref, dattn)
    dheads = contract(dattn, wo_ref[...], 1, 1)
    for pair in range(len(packed) // 2):
        lanes = slice(pair * LANES, (pair + 1) * LANES)
        top, bottom = dheads[:part, lanes], dheads[part:, lanes]
        both = (
            jnp.where(left, top, pltpu.roll(bottom, HD, 1)).astype(low),
            jnp.where(left, pltpu.roll(top, HD, 1), bottom).astype(low),
        )
        for side in range(2):
            turn, head = divmod(2 * pair + side, heads)
            do_refs[turn][head] = both[side]
    sums = jnp.concatenate(sums_a + sums_b, axis=0)

    @pl.when(pl.program_id(0) == 0)
    def _():
        sums_ref[...] = sums

    @pl.when(pl.program_id(0) > 0)
    def _():
        sums_ref[...] += sums


LAYER_STEPS = 4


def layer(o_got, block_in, block_cot, out_rows, up_rows, down_rows, norm_params):
    heads = len(o_got)
    here = block_in.shape[0]
    half = here // 2
    part = half // LAYER_STEPS
    once = pl.Buffered(1)

    def lead(count, width):
        return pl.BlockSpec((count, part, width), lambda step: (0, step, 0))

    def do_part(turns):
        return pl.BlockSpec((turns, heads, part, LANES), lambda step: (0, 0, step, 0))

    def still(rows):
        return pl.BlockSpec((rows, D), lambda step: (0, 0), pipeline_mode=once)

    def pairs(width, kind):
        return jax.ShapeDtypeStruct((2, half, width), kind)

    o_args = [piece for own, near, far in o_got for piece in (own, near, far, near)]
    later = pl.BlockSpec((part, LANES), lambda step: (step + LAYER_STEPS, 0))
    lanes = pl.BlockSpec((part, LANES), lambda step: (step, 0))
    two = lead(2, D)
    wide = lead(2, FF // 2)
    flat = pl.pallas_call(
        lambda *refs: layer_kernel(heads, *refs),
        grid=(LAYER_STEPS,),
        in_specs=[lanes, lanes, lanes, later] * heads
        + [two, two, still(D), still(4)]
        + [still(FF // 4)] * 8,
        out_specs=[do_part(1), do_part(1), do_part(2), two, two] + [wide] * 4 + [two] * 4
        + [pl.BlockSpec((4, D), lambda step: (0, 0))],
        out_shape=[jax.ShapeDtypeStruct((turns, heads, half, LANES), low) for turns in (1, 1, 2)]
        + [
            pairs(D, low),
            pairs(D, full),
            pairs(FF // 2, low),
            pairs(FF // 2, low),
            pairs(FF // 2, low),
            pairs(FF // 2, low),
            pairs(D, low),
            pairs(D, low),
            pairs(D, low),
            pairs(D, low),
            jax.ShapeDtypeStruct((4, D), full),
        ],
        scratch_shapes=[pltpu.VMEM((2 * part, FF), full)],
        compiler_params=pltpu.CompilerParams(vmem_limit_bytes=60 * 2**20),
        cost_estimate=pl.CostEstimate(flops=40 * 10**9, bytes_accessed=1000, transcendentals=0),
        name="layer",
    )(
        *o_args,
        block_in.reshape(2, half, D),
        block_cot.reshape(2, half, D),
        out_rows,
        norm_params,
        *up_rows,
        *down_rows,
    )
    tokenwise = [value.reshape(here, value.shape[2]) for value in flat[3:-1]]
    return flat[:3], tokenwise, flat[-1]


def weight_grad_kernel(left_ref, right_ref, *refs):
    value = contract(left_ref[...], right_ref[...], 0, 0)
    if len(refs) > 1:
        value = value + refs[0][...].astype(full)
    refs[-1][...] = value.astype(low)


def weight_grad(left, right, other=None):
    rows, width = left.shape
    part = 384
    args = [left, right]
    in_specs = [
        pl.BlockSpec((rows, part), lambda step: (0, step)),
        pl.BlockSpec((rows, D), lambda step: (0, 0)),
    ]
    block = pl.BlockSpec((part, D), lambda step: (step, 0))
    if other is not None:
        args.append(other)
        in_specs.append(block)
    return pl.pallas_call(
        weight_grad_kernel,
        grid=(width // part,),
        in_specs=in_specs,
        out_specs=block,
        out_shape=jax.ShapeDtypeStruct((width, D), low),
        compiler_params=pltpu.CompilerParams(vmem_limit_bytes=32 * 2**20),
        cost_estimate=pl.CostEstimate(flops=5 * 10**9, bytes_accessed=1000, transcendentals=0),
        name="weight_grad",
    )(*args)


def packed_gram(matrix):
    gram = contract(matrix, matrix, 0, 0)
    panels = [gram[: at + LANES, at : at + LANES] for at in range(0, D, LANES)]
    return jnp.concatenate(panels, axis=0)


def schulz_kernel(panels_ref, matrix_ref, out_ref, gram_ref, low_ref, mix_ref, once_ref, it_ref):
    one, two, three = schulz_coeffs
    blocks = D // LANES
    diagonal = lax.broadcasted_iota(jnp.int32, (LANES, LANES), 0) == lax.broadcasted_iota(
        jnp.int32, (LANES, LANES), 1
    )
    trace = jnp.zeros((1, 1), full)
    first = 0
    for col in range(blocks):
        for row in range(col + 1):
            block = panels_ref[first : first + LANES, :].astype(full)
            first += LANES
            rows = slice(row * LANES, (row + 1) * LANES)
            cols = slice(col * LANES, (col + 1) * LANES)
            gram_ref[rows, cols] = block
            if row < col:
                gram_ref[cols, rows] = block.T
            else:
                mine = jnp.where(diagonal, block, 0.0)
                trace = trace + jnp.sum(jnp.sum(mine, axis=1, keepdims=True), axis=0, keepdims=True)
    shrink = 1.0 / (jnp.sqrt(trace) + 1e-07)
    cuts = [slice(at, at + SCHULZ_CUT) for at in range(0, D, SCHULZ_CUT)]
    its = [slice(at, at + SCHULZ_ITS) for at in range(0, matrix_ref.shape[0], SCHULZ_ITS)]
    for cut in cuts:
        gram = gram_ref[cut, :] * (shrink * shrink)
        gram_ref[cut, :] = gram
        low_ref[cut, :] = gram.astype(low)
    for part in its:
        it_ref[part, :] = matrix_ref[part, :].astype(full) * shrink
    for step in range(NS_STEPS):
        for cut in cuts:
            square = contract(low_ref[cut, :], low_ref[...], 1, 0)
            mix_ref[cut, :] = (two * gram_ref[cut, :] + three * square).astype(low)
        for part in its:
            iterate = it_ref[part, :]
            iterate = one * iterate + contract(iterate.astype(low), mix_ref[...], 1, 0)
            if step < NS_STEPS - 1:
                it_ref[part, :] = iterate
            else:
                out_ref[part, :] = iterate.astype(low)
        if step < NS_STEPS - 1:
            for cut in cuts:
                once = contract(mix_ref[cut, :], low_ref[...], 1, 0)
                gram_ref[cut, :] = one * one * gram_ref[cut, :] + 2.0 * one * once
                once_ref[cut, :] = once.astype(low)
            for cut in cuts:
                gram = gram_ref[cut, :] + contract(once_ref[cut, :], mix_ref[...], 1, 0)
                gram_ref[cut, :] = gram
            for cut in cuts:
                low_ref[cut, :] = gram_ref[cut, :].astype(low)


SCHULZ_CUT = 256
SCHULZ_ITS = 192


def schulz(panels, matrix):
    in_vmem = pl.BlockSpec(memory_space=pltpu.VMEM)
    return pl.pallas_call(
        schulz_kernel,
        in_specs=[in_vmem, in_vmem],
        out_specs=in_vmem,
        out_shape=jax.ShapeDtypeStruct(matrix.shape, low),
        scratch_shapes=[
            pltpu.VMEM((D, D), full),
            pltpu.VMEM((D, D), low),
            pltpu.VMEM((D, D), low),
            pltpu.VMEM((D, D), low),
            pltpu.VMEM(matrix.shape, full),
        ],
        compiler_params=pltpu.CompilerParams(vmem_limit_bytes=32 * 2**20),
        cost_estimate=pl.CostEstimate(flops=8 * 10**9, bytes_accessed=1000, transcendentals=0),
        name="schulz",
    )(panels, matrix)


def rows_qkv(value):
    kinds, depth, heads, cut = value.shape
    return value.transpose(0, 2, 3, 1).reshape(kinds * heads * cut, depth)


def unrows_qkv(rows, shape):
    kinds, depth, heads, cut = shape
    return rows.reshape(kinds, heads, cut, depth).transpose(0, 3, 1, 2)


def on_device(
    block_in,
    block_cot,
    cluster_perm,
    w_qkv,
    w_out,
    w_up,
    w_down,
    mom_qkv,
    mom_out,
    mom_up,
    mom_down,
    norm_params,
    norm_first,
    norm_second,
):
    ffn_here = lax.axis_index("ffn")
    seqs = lax.axis_size("seq")
    n_bits = len(seq_bits())
    here = block_in.shape[0]
    half = here // 2
    heads = w_out.shape[0]
    cut = w_out.shape[1]
    seq_len = cluster_perm.shape[2]
    clusters = seq_len // CLUSTER

    weights = [rows_qkv(w_qkv), w_out.reshape(heads * cut, D), w_up.T, w_down]
    momenta = [rows_qkv(mom_qkv), mom_out.reshape(heads * cut, D), mom_up.T, mom_down]

    wide_qkv = weights[0].astype(low)
    far = seq_stages()[0]
    first = swap(wide_qkv, *far)
    tokens = [block_in, swap(block_in, "ffn", 1), swap(block_in, "ffn", 2)]
    tokens.append(swap(tokens[2], "ffn", 1))
    wide_qkv = jnp.concatenate([wide_qkv, first], axis=0)
    shards = (weights[2].astype(low), weights[1].astype(low), weights[3].astype(low))
    for stage in seq_stages()[1:]:
        if stage == seq_stages()[-1]:
            shards = after(shards, wide_qkv)
        wide_qkv = spread(wide_qkv, [stage])
    up_rows, out_wide, down_rows = shards
    wide_qkv = wide_qkv.reshape(seqs, 3, heads, cut, D).transpose(1, 2, 0, 3, 4).reshape(3, heads, HD, D)
    head_rows = jnp.stack(
        [wide_qkv[0], wide_qkv[2], wide_qkv[1], jnp.zeros_like(wide_qkv[1])], axis=1
    ).reshape(heads * 2 * LANES, D)
    for stage in far_stages():
        up_rows, out_wide, down_rows = [spread(value, [stage]) for value in (up_rows, out_wide, down_rows)]
    low_rows = down_rows.shape[0]
    shards = (up_rows, jnp.concatenate([down_rows, out_wide], axis=0))
    first_at = (("seq", 1), ("ffn", 2))
    then_at = (("ffn", 2), ("seq", 1))

    def swaps(values, places):
        return tuple(swap(value, *place) for value, place in zip(values, places))

    first_got = swaps(shards, first_at)
    own_got = swaps(shards, then_at)

    perm = jnp.bitwise_xor(cluster_perm[0], ffn_here * here)
    kept = []
    o_sent = []
    far_got = []
    near_got = []
    for head in range(heads):
        mine = head_rows[head * 2 * LANES : (head + 1) * 2 * LANES]
        order_rows = perm[head : head + 1]
        if head == 1:
            order_rows, first_got = after((order_rows, first_got), kept[0])
            other_got = swaps(first_got, then_at)
            up_pieces = [jnp.concatenate([shards[0], first_got[0]], axis=0)]
            up_pieces.append(swap(up_pieces[0], "ffn", 1))
        if head == 2:
            order_rows, own_got, far_got[0], up_pieces[1] = after(
                (order_rows, own_got, far_got[0], up_pieces[1]), kept[1]
            )
            near_got.append(send_on(o_sent[0][0], far_got[0][half:]))
            down_pieces = [jnp.concatenate([shards[1][:low_rows], own_got[1][:low_rows]], axis=0)]
            down_pieces.append(swap(down_pieces[0], "ffn", 1))
        own, near, far, qv, key = attend(order_rows, tokens, mine, "attend")
        kept.append((qv, key))
        o_sent.append((near, own))
        far_got.append(swap(far, "ffn", 2))
    other_got, far_got[1], near_got[0], down_pieces[1] = after(
        (other_got, far_got[1], near_got[0], down_pieces[1]), kept[2]
    )
    up_pieces.insert(1, jnp.concatenate([own_got[0], other_got[0]], axis=0))
    down_pieces.insert(1, jnp.concatenate([first_got[1][:low_rows], other_got[1][:low_rows]], axis=0))
    out_wide = jnp.concatenate(
        [value[low_rows:] for value in (shards[1], own_got[1], first_got[1], other_got[1])], axis=0
    )
    out_wide = spread(out_wide, [("ffn", 1)])
    up_pieces.append(swap(up_pieces[1], "ffn", 1))
    down_pieces.append(swap(down_pieces[1], "ffn", 1))
    near_got += [send_on(o_sent[head][0], far_got[head][half:]) for head in (1, 2)]
    o_got = [(sent[1], near, far) for sent, near, far in zip(o_sent, near_got, far_got)]
    up_rows, down_rows = up_pieces, down_pieces

    digits = (2, 2, 2) + (2,) * (n_bits - 1)
    order = (1, 0, 2 + n_bits, 2) + tuple(range(3, 2 + n_bits)) + (3 + n_bits, 4 + n_bits)
    back = tuple(sorted(range(len(order)), key=lambda at: order[at]))
    sizes = digits + (heads, cut, D)
    out_rows = out_wide.reshape(sizes).transpose(order).reshape(4 * heads * HD, D)

    do_blocks, tokenwise, norm_part = layer(
        o_got, block_in, block_cot, out_rows, up_rows, down_rows, norm_params
    )
    block_out, dresidual, gelu_a, gelu_b, dinner_a, dinner_b, dbranch, hidden_low, dattn, o_rows = tokenwise
    do_far = swap(do_blocks[2], "ffn", 2)
    do_got = (do_blocks[0], send_on(do_blocks[1], do_far[1:]), do_far)

    early_half = (cluster_perm[0] < seq_len // 2).astype(full).reshape(heads, clusters, CLUSTER)
    share = lax.dynamic_update_slice(
        jnp.zeros((4 * heads, clusters), full), jnp.sum(early_half, axis=2) / CLUSTER, (ffn_here * heads, 0)
    ).reshape(1, 4 * heads * clusters)
    small = jnp.concatenate([norm_part, jnp.pad(share, ((0, 0), (0, D - share.shape[1])))])

    down_sent = weight_grad(gelu_b, dbranch)
    up_sent = weight_grad(dinner_b, hidden_low)
    part_out = weight_grad(o_rows, dattn)
    part_out = part_out.reshape(tuple(sizes[at] for at in order)).transpose(back)
    part_out = part_out.reshape(4 * heads * HD, D)
    out_kept, out_sent = cut_outer(part_out)
    down_sum = weight_grad(gelu_a, dbranch, swap(down_sent, "ffn", 1))
    up_sum = weight_grad(dinner_a, hidden_low, swap(up_sent, "ffn", 1))
    out_sum = add_low(out_kept, swap(out_sent, "ffn", 1))
    small = small + swap(small, "ffn", 1)

    def quarters(value):
        rows = value.shape[0] // 4
        return [value[part * rows : (part + 1) * rows] for part in range(4)]

    low_sums = [jnp.concatenate(pair, axis=0) for pair in zip(quarters(down_sum), quarters(out_sum))]
    up_sums = [quarters(up_sum)[part] for part in (0, 2, 1, 3)]
    sums = list(zip(up_sums, low_sums))
    places = (("ffn", 2), ("seq", 1))
    then_places = (("seq", 1), ("ffn", 2))

    def cut_all(values):
        cuts = [cut_outer(value) for value in values]
        return [pair[0] for pair in cuts], jnp.concatenate([pair[1] for pair in cuts], axis=0)

    def add_all(kept_parts, got):
        values = []
        at = 0
        for part in kept_parts:
            values.append(add_low(part, got[at : at + part.shape[0]]))
            at += part.shape[0]
        return values

    do_got = after(do_got, sums)
    far_places = list(reversed(far_stages()))
    part_heads = []
    dboth = []
    for head in range(heads):
        if head == 0:
            first_got = swaps(sums[3], places)
            small_got = swap(small, "ffn", 2)
        if head == 1:
            do_got, first_got, small_got = after((do_got, first_got, small_got), part_heads[0])
            then_sent = [add_low(value, other) for value, other in zip(sums[2], first_got)]
            second_got = swaps(sums[1], places)
            then_got = swaps(then_sent, then_places)
            small = small + small_got
            small_got = swap(small, "seq", 1)
        if head == 2:
            do_got, second_got, then_got, small_got = after(
                (do_got, second_got, then_got, small_got), part_heads[1]
            )
            up_sum, low_sum = [
                (value.astype(full) + second.astype(full) + then.astype(full)).astype(low)
                for value, second, then in zip(sums[0], second_got, then_got)
            ]
            small = small + small_got
            rest, sent = cut_all([up_sum, low_sum[:low_rows], low_sum[low_rows:]])
            rest_got = swap(sent, *far_places[0])
            small_got = swap(small, *far_places[0])
        gw, both = attend_back(perm[head : head + 1], head, kept[head], do_got, tokens)
        part_heads.append(gw)
        dboth.append(both)
    rest_got, small_got, dboth = after((rest_got, small_got, dboth), part_heads[2])
    rest = add_all(rest, rest_got)
    small = small + small_got
    part_qkv = jnp.stack(part_heads).reshape(heads, 4, HD, D)
    part_qkv = jnp.stack([part_qkv[:, 0], part_qkv[:, 2], part_qkv[:, 1]])
    part_qkv = part_qkv.reshape(3, heads, seqs, cut, D).transpose(2, 0, 1, 3, 4)
    qkv_kept, qkv_sent = cut_outer(part_qkv.reshape(seqs * 3 * heads * cut, D))
    qkv_got = swap(qkv_sent, "seq", 1)
    gx_kept, gx_sent = token_grad(dboth, head_rows, here)
    qkv_got, gx_kept, gx_sent = after((qkv_got, gx_kept, gx_sent))
    qkv_sum = add_low(qkv_kept, qkv_got)
    gx_got = swap(gx_sent, "ffn", 1)
    for turn, place in enumerate(far_places):
        qkv_kept, qkv_sent = cut_outer(qkv_sum)
        qkv_got = swap(qkv_sent, *place)
        if turn + 1 < len(far_places):
            kept_parts, sent = cut_all(rest)
            rest_got = swap(sent, *far_places[turn + 1])
            small_got = swap(small, *far_places[turn + 1])
            qkv_got, rest_got, small_got, gx_got = after((qkv_got, rest_got, small_got, gx_got))
            rest = add_all(kept_parts, rest_got)
            small = small + small_got
        qkv_sum = add_low(qkv_kept, qkv_got)
        if turn == 0:
            gx_kept, gx_sent = cut_outer(add_low(gx_kept, gx_got))
            gx_cuts = cut_outer(gx_sent)
            gx_first = swap(gx_cuts[0], "ffn", 2)
    up_sum, down_sum, out_sum = rest
    grad_qkv, grad_out, grad_up, grad_down = [
        value.astype(full) for value in (qkv_sum, out_sum, up_sum, down_sum)
    ]
    grad_norm = small[:4]
    occupancy = small[4, : 4 * heads * clusters].reshape(4 * heads, clusters)

    grads = [grad_qkv, grad_out, grad_up, grad_down]
    moments = [0.5 * mom + grad for mom, grad in zip(momenta, grads)]
    most = max(moment.shape[0] for moment in moments)
    stack = jnp.stack(
        [jnp.pad(moment.astype(low), ((0, most - moment.shape[0]), (0, 0))) for moment in moments]
    )

    def pick(turn):
        return lax.dynamic_index_in_dim(stack, jnp.bitwise_xor(ffn_here, turn), keepdims=False)

    picked = [swap(pick(turn), "ffn", turn) for turn in (1, 2, 3)]
    picked, gx_first = after((picked, gx_first))
    matrix = jnp.concatenate([pick(0)] + picked, axis=0)
    gx_second = swap(gx_cuts[1], "ffn", 2)
    panels = sum_halves(packed_gram(matrix), seq_stages())
    panels = spread_halves(panels, seq_stages())
    panels, gx_second = after((panels, gx_second))
    gx_other = jnp.concatenate([gx_first, gx_second], axis=0)
    steps = schulz(panels, matrix).reshape(4, most, D)
    input_grad = dresidual + (gx_kept.astype(full) + gx_other.astype(full))
    home = jnp.stack([steps[0]] + [swap(steps[turn], "ffn", turn) for turn in (1, 2, 3)])
    step_rates = (
        0.5 * math.sqrt(3.0),
        0.5 * math.sqrt(CLUSTER / 3.0),
        0.5 * math.sqrt(FF / D),
        0.5,
    )
    masters = []
    for member in range(4):
        own = lax.dynamic_index_in_dim(home, jnp.bitwise_xor(ffn_here, member), keepdims=False)
        own = own[: moments[member].shape[0]].astype(full)
        masters.append(weights[member] - step_rates[member] * own)

    first_fix = 1.0 - 0.9**ADAM_STEP
    second_fix = 1.0 - 0.999**ADAM_STEP
    first_new = 0.9 * norm_first + 0.1 * grad_norm
    second_new = 0.999 * norm_second + 0.001 * grad_norm * grad_norm
    first_hat = first_new / first_fix
    second_hat = second_new / second_fix
    norm_new = norm_params - 0.5 * (first_hat / (jnp.sqrt(second_hat) + 1e-08) + 0.01 * norm_params)

    def shaped(four):
        return (unrows_qkv(four[0], w_qkv.shape), four[1].reshape(w_out.shape), four[2].T, four[3])

    return (
        (block_out, input_grad)
        + shaped(grads)
        + (grad_norm,)
        + shaped(moments)
        + shaped(masters)
        + (first_new, second_new, norm_new, occupancy)
    )


def solution(mesh):
    rows = P(("seq", "ffn"), None)
    placed = (
        rows,
        rows,
        P("seq", "ffn", None),
        P(None, None, "ffn", "seq"),
        P("ffn", "seq", None),
        P(None, ("seq", "ffn")),
        rows,
        P(None, None, "ffn", "seq"),
        P("ffn", "seq", None),
        P(None, ("seq", "ffn")),
        rows,
        P(),
        P(),
        P(),
    )
    four = placed[3:7]
    return jax.shard_map(
        on_device,
        mesh=mesh,
        in_specs=placed,
        out_specs=(rows, rows) + four + (P(),) + four + four + (P(), P(), P(), P()),
        check_vma=False,
    )
```

time: 644 us -> 433 us (0.67)
  waiting for transfers between devices: 240 us -> 132 us
  matrix products: 76.3 us -> 0.81 us
  Pallas kernels: 130 us -> 184 us
  local copies, waits for them, and re-layouts: 65.2 us -> 21.6 us
  other arithmetic: 60.8 us -> 24 us
    ppermute x64 -> x65, waiting for transfers between devices: 240 us -> 132 us  [swap(): lax.ppermute(value, axis, [(place, place ^ bit) for place in range(size)])]
    dot_general x19 -> x1, matrix products: 76.3 us -> 0.81 us  [contract(): lax.dot_general(left, right, (((left_axis,), (right_axis,)), ((), ())), p...]
    pallas_call x2 -> x14, Pallas kernels: 130 us -> 184 us  [the longest x3 57.5 us: attend_back(): pl.pallas_call(lambda *refs: attend_back_kernel(1, *refs), grid=(1,), in_...]
    add x23 -> x8, other arithmetic: 18.4 us -> 2.3 us  [the longest x1 2.13 us: on_device(): input_grad = dresidual + (gx_kept.astype(full) + gx_other.astype(full))]
    unnamed x126 -> x173, local copies, waits for them, and re-layouts: 27.2 us -> 15.3 us
    slice x28 -> x25, local copies, waits for them, and re-layouts: 13.7 us -> 2.49 us  [the longest x11 1.88 us: cut_outer(): return (value[:half], value[half:])]
    concatenate x6 -> x1, local copies, waits for them, and re-layouts: 7.22 us -> 0.04 us  [spread(): shard = jnp.concatenate([shard, swap(shard, axis, bit)], axis=0)]
    ppermute x64 -> x65, starting transfers between devices: 60 us -> 59.6 us  [swap(): lax.ppermute(value, axis, [(place, place ^ bit) for place in range(size)])]
  transfers between devices with their start and end apart: 64 -> 65, of which waited for: 32 -> 25; matrix products, arithmetic and copies ran while one was open for 19% -> 6% of each run, Pallas kernels for 20% -> 31%
where the time goes in v2:
time: 433 us; the launch traced here: 425 us
  Pallas kernels  184 us (42%)
  waiting for transfers between devices  132 us (30%)
  starting transfers between devices  59.6 us (14%)
  other arithmetic  24 us (6%)
  local copies, waits for them, and re-layouts  21.6 us (5%)
    ppermute x65, waiting for transfers between devices, swap(): lax.ppermute(value, axis, [(place, place ^ bit) for place in range(size)])  132 us
    ppermute x65, starting transfers between devices, swap(): lax.ppermute(value, axis, [(place, place ^ bit) for place in range(size)])  59.6 us
    pallas_call x3, Pallas kernels, attend_back(): pl.pallas_call(lambda *refs: attend_back_kernel(1, *refs), grid=(1,), in_...  57.5 us
    pallas_call x3, Pallas kernels, attend(): pl.pallas_call(attend_kernel, in_specs=[pl.BlockSpec(memory_space=pltpu.S...  51.3 us
    pallas_call x1, Pallas kernels, layer(): pl.pallas_call(lambda *refs: layer_kernel(heads, *refs), grid=(LAYER_STEP...  39.1 us
    pallas_call x5, Pallas kernels, weight_grad(): pl.pallas_call(weight_grad_kernel, grid=(width // part,), in_specs=in_spe...  19.9 us
    unnamed x173, local copies, waits for them, and re-layouts  15.3 us
  transfers between devices with their start and end apart: 65, of which 25 were waited for; matrix products, arithmetic and copies ran while one was open for 6% of the time, Pallas kernels for 31%

profile of v2, /device:TPU:0, one launch (start us, length us, event | category | flops | bytes accessed | tf_op | source)
XLA Modules:
  0.0 424.7 jit_solution(5081437211397360427)
XLA Ops:
  0.7 3.0 collective-permute-start.1
  4.7 2.7 collective-permute-start.3
  10.2 3.3 collective-permute-done.3
  14.3 6.4 %collective-permute-done.4 = bf16[144,768]{1,0:T(8,128)(2,1)S(1)} collective-permute-done((bf16[144,768]{1,0:T(8,128)(2,1)S(1)}, bf16[144,768]{1,0:T(8,128)(2,1)S(1)}, u32[]{:S(2)}, u32[]{:S(2)}) %collective-permute-start.4) | collective-permute-done | bytes 221216 | tf_op jit(solution)/shard_map/ppermute | solution.py:35
  20.6 2.7 collective-permute-start.9
  23.7 2.7 collective-permute-start.6
  26.4 9.4 %collective-permute-done.11 = bf16[24,768]{1,0:T(8,128)(2,1)S(1)} collective-permute-done((bf16[24,768]{1,0:T(8,128)(2,1)S(1)}, bf16[24,768]{1,0:T(8,128)(2,1)S(1)}, u32[]{:S(2)}, u32[]{:S(2)}) %collective-permute-start.11) | collective-permute-done | bytes 36896 | tf_op jit(solution)/shard_map/ppermute | solution.py:35
  35.8 1.5 collective-permute-start.5
  38.0 1.5 collective-permute-start.10
  39.7 7.1 %collective-permute-done.10 = bf16[192,768]{1,0:T(8,128)(2,1)S(1)} collective-permute-done((bf16[192,768]{1,0:T(8,128)(2,1)S(1)}, bf16[192,768]{1,0:T(8,128)(2,1)S(1)}, u32[]{:S(2)}, u32[]{:S(2)}) %collective-permute-start.10) | collective-permute-done | bytes 294944 | tf_op jit(solution)/shard_map/ppermute | solution.py:35
  48.8 5.2 %collective-permute-done.7 = bf16[192,768]{1,0:T(8,128)(2,1)S(1)} collective-permute-done((bf16[192,768]{1,0:T(8,128)(2,1)S(1)}, bf16[192,768]{1,0:T(8,128)(2,1)S(1)}, u32[]{:S(2)}, u32[]{:S(2)}) %collective-permute-start.7) | collective-permute-done | bytes 294944 | tf_op jit(solution)/shard_map/ppermute | solution.py:35
  54.0 2.1 collective-permute-start.18
  58.4 17.3 %attend.3 = (bf16[512,128]{1,0:T(8,128)(2,1)S(1)}, bf16[512,128]{1,0:T(8,128)(2,1)S(1)}, bf16[1024,128]{1,0:T(8,128)(2,1)S(1)}, bf16[4096,128]{1,0:T(8,128)(2,1)S(1)}, bf16[4096,128]{1,0:T(8,128)(2,1)S(1)}) custom-call(s32[1,4096]{1,0:T(1,128)S(1)} %get-tuple-element.276.perm_ref.refs_0_, bf16[1024,768]{1,0:T(8,128)(2,1)S(1)} %copy-done.2, ...), custom_call_target="tpu_custom_call" | custom-call | flops 17999998976 | bytes 1000 | tf_op jit(solution)/shard_map/attend/pallas_call | solution.py:201
  76.7 6.6 %collective-permute-done.8 = bf16[384,768]{1,0:T(8,128)(2,1)S(1)} collective-permute-done((bf16[384,768]{1,0:T(8,128)(2,1)S(1)}, bf16[384,768]{1,0:T(8,128)(2,1)S(1)}, u32[]{:S(2)}, u32[]{:S(2)}) %collective-permute-start.8) | collective-permute-done | bytes 589856 | tf_op jit(solution)/shard_map/ppermute | solution.py:35
  84.0 1.7 collective-permute-start.15
  85.7 17.0 %attend.4 = (bf16[512,128]{1,0:T(8,128)(2,1)S(1)}, bf16[512,128]{1,0:T(8,128)(2,1)S(1)}, bf16[1024,128]{1,0:T(8,128)(2,1)S(1)}, bf16[4096,128]{1,0:T(8,128)(2,1)S(1)}, bf16[4096,128]{1,0:T(8,128)(2,1)S(1)}) custom-call(s32[1,4096]{1,0:T(1,128)S(1)} %get-tuple-element.115.perm_ref.refs_0_, bf16[1024,768]{1,0:T(8,128)(2,1)S(1)} %copy-done.2, ...), custom_call_target="tpu_custom_call" | custom-call | flops 17999998976 | bytes 1000 | tf_op jit(solution)/shard_map/attend/pallas_call | solution.py:201
  102.8 1.6 collective-permute-start.14
  106.6 17.0 %attend.5 = (bf16[512,128]{1,0:T(8,128)(2,1)S(1)}, bf16[512,128]{1,0:T(8,128)(2,1)S(1)}, bf16[1024,128]{1,0:T(8,128)(2,1)S(1)}, bf16[4096,128]{1,0:T(8,128)(2,1)S(1)}, bf16[4096,128]{1,0:T(8,128)(2,1)S(1)}) custom-call(s32[1,4096]{1,0:T(1,128)S(1)} %get-tuple-element.123.perm_ref.refs_0_, bf16[1024,768]{1,0:T(8,128)(2,1)S(1)} %copy-done.2, ...), custom_call_target="tpu_custom_call" | custom-call | flops 17999998976 | bytes 1000 | tf_op jit(solution)/shard_map/attend/pallas_call | solution.py:201
  123.7 1.6 collective-permute-start.24
  127.2 4.9 %collective-permute-done.24.refs_10_ = bf16[1024,128]{1,0:T(8,128)(2,1)S(1)} collective-permute-done((bf16[1024,128]{1,0:T(8,128)(2,1)S(1)}, bf16[1024,128]{1,0:T(8,128)(2,1)S(1)}, u32[]{:S(2)}, u32[]{:S(2)}) %collective-permute-start.24) | collective-permute-done | bytes 262176 | tf_op jit(solution)/shard_map/ppermute | solution.py:35
  135.5 39.1 %layer.1 = (bf16[1,3,512,128]{3,2,1,0:T(8,128)(2,1)}, bf16[1,3,512,128]{3,2,1,0:T(8,128)(2,1)}, bf16[2,3,512,128]{3,2,1,0:T(8,128)(2,1)}, bf16[2,512,768]{2,1,0:...) custom-call(bf16[512,128]{1,0:T(8,128)(2,1)} %copy-done.35, ...), custom_call_target="tpu_custom_call" | custom-call | flops 40000000000 | bytes 1000 | tf_op jit(solution)/shard_map/layer/pallas_call | solution.py:489
  174.6 1.9 copy-done.11
  176.5 1.4 copy-done.14
  177.9 4.5 %weight_grad.7 = bf16[1536,768]{1,0:T(8,128)(2,1)} custom-call(bf16[1024,1536]{1,0:T(8,128)(2,1)S(1)} %bitcast.151, bf16[1024,768]{1,0:T(8,128)(2,1)S(1)} %bitcast.154), custom_call_target="tpu_custom_call" | custom-call | flops 5000000000 | bytes 1000 | tf_op jit(solution)/shard_map/weight_grad/pallas_call | solution.py:547
  182.6 1.9 weight_grad.9
  186.8 4.5 %weight_grad.5 = bf16[1536,768]{1,0:T(8,128)(2,1)} custom-call(bf16[1024,1536]{1,0:T(8,128)(2,1)S(1)} %bitcast.150, bf16[1024,768]{1,0:T(8,128)(2,1)S(1)} %bitcast.152), custom_call_target="tpu_custom_call" | custom-call | flops 5000000000 | bytes 1000 | tf_op jit(solution)/shard_map/weight_grad/pallas_call | solution.py:547
  192.0 1.5 collective-permute-start.29
  193.6 1.3 copy.35
  195.9 1.6 collective-permute-start.37
  197.5 1.4 fusion
  199.0 13.2 %collective-permute-done.29.refs_5_ = bf16[2,3,512,128]{3,2,1,0:T(8,128)(2,1)S(1)} collective-permute-done((bf16[2,3,512,128]{3,2,1,0:T(8,128)(2,1)}, bf16[2,3,512,128]{3,2,1,0:T(8,128)(2,1)S(1)}, u32[]{:S(2)}, u32[]{:S(2)}) %collective-permute-start.29) | collective-permute-done | bytes 786464 | tf_op jit(solution)/shard_map/ppermute | solution.py:35
  212.4 4.9 %weight_grad.8 = bf16[1536,768]{1,0:T(8,128)(2,1)S(1)} custom-call(bf16[1024,1536]{1,0:T(8,128)(2,1)S(1)} %bitcast.149, bf16[1024,768]{1,0:T(8,128)(2,1)S(1)} %bitcast.155, bf16[1536,768]{1,0:T(8,128)(2,1)} %collective-permute-done.32.refs_0_), custom_call_target="tpu_custom_call" | custom-call | flops 5000000000 | bytes 1000 | tf_op jit(solution)/shard_map/weight_grad/pallas_call | solution.py:547
  217.9 1.3 copy-done.8
  219.7 4.1 weight_grad.6
  223.9 1.6 collective-permute-start.34
  226.4 19.2 %attend_back.3 = (bf16[256,768]{1,0:T(8,128)(2,1)S(1)}, bf16[4096,256]{1,0:T(8,128)(2,1)S(1)}) custom-call(s32[1,4096]{1,0:T(1,128)S(1)} %get-tuple-element.276.perm_ref.refs_0_, bf16[4096,128]{1,0:T(8,128)(2,1)S(1)} %copy-done.31, bf16[4096,128]{1,0:T(8,128)(2,1)S(1)} %copy-done.33, bf16[1,3,512,128]{3,2,1,0:T(8,128)(2,1)S(1)} %copy-done.34, ...), custom_call_target="tpu_custom_call" | custom-call | flops 22000001024 | bytes 1000 | tf_op jit(solution)/shard_map/attend_back/pallas_call | solution.py:294
  245.7 1.8 collective-permute-start.42
  247.7 1.6 collective-permute-start.41
  249.8 19.2 %attend_back.4 = (bf16[256,768]{1,0:T(8,128)(2,1)S(1)}, bf16[4096,256]{1,0:T(8,128)(2,1)S(1)}) custom-call(s32[1,4096]{1,0:T(1,128)S(1)} %get-tuple-element.115.perm_ref.refs_0_, bf16[4096,128]{1,0:T(8,128)(2,1)S(1)} %copy-done.27, bf16[4096,128]{1,0:T(8,128)(2,1)S(1)} %copy-done.29, bf16[1,3,512,128]{3,2,1,0:T(8,128)(2,1)S(1)} %copy-done.34, ...), custom_call_target="tpu_custom_call" | custom-call | flops 22000001024 | bytes 1000 | tf_op jit(solution)/shard_map/attend_back/pallas_call | solution.py:294
  270.3 1.3 collective-permute-start.45
  273.1 19.2 %attend_back.5 = (bf16[256,768]{1,0:T(8,128)(2,1)S(1)}, bf16[4096,256]{1,0:T(8,128)(2,1)S(1)}) custom-call(s32[1,4096]{1,0:T(1,128)S(1)} %get-tuple-element.123.perm_ref.refs_0_, bf16[4096,128]{1,0:T(8,128)(2,1)S(1)} %copy-done.23, bf16[4096,128]{1,0:T(8,128)(2,1)S(1)} %copy-done.25, bf16[1,3,512,128]{3,2,1,0:T(8,128)(2,1)S(1)} %copy-done.34, ...), custom_call_target="tpu_custom_call" | custom-call | flops 22000001024 | bytes 1000 | tf_op jit(solution)/shard_map/attend_back/pallas_call | solution.py:294
  292.5 1.8 collective-permute-start.43
  294.9 8.1 %token_grad.1 = (bf16[2048,768]{1,0:T(8,128)(2,1)S(1)}, bf16[2048,768]{1,0:T(8,128)(2,1)}) custom-call(bf16[4096,256]{1,0:T(8,128)(2,1)S(1)} %copy-done.19, bf16[4096,256]{1,0:T(8,128)(2,1)S(1)} %copy-done.21, bf16[4096,256]{1,0:T(8,128)(2,1)S(1)} %get-tuple-element.177.d2, bf16[768,768]{1,0:T(8,128)(2,1)S(1)} %bitcast.139), custom_call_target="tpu_custom_call" | custom-call | flops 8000000000 | bytes 1000 | tf_op jit(solution)/shard_map/token_grad/pallas_call | solution.py:341
  303.3 4.6 %collective-permute-start.48 = (f32[5,768]{1,0:T(8,128)S(1)}, f32[5,768]{1,0:T(8,128)S(1)}, u32[]{:S(2)}, u32[]{:S(2)}) collective-permute-start(f32[5,768]{1,0:T(8,128)S(1)} %add.149), channel_id=1, source_target_pairs={{0,16},{4,20},{8,24},{12,28},{16,0},{20,4},{24,8},{28,12},{1,17},{... | collective-permute-start | bytes 46088 | tf_op jit(solution)/shard_map/ppermute | solution.py:35
  312.2 9.5 %collective-permute-done.46 = bf16[144,768]{1,0:T(8,128)(2,1)} collective-permute-done((bf16[144,768]{1,0:T(8,128)(2,1)}, bf16[144,768]{1,0:T(8,128)(2,1)}, u32[]{:S(2)}, u32[]{:S(2)}) %collective-permute-start.46) | collective-permute-done | bytes 221216 | tf_op jit(solution)/shard_map/ppermute | solution.py:35
  321.7 5.4 %collective-permute-done.47 = bf16[216,768]{1,0:T(8,128)(2,1)} collective-permute-done((bf16[216,768]{1,0:T(8,128)(2,1)}, bf16[216,768]{1,0:T(8,128)(2,1)}, u32[]{:S(2)}, u32[]{:S(2)}) %collective-permute-start.47) | collective-permute-done | bytes 331808 | tf_op jit(solution)/shard_map/ppermute | solution.py:35
  328.3 2.7 add_convert_fusion
  333.5 1.4 fusion.10
  334.9 2.1 fusion.5
  338.1 1.5 collective-permute-start.52
  339.9 16.6 %collective-permute-done.52 = bf16[96,768]{1,0:T(8,128)(2,1)S(1)} collective-permute-done((bf16[96,768]{1,0:T(8,128)(2,1)S(1)}, bf16[96,768]{1,0:T(8,128)(2,1)S(1)}, u32[]{:S(2)}, u32[]{:S(2)}) %collective-permute-start.52) | collective-permute-done | bytes 147488 | tf_op jit(solution)/shard_map/ppermute | solution.py:35
  358.9 10.0 %collective-permute-done.55 = bf16[1344,128]{1,0:T(8,128)(2,1)S(1)} collective-permute-done((bf16[1344,128]{1,0:T(8,128)(2,1)S(1)}, bf16[1344,128]{1,0:T(8,128)(2,1)S(1)}, u32[]{:S(2)}, u32[]{:S(2)}) %collective-permute-start.55) | collective-permute-done | bytes 344096 | tf_op jit(solution)/shard_map/ppermute | solution.py:35
  369.8 5.7 %collective-permute-done.56 = bf16[672,128]{1,0:T(8,128)(2,1)S(1)} collective-permute-done((bf16[672,128]{1,0:T(8,128)(2,1)S(1)}, bf16[672,128]{1,0:T(8,128)(2,1)S(1)}, u32[]{:S(2)}, u32[]{:S(2)}) %collective-permute-start.56) | collective-permute-done | bytes 172064 | tf_op jit(solution)/shard_map/ppermute | solution.py:35
  375.7 2.3 collective-permute-start.57
  378.0 4.2 collective-permute-done.57
  382.2 1.4 collective-permute-start.58
  383.6 4.5 %collective-permute-done.58 = bf16[336,128]{1,0:T(8,128)(2,1)S(1)} collective-permute-done((bf16[336,128]{1,0:T(8,128)(2,1)S(1)}, bf16[336,128]{1,0:T(8,128)(2,1)S(1)}, u32[]{:S(2)}, u32[]{:S(2)}) %collective-permute-start.58) | collective-permute-done | bytes 86048 | tf_op jit(solution)/shard_map/ppermute | solution.py:35
  390.1 3.6 collective-permute-done.59
  395.2 5.8 %collective-permute-done.60 = bf16[1344,128]{1,0:T(8,128)(2,1)S(1)} collective-permute-done((bf16[1344,128]{1,0:T(8,128)(2,1)S(1)}, bf16[1344,128]{1,0:T(8,128)(2,1)S(1)}, u32[]{:S(2)}, u32[]{:S(2)}) %collective-permute-start.60) | collective-permute-done | bytes 344096 | tf_op jit(solution)/shard_map/ppermute | solution.py:35
  401.3 3.3 collective-permute-done.61
  404.6 8.5 %schulz.1 = bf16[384,768]{1,0:T(8,128)(2,1)S(1)} custom-call(bf16[2688,128]{1,0:T(8,128)(2,1)S(1)} %pad_maximum_fusion.10.panels_ref, bf16[384,768]{1,0:T(8,128)(2,1)S(1)} %pad_maximum_fusion.13.matrix_ref), custom_call_target="tpu_custom_call" | custom-call | flops 8000000000 | bytes 1000 | tf_op jit(solution)/shard_map/schulz/pallas_call | solution.py:623
  415.0 2.1 bitcast_add_fusion
  417.2 2.7 collective-permute-done.63
  419.9 2.3 collective-permute-done.64
  (366 shorter events, 50.6 us)
Async XLA Ops:
  0.7 38.9 %collective-permute-start.1 = (bf16[1024,768]{1,0:T(8,128)(2,1)}, bf16[1024,768]{1,0:T(8,128)(2,1)S(1)}, u32[]{:S(2)}, u32[]{:S(2)}) collective-permute-start(bf16[1024,768]{1,0:T(8,128)(2,1)} %refs_7_.5), channel_id=1, source_target_pairs={{0,2},{1,3},{2,0},{3,1},{4,6},{5,7},{6,4},{7,5},{8,10},{9,11},{10,... | collective-permute-start | bytes 4718600 | tf_op jit(solution)/shard_map/ppermute | solution.py:35
  3.7 54.0 %collective-permute-start = (bf16[1024,768]{1,0:T(8,128)(2,1)}, bf16[1024,768]{1,0:T(8,128)(2,1)}, u32[]{:S(2)}, u32[]{:S(2)}) collective-permute-start(bf16[1024,768]{1,0:T(8,128)(2,1)} %refs_7_.5), channel_id=1, source_target_pairs={{0,1},{1,0},{2,3},{3,2},{4,5},{5,4},{6,7},{7,6},{8,9},{9,8},{10,11... | collective-permute-start | bytes 4718600 | tf_op jit(solution)/shard_map/ppermute | solution.py:35
  4.7 8.8 %collective-permute-start.3 = (bf16[72,768]{1,0:T(8,128)(2,1)S(1)}, bf16[72,768]{1,0:T(8,128)(2,1)S(1)}, u32[]{:S(2)}, u32[]{:S(2)}) collective-permute-start(bf16[72,768]{1,0:T(8,128)(2,1)S(1)} %bitcast.160), channel_id=1, source_target_pairs={{0,16},{4,20},{8,24},{12,28},{16,0},{20,4},{24,8},{28,12},{1,17},{... | collective-permute-start | bytes 331784 | tf_op jit(solution)/shard_map/ppermute | solution.py:35
  13.5 7.1 %collective-permute-start.4 = (bf16[144,768]{1,0:T(8,128)(2,1)S(1)}, bf16[144,768]{1,0:T(8,128)(2,1)S(1)}, u32[]{:S(2)}, u32[]{:S(2)}) collective-permute-start(bf16[144,768]{1,0:T(8,128)(2,1)S(1)} %pad_maximum_fusion.25), channel_id=1, source_target_pairs={{0,8},{4,12},{8,0},{12,4},{16,24},{20,28},{24,16},{28,20},{1,9},{5... | collective-permute-start | bytes 663560 | tf_op jit(solution)/shard_map/ppermute | solution.py:35
  20.6 16.7 %collective-permute-start.9 = (bf16[96,768]{1,0:T(8,128)(2,1)S(1)}, bf16[96,768]{1,0:T(8,128)(2,1)S(1)}, u32[]{:S(2)}, u32[]{:S(2)}) collective-permute-start(bf16[96,768]{1,0:T(8,128)(2,1)S(1)} %convert_element_type.258), channel_id=1, source_target_pairs={{0,16},{4,20},{8,24},{12,28},{16,0},{20,4},{24,8},{28,12},{1,17},{... | collective-permute-start | bytes 442376 | tf_op jit(solution)/shard_map/ppermute | solution.py:35
  23.4 12.5 %collective-permute-start.11 = (bf16[24,768]{1,0:T(8,128)(2,1)S(1)}, bf16[24,768]{1,0:T(8,128)(2,1)S(1)}, u32[]{:S(2)}, u32[]{:S(2)}) collective-permute-start(bf16[24,768]{1,0:T(8,128)(2,1)S(1)} %convert_bitcast_fusion.3), channel_id=1, source_target_pairs={{0,16},{4,20},{8,24},{12,28},{16,0},{20,4},{24,8},{28,12},{1,17},{... | collective-permute-start | bytes 110600 | tf_op jit(solution)/shard_map/ppermute | solution.py:35
  23.7 14.3 %collective-permute-start.6 = (bf16[96,768]{1,0:T(8,128)(2,1)S(1)}, bf16[96,768]{1,0:T(8,128)(2,1)S(1)}, u32[]{:S(2)}, u32[]{:S(2)}) collective-permute-start(bf16[96,768]{1,0:T(8,128)(2,1)S(1)} %bitcast_convert_fusion), channel_id=1, source_target_pairs={{0,16},{4,20},{8,24},{12,28},{16,0},{20,4},{24,8},{28,12},{1,17},{... | collective-permute-start | bytes 442376 | tf_op jit(solution)/shard_map/ppermute | solution.py:35
  35.8 20.3 %collective-permute-start.5 = (bf16[288,768]{1,0:T(8,128)(2,1)S(1)}, bf16[288,768]{1,0:T(8,128)(2,1)S(1)}, u32[]{:S(2)}, u32[]{:S(2)}) collective-permute-start(bf16[288,768]{1,0:T(8,128)(2,1)S(1)} %pad_maximum_fusion.15), channel_id=1, source_target_pairs={{0,4},{4,0},{8,12},{12,8},{16,20},{20,16},{24,28},{28,24},{1,5},{5... | collective-permute-start | bytes 1327112 | tf_op jit(solution)/shard_map/ppermute | solution.py:35
  37.3 10.8 %collective-permute-start.12 = (bf16[48,768]{1,0:T(8,128)(2,1)S(1)}, bf16[48,768]{1,0:T(8,128)(2,1)S(1)}, u32[]{:S(2)}, u32[]{:S(2)}) collective-permute-start(bf16[48,768]{1,0:T(8,128)(2,1)S(1)} %pad_maximum_fusion.27), channel_id=1, source_target_pairs={{0,8},{4,12},{8,0},{12,4},{16,24},{20,28},{24,16},{28,20},{1,9},{5... | collective-permute-start | bytes 221192 | tf_op jit(solution)/shard_map/ppermute | solution.py:35
  38.0 8.8 %collective-permute-start.10 = (bf16[192,768]{1,0:T(8,128)(2,1)S(1)}, bf16[192,768]{1,0:T(8,128)(2,1)S(1)}, u32[]{:S(2)}, u32[]{:S(2)}) collective-permute-start(bf16[192,768]{1,0:T(8,128)(2,1)S(1)} %pad_maximum_fusion.21), channel_id=1, source_target_pairs={{0,8},{4,12},{8,0},{12,4},{16,24},{20,28},{24,16},{28,20},{1,9},{5... | collective-permute-start | bytes 884744 | tf_op jit(solution)/shard_map/ppermute | solution.py:35
  39.6 18.6 %collective-permute-start.2 = (bf16[1024,768]{1,0:T(8,128)(2,1)S(1)}, bf16[1024,768]{1,0:T(8,128)(2,1)S(1)}, u32[]{:S(2)}, u32[]{:S(2)}) collective-permute-start(bf16[1024,768]{1,0:T(8,128)(2,1)S(1)} %collective-permute-done.1.x2.refs_9_), channel_id=1, source_target_pairs={{0,1},{1,0},{2,3},{3,2},{4,5},{5,4},{6,7},{7,6},{8,9},{9,8},{10,11... | collective-permute-start | bytes 4718600 | tf_op jit(solution)/shard_map/ppermute | solution.py:35
  46.8 7.2 %collective-permute-start.7 = (bf16[192,768]{1,0:T(8,128)(2,1)S(1)}, bf16[192,768]{1,0:T(8,128)(2,1)S(1)}, u32[]{:S(2)}, u32[]{:S(2)}) collective-permute-start(bf16[192,768]{1,0:T(8,128)(2,1)S(1)} %pad_maximum_fusion.20), channel_id=1, source_target_pairs={{0,8},{4,12},{8,0},{12,4},{16,24},{20,28},{24,16},{28,20},{1,9},{5... | collective-permute-start | bytes 884744 | tf_op jit(solution)/shard_map/ppermute | solution.py:35
  48.2 35.1 %collective-permute-start.13 = (bf16[480,768]{1,0:T(8,128)(2,1)S(1)}, bf16[480,768]{1,0:T(8,128)(2,1)S(1)}, u32[]{:S(2)}, u32[]{:S(2)}) collective-permute-start(bf16[480,768]{1,0:T(8,128)(2,1)S(1)} %get-tuple-element.273), channel_id=1, source_target_pairs={{0,2},{1,3},{2,0},{3,1},{4,6},{5,7},{6,4},{7,5},{8,10},{9,11},{10,... | collective-permute-start | bytes 2211848 | tf_op jit(solution)/shard_map/ppermute | solution.py:35
  54.0 50.4 %collective-permute-start.18 = (bf16[480,768]{1,0:T(8,128)(2,1)S(1)}, bf16[480,768]{1,0:T(8,128)(2,1)S(1)}, u32[]{:S(2)}, u32[]{:S(2)}) collective-permute-start(bf16[480,768]{1,0:T(8,128)(2,1)S(1)} %get-tuple-element.273), channel_id=1, source_target_pairs={{0,4},{4,0},{8,12},{12,8},{16,20},{20,16},{24,28},{28,24},{1,5},{5... | collective-permute-start | bytes 2211848 | tf_op jit(solution)/shard_map/ppermute | solution.py:35
  56.1 27.2 %collective-permute-start.8 = (bf16[384,768]{1,0:T(8,128)(2,1)S(1)}, bf16[384,768]{1,0:T(8,128)(2,1)S(1)}, u32[]{:S(2)}, u32[]{:S(2)}) collective-permute-start(bf16[384,768]{1,0:T(8,128)(2,1)S(1)} %get-tuple-element.264), channel_id=1, source_target_pairs={{0,4},{4,0},{8,12},{12,8},{16,20},{20,16},{24,28},{28,24},{1,5},{5... | collective-permute-start | bytes 1769480 | tf_op jit(solution)/shard_map/ppermute | solution.py:35
  57.7 45.1 %collective-permute-start.17 = (bf16[384,768]{1,0:T(8,128)(2,1)S(1)}, bf16[384,768]{1,0:T(8,128)(2,1)S(1)}, u32[]{:S(2)}, u32[]{:S(2)}) collective-permute-start(bf16[384,768]{1,0:T(8,128)(2,1)S(1)} %get-tuple-element.264), channel_id=1, source_target_pairs={{0,2},{1,3},{2,0},{3,1},{4,6},{5,7},{6,4},{7,5},{8,10},{9,11},{10,... | collective-permute-start | bytes 1769480 | tf_op jit(solution)/shard_map/ppermute | solution.py:35
  83.3 21.6 %collective-permute-start.20 = (bf16[768,768]{1,0:T(8,128)(2,1)S(1)}, bf16[768,768]{1,0:T(8,128)(2,1)S(1)}, u32[]{:S(2)}, u32[]{:S(2)}) collective-permute-start(bf16[768,768]{1,0:T(8,128)(2,1)S(1)} %constant_dynamic-update-slice_fusion.9.refs_16_), channel_id=1, source_target_pairs={{0,1},{1,0},{2,3},{3,2},{4,5},{5,4},{6,7},{7,6},{8,9},{9,8},{10,11... | collective-permute-start | bytes 3538952 | tf_op jit(solution)/shard_map/ppermute | solution.py:35
  83.4 21.5 %collective-permute-start.19 = (bf16[1024,128]{1,0:T(8,128)(2,1)S(1)}, bf16[1024,128]{1,0:T(8,128)(2,1)S(1)}, u32[]{:S(2)}, u32[]{:S(2)}) collective-permute-start(bf16[1024,128]{1,0:T(8,128)(2,1)S(1)} %get-tuple-element.118), channel_id=1, source_target_pairs={{0,2},{1,3},{2,0},{3,1},{4,6},{5,7},{6,4},{7,5},{8,10},{9,11},{10,... | collective-permute-start | bytes 786440 | tf_op jit(solution)/shard_map/ppermute | solution.py:35
  84.0 41.3 %collective-permute-start.15 = (bf16[480,768]{1,0:T(8,128)(2,1)S(1)}, bf16[480,768]{1,0:T(8,128)(2,1)S(1)}, u32[]{:S(2)}, u32[]{:S(2)}) collective-permute-start(bf16[480,768]{1,0:T(8,128)(2,1)S(1)} %collective-permute-done.13), channel_id=1, source_target_pairs={{0,4},{4,0},{8,12},{12,8},{16,20},{20,16},{24,28},{28,24},{1,5},{5... | collective-permute-start | bytes 2211848 | tf_op jit(solution)/shard_map/ppermute | solution.py:35
  102.8 22.5 %collective-permute-start.14 = (bf16[384,768]{1,0:T(8,128)(2,1)S(1)}, bf16[384,768]{1,0:T(8,128)(2,1)S(1)}, u32[]{:S(2)}, u32[]{:S(2)}) collective-permute-start(bf16[384,768]{1,0:T(8,128)(2,1)S(1)} %collective-permute-done.8), channel_id=1, source_target_pairs={{0,2},{1,3},{2,0},{3,1},{4,6},{5,7},{6,4},{7,5},{8,10},{9,11},{10,... | collective-permute-start | bytes 1769480 | tf_op jit(solution)/shard_map/ppermute | solution.py:35
  104.4 19.3 %collective-permute-start.16 = (bf16[1024,128]{1,0:T(8,128)(2,1)S(1)}, bf16[1024,128]{1,0:T(8,128)(2,1)S(1)}, u32[]{:S(2)}, u32[]{:S(2)}) collective-permute-start(bf16[1024,128]{1,0:T(8,128)(2,1)S(1)} %get-tuple-element.116), channel_id=1, source_target_pairs={{0,2},{1,3},{2,0},{3,1},{4,6},{5,7},{6,4},{7,5},{8,10},{9,11},{10,... | collective-permute-start | bytes 786440 | tf_op jit(solution)/shard_map/ppermute | solution.py:35
  106.0 19.4 %collective-permute-start.22 = (bf16[768,768]{1,0:T(8,128)(2,1)S(1)}, bf16[768,768]{1,0:T(8,128)(2,1)S(1)}, u32[]{:S(2)}, u32[]{:S(2)}) collective-permute-start(bf16[768,768]{1,0:T(8,128)(2,1)S(1)} %pad_maximum_fusion.refs_20_), channel_id=1, source_target_pairs={{0,1},{1,0},{2,3},{3,2},{4,5},{5,4},{6,7},{7,6},{8,9},{9,8},{10,11... | collective-permute-start | bytes 3538952 | tf_op jit(solution)/shard_map/ppermute | solution.py:35
  106.0 19.3 %collective-permute-start.21 = (bf16[1024,128]{1,0:T(8,128)(2,1)S(1)}, bf16[1024,128]{1,0:T(8,128)(2,1)S(1)}, u32[]{:S(2)}, u32[]{:S(2)}) collective-permute-start(bf16[1024,128]{1,0:T(8,128)(2,1)S(1)} %pad_maximum_fusion.22), channel_id=1, source_target_pairs={{0,1},{1,0},{2,3},{3,2},{4,5},{5,4},{6,7},{7,6},{8,9},{9,8},{10,11... | collective-permute-start | bytes 786440 | tf_op jit(solution)/shard_map/ppermute | solution.py:35
  123.7 8.3 %collective-permute-start.24 = (bf16[1024,128]{1,0:T(8,128)(2,1)S(1)}, bf16[1024,128]{1,0:T(8,128)(2,1)S(1)}, u32[]{:S(2)}, u32[]{:S(2)}) collective-permute-start(bf16[1024,128]{1,0:T(8,128)(2,1)S(1)} %get-tuple-element.132), channel_id=1, source_target_pairs={{0,2},{1,3},{2,0},{3,1},{4,6},{5,7},{6,4},{7,5},{8,10},{9,11},{10,... | collective-permute-start | bytes 786440 | tf_op jit(solution)/shard_map/ppermute | solution.py:35
  126.4 7.7 %collective-permute-start.28 = (bf16[768,768]{1,0:T(8,128)(2,1)S(1)}, bf16[768,768]{1,0:T(8,128)(2,1)S(1)}, u32[]{:S(2)}, u32[]{:S(2)}) collective-permute-start(bf16[768,768]{1,0:T(8,128)(2,1)S(1)} %pad_maximum_fusion.1.refs_21_), channel_id=1, source_target_pairs={{0,1},{1,0},{2,3},{3,2},{4,5},{5,4},{6,7},{7,6},{8,9},{9,8},{10,11... | collective-permute-start | bytes 3538952 | tf_op jit(solution)/shard_map/ppermute | solution.py:35
  126.5 7.6 %collective-permute-start.27 = (bf16[768,768]{1,0:T(8,128)(2,1)S(1)}, bf16[768,768]{1,0:T(8,128)(2,1)S(1)}, u32[]{:S(2)}, u32[]{:S(2)}) collective-permute-start(bf16[768,768]{1,0:T(8,128)(2,1)S(1)} %constant_dynamic-update-slice_fusion.20.refs_17_), channel_id=1, source_target_pairs={{0,1},{1,0},{2,3},{3,2},{4,5},{5,4},{6,7},{7,6},{8,9},{9,8},{10,11... | collective-permute-start | bytes 3538952 | tf_op jit(solution)/shard_map/ppermute | solution.py:35
  127.1 5.7 %collective-permute-start.26 = (bf16[384,768]{1,0:T(8,128)(2,1)S(1)}, bf16[384,768]{1,0:T(8,128)(2,1)S(1)}, u32[]{:S(2)}, u32[]{:S(2)}) collective-permute-start(bf16[384,768]{1,0:T(8,128)(2,1)S(1)} %get-tuple-element.229), channel_id=1, source_target_pairs={{0,1},{1,0},{2,3},{3,2},{4,5},{5,4},{6,7},{7,6},{8,9},{9,8},{10,11... | collective-permute-start | bytes 1769480 | tf_op jit(solution)/shard_map/ppermute | solution.py:35
  132.1 1.9 collective-permute-start.25
  182.4 29.9 %collective-permute-start.32 = (bf16[1536,768]{1,0:T(8,128)(2,1)}, bf16[1536,768]{1,0:T(8,128)(2,1)}, u32[]{:S(2)}, u32[]{:S(2)}) collective-permute-start(bf16[1536,768]{1,0:T(8,128)(2,1)} %weight_grad.7), channel_id=1, source_target_pairs={{0,1},{1,0},{2,3},{3,2},{4,5},{5,4},{6,7},{7,6},{8,9},{9,8},{10,11... | collective-permute-start | bytes 7077896 | tf_op jit(solution)/shard_map/ppermute | solution.py:35
  185.8 11.7 %collective-permute-start.33 = (bf16[384,768]{1,0:T(8,128)(2,1)S(1)}, bf16[384,768]{1,0:T(8,128)(2,1)}, u32[]{:S(2)}, u32[]{:S(2)}) collective-permute-start(bf16[384,768]{1,0:T(8,128)(2,1)S(1)} %bitcast.167), channel_id=1, source_target_pairs={{0,1},{1,0},{2,3},{3,2},{4,5},{5,4},{6,7},{7,6},{8,9},{9,8},{10,11... | collective-permute-start | bytes 1769480 | tf_op jit(solution)/shard_map/ppermute | solution.py:35
  191.3 26.6 %collective-permute-start.31 = (bf16[1536,768]{1,0:T(8,128)(2,1)}, bf16[1536,768]{1,0:T(8,128)(2,1)S(1)}, u32[]{:S(2)}, u32[]{:S(2)}) collective-permute-start(bf16[1536,768]{1,0:T(8,128)(2,1)} %weight_grad.5), channel_id=1, source_target_pairs={{0,1},{1,0},{2,3},{3,2},{4,5},{5,4},{6,7},{7,6},{8,9},{9,8},{10,11... | collective-permute-start | bytes 7077896 | tf_op jit(solution)/shard_map/ppermute | solution.py:35
  192.0 20.2 %collective-permute-start.29 = (bf16[2,3,512,128]{3,2,1,0:T(8,128)(2,1)}, bf16[2,3,512,128]{3,2,1,0:T(8,128)(2,1)S(1)}, u32[]{:S(2)}, u32[]{:S(2)}) collective-permute-start(bf16[2,3,512,128]{3,2,1,0:T(8,128)(2,1)} %get-tuple-element.142), channel_id=1, source_target_pairs={{0,2},{1,3},{2,0},{3,1},{4,6},{5,7},{6,4},{7,5},{8,10},{9,11},{10,... | collective-permute-start | bytes 2359304 | tf_op jit(solution)/shard_map/ppermute | solution.py:35
  193.5 2.4 collective-permute-start.36
  195.9 49.7 %collective-permute-start.37 = (f32[5,768]{1,0:T(8,128)S(1)}, f32[5,768]{1,0:T(8,128)S(1)}, u32[]{:S(2)}, u32[]{:S(2)}) collective-permute-start(f32[5,768]{1,0:T(8,128)S(1)} %fusion.13), channel_id=1, source_target_pairs={{0,2},{1,3},{2,0},{3,1},{4,6},{5,7},{6,4},{7,5},{8,10},{9,11},{10,... | collective-permute-start | bytes 46088 | tf_op jit(solution)/shard_map/ppermute | solution.py:35
  212.3 13.6 %collective-permute-start.30 = (bf16[2,3,512,128]{3,2,1,0:T(8,128)(2,1)S(1)}, bf16[2,3,512,128]{3,2,1,0:T(8,128)(2,1)S(1)}, u32[]{:S(2)}, u32[]{:S(2)}) collective-permute-start(bf16[2,3,512,128]{3,2,1,0:T(8,128)(2,1)S(1)} %pad_maximum_fusion.4), channel_id=1, source_target_pairs={{0,1},{1,0},{2,3},{3,2},{4,5},{5,4},{6,7},{7,6},{8,9},{9,8},{10,11... | collective-permute-start | bytes 2359304 | tf_op jit(solution)/shard_map/ppermute | solution.py:35
  217.5 28.1 %collective-permute-start.35 = (bf16[480,768]{1,0:T(8,128)(2,1)S(1)}, bf16[480,768]{1,0:T(8,128)(2,1)S(1)}, u32[]{:S(2)}, u32[]{:S(2)}) collective-permute-start(bf16[480,768]{1,0:T(8,128)(2,1)S(1)} %pad_maximum_fusion.8), channel_id=1, source_target_pairs={{0,4},{4,0},{8,12},{12,8},{16,20},{20,16},{24,28},{28,24},{1,5},{5... | collective-permute-start | bytes 2211848 | tf_op jit(solution)/shard_map/ppermute | solution.py:35
  223.9 21.7 %collective-permute-start.34 = (bf16[384,768]{1,0:T(8,128)(2,1)S(1)}, bf16[384,768]{1,0:T(8,128)(2,1)S(1)}, u32[]{:S(2)}, u32[]{:S(2)}) collective-permute-start(bf16[384,768]{1,0:T(8,128)(2,1)S(1)} %get-tuple-element.212), channel_id=1, source_target_pairs={{0,2},{1,3},{2,0},{3,1},{4,6},{5,7},{6,4},{7,5},{8,10},{9,11},{10,... | collective-permute-start | bytes 1769480 | tf_op jit(solution)/shard_map/ppermute | solution.py:35
  225.6 43.4 %collective-permute-start.39 = (bf16[480,768]{1,0:T(8,128)(2,1)S(1)}, bf16[480,768]{1,0:T(8,128)(2,1)S(1)}, u32[]{:S(2)}, u32[]{:S(2)}) collective-permute-start(bf16[480,768]{1,0:T(8,128)(2,1)S(1)} %pad_maximum_fusion.6), channel_id=1, source_target_pairs={{0,4},{4,0},{8,12},{12,8},{16,20},{20,16},{24,28},{28,24},{1,5},{5... | collective-permute-start | bytes 2211848 | tf_op jit(solution)/shard_map/ppermute | solution.py:35
  225.9 43.1 %collective-permute-start.38 = (bf16[384,768]{1,0:T(8,128)(2,1)S(1)}, bf16[384,768]{1,0:T(8,128)(2,1)S(1)}, u32[]{:S(2)}, u32[]{:S(2)}) collective-permute-start(bf16[384,768]{1,0:T(8,128)(2,1)S(1)} %get-tuple-element.213), channel_id=1, source_target_pairs={{0,2},{1,3},{2,0},{3,1},{4,6},{5,7},{6,4},{7,5},{8,10},{9,11},{10,... | collective-permute-start | bytes 1769480 | tf_op jit(solution)/shard_map/ppermute | solution.py:35
  245.7 23.3 %collective-permute-start.42 = (f32[5,768]{1,0:T(8,128)S(1)}, f32[5,768]{1,0:T(8,128)S(1)}, u32[]{:S(2)}, u32[]{:S(2)}) collective-permute-start(f32[5,768]{1,0:T(8,128)S(1)} %add.139), channel_id=1, source_target_pairs={{0,4},{4,0},{8,12},{12,8},{16,20},{20,16},{24,28},{28,24},{1,5},{5... | collective-permute-start | bytes 46088 | tf_op jit(solution)/shard_map/ppermute | solution.py:35
  247.7 21.3 %collective-permute-start.41 = (bf16[480,768]{1,0:T(8,128)(2,1)S(1)}, bf16[480,768]{1,0:T(8,128)(2,1)S(1)}, u32[]{:S(2)}, u32[]{:S(2)}) collective-permute-start(bf16[480,768]{1,0:T(8,128)(2,1)S(1)} %add_convert_fusion.2), channel_id=1, source_target_pairs={{0,2},{1,3},{2,0},{3,1},{4,6},{5,7},{6,4},{7,5},{8,10},{9,11},{10,... | collective-permute-start | bytes 2211848 | tf_op jit(solution)/shard_map/ppermute | solution.py:35
  249.4 19.6 %collective-permute-start.40 = (bf16[384,768]{1,0:T(8,128)(2,1)S(1)}, bf16[384,768]{1,0:T(8,128)(2,1)S(1)}, u32[]{:S(2)}, u32[]{:S(2)}) collective-permute-start(bf16[384,768]{1,0:T(8,128)(2,1)S(1)} %add_convert_fusion.4), channel_id=1, source_target_pairs={{0,4},{4,0},{8,12},{12,8},{16,20},{20,16},{24,28},{28,24},{1,5},{5... | collective-permute-start | bytes 1769480 | tf_op jit(solution)/shard_map/ppermute | solution.py:35
  270.3 24.0 %collective-permute-start.45 = (f32[5,768]{1,0:T(8,128)S(1)}, f32[5,768]{1,0:T(8,128)S(1)}, u32[]{:S(2)}, u32[]{:S(2)}) collective-permute-start(f32[5,768]{1,0:T(8,128)S(1)} %add.144), channel_id=1, source_target_pairs={{0,8},{4,12},{8,0},{12,4},{16,24},{20,28},{24,16},{28,20},{1,9},{5... | collective-permute-start | bytes 46088 | tf_op jit(solution)/shard_map/ppermute | solution.py:35
  272.0 22.4 %collective-permute-start.44 = (bf16[432,768]{1,0:T(8,128)(2,1)S(1)}, bf16[432,768]{1,0:T(8,128)(2,1)S(1)}, u32[]{:S(2)}, u32[]{:S(2)}) collective-permute-start(bf16[432,768]{1,0:T(8,128)(2,1)S(1)} %pad_maximum_fusion.11), channel_id=1, source_target_pairs={{0,8},{4,12},{8,0},{12,4},{16,24},{20,28},{24,16},{28,20},{1,9},{5... | collective-permute-start | bytes 1990664 | tf_op jit(solution)/shard_map/ppermute | solution.py:35
  292.5 10.8 %collective-permute-start.43 = (bf16[288,768]{1,0:T(8,128)(2,1)S(1)}, bf16[288,768]{1,0:T(8,128)(2,1)S(1)}, u32[]{:S(2)}, u32[]{:S(2)}) collective-permute-start(bf16[288,768]{1,0:T(8,128)(2,1)S(1)} %bitcast.168), channel_id=1, source_target_pairs={{0,4},{4,0},{8,12},{12,8},{16,20},{20,16},{24,28},{28,24},{1,5},{5... | collective-permute-start | bytes 1327112 | tf_op jit(solution)/shard_map/ppermute | solution.py:35
  303.3 23.8 %collective-permute-start.49 = (bf16[2048,768]{1,0:T(8,128)(2,1)}, bf16[2048,768]{1,0:T(8,128)(2,1)}, u32[]{:S(2)}, u32[]{:S(2)}) collective-permute-start(bf16[2048,768]{1,0:T(8,128)(2,1)} %get-tuple-element.184), channel_id=1, source_target_pairs={{0,1},{1,0},{2,3},{3,2},{4,5},{5,4},{6,7},{7,6},{8,9},{9,8},{10,11... | collective-permute-start | bytes 9437192 | tf_op jit(solution)/shard_map/ppermute | solution.py:35
  303.3 8.8 %collective-permute-start.48 = (f32[5,768]{1,0:T(8,128)S(1)}, f32[5,768]{1,0:T(8,128)S(1)}, u32[]{:S(2)}, u32[]{:S(2)}) collective-permute-start(f32[5,768]{1,0:T(8,128)S(1)} %add.149), channel_id=1, source_target_pairs={{0,16},{4,20},{8,24},{12,28},{16,0},{20,4},{24,8},{28,12},{1,17},{... | collective-permute-start | bytes 46088 | tf_op jit(solution)/shard_map/ppermute | solution.py:35
  308.9 18.2 %collective-permute-start.47 = (bf16[216,768]{1,0:T(8,128)(2,1)}, bf16[216,768]{1,0:T(8,128)(2,1)}, u32[]{:S(2)}, u32[]{:S(2)}) collective-permute-start(bf16[216,768]{1,0:T(8,128)(2,1)} %pad_maximum_fusion.17), channel_id=1, source_target_pairs={{0,16},{4,20},{8,24},{12,28},{16,0},{20,4},{24,8},{28,12},{1,17},{... | collective-permute-start | bytes 995336 | tf_op jit(solution)/shard_map/ppermute | solution.py:35
  310.5 11.1 %collective-permute-start.46 = (bf16[144,768]{1,0:T(8,128)(2,1)}, bf16[144,768]{1,0:T(8,128)(2,1)}, u32[]{:S(2)}, u32[]{:S(2)}) collective-permute-start(bf16[144,768]{1,0:T(8,128)(2,1)} %slice.428), channel_id=1, source_target_pairs={{0,8},{4,12},{8,0},{12,4},{16,24},{20,28},{24,16},{28,20},{1,9},{5... | collective-permute-start | bytes 663560 | tf_op jit(solution)/shard_map/ppermute | solution.py:35
  328.2 8.8 %collective-permute-start.50 = (bf16[72,768]{1,0:T(8,128)(2,1)S(1)}, bf16[72,768]{1,0:T(8,128)(2,1)S(1)}, u32[]{:S(2)}, u32[]{:S(2)}) collective-permute-start(bf16[72,768]{1,0:T(8,128)(2,1)S(1)} %slice.438), channel_id=1, source_target_pairs={{0,16},{4,20},{8,24},{12,28},{16,0},{20,4},{24,8},{28,12},{1,17},{... | collective-permute-start | bytes 331784 | tf_op jit(solution)/shard_map/ppermute | solution.py:35
  332.9 24.1 %collective-permute-start.54 = (bf16[512,768]{1,0:T(8,128)(2,1)S(1)}, bf16[512,768]{1,0:T(8,128)(2,1)S(1)}, u32[]{:S(2)}, u32[]{:S(2)}) collective-permute-start(bf16[512,768]{1,0:T(8,128)(2,1)S(1)} %get-tuple-element.205), channel_id=1, source_target_pairs={{0,2},{1,3},{2,0},{3,1},{4,6},{5,7},{6,4},{7,5},{8,10},{9,11},{10,... | collective-permute-start | bytes 2359304 | tf_op jit(solution)/shard_map/ppermute | solution.py:35
  338.0 1.9 collective-permute-start.51
  338.1 18.4 %collective-permute-start.52 = (bf16[96,768]{1,0:T(8,128)(2,1)S(1)}, bf16[96,768]{1,0:T(8,128)(2,1)S(1)}, u32[]{:S(2)}, u32[]{:S(2)}) collective-permute-start(bf16[96,768]{1,0:T(8,128)(2,1)S(1)} %get-tuple-element.248), channel_id=1, source_target_pairs={{0,2},{1,3},{2,0},{3,1},{4,6},{5,7},{6,4},{7,5},{8,10},{9,11},{10,... | collective-permute-start | bytes 442376 | tf_op jit(solution)/shard_map/ppermute | solution.py:35
  339.6 17.4 %collective-permute-start.53 = (bf16[96,768]{1,0:T(8,128)(2,1)S(1)}, bf16[96,768]{1,0:T(8,128)(2,1)S(1)}, u32[]{:S(2)}, u32[]{:S(2)}) collective-permute-start(bf16[96,768]{1,0:T(8,128)(2,1)S(1)} %get-tuple-element.247), channel_id=1, source_target_pairs={{0,3},{1,2},{2,1},{3,0},{4,7},{5,6},{6,5},{7,4},{8,11},{9,10},{10,... | collective-permute-start | bytes 442376 | tf_op jit(solution)/shard_map/ppermute | solution.py:35
  358.1 10.8 %collective-permute-start.55 = (bf16[1344,128]{1,0:T(8,128)(2,1)S(1)}, bf16[1344,128]{1,0:T(8,128)(2,1)S(1)}, u32[]{:S(2)}, u32[]{:S(2)}) collective-permute-start(bf16[1344,128]{1,0:T(8,128)(2,1)S(1)} %select_convert_fusion), channel_id=1, source_target_pairs={{0,4},{4,0},{8,12},{12,8},{16,20},{20,16},{24,28},{28,24},{1,5},{5... | collective-permute-start | bytes 1032200 | tf_op jit(solution)/shard_map/ppermute | solution.py:35
  369.1 6.5 %collective-permute-start.56 = (bf16[672,128]{1,0:T(8,128)(2,1)S(1)}, bf16[672,128]{1,0:T(8,128)(2,1)S(1)}, u32[]{:S(2)}, u32[]{:S(2)}) collective-permute-start(bf16[672,128]{1,0:T(8,128)(2,1)S(1)} %select_convert_fusion.1), channel_id=1, source_target_pairs={{0,8},{4,12},{8,0},{12,4},{16,24},{20,28},{24,16},{28,20},{1,9},{5... | collective-permute-start | bytes 516104 | tf_op jit(solution)/shard_map/ppermute | solution.py:35
  375.7 6.5 %collective-permute-start.57 = (bf16[336,128]{1,0:T(8,128)(2,1)S(1)}, bf16[336,128]{1,0:T(8,128)(2,1)S(1)}, u32[]{:S(2)}, u32[]{:S(2)}) collective-permute-start(bf16[336,128]{1,0:T(8,128)(2,1)S(1)} %select_convert_fusion.2), channel_id=1, source_target_pairs={{0,16},{4,20},{8,24},{12,28},{16,0},{20,4},{24,8},{28,12},{1,17},{... | collective-permute-start | bytes 258056 | tf_op jit(solution)/shard_map/ppermute | solution.py:35
  382.2 5.9 %collective-permute-start.58 = (bf16[336,128]{1,0:T(8,128)(2,1)S(1)}, bf16[336,128]{1,0:T(8,128)(2,1)S(1)}, u32[]{:S(2)}, u32[]{:S(2)}) collective-permute-start(bf16[336,128]{1,0:T(8,128)(2,1)S(1)} %add_convert_fusion.11), channel_id=1, source_target_pairs={{0,16},{4,20},{8,24},{12,28},{16,0},{20,4},{24,8},{28,12},{1,17},{... | collective-permute-start | bytes 258056 | tf_op jit(solution)/shard_map/ppermute | solution.py:35
  388.1 5.5 %collective-permute-start.59 = (bf16[672,128]{1,0:T(8,128)(2,1)S(1)}, bf16[672,128]{1,0:T(8,128)(2,1)S(1)}, u32[]{:S(2)}, u32[]{:S(2)}) collective-permute-start(bf16[672,128]{1,0:T(8,128)(2,1)S(1)} %pad_maximum_fusion.26), channel_id=1, source_target_pairs={{0,8},{4,12},{8,0},{12,4},{16,24},{20,28},{24,16},{28,20},{1,9},{5... | collective-permute-start | bytes 516104 | tf_op jit(solution)/shard_map/ppermute | solution.py:35
  388.2 16.3 %collective-permute-start.61 = (bf16[512,768]{1,0:T(8,128)(2,1)S(1)}, bf16[512,768]{1,0:T(8,128)(2,1)S(1)}, u32[]{:S(2)}, u32[]{:S(2)}) collective-permute-start(bf16[512,768]{1,0:T(8,128)(2,1)S(1)} %copy-done.52), channel_id=1, source_target_pairs={{0,2},{1,3},{2,0},{3,1},{4,6},{5,7},{6,4},{7,5},{8,10},{9,11},{10,... | collective-permute-start | bytes 2359304 | tf_op jit(solution)/shard_map/ppermute | solution.py:35
  393.7 7.3 %collective-permute-start.60 = (bf16[1344,128]{1,0:T(8,128)(2,1)S(1)}, bf16[1344,128]{1,0:T(8,128)(2,1)S(1)}, u32[]{:S(2)}, u32[]{:S(2)}) collective-permute-start(bf16[1344,128]{1,0:T(8,128)(2,1)S(1)} %pad_maximum_fusion.16), channel_id=1, source_target_pairs={{0,4},{4,0},{8,12},{12,8},{16,20},{20,16},{24,28},{28,24},{1,5},{5... | collective-permute-start | bytes 1032200 | tf_op jit(solution)/shard_map/ppermute | solution.py:35
  413.1 4.1 collective-permute-start.62
  413.2 6.7 %collective-permute-start.63 = (bf16[96,768]{1,0:T(8,128)(2,1)S(1)}, bf16[96,768]{1,0:T(8,128)(2,1)S(1)}, u32[]{:S(2)}, u32[]{:S(2)}) collective-permute-start(bf16[96,768]{1,0:T(8,128)(2,1)S(1)} %get-tuple-element.244), channel_id=1, source_target_pairs={{0,2},{1,3},{2,0},{3,1},{4,6},{5,7},{6,4},{7,5},{8,10},{9,11},{10,... | collective-permute-start | bytes 442376 | tf_op jit(solution)/shard_map/ppermute | solution.py:35
  414.2 7.9 %collective-permute-start.64 = (bf16[96,768]{1,0:T(8,128)(2,1)S(1)}, bf16[96,768]{1,0:T(8,128)(2,1)S(1)}, u32[]{:S(2)}, u32[]{:S(2)}) collective-permute-start(bf16[96,768]{1,0:T(8,128)(2,1)S(1)} %get-tuple-element.243), channel_id=1, source_target_pairs={{0,3},{1,2},{2,1},{3,0},{4,7},{5,6},{6,5},{7,4},{8,11},{9,10},{10,... | collective-permute-start | bytes 442376 | tf_op jit(solution)/shard_map/ppermute | solution.py:35
  (80 other events, 499.6 us)

commit v3 on v2

--- a/solution.py
+++ b/solution.py
@@ -19,8 +19,7 @@
 low = jnp.bfloat16
 full = jnp.float32
 LANES = 128
-GROUP = 8
-UNROLL = 32
+GROUP = 4
 score_scale = 1.0 / math.sqrt(HD)
 
 
@@ -96,38 +95,104 @@
     return add_low(kept, swap(sent, axis, bit))
 
 
-def send_on(near, far_got):
-    return swap(jnp.concatenate([near, far_got], axis=0), "ffn", 1)
-
-
-def sides_of(stages):
-    return [(axis, bit, (lax.axis_index(axis) & bit) != 0) for axis, bit in stages]
-
-
-def sum_halves(value, stages):
-    for axis, bit, side in reversed(sides_of(stages)):
-        half = value.shape[0] // 2
-        kept = jnp.where(side, value[half:], value[:half])
-        sent = jnp.where(side, value[:half], value[half:]).astype(low)
-        value = kept.astype(full) + swap(sent, axis, bit).astype(full)
-    return value.astype(low)
-
-
-def spread_halves(value, stages):
-    for axis, bit, side in sides_of(stages):
-        other = swap(value, axis, bit)
-        value = jnp.concatenate([jnp.where(side, other, value), jnp.where(side, value, other)], axis=0)
+def send_on(near, far_got, axis=0):
+    return swap(jnp.concatenate([near, far_got], axis=axis), "ffn", 1)
+
+
+def add_many(first, others):
+    value = first.astype(full)
+    for other in others:
+        value = value + other.astype(full)
     return value
 
 
-def move_rows(perm_ref, head, base, count, move):
-    def step(turn, carry):
-        for inner in range(UNROLL):
-            row = turn * UNROLL + inner
-            move(perm_ref[head, base + row], row)
+def seq_groups():
+    bits = sorted(seq_bits())
+    return [tuple(bits[:1])] + [tuple(bits[at : at + 2]) for at in range(1, len(bits), 2)]
+
+
+def masks_of(bits):
+    masks = [0]
+    for bit in bits:
+        masks = [mask | more for mask in masks for more in (0, bit)]
+    return masks
+
+
+def cut_many(value, count):
+    rows = value.shape[0] // count
+    return [value[part * rows : (part + 1) * rows] for part in range(count)]
+
+
+def place_in(bits):
+    me = lax.axis_index("seq")
+    place = 0
+    for bit in bits:
+        place = 2 * place + ((me & bit) != 0).astype(jnp.int32)
+    return place
+
+
+def sum_parts(value):
+    for bits in seq_groups():
+        masks = masks_of(bits)
+        place = place_in(bits)
+        parts = value.reshape((len(masks), value.shape[0] // len(masks)) + value.shape[1:])
+
+        def part(turn):
+            return lax.dynamic_index_in_dim(parts, jnp.bitwise_xor(place, turn), keepdims=False)
+
+        got = [swap(part(turn), "seq", masks[turn]) for turn in range(1, len(masks))]
+        value = add_many(part(0), got).astype(low)
+    return value
+
+
+def spread_parts(value, beside):
+    for turn, bits in enumerate(reversed(seq_groups())):
+        masks = masks_of(bits)
+        got = [value] + [swap(value, "seq", mask) for mask in masks[1:]]
+        if turn == 0:
+            got, beside = after((got, beside))
+        me = lax.axis_index("seq")
+        for at, bit in enumerate(bits):
+            flip = 2 ** (len(bits) - 1 - at)
+            side = (me & bit) != 0
+            got = [jnp.where(side, got[turn ^ flip], got[turn]) for turn in range(len(masks))]
+        value = jnp.concatenate(got, axis=0)
+    return value, beside
+
+
+def in_turns(perm_ref, seq_len, fetch, work, place):
+    count = GROUP * CLUSTER
+    groups = seq_len // count
+
+    def rows_of(turn):
+        return pl.multiple_of(jnp.clip(turn, 0, groups - 1) * count, count)
+
+    def fetch_some(side, turn, rows):
+        base = rows_of(turn)
+        for row in rows:
+            fetch(side, perm_ref[0, base + row], row)
+
+    def place_some(side, turn, rows):
+        base = rows_of(turn)
+        for row in rows:
+            place(side, perm_ref[0, base + row], row)
+
+    def step(pair, carry):
+        for side in range(2):
+            turn = 2 * pair + side
+            done = 0
+            for at in work(side, rows_of(turn)):
+                rows = range(done, min(count, int(at * count)))
+                fetch_some(1 - side, turn + 1, rows)
+                place_some(1 - side, turn - 1, rows)
+                done = max(done, rows.stop)
+            fetch_some(1 - side, turn + 1, range(done, count))
+            place_some(1 - side, turn - 1, range(done, count))
         return carry
 
-    lax.fori_loop(0, count // UNROLL, step, 0)
+    fetch_some(0, 0, range(count))
+    lax.fori_loop(0, groups // 2, step, 0)
+    place_some(1, groups - 1, range(count))
 
 
 def softmax_rows(scores):
@@ -141,8 +206,9 @@
 
 
 def attend_kernel(
-    perm_ref, x0, x1, x2, x3, w_ref, own_ref, near_ref, far_ref, qv_ref, key_ref, qv_rows, key_rows, qv_got, key_got, o_got, o_rows
+    perm_ref, x0, x1, x2, x3, w_ref, own_ref, near_ref, far_ref, qv_ref, key_ref, qv_rows, key_rows, o_rows, *got
 ):
+    qv_got, key_got, o_got = got[0:2], got[2:4], got[4:6]
     here = x0.shape[0]
     seq_len = 4 * here
     half = here // 2
@@ -152,35 +218,32 @@
             rows = pl.ds(block * here + cut * half, half)
             qv_rows[rows, :] = both[:, :LANES]
             key_rows[rows, :] = both[:, LANES:]
-    count = GROUP * CLUSTER
-
-    def group(turn, carry):
-        base = turn * count
-
-        def fetch(index, row):
-            qv_got[pl.ds(row, 1), :] = qv_rows[pl.ds(index, 1), :]
-            key_got[pl.ds(row, 1), :] = key_rows[pl.ds(index, 1), :]
-
-        move_rows(perm_ref, 0, base, count, fetch)
-        spans = [slice(part * CLUSTER, (part + 1) * CLUSTER) for part in range(GROUP)]
-        qvs = [qv_got[span].astype(low) for span in spans]
-        keys = [key_got[span].astype(low) for span in spans]
+    spans = [slice(part * CLUSTER, (part + 1) * CLUSTER) for part in range(GROUP)]
+
+    def fetch(side, index, row):
+        qv_got[side][pl.ds(row, 1), :] = qv_rows[pl.ds(index, 1), :]
+        key_got[side][pl.ds(row, 1), :] = key_rows[pl.ds(index, 1), :]
+
+    def work(side, base):
+        qvs = [qv_got[side][span].astype(low) for span in spans]
+        keys = [key_got[side][span].astype(low) for span in spans]
         for part in range(GROUP):
             rows = pl.ds(base + part * CLUSTER, CLUSTER)
             qv_ref[rows, :] = qvs[part]
             key_ref[rows, :] = keys[part]
         scores = [contract(qv, key, 1, 1) for qv, key in zip(qvs, keys)]
-        probs = [softmax_rows(score).astype(low) for score in scores]
+        yield 0.3
+        probs = []
         for part in range(GROUP):
-            o_got[spans[part]] = contract(probs[part], qvs[part], 1, 0)
-
-        def place(index, row):
-            o_rows[pl.ds(index, 1), :] = o_got[pl.ds(row, 1), :]
-
-        move_rows(perm_ref, 0, base, count, place)
-        return carry
-
-    lax.fori_loop(0, seq_len // count, group, 0)
+            probs.append(softmax_rows(scores[part]).astype(low))
+            yield 0.3 + 0.6 * (part + 1) / GROUP
+        for part in range(GROUP):
+            o_got[side][spans[part]] = contract(probs[part], qvs[part], 1, 0)
+
+    def place(side, index, row):
+        o_rows[pl.ds(index, 1), :] = o_got[side][pl.ds(row, 1), :]
+
+    in_turns(perm_ref, seq_len, fetch, work, place)
     outs = (own_ref, near_ref, far_ref.at[pl.ds(0, half), :], far_ref.at[pl.ds(half, half), :])
     for block, out_ref in enumerate(outs):
         top = pltpu.roll(o_rows[pl.ds(block * here, half), :], HD, 1)
@@ -209,74 +272,65 @@
             jax.ShapeDtypeStruct((seq_len, LANES), low),
             jax.ShapeDtypeStruct((seq_len, LANES), low),
         ],
-        scratch_shapes=[rows_all, rows_all, rows_got, rows_got, rows_got, rows_all],
+        scratch_shapes=[rows_all] * 3 + [rows_got] * 6,
         compiler_params=pltpu.CompilerParams(vmem_limit_bytes=40 * 2**20),
         cost_estimate=pl.CostEstimate(flops=18 * 10**9, bytes_accessed=1000, transcendentals=0),
         name=name,
     )(perm, *tokens, weights)
 
 
-def attend_back_kernel(heads, *refs):
-    perm_ref = refs[0]
-    per_head = [refs[1 + 6 * head : 7 + 6 * head] for head in range(heads)]
-    x_refs = refs[1 + 6 * heads : 5 + 6 * heads]
-    outs = refs[5 + 6 * heads : 5 + 8 * heads]
-    d_rows, d_got, dqv_got, dkey_got, dqv_rows, dkey_rows = refs[5 + 8 * heads :]
-    here = x_refs[0].shape[0]
+def attend_back_kernel(
+    perm_ref, qv_ref, key_ref, do0, do1, do2, do3, x0, x1, x2, x3, gw_ref, dboth_ref, d_rows, dqv_rows, dkey_rows, *got
+):
+    d_got, dqv_got, dkey_got = got[0:2], got[2:4], got[4:6]
+    here = x0.shape[0]
     seq_len = 4 * here
     half = here // 2
-    count = GROUP * CLUSTER
-    for head in range(heads):
-        qv_ref, key_ref, *do_refs = per_head[head]
-        gw_ref, dboth_ref = outs[2 * head : 2 * head + 2]
-        for block, do_ref in enumerate(do_refs):
-            rows = do_ref[...].astype(full)
-            top = pltpu.roll(rows, HD, 1)
-            d_rows[pl.ds(block * here, half), :] = jnp.where(left_half(half), 0.0, top)
-            d_rows[pl.ds(block * here + half, half), :] = jnp.where(left_half(half), 0.0, rows)
-
-        def group(turn, carry):
-            base = turn * count
-
-            def fetch(index, row):
-                d_got[pl.ds(row, 1), :] = d_rows[pl.ds(index, 1), :]
-
-            move_rows(perm_ref, head, base, count, fetch)
-            spans = [slice(part * CLUSTER, (part + 1) * CLUSTER) for part in range(GROUP)]
-            rows = [pl.ds(base + part * CLUSTER, CLUSTER) for part in range(GROUP)]
-            qvs = [qv_ref[span, :] for span in rows]
-            keys = [key_ref[span, :] for span in rows]
-            dos = [d_got[span].astype(low) for span in spans]
-            scores = [contract(qv, key, 1, 1) for qv, key in zip(qvs, keys)]
-            dprobs = [contract(do, qv, 1, 1) for do, qv in zip(dos, qvs)]
-            probs = [softmax_rows(score) for score in scores]
-            probs_low = [prob.astype(low) for prob in probs]
-            dscores = [
-                (prob * (dprob - jnp.sum(prob * dprob, axis=1, keepdims=True))).astype(low)
-                for prob, dprob in zip(probs, dprobs)
-            ]
-            for part in range(GROUP):
-                dqv_got[spans[part]] = score_scale * contract(dscores[part], keys[part], 1, 0) + contract(
-                    probs_low[part], dos[part], 0, 0
-                )
-                dkey_got[spans[part]] = score_scale * contract(dscores[part], qvs[part], 0, 0)
-
-            def place(index, row):
-                dqv_rows[pl.ds(index, 1), :] = dqv_got[pl.ds(row, 1), :]
-                dkey_rows[pl.ds(index, 1), :] = dkey_got[pl.ds(row, 1), :]
-
-            move_rows(perm_ref, head, base, count, place)
-            return carry
-
-        lax.fori_loop(0, seq_len // count, group, 0)
-
-        gw = jnp.zeros((2 * LANES, D), full)
-        for block, x_ref in enumerate(x_refs):
-            rows = pl.ds(block * here, here)
-            dboth_ref[rows, :LANES] = dqv_rows[rows, :].astype(low)
-            dboth_ref[rows, LANES:] = dkey_rows[rows, :].astype(low)
-            gw = gw + contract(dboth_ref[rows, :], x_ref[...], 0, 0)
-        gw_ref[...] = gw.astype(low)
+    for block, do_ref in enumerate((do0, do1, do2, do3)):
+        rows = do_ref[...].astype(full)
+        top = pltpu.roll(rows, HD, 1)
+        d_rows[pl.ds(block * here, half), :] = jnp.where(left_half(half), 0.0, top)
+        d_rows[pl.ds(block * here + half, half), :] = jnp.where(left_half(half), 0.0, rows)
+    spans = [slice(part * CLUSTER, (part + 1) * CLUSTER) for part in range(GROUP)]
+
+    def fetch(side, index, row):
+        d_got[side][pl.ds(row, 1), :] = d_rows[pl.ds(index, 1), :]
+
+    def work(side, base):
+        rows = [pl.ds(base + part * CLUSTER, CLUSTER) for part in range(GROUP)]
+        qvs = [qv_ref[span, :] for span in rows]
+        keys = [key_ref[span, :] for span in rows]
+        dos = [d_got[side][span].astype(low) for span in spans]
+        scores = [contract(qv, key, 1, 1) for qv, key in zip(qvs, keys)]
+        dprobs = [contract(do, qv, 1, 1) for do, qv in zip(dos, qvs)]
+        yield 0.2
+        probs = []
+        for part in range(GROUP):
+            probs.append(softmax_rows(scores[part]))
+            yield 0.2 + 0.3 * (part + 1) / GROUP
+        probs_low = [prob.astype(low) for prob in probs]
+        dscores = []
+        for prob, dprob in zip(probs, dprobs):
+            dscores.append((prob * (dprob - jnp.sum(prob * dprob, axis=1, keepdims=True))).astype(low))
+            yield 0.5 + 0.3 * len(dscores) / GROUP
+        for part in range(GROUP):
+            dqv_got[side][spans[part]] = score_scale * contract(dscores[part], keys[part], 1, 0) + contract(
+                probs_low[part], dos[part], 0, 0
+            )
+            dkey_got[side][spans[part]] = score_scale * contract(dscores[part], qvs[part], 0, 0)
+
+    def place(side, index, row):
+        dqv_rows[pl.ds(index, 1), :] = dqv_got[side][pl.ds(row, 1), :]
+        dkey_rows[pl.ds(index, 1), :] = dkey_got[side][pl.ds(row, 1), :]
+
+    in_turns(perm_ref, seq_len, fetch, work, place)
+    gw = jnp.zeros((2 * LANES, D), full)
+    for block, x_ref in enumerate((x0, x1, x2, x3)):
+        rows = pl.ds(block * here, here)
+        dboth_ref[rows, :LANES] = dqv_rows[rows, :].astype(low)
+        dboth_ref[rows, LANES:] = dkey_rows[rows, :].astype(low)
+        gw = gw + contract(dboth_ref[rows, :], x_ref[...], 0, 0)
+    gw_ref[...] = gw.astype(low)
 
 
 def attend_back(perm, head, kept, do, tokens):
@@ -288,22 +342,24 @@
     in_vmem = pl.BlockSpec(memory_space=pltpu.VMEM)
     own, near, far = do
 
-    def part(turn):
-        return pl.BlockSpec((None, None, half, LANES), lambda step: (turn, head, 0, 0))
+    def part(at, turn):
+        return pl.BlockSpec((None, None, half, LANES), lambda step: (at, turn, 0, 0))
+
+    at = 0 if head == 0 else head - 1
 
     return pl.pallas_call(
-        lambda *refs: attend_back_kernel(1, *refs),
+        attend_back_kernel,
         grid=(1,),
         in_specs=[pl.BlockSpec(memory_space=pltpu.SMEM)]
         + [in_vmem] * 2
-        + [part(0), part(0), part(0), part(1)]
+        + [part(head, 0), part(at, 0), part(at, 0), part(at, 1)]
         + [in_vmem] * 4,
         out_specs=[in_vmem] * 2,
         out_shape=[
             jax.ShapeDtypeStruct((2 * LANES, D), low),
             jax.ShapeDtypeStruct((seq_len, 2 * LANES), low),
         ],
-        scratch_shapes=[rows_all, rows_got, rows_got, rows_got, rows_all, rows_all],
+        scratch_shapes=[rows_all] * 3 + [rows_got] * 6,
         compiler_params=pltpu.CompilerParams(vmem_limit_bytes=40 * 2**20),
         cost_estimate=pl.CostEstimate(flops=22 * 10**9, bytes_accessed=1000, transcendentals=0),
         name="attend_back",
@@ -375,11 +431,19 @@
     up_refs = refs[4 * heads + 4 : 4 * heads + 8]
     down_refs = refs[4 * heads + 8 : 4 * heads + 12]
     outs = refs[4 * heads + 12 :]
-    (do_own, do_near, do_far, block_ref, da_ref) = outs[:5]
-    do_refs = (do_own.at[0], do_near.at[0], do_far.at[0], do_far.at[1])
-    g_refs = outs[5:7]
-    du_refs = outs[7:9]
-    (df_ref, hb_ref, dattn_ref, o_ref, sums_ref, slope_ref) = outs[9:]
+    (do_own, near_first, near_rest, far_first, far_rest, block_ref, da_ref) = outs[:7]
+    g_refs = outs[7:9]
+    du_refs = outs[9:11]
+    (df_ref, hb_ref, dattn_ref, o_ref, sums_ref, slope_ref) = outs[11:]
+
+    def store_do(head, turn, value):
+        near, far, at = (near_first, far_first, 0) if head == 0 else (near_rest, far_rest, head - 1)
+        if turn == 0:
+            do_own[head, 0] = value
+        elif turn == 1:
+            near[at, 0] = value
+        else:
+            far[at, turn - 2] = value
     part = x_ref.shape[1]
     rows = 2 * part
     left = left_half(part)
@@ -447,7 +511,7 @@
         )
         for side in range(2):
             turn, head = divmod(2 * pair + side, heads)
-            do_refs[turn][head] = both[side]
+            store_do(head, turn, both[side])
     sums = jnp.concatenate(sums_a + sums_b, axis=0)
 
     @pl.when(pl.program_id(0) == 0)
@@ -472,8 +536,10 @@
     def lead(count, width):
         return pl.BlockSpec((count, part, width), lambda step: (0, step, 0))
 
-    def do_part(turns):
-        return pl.BlockSpec((turns, heads, part, LANES), lambda step: (0, 0, step, 0))
+    do_sizes = ((heads, 1), (1, 1), (heads - 1, 1), (1, 2), (heads - 1, 2))
+
+    def do_part(count, turns):
+        return pl.BlockSpec((count, turns, part, LANES), lambda step: (0, 0, step, 0))
 
     def still(rows):
         return pl.BlockSpec((rows, D), lambda step: (0, 0), pipeline_mode=once)
@@ -492,9 +558,9 @@
         in_specs=[lanes, lanes, lanes, later] * heads
         + [two, two, still(D), still(4)]
         + [still(FF // 4)] * 8,
-        out_specs=[do_part(1), do_part(1), do_part(2), two, two] + [wide] * 4 + [two] * 4
+        out_specs=[do_part(*sizes) for sizes in do_sizes] + [two, two] + [wide] * 4 + [two] * 4
         + [pl.BlockSpec((4, D), lambda step: (0, 0))],
-        out_shape=[jax.ShapeDtypeStruct((turns, heads, half, LANES), low) for turns in (1, 1, 2)]
+        out_shape=[jax.ShapeDtypeStruct((count, turns, half, LANES), low) for count, turns in do_sizes]
         + [
             pairs(D, low),
             pairs(D, full),
@@ -521,8 +587,8 @@
         *up_rows,
         *down_rows,
     )
-    tokenwise = [value.reshape(here, value.shape[2]) for value in flat[3:-1]]
-    return flat[:3], tokenwise, flat[-1]
+    tokenwise = [value.reshape(here, value.shape[2]) for value in flat[5:-1]]
+    return flat[:5], tokenwise, flat[-1]
 
 
 def weight_grad_kernel(left_ref, right_ref, *refs):
@@ -551,7 +617,7 @@
         out_specs=block,
         out_shape=jax.ShapeDtypeStruct((width, D), low),
         compiler_params=pltpu.CompilerParams(vmem_limit_bytes=32 * 2**20),
-        cost_estimate=pl.CostEstimate(flops=5 * 10**9, bytes_accessed=1000, transcendentals=0),
+        cost_estimate=pl.CostEstimate(flops=4 * 10**9, bytes_accessed=1000, transcendentals=0),
         name="weight_grad",
     )(*args)
 
@@ -678,23 +744,41 @@
     momenta = [rows_qkv(mom_qkv), mom_out.reshape(heads * cut, D), mom_up.T, mom_down]
 
     wide_qkv = weights[0].astype(low)
-    far = seq_stages()[0]
-    first = swap(wide_qkv, *far)
+    far_groups = seq_groups()[1:]
+
+    def gather_group(values, bits):
+        sent = jnp.concatenate(values, axis=0)
+        return [swap(sent, "seq", mask) for mask in masks_of(bits)[1:]]
+
+    def join_group(values, got):
+        joined = []
+        at = 0
+        for value in values:
+            joined.append(jnp.concatenate([value] + [other[at : at + value.shape[0]] for other in got], axis=0))
+            at += value.shape[0]
+        return joined
+
+    got = gather_group([wide_qkv], far_groups[-1])
     tokens = [block_in, swap(block_in, "ffn", 1), swap(block_in, "ffn", 2)]
     tokens.append(swap(tokens[2], "ffn", 1))
-    wide_qkv = jnp.concatenate([wide_qkv, first], axis=0)
-    shards = (weights[2].astype(low), weights[1].astype(low), weights[3].astype(low))
-    for stage in seq_stages()[1:]:
-        if stage == seq_stages()[-1]:
-            shards = after(shards, wide_qkv)
-        wide_qkv = spread(wide_qkv, [stage])
-    up_rows, out_wide, down_rows = shards
+    for bits in reversed(far_groups[:-1]):
+        (wide_qkv,) = join_group([wide_qkv], got)
+        got = gather_group([wide_qkv], bits)
+    shards = [weights[2].astype(low), weights[3].astype(low), weights[1].astype(low)]
+    shards, got = after((shards, got))
+    (wide_qkv,) = join_group([wide_qkv], got)
+    last_got = swap(wide_qkv, "seq", 1)
+    for turn, bits in enumerate(reversed(far_groups)):
+        got = gather_group(shards, bits)
+        if turn == 0:
+            got, last_got = after((got, last_got))
+        shards = join_group(shards, got)
+    up_rows, down_rows, out_wide = shards
+    wide_qkv = jnp.concatenate([wide_qkv, last_got], axis=0)
     wide_qkv = wide_qkv.reshape(seqs, 3, heads, cut, D).transpose(1, 2, 0, 3, 4).reshape(3, heads, HD, D)
     head_rows = jnp.stack(
         [wide_qkv[0], wide_qkv[2], wide_qkv[1], jnp.zeros_like(wide_qkv[1])], axis=1
     ).reshape(heads * 2 * LANES, D)
-    for stage in far_stages():
-        up_rows, out_wide, down_rows = [spread(value, [stage]) for value in (up_rows, out_wide, down_rows)]
     low_rows = down_rows.shape[0]
     shards = (up_rows, jnp.concatenate([down_rows, out_wide], axis=0))
     first_at = (("seq", 1), ("ffn", 2))
@@ -704,7 +788,6 @@
         return tuple(swap(value, *place) for value, place in zip(values, places))
 
     first_got = swaps(shards, first_at)
-    own_got = swaps(shards, then_at)
 
     perm = jnp.bitwise_xor(cluster_perm[0], ffn_here * here)
     kept = []
@@ -715,14 +798,15 @@
         mine = head_rows[head * 2 * LANES : (head + 1) * 2 * LANES]
         order_rows = perm[head : head + 1]
         if head == 1:
-            order_rows, first_got = after((order_rows, first_got), kept[0])
-            other_got = swaps(first_got, then_at)
+            order_rows, first_got, shards = after((order_rows, first_got, shards), kept[0])
+            own_got = swaps(shards, then_at)
             up_pieces = [jnp.concatenate([shards[0], first_got[0]], axis=0)]
             up_pieces.append(swap(up_pieces[0], "ffn", 1))
         if head == 2:
-            order_rows, own_got, far_got[0], up_pieces[1] = after(
-                (order_rows, own_got, far_got[0], up_pieces[1]), kept[1]
+            order_rows, own_got, first_got, far_got[0], up_pieces[1] = after(
+                (order_rows, own_got, first_got, far_got[0], up_pieces[1]), kept[1]
             )
+            other_got = swaps(first_got, then_at)
             near_got.append(send_on(o_sent[0][0], far_got[0][half:]))
             down_pieces = [jnp.concatenate([shards[1][:low_rows], own_got[1][:low_rows]], axis=0)]
             down_pieces.append(swap(down_pieces[0], "ffn", 1))
@@ -755,8 +839,8 @@
         o_got, block_in, block_cot, out_rows, up_rows, down_rows, norm_params
     )
     block_out, dresidual, gelu_a, gelu_b, dinner_a, dinner_b, dbranch, hidden_low, dattn, o_rows = tokenwise
-    do_far = swap(do_blocks[2], "ffn", 2)
-    do_got = (do_blocks[0], send_on(do_blocks[1], do_far[1:]), do_far)
+    do_own, *do_near, far_first, far_rest = do_blocks
+    do_far = [swap(far_first, "ffn", 2), swap(far_rest, "ffn", 2)]
 
     early_half = (cluster_perm[0] < seq_len // 2).astype(full).reshape(heads, clusters, CLUSTER)
     share = lax.dynamic_update_slice(
@@ -765,15 +849,21 @@
     small = jnp.concatenate([norm_part, jnp.pad(share, ((0, 0), (0, D - share.shape[1])))])
 
     down_sent = weight_grad(gelu_b, dbranch)
+    dinner_b, do_far[0] = after((dinner_b, do_far[0]), down_sent)
+    do_near[0] = send_on(do_near[0], do_far[0][:, 1:], 1)
     up_sent = weight_grad(dinner_b, hidden_low)
     part_out = weight_grad(o_rows, dattn)
     part_out = part_out.reshape(tuple(sizes[at] for at in order)).transpose(back)
     part_out = part_out.reshape(4 * heads * HD, D)
     out_kept, out_sent = cut_outer(part_out)
-    down_sum = weight_grad(gelu_a, dbranch, swap(down_sent, "ffn", 1))
-    up_sum = weight_grad(dinner_a, hidden_low, swap(up_sent, "ffn", 1))
-    out_sum = add_low(out_kept, swap(out_sent, "ffn", 1))
-    small = small + swap(small, "ffn", 1)
+    down_got, up_got, out_got = [swap(value, "ffn", 1) for value in (down_sent, up_sent, out_sent)]
+    down_got, do_far[1] = after((down_got, do_far[1]))
+    do_near[1] = send_on(do_near[1], do_far[1][:, 1:], 1)
+    small = small + swap(after(small, down_got), "ffn", 1)
+    down_sum = weight_grad(gelu_a, dbranch, down_got)
+    up_got, do_near[0], out_got = after((up_got, do_near[0], out_got), down_sum)
+    up_sum = weight_grad(dinner_a, hidden_low, up_got)
+    out_sum = add_low(out_kept, out_got)
 
     def quarters(value):
         rows = value.shape[0] // 4
@@ -785,20 +875,25 @@
     places = (("ffn", 2), ("seq", 1))
     then_places = (("seq", 1), ("ffn", 2))
 
-    def cut_all(values):
-        cuts = [cut_outer(value) for value in values]
-        return [pair[0] for pair in cuts], jnp.concatenate([pair[1] for pair in cuts], axis=0)
-
-    def add_all(kept_parts, got):
+    def send_groups(values, bits):
+        masks = masks_of(bits)
+        cuts = [cut_many(value, len(masks)) for value in values]
+        sent = [jnp.concatenate([parts[turn] for parts in cuts], axis=0) for turn in range(1, len(masks))]
+        got = [swap(value, "seq", mask) for value, mask in zip(sent, masks[1:])]
+        return [parts[0] for parts in cuts], got
+
+    def add_groups(own, got):
         values = []
         at = 0
-        for part in kept_parts:
-            values.append(add_low(part, got[at : at + part.shape[0]]))
+        for part in own:
+            values.append(add_many(part, [other[at : at + part.shape[0]] for other in got]).astype(low))
             at += part.shape[0]
         return values
 
-    do_got = after(do_got, sums)
-    far_places = list(reversed(far_stages()))
+    def small_step(bit):
+        return small + swap(small, "seq", bit)
+
+    do_near[0] = after(do_near[0], sums)
     part_heads = []
     dboth = []
     for head in range(heads):
@@ -806,29 +901,29 @@
             first_got = swaps(sums[3], places)
             small_got = swap(small, "ffn", 2)
         if head == 1:
-            do_got, first_got, small_got = after((do_got, first_got, small_got), part_heads[0])
+            do_near[1], first_got, small_got = after((do_near[1], first_got, small_got), part_heads[0])
             then_sent = [add_low(value, other) for value, other in zip(sums[2], first_got)]
             second_got = swaps(sums[1], places)
             then_got = swaps(then_sent, then_places)
             small = small + small_got
             small_got = swap(small, "seq", 1)
         if head == 2:
-            do_got, second_got, then_got, small_got = after(
-                (do_got, second_got, then_got, small_got), part_heads[1]
+            do_near[1], second_got, then_got, small_got = after(
+                (do_near[1], second_got, then_got, small_got), part_heads[1]
             )
             up_sum, low_sum = [
                 (value.astype(full) + second.astype(full) + then.astype(full)).astype(low)
                 for value, second, then in zip(sums[0], second_got, then_got)
             ]
             small = small + small_got
-            rest, sent = cut_all([up_sum, low_sum[:low_rows], low_sum[low_rows:]])
-            rest_got = swap(sent, *far_places[0])
-            small_got = swap(small, *far_places[0])
-        gw, both = attend_back(perm[head : head + 1], head, kept[head], do_got, tokens)
+            rest = [up_sum, low_sum[:low_rows], low_sum[low_rows:]]
+            own, rest_got = send_groups(rest, far_groups[0])
+            small_got = swap(small, "seq", 2)
+        do = (do_own, do_near[min(head, 1)], do_far[min(head, 1)])
+        gw, both = attend_back(perm[head : head + 1], head, kept[head], do, tokens)
         part_heads.append(gw)
         dboth.append(both)
-    rest_got, small_got, dboth = after((rest_got, small_got, dboth), part_heads[2])
-    rest = add_all(rest, rest_got)
+    small_got, dboth = after((small_got, dboth), part_heads[2])
     small = small + small_got
     part_qkv = jnp.stack(part_heads).reshape(heads, 4, HD, D)
     part_qkv = jnp.stack([part_qkv[:, 0], part_qkv[:, 2], part_qkv[:, 1]])
@@ -836,31 +931,25 @@
     qkv_kept, qkv_sent = cut_outer(part_qkv.reshape(seqs * 3 * heads * cut, D))
     qkv_got = swap(qkv_sent, "seq", 1)
     gx_kept, gx_sent = token_grad(dboth, head_rows, here)
-    qkv_got, gx_kept, gx_sent = after((qkv_got, gx_kept, gx_sent))
+    qkv_got, gx_kept, gx_sent, rest_got = after((qkv_got, gx_kept, gx_sent, rest_got))
     qkv_sum = add_low(qkv_kept, qkv_got)
+    rest = add_groups(own, rest_got)
     gx_got = swap(gx_sent, "ffn", 1)
-    for turn, place in enumerate(far_places):
-        qkv_kept, qkv_sent = cut_outer(qkv_sum)
-        qkv_got = swap(qkv_sent, *place)
-        if turn + 1 < len(far_places):
-            kept_parts, sent = cut_all(rest)
-            rest_got = swap(sent, *far_places[turn + 1])
-            small_got = swap(small, *far_places[turn + 1])
-            qkv_got, rest_got, small_got, gx_got = after((qkv_got, rest_got, small_got, gx_got))
-            rest = add_all(kept_parts, rest_got)
-            small = small + small_got
-        qkv_sum = add_low(qkv_kept, qkv_got)
+    for turn, bits in enumerate(far_groups):
+        if turn > 0:
+            rest = add_groups(*send_groups(rest, bits))
+        qkv_own, qkv_got = send_groups([qkv_sum], bits)
         if turn == 0:
+            qkv_got, gx_got = after((qkv_got, gx_got))
             gx_kept, gx_sent = cut_outer(add_low(gx_kept, gx_got))
-            gx_cuts = cut_outer(gx_sent)
-            gx_first = swap(gx_cuts[0], "ffn", 2)
+        (qkv_sum,) = add_groups(qkv_own, qkv_got)
+        for bit in bits:
+            if bit > 2:
+                small = small_step(bit)
     up_sum, down_sum, out_sum = rest
     grad_qkv, grad_out, grad_up, grad_down = [
         value.astype(full) for value in (qkv_sum, out_sum, up_sum, down_sum)
     ]
-    grad_norm = small[:4]
-    occupancy = small[4, : 4 * heads * clusters].reshape(4 * heads, clusters)
-
     grads = [grad_qkv, grad_out, grad_up, grad_down]
     moments = [0.5 * mom + grad for mom, grad in zip(momenta, grads)]
     most = max(moment.shape[0] for moment in moments)
@@ -872,12 +961,13 @@
         return lax.dynamic_index_in_dim(stack, jnp.bitwise_xor(ffn_here, turn), keepdims=False)
 
     picked = [swap(pick(turn), "ffn", turn) for turn in (1, 2, 3)]
-    picked, gx_first = after((picked, gx_first))
+    picked, gx_sent = after((picked, gx_sent))
     matrix = jnp.concatenate([pick(0)] + picked, axis=0)
-    gx_second = swap(gx_cuts[1], "ffn", 2)
-    panels = sum_halves(packed_gram(matrix), seq_stages())
-    panels = spread_halves(panels, seq_stages())
-    panels, gx_second = after((panels, gx_second))
+    gx_first, gx_second = [swap(value, "ffn", 2) for value in cut_outer(gx_sent)]
+    panels = sum_parts(packed_gram(matrix).astype(low))
+    panels, gx_first = after((panels, gx_first))
+    panels, gx_second = spread_parts(panels, gx_second)
+    panels, small = after((panels, small))
     gx_other = jnp.concatenate([gx_first, gx_second], axis=0)
     steps = schulz(panels, matrix).reshape(4, most, D)
     input_grad = dresidual + (gx_kept.astype(full) + gx_other.astype(full))
@@ -894,6 +984,8 @@
         own = own[: moments[member].shape[0]].astype(full)
         masters.append(weights[member] - step_rates[member] * own)
 
+    grad_norm = small[:4]
+    occupancy = small[4, : 4 * heads * clusters].reshape(4 * heads, clusters)
     first_fix = 1.0 - 0.9**ADAM_STEP
     second_fix = 1.0 - 0.999**ADAM_STEP
     first_new = 0.9 * norm_first + 0.1 * grad_norm

time: 433 us -> 389 us (0.90)
  waiting for transfers between devices: 132 us -> 97.1 us
  Pallas kernels: 184 us -> 167 us
  starting transfers between devices: 59.6 us -> 70 us
    ppermute x65 -> x69, waiting for transfers between devices: 132 us -> 97.1 us  [swap(): lax.ppermute(value, axis, [(place, place ^ bit) for place in range(size)])]
    ppermute x65 -> x69, starting transfers between devices: 59.6 us -> 70 us  [swap(): lax.ppermute(value, axis, [(place, place ^ bit) for place in range(size)])]
    pallas_call x3, Pallas kernels: 57.5 us -> 48.5 us  [attend_back(): pl.pallas_call(attend_back_kernel, grid=(1,), in_specs=[pl.BlockSpec(memo...]
    pallas_call x3, Pallas kernels: 51.3 us -> 42.9 us  [attend(): pl.pallas_call(attend_kernel, in_specs=[pl.BlockSpec(memory_space=pltpu.S...]
    unnamed x173 -> x181, local copies, waits for them, and re-layouts: 15.3 us -> 21 us
  transfers between devices with their start and end apart: 65 -> 69, of which waited for: 25 -> 26; matrix products, arithmetic and copies ran while one was open for 6% -> 6% of each run, Pallas kernels for 31% -> 31%
where the time goes in v3:
time: 389 us; the launch traced here: 385 us
  Pallas kernels  167 us (43%)
  waiting for transfers between devices  97.1 us (25%)
  starting transfers between devices  70 us (18%)
  local copies, waits for them, and re-layouts  25.5 us (7%)
  other arithmetic  22.1 us (6%)
    ppermute x69, waiting for transfers between devices, swap(): lax.ppermute(value, axis, [(place, place ^ bit) for place in range(size)])  97.1 us
    ppermute x69, starting transfers between devices, swap(): lax.ppermute(value, axis, [(place, place ^ bit) for place in range(size)])  70 us
    pallas_call x3, Pallas kernels, attend_back(): pl.pallas_call(attend_back_kernel, grid=(1,), in_specs=[pl.BlockSpec(memo...  48.5 us
    pallas_call x3, Pallas kernels, attend(): pl.pallas_call(attend_kernel, in_specs=[pl.BlockSpec(memory_space=pltpu.S...  42.9 us
    pallas_call x1, Pallas kernels, layer(): pl.pallas_call(lambda *refs: layer_kernel(heads, *refs), grid=(LAYER_STEP...  38.9 us
    unnamed x181, local copies, waits for them, and re-layouts  21 us
    pallas_call x5, Pallas kernels, weight_grad(): pl.pallas_call(weight_grad_kernel, grid=(width // part,), in_specs=in_spe...  19.9 us
    pallas_call x1, Pallas kernels, schulz(): pl.pallas_call(schulz_kernel, in_specs=[in_vmem, in_vmem], out_specs=in_v...  8.46 us
  transfers between devices with their start and end apart: 69, of which 26 were waited for; matrix products, arithmetic and copies ran while one was open for 6% of the time, Pallas kernels for 31%

profile of v3, /device:TPU:0, one launch (start us, length us, event | category | flops | bytes accessed | tf_op | source)
XLA Modules:
  0.0 384.8 jit_solution(13802632858149677364)
XLA Ops:
  1.7 4.1 %collective-permute-start.3 = (bf16[72,768]{1,0:T(8,128)(2,1)S(1)}, bf16[72,768]{1,0:T(8,128)(2,1)}, u32[]{:S(2)}, u32[]{:S(2)}) collective-permute-start(bf16[72,768]{1,0:T(8,128)(2,1)S(1)} %bitcast.181), channel_id=1, source_target_pairs={{0,16},{4,20},{8,24},{12,28},{16,0},{20,4},{24,8},{28,12},{1,17},{... | collective-permute-start | bytes 331784 | tf_op jit(solution)/shard_map/ppermute | solution.py:34
  5.8 1.6 collective-permute-start.4
  7.3 1.7 collective-permute-start.1
  10.1 1.6 convert_element_type.265
  13.0 1.9 collective-permute-done.5
  15.9 1.6 collective-permute-start.9
  17.5 3.9 %collective-permute-start.6 = (bf16[216,768]{1,0:T(8,128)(2,1)S(1)}, bf16[216,768]{1,0:T(8,128)(2,1)S(1)}, u32[]{:S(2)}, u32[]{:S(2)}) collective-permute-start(bf16[216,768]{1,0:T(8,128)(2,1)S(1)} %constant_dynamic-update-slice_fusion), channel_id=1, source_target_pairs={{0,16},{4,20},{8,24},{12,28},{16,0},{20,4},{24,8},{28,12},{1,17},{... | collective-permute-start | bytes 995336 | tf_op jit(solution)/shard_map/ppermute | solution.py:34
  21.4 1.5 collective-permute-start.8
  25.7 12.0 %collective-permute-done.6 = bf16[216,768]{1,0:T(8,128)(2,1)S(1)} collective-permute-done((bf16[216,768]{1,0:T(8,128)(2,1)S(1)}, bf16[216,768]{1,0:T(8,128)(2,1)S(1)}, u32[]{:S(2)}, u32[]{:S(2)}) %collective-permute-start.6) | collective-permute-done | bytes 331808 | tf_op jit(solution)/shard_map/ppermute | solution.py:34
  37.6 7.0 %collective-permute-done.7 = bf16[216,768]{1,0:T(8,128)(2,1)S(1)} collective-permute-done((bf16[216,768]{1,0:T(8,128)(2,1)S(1)}, bf16[216,768]{1,0:T(8,128)(2,1)S(1)}, u32[]{:S(2)}, u32[]{:S(2)}) %collective-permute-start.7) | collective-permute-done | bytes 331808 | tf_op jit(solution)/shard_map/ppermute | solution.py:34
  44.9 1.6 collective-permute-start.11
  48.5 14.3 %attend.3 = (bf16[512,128]{1,0:T(8,128)(2,1)S(1)}, bf16[512,128]{1,0:T(8,128)(2,1)S(1)}, bf16[1024,128]{1,0:T(8,128)(2,1)S(1)}, bf16[4096,128]{1,0:T(8,128)(2,1)S(1)}, bf16[4096,128]{1,0:T(8,128)(2,1)S(1)}) custom-call(s32[1,4096]{1,0:T(1,128)S(1)} %get-tuple-element.334.perm_ref, bf16[1024,768]{1,0:T(8,128)(2,1)S(1)} %copy-done.2, ...), custom_call_target="tpu_custom_call" | custom-call | flops 17999998976 | bytes 1000 | tf_op jit(solution)/shard_map/attend/pallas_call | solution.py:264
  63.9 1.6 collective-permute-start.12
  66.7 14.2 %attend.4 = (bf16[512,128]{1,0:T(8,128)(2,1)S(1)}, bf16[512,128]{1,0:T(8,128)(2,1)S(1)}, bf16[1024,128]{1,0:T(8,128)(2,1)S(1)}, bf16[4096,128]{1,0:T(8,128)(2,1)S(1)}, bf16[4096,128]{1,0:T(8,128)(2,1)S(1)}) custom-call(s32[1,4096]{1,0:T(1,128)S(1)} %get-tuple-element.149.perm_ref, bf16[1024,768]{1,0:T(8,128)(2,1)S(1)} %copy-done.2, ...), custom_call_target="tpu_custom_call" | custom-call | flops 17999998976 | bytes 1000 | tf_op jit(solution)/shard_map/attend/pallas_call | solution.py:264
  81.0 1.6 collective-permute-start.18
  82.6 2.7 collective-permute-done.14.refs_2_
  88.6 14.4 %attend.5 = (bf16[512,128]{1,0:T(8,128)(2,1)S(1)}, bf16[512,128]{1,0:T(8,128)(2,1)S(1)}, bf16[1024,128]{1,0:T(8,128)(2,1)S(1)}, bf16[4096,128]{1,0:T(8,128)(2,1)S(1)}, bf16[4096,128]{1,0:T(8,128)(2,1)S(1)}) custom-call(s32[1,4096]{1,0:T(1,128)S(1)} %get-tuple-element.158.perm_ref, bf16[1024,768]{1,0:T(8,128)(2,1)S(1)} %copy-done.2, ...), custom_call_target="tpu_custom_call" | custom-call | flops 17999998976 | bytes 1000 | tf_op jit(solution)/shard_map/attend/pallas_call | solution.py:264
  107.2 1.6 collective-permute-start.22
  109.0 6.5 %collective-permute-done.22.refs_10_ = bf16[1024,128]{1,0:T(8,128)(2,1)S(1)} collective-permute-done((bf16[1024,128]{1,0:T(8,128)(2,1)S(1)}, bf16[1024,128]{1,0:T(8,128)(2,1)S(1)}, u32[]{:S(2)}, u32[]{:S(2)}) %collective-permute-start.22) | collective-permute-done | bytes 262176 | tf_op jit(solution)/shard_map/ppermute | solution.py:34
  119.7 38.9 %layer.1 = (bf16[3,1,512,128]{3,2,1,0:T(8,128)(2,1)}, bf16[1,1,512,128]{3,2,1,0:T(8,128)(2,1)}, bf16[2,1,512,128]{3,2,1,0:T(8,128)(2,1)}, bf16[1,2,512,128]{3,2,...) custom-call(bf16[512,128]{1,0:T(8,128)(2,1)} %copy-done.35, ...), custom_call_target="tpu_custom_call" | custom-call | flops 40000000000 | bytes 1000 | tf_op jit(solution)/shard_map/layer/pallas_call | solution.py:555
  158.6 1.6 collective-permute-start.27
  160.2 1.9 copy-done.13
  163.5 5.0 %weight_grad.5 = bf16[1536,768]{1,0:T(8,128)(2,1)} custom-call(bf16[1024,1536]{1,0:T(8,128)(2,1)S(1)} %bitcast.167, bf16[1024,768]{1,0:T(8,128)(2,1)S(1)} %bitcast.170), custom_call_target="tpu_custom_call" | custom-call | flops 4000000000 | bytes 1000 | tf_op jit(solution)/shard_map/weight_grad/pallas_call | solution.py:613
  168.4 4.5 %weight_grad.6 = bf16[1536,768]{1,0:T(8,128)(2,1)} custom-call(bf16[1024,1536]{1,0:T(8,128)(2,1)S(1)} %bitcast.166, bf16[1024,768]{1,0:T(8,128)(2,1)S(1)} %bitcast.168), custom_call_target="tpu_custom_call" | custom-call | flops 4000000000 | bytes 1000 | tf_op jit(solution)/shard_map/weight_grad/pallas_call | solution.py:613
  177.2 1.8 weight_grad.7
  180.1 7.8 %collective-permute-done.32.do2 = bf16[2,2,512,128]{3,2,1,0:T(8,128)(2,1)S(1)} collective-permute-done((bf16[2,2,512,128]{3,2,1,0:T(8,128)(2,1)}, bf16[2,2,512,128]{3,2,1,0:T(8,128)(2,1)S(1)}, u32[]{:S(2)}, u32[]{:S(2)}) %collective-permute-start.32) | collective-permute-done | bytes 524320 | tf_op jit(solution)/shard_map/ppermute | solution.py:34
  188.0 4.9 %weight_grad.8 = bf16[1536,768]{1,0:T(8,128)(2,1)S(1)} custom-call(bf16[1024,1536]{1,0:T(8,128)(2,1)S(1)} %bitcast.165, bf16[1024,768]{1,0:T(8,128)(2,1)S(1)} %bitcast.171, bf16[1536,768]{1,0:T(8,128)(2,1)} %collective-permute-done.31.refs_0_), custom_call_target="tpu_custom_call" | custom-call | flops 4000000000 | bytes 1000 | tf_op jit(solution)/shard_map/weight_grad/pallas_call | solution.py:613
  195.9 3.7 weight_grad.9
  201.3 1.6 collective-permute-start.39
  203.0 16.3 %attend_back.3 = (bf16[256,768]{1,0:T(8,128)(2,1)S(1)}, bf16[4096,256]{1,0:T(8,128)(2,1)S(1)}) custom-call(s32[1,4096]{1,0:T(1,128)S(1)} %get-tuple-element.334.perm_ref, bf16[4096,128]{1,0:T(8,128)(2,1)S(1)} %copy-done.31, bf16[4096,128]{1,0:T(8,128)(2,1)S(1)} %copy-done.33, bf16[3,1,512,128]{3,2,1,0:T(8,128)(2,1)S(1)} %copy-done.34, ...), custom_call_target="tpu_custom_call" | custom-call | flops 22000001024 | bytes 1000 | tf_op jit(solution)/shard_map/attend_back/pallas_call | solution.py:350
  222.3 1.6 collective-permute-start.40
  224.0 16.1 %attend_back.4 = (bf16[256,768]{1,0:T(8,128)(2,1)S(1)}, bf16[4096,256]{1,0:T(8,128)(2,1)S(1)}) custom-call(s32[1,4096]{1,0:T(1,128)S(1)} %get-tuple-element.149.perm_ref, bf16[4096,128]{1,0:T(8,128)(2,1)S(1)} %copy-done.27, bf16[4096,128]{1,0:T(8,128)(2,1)S(1)} %copy-done.29, bf16[3,1,512,128]{3,2,1,0:T(8,128)(2,1)S(1)} %copy-done.34, ...), custom_call_target="tpu_custom_call" | custom-call | flops 22000001024 | bytes 1000 | tf_op jit(solution)/shard_map/attend_back/pallas_call | solution.py:350
  240.1 7.5 %collective-permute-done.40 = bf16[384,768]{1,0:T(8,128)(2,1)S(1)} collective-permute-done((bf16[384,768]{1,0:T(8,128)(2,1)S(1)}, bf16[384,768]{1,0:T(8,128)(2,1)S(1)}, u32[]{:S(2)}, u32[]{:S(2)}) %collective-permute-start.40) | collective-permute-done | bytes 589856 | tf_op jit(solution)/shard_map/ppermute | solution.py:34
  247.7 2.2 collective-permute-done.41
  251.9 1.9 collective-permute-start.47
  253.9 4.5 %collective-permute-start.46 = (bf16[216,768]{1,0:T(8,128)(2,1)S(1)}, bf16[216,768]{1,0:T(8,128)(2,1)S(1)}, u32[]{:S(2)}, u32[]{:S(2)}) collective-permute-start(bf16[216,768]{1,0:T(8,128)(2,1)S(1)} %pad_maximum_fusion.17), channel_id=1, source_target_pairs={{0,8},{4,12},{8,0},{12,4},{16,24},{20,28},{24,16},{28,20},{1,9},{5... | collective-permute-start | bytes 995336 | tf_op jit(solution)/shard_map/ppermute | solution.py:34
  258.4 1.5 collective-permute-start.45
  260.0 2.0 collective-permute-start.44
  262.0 16.1 %attend_back.5 = (bf16[256,768]{1,0:T(8,128)(2,1)S(1)}, bf16[4096,256]{1,0:T(8,128)(2,1)S(1)}) custom-call(s32[1,4096]{1,0:T(1,128)S(1)} %get-tuple-element.158.perm_ref, bf16[4096,128]{1,0:T(8,128)(2,1)S(1)} %copy-done.23, bf16[4096,128]{1,0:T(8,128)(2,1)S(1)} %copy-done.25, bf16[3,1,512,128]{3,2,1,0:T(8,128)(2,1)S(1)} %copy-done.34, ...), custom_call_target="tpu_custom_call" | custom-call | flops 22000001024 | bytes 1000 | tf_op jit(solution)/shard_map/attend_back/pallas_call | solution.py:350
  280.3 8.0 %token_grad.1 = (bf16[2048,768]{1,0:T(8,128)(2,1)S(1)}, bf16[2048,768]{1,0:T(8,128)(2,1)}) custom-call(bf16[4096,256]{1,0:T(8,128)(2,1)S(1)} %get-tuple-element.210.d0, bf16[4096,256]{1,0:T(8,128)(2,1)S(1)} %copy-done.21, bf16[4096,256]{1,0:T(8,128)(2,1)S(1)} %get-tuple-element.212.d2, bf16[768,768]{1,0:T(8,128)(2,1)S(1)} %bitcast.155), custom_call_target="tpu_custom_call" | custom-call | flops 8000000000 | bytes 1000 | tf_op jit(solution)/shard_map/token_grad/pallas_call | solution.py:397
  289.9 4.2 %collective-permute-done.65 = f32[5,768]{1,0:T(8,128)S(1)} collective-permute-done((f32[5,768]{1,0:T(8,128)S(1)}, f32[5,768]{1,0:T(8,128)S(1)}, u32[]{:S(2)}, u32[]{:S(2)}) %collective-permute-start.65) | collective-permute-done | bytes 15392 | tf_op jit(solution)/shard_map/ppermute | solution.py:34
  296.0 1.5 collective-permute-start.49
  297.6 2.4 collective-permute-start.50
  300.0 1.4 fusion.14
  301.5 2.0 fusion.6
  303.5 2.2 collective-permute-done.48
  306.9 1.5 collective-permute-start.53
  308.7 2.7 add_convert_fusion
  311.4 1.7 copy-done.38
  313.6 2.3 collective-permute-done.54
  320.8 6.4 %collective-permute-done.55 = bf16[1344,128]{1,0:T(8,128)(2,1)S(1)} collective-permute-done((bf16[1344,128]{1,0:T(8,128)(2,1)S(1)}, bf16[1344,128]{1,0:T(8,128)(2,1)S(1)}, u32[]{:S(2)}, u32[]{:S(2)}) %collective-permute-start.55) | collective-permute-done | bytes 344096 | tf_op jit(solution)/shard_map/ppermute | solution.py:34
  327.3 2.0 collective-permute-start.56
  329.6 2.2 collective-permute-start.58
  332.4 3.7 collective-permute-done.56
  337.2 1.9 collective-permute-done.59
  339.1 1.9 collective-permute-start.60
  341.4 2.1 collective-permute-start.62
  343.6 11.5 %collective-permute-done.63 = bf16[512,768]{1,0:T(8,128)(2,1)S(1)} collective-permute-done((bf16[512,768]{1,0:T(8,128)(2,1)S(1)}, bf16[512,768]{1,0:T(8,128)(2,1)S(1)}, u32[]{:S(2)}, u32[]{:S(2)}) %collective-permute-start.63) | collective-permute-done | bytes 786464 | tf_op jit(solution)/shard_map/ppermute | solution.py:34
  356.3 2.2 bitcast_add_fusion
  358.5 5.8 %collective-permute-done.64 = bf16[1344,128]{1,0:T(8,128)(2,1)S(1)} collective-permute-done((bf16[1344,128]{1,0:T(8,128)(2,1)S(1)}, bf16[1344,128]{1,0:T(8,128)(2,1)S(1)}, u32[]{:S(2)}, u32[]{:S(2)}) %collective-permute-start.64) | collective-permute-done | bytes 344096 | tf_op jit(solution)/shard_map/ppermute | solution.py:34
  364.5 8.5 %schulz.1 = bf16[384,768]{1,0:T(8,128)(2,1)S(1)} custom-call(bf16[2688,128]{1,0:T(8,128)(2,1)S(1)} %pad_maximum_fusion.7.panels_ref, bf16[384,768]{1,0:T(8,128)(2,1)S(1)} %pad_maximum_fusion.11.matrix_ref), custom_call_target="tpu_custom_call" | custom-call | flops 8000000000 | bytes 1000 | tf_op jit(solution)/shard_map/schulz/pallas_call | solution.py:689
  373.2 1.8 collective-permute-start.67
  376.4 3.5 collective-permute-done.67
  379.9 2.3 collective-permute-done.68
  (381 shorter events, 59.4 us)
Async XLA Ops:
  1.7 11.3 %collective-permute-start.3 = (bf16[72,768]{1,0:T(8,128)(2,1)S(1)}, bf16[72,768]{1,0:T(8,128)(2,1)}, u32[]{:S(2)}, u32[]{:S(2)}) collective-permute-start(bf16[72,768]{1,0:T(8,128)(2,1)S(1)} %bitcast.181), channel_id=1, source_target_pairs={{0,16},{4,20},{8,24},{12,28},{16,0},{20,4},{24,8},{28,12},{1,17},{... | collective-permute-start | bytes 331784 | tf_op jit(solution)/shard_map/ppermute | solution.py:34
  5.8 7.2 %collective-permute-start.4 = (bf16[72,768]{1,0:T(8,128)(2,1)S(1)}, bf16[72,768]{1,0:T(8,128)(2,1)}, u32[]{:S(2)}, u32[]{:S(2)}) collective-permute-start(bf16[72,768]{1,0:T(8,128)(2,1)S(1)} %bitcast.182), channel_id=1, source_target_pairs={{0,8},{4,12},{8,0},{12,4},{16,24},{20,28},{24,16},{28,20},{1,9},{5... | collective-permute-start | bytes 331784 | tf_op jit(solution)/shard_map/ppermute | solution.py:34
  7.3 7.5 %collective-permute-start.5 = (bf16[72,768]{1,0:T(8,128)(2,1)S(1)}, bf16[72,768]{1,0:T(8,128)(2,1)}, u32[]{:S(2)}, u32[]{:S(2)}) collective-permute-start(bf16[72,768]{1,0:T(8,128)(2,1)S(1)} %bitcast.183), channel_id=1, source_target_pairs={{0,24},{4,28},{8,16},{12,20},{16,8},{20,12},{24,0},{28,4},{1,25},{... | collective-permute-start | bytes 331784 | tf_op jit(solution)/shard_map/ppermute | solution.py:34
  7.3 37.4 %collective-permute-start.1 = (bf16[1024,768]{1,0:T(8,128)(2,1)}, bf16[1024,768]{1,0:T(8,128)(2,1)S(1)}, u32[]{:S(2)}, u32[]{:S(2)}) collective-permute-start(bf16[1024,768]{1,0:T(8,128)(2,1)} %x0.11), channel_id=1, source_target_pairs={{0,2},{1,3},{2,0},{3,1},{4,6},{5,7},{6,4},{7,5},{8,10},{9,11},{10,... | collective-permute-start | bytes 4718600 | tf_op jit(solution)/shard_map/ppermute | solution.py:34
  15.9 28.8 %collective-permute-start.9 = (bf16[288,768]{1,0:T(8,128)(2,1)S(1)}, bf16[288,768]{1,0:T(8,128)(2,1)S(1)}, u32[]{:S(2)}, u32[]{:S(2)}) collective-permute-start(bf16[288,768]{1,0:T(8,128)(2,1)S(1)} %pad_maximum_fusion.14), channel_id=1, source_target_pairs={{0,4},{4,0},{8,12},{12,8},{16,20},{20,16},{24,28},{28,24},{1,5},{5... | collective-permute-start | bytes 1327112 | tf_op jit(solution)/shard_map/ppermute | solution.py:34
  17.5 20.1 %collective-permute-start.6 = (bf16[216,768]{1,0:T(8,128)(2,1)S(1)}, bf16[216,768]{1,0:T(8,128)(2,1)S(1)}, u32[]{:S(2)}, u32[]{:S(2)}) collective-permute-start(bf16[216,768]{1,0:T(8,128)(2,1)S(1)} %constant_dynamic-update-slice_fusion), channel_id=1, source_target_pairs={{0,16},{4,20},{8,24},{12,28},{16,0},{20,4},{24,8},{28,12},{1,17},{... | collective-permute-start | bytes 995336 | tf_op jit(solution)/shard_map/ppermute | solution.py:34
  21.4 23.2 %collective-permute-start.7 = (bf16[216,768]{1,0:T(8,128)(2,1)S(1)}, bf16[216,768]{1,0:T(8,128)(2,1)S(1)}, u32[]{:S(2)}, u32[]{:S(2)}) collective-permute-start(bf16[216,768]{1,0:T(8,128)(2,1)S(1)} %constant_dynamic-update-slice_fusion), channel_id=1, source_target_pairs={{0,8},{4,12},{8,0},{12,4},{16,24},{20,28},{24,16},{28,20},{1,9},{5... | collective-permute-start | bytes 995336 | tf_op jit(solution)/shard_map/ppermute | solution.py:34
  21.4 23.2 %collective-permute-start.8 = (bf16[216,768]{1,0:T(8,128)(2,1)S(1)}, bf16[216,768]{1,0:T(8,128)(2,1)S(1)}, u32[]{:S(2)}, u32[]{:S(2)}) collective-permute-start(bf16[216,768]{1,0:T(8,128)(2,1)S(1)} %constant_dynamic-update-slice_fusion), channel_id=1, source_target_pairs={{0,24},{4,28},{8,16},{12,20},{16,8},{20,12},{24,0},{28,4},{1,25},{... | collective-permute-start | bytes 995336 | tf_op jit(solution)/shard_map/ppermute | solution.py:34
  37.6 9.9 %collective-permute-start = (bf16[1024,768]{1,0:T(8,128)(2,1)S(1)}, bf16[1024,768]{1,0:T(8,128)(2,1)S(1)}, u32[]{:S(2)}, u32[]{:S(2)}) collective-permute-start(bf16[1024,768]{1,0:T(8,128)(2,1)S(1)} %copy-done.2), channel_id=1, source_target_pairs={{0,1},{1,0},{2,3},{3,2},{4,5},{5,4},{6,7},{7,6},{8,9},{9,8},{10,11... | collective-permute-start | bytes 4718600 | tf_op jit(solution)/shard_map/ppermute | solution.py:34
  44.9 18.9 %collective-permute-start.11 = (bf16[480,768]{1,0:T(8,128)(2,1)S(1)}, bf16[480,768]{1,0:T(8,128)(2,1)S(1)}, u32[]{:S(2)}, u32[]{:S(2)}) collective-permute-start(bf16[480,768]{1,0:T(8,128)(2,1)S(1)} %constant_dynamic-update-slice_fusion.8), channel_id=1, source_target_pairs={{0,2},{1,3},{2,0},{3,1},{4,6},{5,7},{6,4},{7,5},{8,10},{9,11},{10,... | collective-permute-start | bytes 2211848 | tf_op jit(solution)/shard_map/ppermute | solution.py:34
  46.5 16.4 %collective-permute-start.10 = (bf16[384,768]{1,0:T(8,128)(2,1)S(1)}, bf16[384,768]{1,0:T(8,128)(2,1)S(1)}, u32[]{:S(2)}, u32[]{:S(2)}) collective-permute-start(bf16[384,768]{1,0:T(8,128)(2,1)S(1)} %pad_maximum_fusion.8), channel_id=1, source_target_pairs={{0,4},{4,0},{8,12},{12,8},{16,20},{20,16},{24,28},{28,24},{1,5},{5... | collective-permute-start | bytes 1769480 | tf_op jit(solution)/shard_map/ppermute | solution.py:34
  63.9 21.4 %collective-permute-start.12 = (bf16[384,768]{1,0:T(8,128)(2,1)S(1)}, bf16[384,768]{1,0:T(8,128)(2,1)S(1)}, u32[]{:S(2)}, u32[]{:S(2)}) collective-permute-start(bf16[384,768]{1,0:T(8,128)(2,1)S(1)} %pad_maximum_fusion.8), channel_id=1, source_target_pairs={{0,2},{1,3},{2,0},{3,1},{4,6},{5,7},{6,4},{7,5},{8,10},{9,11},{10,... | collective-permute-start | bytes 1769480 | tf_op jit(solution)/shard_map/ppermute | solution.py:34
  65.5 19.8 %collective-permute-start.15 = (bf16[768,768]{1,0:T(8,128)(2,1)S(1)}, bf16[768,768]{1,0:T(8,128)(2,1)S(1)}, u32[]{:S(2)}, u32[]{:S(2)}) collective-permute-start(bf16[768,768]{1,0:T(8,128)(2,1)S(1)} %constant_dynamic-update-slice_fusion.13.refs_16_), channel_id=1, source_target_pairs={{0,1},{1,0},{2,3},{3,2},{4,5},{5,4},{6,7},{7,6},{8,9},{9,8},{10,11... | collective-permute-start | bytes 3538952 | tf_op jit(solution)/shard_map/ppermute | solution.py:34
  65.6 19.7 %collective-permute-start.13 = (bf16[480,768]{1,0:T(8,128)(2,1)S(1)}, bf16[480,768]{1,0:T(8,128)(2,1)S(1)}, u32[]{:S(2)}, u32[]{:S(2)}) collective-permute-start(bf16[480,768]{1,0:T(8,128)(2,1)S(1)} %constant_dynamic-update-slice_fusion.8), channel_id=1, source_target_pairs={{0,4},{4,0},{8,12},{12,8},{16,20},{20,16},{24,28},{28,24},{1,5},{5... | collective-permute-start | bytes 2211848 | tf_op jit(solution)/shard_map/ppermute | solution.py:34
  66.2 19.1 %collective-permute-start.14 = (bf16[1024,128]{1,0:T(8,128)(2,1)S(1)}, bf16[1024,128]{1,0:T(8,128)(2,1)S(1)}, u32[]{:S(2)}, u32[]{:S(2)}) collective-permute-start(bf16[1024,128]{1,0:T(8,128)(2,1)S(1)} %get-tuple-element.148), channel_id=1, source_target_pairs={{0,2},{1,3},{2,0},{3,1},{4,6},{5,7},{6,4},{7,5},{8,10},{9,11},{10,... | collective-permute-start | bytes 786440 | tf_op jit(solution)/shard_map/ppermute | solution.py:34
  81.0 23.4 %collective-permute-start.18 = (bf16[1024,128]{1,0:T(8,128)(2,1)S(1)}, bf16[1024,128]{1,0:T(8,128)(2,1)S(1)}, u32[]{:S(2)}, u32[]{:S(2)}) collective-permute-start(bf16[1024,128]{1,0:T(8,128)(2,1)S(1)} %get-tuple-element.154), channel_id=1, source_target_pairs={{0,2},{1,3},{2,0},{3,1},{4,6},{5,7},{6,4},{7,5},{8,10},{9,11},{10,... | collective-permute-start | bytes 786440 | tf_op jit(solution)/shard_map/ppermute | solution.py:34
  86.4 19.1 %collective-permute-start.20 = (bf16[768,768]{1,0:T(8,128)(2,1)S(1)}, bf16[768,768]{1,0:T(8,128)(2,1)S(1)}, u32[]{:S(2)}, u32[]{:S(2)}) collective-permute-start(bf16[768,768]{1,0:T(8,128)(2,1)S(1)} %pad_maximum_fusion.refs_20_), channel_id=1, source_target_pairs={{0,1},{1,0},{2,3},{3,2},{4,5},{5,4},{6,7},{7,6},{8,9},{9,8},{10,11... | collective-permute-start | bytes 3538952 | tf_op jit(solution)/shard_map/ppermute | solution.py:34
  86.4 18.0 %collective-permute-start.19 = (bf16[1024,128]{1,0:T(8,128)(2,1)S(1)}, bf16[1024,128]{1,0:T(8,128)(2,1)S(1)}, u32[]{:S(2)}, u32[]{:S(2)}) collective-permute-start(bf16[1024,128]{1,0:T(8,128)(2,1)S(1)} %pad_maximum_fusion.21), channel_id=1, source_target_pairs={{0,1},{1,0},{2,3},{3,2},{4,5},{5,4},{6,7},{7,6},{8,9},{9,8},{10,11... | collective-permute-start | bytes 786440 | tf_op jit(solution)/shard_map/ppermute | solution.py:34
  87.0 18.5 %collective-permute-start.17 = (bf16[480,768]{1,0:T(8,128)(2,1)S(1)}, bf16[480,768]{1,0:T(8,128)(2,1)S(1)}, u32[]{:S(2)}, u32[]{:S(2)}) collective-permute-start(bf16[480,768]{1,0:T(8,128)(2,1)S(1)} %collective-permute-done.11), channel_id=1, source_target_pairs={{0,4},{4,0},{8,12},{12,8},{16,20},{20,16},{24,28},{28,24},{1,5},{5... | collective-permute-start | bytes 2211848 | tf_op jit(solution)/shard_map/ppermute | solution.py:34
  87.2 17.3 %collective-permute-start.16 = (bf16[384,768]{1,0:T(8,128)(2,1)S(1)}, bf16[384,768]{1,0:T(8,128)(2,1)S(1)}, u32[]{:S(2)}, u32[]{:S(2)}) collective-permute-start(bf16[384,768]{1,0:T(8,128)(2,1)S(1)} %collective-permute-done.10), channel_id=1, source_target_pairs={{0,2},{1,3},{2,0},{3,1},{4,6},{5,7},{6,4},{7,5},{8,10},{9,11},{10,... | collective-permute-start | bytes 1769480 | tf_op jit(solution)/shard_map/ppermute | solution.py:34
  106.5 11.0 %collective-permute-start.26 = (bf16[768,768]{1,0:T(8,128)(2,1)S(1)}, bf16[768,768]{1,0:T(8,128)(2,1)S(1)}, u32[]{:S(2)}, u32[]{:S(2)}) collective-permute-start(bf16[768,768]{1,0:T(8,128)(2,1)S(1)} %pad_maximum_fusion.1.refs_21_), channel_id=1, source_target_pairs={{0,1},{1,0},{2,3},{3,2},{4,5},{5,4},{6,7},{7,6},{8,9},{9,8},{10,11... | collective-permute-start | bytes 3538952 | tf_op jit(solution)/shard_map/ppermute | solution.py:34
  106.6 10.9 %collective-permute-start.25 = (bf16[768,768]{1,0:T(8,128)(2,1)S(1)}, bf16[768,768]{1,0:T(8,128)(2,1)S(1)}, u32[]{:S(2)}, u32[]{:S(2)}) collective-permute-start(bf16[768,768]{1,0:T(8,128)(2,1)S(1)} %constant_dynamic-update-slice_fusion.20.refs_17_), channel_id=1, source_target_pairs={{0,1},{1,0},{2,3},{3,2},{4,5},{5,4},{6,7},{7,6},{8,9},{9,8},{10,11... | collective-permute-start | bytes 3538952 | tf_op jit(solution)/shard_map/ppermute | solution.py:34
  107.2 8.3 %collective-permute-start.22 = (bf16[1024,128]{1,0:T(8,128)(2,1)S(1)}, bf16[1024,128]{1,0:T(8,128)(2,1)S(1)}, u32[]{:S(2)}, u32[]{:S(2)}) collective-permute-start(bf16[1024,128]{1,0:T(8,128)(2,1)S(1)} %get-tuple-element.167), channel_id=1, source_target_pairs={{0,2},{1,3},{2,0},{3,1},{4,6},{5,7},{6,4},{7,5},{8,10},{9,11},{10,... | collective-permute-start | bytes 786440 | tf_op jit(solution)/shard_map/ppermute | solution.py:34
  108.9 7.3 %collective-permute-start.24 = (bf16[384,768]{1,0:T(8,128)(2,1)S(1)}, bf16[384,768]{1,0:T(8,128)(2,1)S(1)}, u32[]{:S(2)}, u32[]{:S(2)}) collective-permute-start(bf16[384,768]{1,0:T(8,128)(2,1)S(1)} %pad_maximum_fusion.9), channel_id=1, source_target_pairs={{0,1},{1,0},{2,3},{3,2},{4,5},{5,4},{6,7},{7,6},{8,9},{9,8},{10,11... | collective-permute-start | bytes 1769480 | tf_op jit(solution)/shard_map/ppermute | solution.py:34
  158.6 9.9 %collective-permute-start.27 = (bf16[1,2,512,128]{3,2,1,0:T(8,128)(2,1)}, bf16[1,2,512,128]{3,2,1,0:T(8,128)(2,1)S(1)}, u32[]{:S(2)}, u32[]{:S(2)}) collective-permute-start(bf16[1,2,512,128]{3,2,1,0:T(8,128)(2,1)} %get-tuple-element.177), channel_id=1, source_target_pairs={{0,2},{1,3},{2,0},{3,1},{4,6},{5,7},{6,4},{7,5},{8,10},{9,11},{10,... | collective-permute-start | bytes 786440 | tf_op jit(solution)/shard_map/ppermute | solution.py:34
  168.4 19.5 %collective-permute-start.31 = (bf16[1536,768]{1,0:T(8,128)(2,1)}, bf16[1536,768]{1,0:T(8,128)(2,1)}, u32[]{:S(2)}, u32[]{:S(2)}) collective-permute-start(bf16[1536,768]{1,0:T(8,128)(2,1)} %weight_grad.5), channel_id=1, source_target_pairs={{0,1},{1,0},{2,3},{3,2},{4,5},{5,4},{6,7},{7,6},{8,9},{9,8},{10,11... | collective-permute-start | bytes 7077896 | tf_op jit(solution)/shard_map/ppermute | solution.py:34
  173.0 22.1 %collective-permute-start.28 = (bf16[1536,768]{1,0:T(8,128)(2,1)}, bf16[1536,768]{1,0:T(8,128)(2,1)S(1)}, u32[]{:S(2)}, u32[]{:S(2)}) collective-permute-start(bf16[1536,768]{1,0:T(8,128)(2,1)} %weight_grad.6), channel_id=1, source_target_pairs={{0,1},{1,0},{2,3},{3,2},{4,5},{5,4},{6,7},{7,6},{8,9},{9,8},{10,11... | collective-permute-start | bytes 7077896 | tf_op jit(solution)/shard_map/ppermute | solution.py:34
  173.9 14.1 %collective-permute-start.32 = (bf16[2,2,512,128]{3,2,1,0:T(8,128)(2,1)}, bf16[2,2,512,128]{3,2,1,0:T(8,128)(2,1)S(1)}, u32[]{:S(2)}, u32[]{:S(2)}) collective-permute-start(bf16[2,2,512,128]{3,2,1,0:T(8,128)(2,1)} %get-tuple-element.187), channel_id=1, source_target_pairs={{0,2},{1,3},{2,0},{3,1},{4,6},{5,7},{6,4},{7,5},{8,10},{9,11},{10,... | collective-permute-start | bytes 1572872 | tf_op jit(solution)/shard_map/ppermute | solution.py:34
  179.2 15.8 %collective-permute-start.30 = (bf16[384,768]{1,0:T(8,128)(2,1)S(1)}, bf16[384,768]{1,0:T(8,128)(2,1)S(1)}, u32[]{:S(2)}, u32[]{:S(2)}) collective-permute-start(bf16[384,768]{1,0:T(8,128)(2,1)S(1)} %bitcast.189), channel_id=1, source_target_pairs={{0,1},{1,0},{2,3},{3,2},{4,5},{5,4},{6,7},{7,6},{8,9},{9,8},{10,11... | collective-permute-start | bytes 1769480 | tf_op jit(solution)/shard_map/ppermute | solution.py:34
  180.0 15.1 %collective-permute-start.29 = (bf16[1,2,512,128]{3,2,1,0:T(8,128)(2,1)S(1)}, bf16[1,2,512,128]{3,2,1,0:T(8,128)(2,1)S(1)}, u32[]{:S(2)}, u32[]{:S(2)}) collective-permute-start(bf16[1,2,512,128]{3,2,1,0:T(8,128)(2,1)S(1)} %pad_maximum_fusion.24), channel_id=1, source_target_pairs={{0,1},{1,0},{2,3},{3,2},{4,5},{5,4},{6,7},{7,6},{8,9},{9,8},{10,11... | collective-permute-start | bytes 786440 | tf_op jit(solution)/shard_map/ppermute | solution.py:34
  187.9 6.6 %collective-permute-start.36 = (f32[5,768]{1,0:T(8,128)S(1)}, f32[5,768]{1,0:T(8,128)S(1)}, u32[]{:S(2)}, u32[]{:S(2)}) collective-permute-start(f32[5,768]{1,0:T(8,128)S(1)} %select_maximum_fusion), channel_id=1, source_target_pairs={{0,1},{1,0},{2,3},{3,2},{4,5},{5,4},{6,7},{7,6},{8,9},{9,8},{10,11... | collective-permute-start | bytes 46088 | tf_op jit(solution)/shard_map/ppermute | solution.py:34
  193.9 26.5 %collective-permute-start.33 = (bf16[2,2,512,128]{3,2,1,0:T(8,128)(2,1)S(1)}, bf16[2,2,512,128]{3,2,1,0:T(8,128)(2,1)S(1)}, u32[]{:S(2)}, u32[]{:S(2)}) collective-permute-start(bf16[2,2,512,128]{3,2,1,0:T(8,128)(2,1)S(1)} %pad_maximum_fusion.13), channel_id=1, source_target_pairs={{0,1},{1,0},{2,3},{3,2},{4,5},{5,4},{6,7},{7,6},{8,9},{9,8},{10,11... | collective-permute-start | bytes 1572872 | tf_op jit(solution)/shard_map/ppermute | solution.py:34
  194.5 24.8 %collective-permute-start.37 = (f32[5,768]{1,0:T(8,128)S(1)}, f32[5,768]{1,0:T(8,128)S(1)}, u32[]{:S(2)}, u32[]{:S(2)}) collective-permute-start(f32[5,768]{1,0:T(8,128)S(1)} %fusion.17), channel_id=1, source_target_pairs={{0,2},{1,3},{2,0},{3,1},{4,6},{5,7},{6,4},{7,5},{8,10},{9,11},{10,... | collective-permute-start | bytes 46088 | tf_op jit(solution)/shard_map/ppermute | solution.py:34
  199.7 20.7 %collective-permute-start.35 = (bf16[480,768]{1,0:T(8,128)(2,1)S(1)}, bf16[480,768]{1,0:T(8,128)(2,1)S(1)}, u32[]{:S(2)}, u32[]{:S(2)}) collective-permute-start(bf16[480,768]{1,0:T(8,128)(2,1)S(1)} %pad_maximum_fusion.6), channel_id=1, source_target_pairs={{0,4},{4,0},{8,12},{12,8},{16,20},{20,16},{24,28},{28,24},{1,5},{5... | collective-permute-start | bytes 2211848 | tf_op jit(solution)/shard_map/ppermute | solution.py:34
  200.3 20.1 %collective-permute-start.34 = (bf16[384,768]{1,0:T(8,128)(2,1)S(1)}, bf16[384,768]{1,0:T(8,128)(2,1)S(1)}, u32[]{:S(2)}, u32[]{:S(2)}) collective-permute-start(bf16[384,768]{1,0:T(8,128)(2,1)S(1)} %get-tuple-element.262), channel_id=1, source_target_pairs={{0,2},{1,3},{2,0},{3,1},{4,6},{5,7},{6,4},{7,5},{8,10},{9,11},{10,... | collective-permute-start | bytes 1769480 | tf_op jit(solution)/shard_map/ppermute | solution.py:34
  201.3 38.8 %collective-permute-start.39 = (bf16[480,768]{1,0:T(8,128)(2,1)S(1)}, bf16[480,768]{1,0:T(8,128)(2,1)S(1)}, u32[]{:S(2)}, u32[]{:S(2)}) collective-permute-start(bf16[480,768]{1,0:T(8,128)(2,1)S(1)} %pad_maximum_fusion.4), channel_id=1, source_target_pairs={{0,4},{4,0},{8,12},{12,8},{16,20},{20,16},{24,28},{28,24},{1,5},{5... | collective-permute-start | bytes 2211848 | tf_op jit(solution)/shard_map/ppermute | solution.py:34
  219.3 20.8 %collective-permute-start.38 = (bf16[384,768]{1,0:T(8,128)(2,1)S(1)}, bf16[384,768]{1,0:T(8,128)(2,1)S(1)}, u32[]{:S(2)}, u32[]{:S(2)}) collective-permute-start(bf16[384,768]{1,0:T(8,128)(2,1)S(1)} %get-tuple-element.261), channel_id=1, source_target_pairs={{0,2},{1,3},{2,0},{3,1},{4,6},{5,7},{6,4},{7,5},{8,10},{9,11},{10,... | collective-permute-start | bytes 1769480 | tf_op jit(solution)/shard_map/ppermute | solution.py:34
  220.4 19.7 %collective-permute-start.42 = (f32[5,768]{1,0:T(8,128)S(1)}, f32[5,768]{1,0:T(8,128)S(1)}, u32[]{:S(2)}, u32[]{:S(2)}) collective-permute-start(f32[5,768]{1,0:T(8,128)S(1)} %add.177), channel_id=1, source_target_pairs={{0,4},{4,0},{8,12},{12,8},{16,20},{20,16},{24,28},{28,24},{1,5},{5... | collective-permute-start | bytes 46088 | tf_op jit(solution)/shard_map/ppermute | solution.py:34
  221.2 28.7 %collective-permute-start.41 = (bf16[480,768]{1,0:T(8,128)(2,1)S(1)}, bf16[480,768]{1,0:T(8,128)(2,1)S(1)}, u32[]{:S(2)}, u32[]{:S(2)}) collective-permute-start(bf16[480,768]{1,0:T(8,128)(2,1)S(1)} %add_convert_fusion.2), channel_id=1, source_target_pairs={{0,2},{1,3},{2,0},{3,1},{4,6},{5,7},{6,4},{7,5},{8,10},{9,11},{10,... | collective-permute-start | bytes 2211848 | tf_op jit(solution)/shard_map/ppermute | solution.py:34
  222.3 25.3 %collective-permute-start.40 = (bf16[384,768]{1,0:T(8,128)(2,1)S(1)}, bf16[384,768]{1,0:T(8,128)(2,1)S(1)}, u32[]{:S(2)}, u32[]{:S(2)}) collective-permute-start(bf16[384,768]{1,0:T(8,128)(2,1)S(1)} %add_convert_fusion.4), channel_id=1, source_target_pairs={{0,4},{4,0},{8,12},{12,8},{16,20},{20,16},{24,28},{28,24},{1,5},{5... | collective-permute-start | bytes 1769480 | tf_op jit(solution)/shard_map/ppermute | solution.py:34
  251.9 36.4 %collective-permute-start.47 = (bf16[216,768]{1,0:T(8,128)(2,1)S(1)}, bf16[216,768]{1,0:T(8,128)(2,1)S(1)}, u32[]{:S(2)}, u32[]{:S(2)}) collective-permute-start(bf16[216,768]{1,0:T(8,128)(2,1)S(1)} %pad_maximum_fusion.18), channel_id=1, source_target_pairs={{0,24},{4,28},{8,16},{12,20},{16,8},{20,12},{24,0},{28,4},{1,25},{... | collective-permute-start | bytes 995336 | tf_op jit(solution)/shard_map/ppermute | solution.py:34
  253.9 34.5 %collective-permute-start.46 = (bf16[216,768]{1,0:T(8,128)(2,1)S(1)}, bf16[216,768]{1,0:T(8,128)(2,1)S(1)}, u32[]{:S(2)}, u32[]{:S(2)}) collective-permute-start(bf16[216,768]{1,0:T(8,128)(2,1)S(1)} %pad_maximum_fusion.17), channel_id=1, source_target_pairs={{0,8},{4,12},{8,0},{12,4},{16,24},{20,28},{24,16},{28,20},{1,9},{5... | collective-permute-start | bytes 995336 | tf_op jit(solution)/shard_map/ppermute | solution.py:34
  258.4 29.9 %collective-permute-start.45 = (bf16[216,768]{1,0:T(8,128)(2,1)S(1)}, bf16[216,768]{1,0:T(8,128)(2,1)S(1)}, u32[]{:S(2)}, u32[]{:S(2)}) collective-permute-start(bf16[216,768]{1,0:T(8,128)(2,1)S(1)} %pad_maximum_fusion.16), channel_id=1, source_target_pairs={{0,16},{4,20},{8,24},{12,28},{16,0},{20,4},{24,8},{28,12},{1,17},{... | collective-permute-start | bytes 995336 | tf_op jit(solution)/shard_map/ppermute | solution.py:34
  260.0 19.9 %collective-permute-start.44 = (f32[5,768]{1,0:T(8,128)S(1)}, f32[5,768]{1,0:T(8,128)S(1)}, u32[]{:S(2)}, u32[]{:S(2)}) collective-permute-start(f32[5,768]{1,0:T(8,128)S(1)} %add.178), channel_id=1, source_target_pairs={{0,8},{4,12},{8,0},{12,4},{16,24},{20,28},{24,16},{28,20},{1,9},{5... | collective-permute-start | bytes 46088 | tf_op jit(solution)/shard_map/ppermute | solution.py:34
  279.2 9.5 %collective-permute-start.43 = (bf16[288,768]{1,0:T(8,128)(2,1)S(1)}, bf16[288,768]{1,0:T(8,128)(2,1)S(1)}, u32[]{:S(2)}, u32[]{:S(2)}) collective-permute-start(bf16[288,768]{1,0:T(8,128)(2,1)S(1)} %bitcast.190), channel_id=1, source_target_pairs={{0,4},{4,0},{8,12},{12,8},{16,20},{20,16},{24,28},{28,24},{1,5},{5... | collective-permute-start | bytes 1327112 | tf_op jit(solution)/shard_map/ppermute | solution.py:34
  288.6 17.1 %collective-permute-start.51 = (bf16[2048,768]{1,0:T(8,128)(2,1)}, bf16[2048,768]{1,0:T(8,128)(2,1)}, u32[]{:S(2)}, u32[]{:S(2)}) collective-permute-start(bf16[2048,768]{1,0:T(8,128)(2,1)} %get-tuple-element.221), channel_id=1, source_target_pairs={{0,1},{1,0},{2,3},{3,2},{4,5},{5,4},{6,7},{7,6},{8,9},{9,8},{10,11... | collective-permute-start | bytes 9437192 | tf_op jit(solution)/shard_map/ppermute | solution.py:34
  295.5 10.2 %collective-permute-start.48 = (bf16[72,768]{1,0:T(8,128)(2,1)S(1)}, bf16[72,768]{1,0:T(8,128)(2,1)S(1)}, u32[]{:S(2)}, u32[]{:S(2)}) collective-permute-start(bf16[72,768]{1,0:T(8,128)(2,1)S(1)} %get-tuple-element.316), channel_id=1, source_target_pairs={{0,16},{4,20},{8,24},{12,28},{16,0},{20,4},{24,8},{28,12},{1,17},{... | collective-permute-start | bytes 331784 | tf_op jit(solution)/shard_map/ppermute | solution.py:34
  296.0 9.7 %collective-permute-start.49 = (bf16[72,768]{1,0:T(8,128)(2,1)S(1)}, bf16[72,768]{1,0:T(8,128)(2,1)S(1)}, u32[]{:S(2)}, u32[]{:S(2)}) collective-permute-start(bf16[72,768]{1,0:T(8,128)(2,1)S(1)} %get-tuple-element.315), channel_id=1, source_target_pairs={{0,8},{4,12},{8,0},{12,4},{16,24},{20,28},{24,16},{28,20},{1,9},{5... | collective-permute-start | bytes 331784 | tf_op jit(solution)/shard_map/ppermute | solution.py:34
  297.6 8.2 %collective-permute-start.50 = (bf16[72,768]{1,0:T(8,128)(2,1)S(1)}, bf16[72,768]{1,0:T(8,128)(2,1)S(1)}, u32[]{:S(2)}, u32[]{:S(2)}) collective-permute-start(bf16[72,768]{1,0:T(8,128)(2,1)S(1)} %get-tuple-element.314), channel_id=1, source_target_pairs={{0,24},{4,28},{8,16},{12,20},{16,8},{20,12},{24,0},{28,4},{1,25},{... | collective-permute-start | bytes 331784 | tf_op jit(solution)/shard_map/ppermute | solution.py:34
  306.8 6.3 %collective-permute-start.52 = (bf16[96,768]{1,0:T(8,128)(2,1)S(1)}, bf16[96,768]{1,0:T(8,128)(2,1)S(1)}, u32[]{:S(2)}, u32[]{:S(2)}) collective-permute-start(bf16[96,768]{1,0:T(8,128)(2,1)S(1)} %get-tuple-element.306), channel_id=1, source_target_pairs={{0,1},{1,0},{2,3},{3,2},{4,5},{5,4},{6,7},{7,6},{8,9},{9,8},{10,11... | collective-permute-start | bytes 442376 | tf_op jit(solution)/shard_map/ppermute | solution.py:34
  306.9 6.7 %collective-permute-start.53 = (bf16[96,768]{1,0:T(8,128)(2,1)S(1)}, bf16[96,768]{1,0:T(8,128)(2,1)S(1)}, u32[]{:S(2)}, u32[]{:S(2)}) collective-permute-start(bf16[96,768]{1,0:T(8,128)(2,1)S(1)} %get-tuple-element.305), channel_id=1, source_target_pairs={{0,2},{1,3},{2,0},{3,1},{4,6},{5,7},{6,4},{7,5},{8,10},{9,11},{10,... | collective-permute-start | bytes 442376 | tf_op jit(solution)/shard_map/ppermute | solution.py:34
  308.4 7.5 %collective-permute-start.54 = (bf16[96,768]{1,0:T(8,128)(2,1)S(1)}, bf16[96,768]{1,0:T(8,128)(2,1)S(1)}, u32[]{:S(2)}, u32[]{:S(2)}) collective-permute-start(bf16[96,768]{1,0:T(8,128)(2,1)S(1)} %get-tuple-element.304), channel_id=1, source_target_pairs={{0,3},{1,2},{2,1},{3,0},{4,7},{5,6},{6,5},{7,4},{8,11},{9,10},{10,... | collective-permute-start | bytes 442376 | tf_op jit(solution)/shard_map/ppermute | solution.py:34
  316.8 10.3 %collective-permute-start.55 = (bf16[1344,128]{1,0:T(8,128)(2,1)S(1)}, bf16[1344,128]{1,0:T(8,128)(2,1)S(1)}, u32[]{:S(2)}, u32[]{:S(2)}) collective-permute-start(bf16[1344,128]{1,0:T(8,128)(2,1)S(1)} %dynamic-slice_bitcast_fusion), channel_id=1, source_target_pairs={{0,4},{4,0},{8,12},{12,8},{16,20},{20,16},{24,28},{28,24},{1,5},{5... | collective-permute-start | bytes 1032200 | tf_op jit(solution)/shard_map/ppermute | solution.py:34
  318.7 20.5 %collective-permute-start.59 = (bf16[512,768]{1,0:T(8,128)(2,1)S(1)}, bf16[512,768]{1,0:T(8,128)(2,1)S(1)}, u32[]{:S(2)}, u32[]{:S(2)}) collective-permute-start(bf16[512,768]{1,0:T(8,128)(2,1)S(1)} %get-tuple-element.264), channel_id=1, source_target_pairs={{0,2},{1,3},{2,0},{3,1},{4,6},{5,7},{6,4},{7,5},{8,10},{9,11},{10,... | collective-permute-start | bytes 2359304 | tf_op jit(solution)/shard_map/ppermute | solution.py:34
  319.7 35.3 %collective-permute-start.63 = (bf16[512,768]{1,0:T(8,128)(2,1)S(1)}, bf16[512,768]{1,0:T(8,128)(2,1)S(1)}, u32[]{:S(2)}, u32[]{:S(2)}) collective-permute-start(bf16[512,768]{1,0:T(8,128)(2,1)S(1)} %get-tuple-element.263), channel_id=1, source_target_pairs={{0,2},{1,3},{2,0},{3,1},{4,6},{5,7},{6,4},{7,5},{8,10},{9,11},{10,... | collective-permute-start | bytes 2359304 | tf_op jit(solution)/shard_map/ppermute | solution.py:34
  327.3 8.8 %collective-permute-start.56 = (bf16[336,128]{1,0:T(8,128)(2,1)S(1)}, bf16[336,128]{1,0:T(8,128)(2,1)S(1)}, u32[]{:S(2)}, u32[]{:S(2)}) collective-permute-start(bf16[336,128]{1,0:T(8,128)(2,1)S(1)} %get-tuple-element.321), channel_id=1, source_target_pairs={{0,16},{4,20},{8,24},{12,28},{16,0},{20,4},{24,8},{28,12},{1,17},{... | collective-permute-start | bytes 258056 | tf_op jit(solution)/shard_map/ppermute | solution.py:34
  329.3 6.8 %collective-permute-start.57 = (bf16[336,128]{1,0:T(8,128)(2,1)S(1)}, bf16[336,128]{1,0:T(8,128)(2,1)S(1)}, u32[]{:S(2)}, u32[]{:S(2)}) collective-permute-start(bf16[336,128]{1,0:T(8,128)(2,1)S(1)} %get-tuple-element.323), channel_id=1, source_target_pairs={{0,8},{4,12},{8,0},{12,4},{16,24},{20,28},{24,16},{28,20},{1,9},{5... | collective-permute-start | bytes 258056 | tf_op jit(solution)/shard_map/ppermute | solution.py:34
  329.6 7.6 %collective-permute-start.58 = (bf16[336,128]{1,0:T(8,128)(2,1)S(1)}, bf16[336,128]{1,0:T(8,128)(2,1)S(1)}, u32[]{:S(2)}, u32[]{:S(2)}) collective-permute-start(bf16[336,128]{1,0:T(8,128)(2,1)S(1)} %get-tuple-element.322), channel_id=1, source_target_pairs={{0,24},{4,28},{8,16},{12,20},{16,8},{20,12},{24,0},{28,4},{1,25},{... | collective-permute-start | bytes 258056 | tf_op jit(solution)/shard_map/ppermute | solution.py:34
  339.1 15.9 %collective-permute-start.60 = (bf16[336,128]{1,0:T(8,128)(2,1)S(1)}, bf16[336,128]{1,0:T(8,128)(2,1)S(1)}, u32[]{:S(2)}, u32[]{:S(2)}) collective-permute-start(bf16[336,128]{1,0:T(8,128)(2,1)S(1)} %fusion.10), channel_id=1, source_target_pairs={{0,16},{4,20},{8,24},{12,28},{16,0},{20,4},{24,8},{28,12},{1,17},{... | collective-permute-start | bytes 258056 | tf_op jit(solution)/shard_map/ppermute | solution.py:34
  341.1 13.9 %collective-permute-start.61 = (bf16[336,128]{1,0:T(8,128)(2,1)S(1)}, bf16[336,128]{1,0:T(8,128)(2,1)S(1)}, u32[]{:S(2)}, u32[]{:S(2)}) collective-permute-start(bf16[336,128]{1,0:T(8,128)(2,1)S(1)} %fusion.10), channel_id=1, source_target_pairs={{0,8},{4,12},{8,0},{12,4},{16,24},{20,28},{24,16},{28,20},{1,9},{5... | collective-permute-start | bytes 258056 | tf_op jit(solution)/shard_map/ppermute | solution.py:34
  341.4 13.7 %collective-permute-start.62 = (bf16[336,128]{1,0:T(8,128)(2,1)S(1)}, bf16[336,128]{1,0:T(8,128)(2,1)S(1)}, u32[]{:S(2)}, u32[]{:S(2)}) collective-permute-start(bf16[336,128]{1,0:T(8,128)(2,1)S(1)} %fusion.10), channel_id=1, source_target_pairs={{0,24},{4,28},{8,16},{12,20},{16,8},{20,12},{24,0},{28,4},{1,25},{... | collective-permute-start | bytes 258056 | tf_op jit(solution)/shard_map/ppermute | solution.py:34
  355.1 9.2 %collective-permute-start.64 = (bf16[1344,128]{1,0:T(8,128)(2,1)S(1)}, bf16[1344,128]{1,0:T(8,128)(2,1)S(1)}, u32[]{:S(2)}, u32[]{:S(2)}) collective-permute-start(bf16[1344,128]{1,0:T(8,128)(2,1)S(1)} %pad_maximum_fusion.15), channel_id=1, source_target_pairs={{0,4},{4,0},{8,12},{12,8},{16,20},{20,16},{24,28},{28,24},{1,5},{5... | collective-permute-start | bytes 1032200 | tf_op jit(solution)/shard_map/ppermute | solution.py:34
  373.2 6.7 %collective-permute-start.67 = (bf16[96,768]{1,0:T(8,128)(2,1)S(1)}, bf16[96,768]{1,0:T(8,128)(2,1)S(1)}, u32[]{:S(2)}, u32[]{:S(2)}) collective-permute-start(bf16[96,768]{1,0:T(8,128)(2,1)S(1)} %get-tuple-element.301), channel_id=1, source_target_pairs={{0,2},{1,3},{2,0},{3,1},{4,6},{5,7},{6,4},{7,5},{8,10},{9,11},{10,... | collective-permute-start | bytes 442376 | tf_op jit(solution)/shard_map/ppermute | solution.py:34
  375.0 7.2 %collective-permute-start.68 = (bf16[96,768]{1,0:T(8,128)(2,1)S(1)}, bf16[96,768]{1,0:T(8,128)(2,1)S(1)}, u32[]{:S(2)}, u32[]{:S(2)}) collective-permute-start(bf16[96,768]{1,0:T(8,128)(2,1)S(1)} %get-tuple-element.300), channel_id=1, source_target_pairs={{0,3},{1,2},{2,1},{3,0},{4,7},{5,6},{6,5},{7,4},{8,11},{9,10},{10,... | collective-permute-start | bytes 442376 | tf_op jit(solution)/shard_map/ppermute | solution.py:34
  (87 other events, 574.2 us)

commit v4 on v3

--- a/solution.py
+++ b/solution.py
@@ -145,19 +145,21 @@
     return value
 
 
-def spread_parts(value, beside):
+def spread_parts(value, beside, later):
     for turn, bits in enumerate(reversed(seq_groups())):
         masks = masks_of(bits)
         got = [value] + [swap(value, "seq", mask) for mask in masks[1:]]
         if turn == 0:
             got, beside = after((got, beside))
+        if turn == len(seq_groups()) - 1:
+            got, later = after((got, later))
         me = lax.axis_index("seq")
         for at, bit in enumerate(bits):
             flip = 2 ** (len(bits) - 1 - at)
             side = (me & bit) != 0
             got = [jnp.where(side, got[turn ^ flip], got[turn]) for turn in range(len(masks))]
         value = jnp.concatenate(got, axis=0)
-    return value, beside
+    return value, beside, later
 
 
 def in_turns(perm_ref, seq_len, fetch, work, place):
@@ -342,10 +344,11 @@
     in_vmem = pl.BlockSpec(memory_space=pltpu.VMEM)
     own, near, far = do
 
+    at = head if near.shape[0] > 1 else 0
+
     def part(at, turn):
         return pl.BlockSpec((None, None, half, LANES), lambda step: (at, turn, 0, 0))
 
-    at = 0 if head == 0 else head - 1
 
     return pl.pallas_call(
         attend_back_kernel,
@@ -431,13 +434,13 @@
     up_refs = refs[4 * heads + 4 : 4 * heads + 8]
     down_refs = refs[4 * heads + 8 : 4 * heads + 12]
     outs = refs[4 * heads + 12 :]
-    (do_own, near_first, near_rest, far_first, far_rest, block_ref, da_ref) = outs[:7]
+    do_own, near_first, near_last, far_first, far_last, block_ref, da_ref = outs[:7]
     g_refs = outs[7:9]
     du_refs = outs[9:11]
     (df_ref, hb_ref, dattn_ref, o_ref, sums_ref, slope_ref) = outs[11:]
 
     def store_do(head, turn, value):
-        near, far, at = (near_first, far_first, 0) if head == 0 else (near_rest, far_rest, head - 1)
+        near, far, at = (near_first, far_first, head) if head < heads - 1 else (near_last, far_last, 0)
         if turn == 0:
             do_own[head, 0] = value
         elif turn == 1:
@@ -536,7 +539,7 @@
     def lead(count, width):
         return pl.BlockSpec((count, part, width), lambda step: (0, step, 0))
 
-    do_sizes = ((heads, 1), (1, 1), (heads - 1, 1), (1, 2), (heads - 1, 2))
+    do_sizes = ((heads, 1), (heads - 1, 1), (1, 1), (heads - 1, 2), (1, 2))
 
     def do_part(count, turns):
         return pl.BlockSpec((count, turns, part, LANES), lambda step: (0, 0, step, 0))
@@ -839,8 +842,8 @@
         o_got, block_in, block_cot, out_rows, up_rows, down_rows, norm_params
     )
     block_out, dresidual, gelu_a, gelu_b, dinner_a, dinner_b, dbranch, hidden_low, dattn, o_rows = tokenwise
-    do_own, *do_near, far_first, far_rest = do_blocks
-    do_far = [swap(far_first, "ffn", 2), swap(far_rest, "ffn", 2)]
+    do_own, *do_near = do_blocks[:3]
+    do_far = [swap(value, "ffn", 2) for value in do_blocks[3:]]
 
     early_half = (cluster_perm[0] < seq_len // 2).astype(full).reshape(heads, clusters, CLUSTER)
     share = lax.dynamic_update_slice(
@@ -857,7 +860,7 @@
     part_out = part_out.reshape(4 * heads * HD, D)
     out_kept, out_sent = cut_outer(part_out)
     down_got, up_got, out_got = [swap(value, "ffn", 1) for value in (down_sent, up_sent, out_sent)]
-    down_got, do_far[1] = after((down_got, do_far[1]))
+    down_got, do_far[1] = after((down_got, do_far[1]), part_out)
     do_near[1] = send_on(do_near[1], do_far[1][:, 1:], 1)
     small = small + swap(after(small, down_got), "ffn", 1)
     down_sum = weight_grad(gelu_a, dbranch, down_got)
@@ -901,7 +904,7 @@
             first_got = swaps(sums[3], places)
             small_got = swap(small, "ffn", 2)
         if head == 1:
-            do_near[1], first_got, small_got = after((do_near[1], first_got, small_got), part_heads[0])
+            do_near[0], first_got, small_got = after((do_near[0], first_got, small_got), part_heads[0])
             then_sent = [add_low(value, other) for value, other in zip(sums[2], first_got)]
             second_got = swaps(sums[1], places)
             then_got = swaps(then_sent, then_places)
@@ -919,7 +922,7 @@
             rest = [up_sum, low_sum[:low_rows], low_sum[low_rows:]]
             own, rest_got = send_groups(rest, far_groups[0])
             small_got = swap(small, "seq", 2)
-        do = (do_own, do_near[min(head, 1)], do_far[min(head, 1)])
+        do = (do_own, do_near[head // (heads - 1)], do_far[head // (heads - 1)])
         gw, both = attend_back(perm[head : head + 1], head, kept[head], do, tokens)
         part_heads.append(gw)
         dboth.append(both)
@@ -943,9 +946,6 @@
             qkv_got, gx_got = after((qkv_got, gx_got))
             gx_kept, gx_sent = cut_outer(add_low(gx_kept, gx_got))
         (qkv_sum,) = add_groups(qkv_own, qkv_got)
-        for bit in bits:
-            if bit > 2:
-                small = small_step(bit)
     up_sum, down_sum, out_sum = rest
     grad_qkv, grad_out, grad_up, grad_down = [
         value.astype(full) for value in (qkv_sum, out_sum, up_sum, down_sum)
@@ -963,12 +963,18 @@
     picked = [swap(pick(turn), "ffn", turn) for turn in (1, 2, 3)]
     picked, gx_sent = after((picked, gx_sent))
     matrix = jnp.concatenate([pick(0)] + picked, axis=0)
-    gx_first, gx_second = [swap(value, "ffn", 2) for value in cut_outer(gx_sent)]
+    *middle_bits, last_bit = [bit for bits in far_groups for bit in bits][1:]
+    for bit in middle_bits:
+        small = small_step(bit)
+    ends = (0, here * 7 // 16, here * 49 // 64, here)
+    gx_got = [swap(gx_sent[at:to], "ffn", 2) for at, to in zip(ends, ends[1:])]
     panels = sum_parts(packed_gram(matrix).astype(low))
-    panels, gx_first = after((panels, gx_first))
-    panels, gx_second = spread_parts(panels, gx_second)
-    panels, small = after((panels, small))
-    gx_other = jnp.concatenate([gx_first, gx_second], axis=0)
+    panels, gx_got[0] = after((panels, gx_got[0]))
+    panels, gx_got[1], (gx_got[2], small_got) = spread_parts(
+        panels, gx_got[1], (gx_got[2], swap(small, "seq", last_bit))
+    )
+    small = small + small_got
+    gx_other = jnp.concatenate(gx_got, axis=0)
     steps = schulz(panels, matrix).reshape(4, most, D)
     input_grad = dresidual + (gx_kept.astype(full) + gx_other.astype(full))
     home = jnp.stack([steps[0]] + [swap(steps[turn], "ffn", turn) for turn in (1, 2, 3)])

time: 389 us -> 380 us (0.977)
  waiting for transfers between devices: 97.1 us -> 76.1 us
  starting transfers between devices: 70 us -> 76.8 us
  Pallas kernels: 167 us -> 171 us
    ppermute x69 -> x70, waiting for transfers between devices: 97.1 us -> 76.1 us  [swap(): lax.ppermute(value, axis, [(place, place ^ bit) for place in range(size)])]
    ppermute x69 -> x70, starting transfers between devices: 70 us -> 76.8 us  [swap(): lax.ppermute(value, axis, [(place, place ^ bit) for place in range(size)])]
    unnamed x181 -> x187, local copies, waits for them, and re-layouts: 21 us -> 17.2 us
  transfers between devices with their start and end apart: 69 -> 70, of which waited for: 26 -> 25; matrix products, arithmetic and copies ran while one was open for 6% -> 7% of each run, Pallas kernels for 31% -> 33%
where the time goes in v4:
time: 380 us; the launch traced here: 376 us
  Pallas kernels  171 us (45%)
  starting transfers between devices  76.8 us (20%)
  waiting for transfers between devices  76.1 us (20%)
  other arithmetic  24.6 us (6%)
  local copies, waits for them, and re-layouts  24 us (6%)
    ppermute x70, starting transfers between devices, swap(): lax.ppermute(value, axis, [(place, place ^ bit) for place in range(size)])  76.8 us
    ppermute x70, waiting for transfers between devices, swap(): lax.ppermute(value, axis, [(place, place ^ bit) for place in range(size)])  76.1 us
    pallas_call x3, Pallas kernels, attend_back(): pl.pallas_call(attend_back_kernel, grid=(1,), in_specs=[pl.BlockSpec(memo...  50.3 us
    pallas_call x3, Pallas kernels, attend(): pl.pallas_call(attend_kernel, in_specs=[pl.BlockSpec(memory_space=pltpu.S...  45.2 us
    pallas_call x1, Pallas kernels, layer(): pl.pallas_call(lambda *refs: layer_kernel(heads, *refs), grid=(LAYER_STEP...  38.9 us
    pallas_call x5, Pallas kernels, weight_grad(): pl.pallas_call(weight_grad_kernel, grid=(width // part,), in_specs=in_spe...  19.9 us
    unnamed x187, local copies, waits for them, and re-layouts  17.2 us
    pallas_call x1, Pallas kernels, schulz(): pl.pallas_call(schulz_kernel, in_specs=[in_vmem, in_vmem], out_specs=in_v...  8.46 us
  transfers between devices with their start and end apart: 70, of which 25 were waited for; matrix products, arithmetic and copies ran while one was open for 7% of the time, Pallas kernels for 33%

profile of v4, /device:TPU:0, one launch (start us, length us, event | category | flops | bytes accessed | tf_op | source)
XLA Modules:
  0.0 375.9 jit_solution(3593692036193537206)
XLA Ops:
  1.7 4.1 %collective-permute-start.3 = (bf16[72,768]{1,0:T(8,128)(2,1)S(1)}, bf16[72,768]{1,0:T(8,128)(2,1)S(1)}, u32[]{:S(2)}, u32[]{:S(2)}) collective-permute-start(bf16[72,768]{1,0:T(8,128)(2,1)S(1)} %bitcast.181), channel_id=1, source_target_pairs={{0,16},{4,20},{8,24},{12,28},{16,0},{20,4},{24,8},{28,12},{1,17},{... | collective-permute-start | bytes 331784 | tf_op jit(solution)/shard_map/ppermute | solution.py:34
  5.8 1.6 collective-permute-start.4
  7.3 1.7 collective-permute-start.1
  11.2 1.6 collective-permute-done.3
  12.8 1.9 collective-permute-done.5
  14.8 1.6 collective-permute-start.9
  16.4 3.9 %collective-permute-start.6 = (bf16[216,768]{1,0:T(8,128)(2,1)S(1)}, bf16[216,768]{1,0:T(8,128)(2,1)S(1)}, u32[]{:S(2)}, u32[]{:S(2)}) collective-permute-start(bf16[216,768]{1,0:T(8,128)(2,1)S(1)} %constant_dynamic-update-slice_fusion), channel_id=1, source_target_pairs={{0,16},{4,20},{8,24},{12,28},{16,0},{20,4},{24,8},{28,12},{1,17},{... | collective-permute-start | bytes 995336 | tf_op jit(solution)/shard_map/ppermute | solution.py:34
  20.3 1.5 collective-permute-start.8
  21.9 14.7 %collective-permute-done.6 = bf16[216,768]{1,0:T(8,128)(2,1)S(1)} collective-permute-done((bf16[216,768]{1,0:T(8,128)(2,1)S(1)}, bf16[216,768]{1,0:T(8,128)(2,1)S(1)}, u32[]{:S(2)}, u32[]{:S(2)}) %collective-permute-start.6) | collective-permute-done | bytes 331808 | tf_op jit(solution)/shard_map/ppermute | solution.py:34
  36.6 7.0 %collective-permute-done.7 = bf16[216,768]{1,0:T(8,128)(2,1)S(1)} collective-permute-done((bf16[216,768]{1,0:T(8,128)(2,1)S(1)}, bf16[216,768]{1,0:T(8,128)(2,1)S(1)}, u32[]{:S(2)}, u32[]{:S(2)}) %collective-permute-start.7) | collective-permute-done | bytes 331808 | tf_op jit(solution)/shard_map/ppermute | solution.py:34
  43.9 1.6 collective-permute-start.11
  47.8 15.4 %attend.3 = (bf16[512,128]{1,0:T(8,128)(2,1)S(1)}, bf16[512,128]{1,0:T(8,128)(2,1)S(1)}, bf16[1024,128]{1,0:T(8,128)(2,1)S(1)}, bf16[4096,128]{1,0:T(8,128)(2,1)S(1)}, bf16[4096,128]{1,0:T(8,128)(2,1)S(1)}) custom-call(s32[1,4096]{1,0:T(1,128)S(1)} %get-tuple-element.336.perm_ref, bf16[1024,768]{1,0:T(8,128)(2,1)S(1)} %copy-done.2, ...), custom_call_target="tpu_custom_call" | custom-call | flops 17999998976 | bytes 1000 | tf_op jit(solution)/shard_map/attend/pallas_call | solution.py:266
  63.4 1.3 collective-permute-start.12
  66.9 14.8 %attend.4 = (bf16[512,128]{1,0:T(8,128)(2,1)S(1)}, bf16[512,128]{1,0:T(8,128)(2,1)S(1)}, bf16[1024,128]{1,0:T(8,128)(2,1)S(1)}, bf16[4096,128]{1,0:T(8,128)(2,1)S(1)}, bf16[4096,128]{1,0:T(8,128)(2,1)S(1)}) custom-call(s32[1,4096]{1,0:T(1,128)S(1)} %get-tuple-element.151.perm_ref, bf16[1024,768]{1,0:T(8,128)(2,1)S(1)} %copy-done.2, ...), custom_call_target="tpu_custom_call" | custom-call | flops 17999998976 | bytes 1000 | tf_op jit(solution)/shard_map/attend/pallas_call | solution.py:266
  82.8 1.4 collective-permute-done.14.refs_2_
  87.1 1.4 collective-permute-start.16
  88.4 15.0 %attend.5 = (bf16[512,128]{1,0:T(8,128)(2,1)S(1)}, bf16[512,128]{1,0:T(8,128)(2,1)S(1)}, bf16[1024,128]{1,0:T(8,128)(2,1)S(1)}, bf16[4096,128]{1,0:T(8,128)(2,1)S(1)}, bf16[4096,128]{1,0:T(8,128)(2,1)S(1)}) custom-call(s32[1,4096]{1,0:T(1,128)S(1)} %get-tuple-element.160.perm_ref, bf16[1024,768]{1,0:T(8,128)(2,1)S(1)} %copy-done.2, ...), custom_call_target="tpu_custom_call" | custom-call | flops 17999998976 | bytes 1000 | tf_op jit(solution)/shard_map/attend/pallas_call | solution.py:266
  108.1 6.9 %collective-permute-done.22.refs_10_ = bf16[1024,128]{1,0:T(8,128)(2,1)S(1)} collective-permute-done((bf16[1024,128]{1,0:T(8,128)(2,1)S(1)}, bf16[1024,128]{1,0:T(8,128)(2,1)S(1)}, u32[]{:S(2)}, u32[]{:S(2)}) %collective-permute-start.22) | collective-permute-done | bytes 262176 | tf_op jit(solution)/shard_map/ppermute | solution.py:34
  119.1 38.9 %layer.1 = (bf16[3,1,512,128]{3,2,1,0:T(8,128)(2,1)}, bf16[2,1,512,128]{3,2,1,0:T(8,128)(2,1)}, bf16[1,1,512,128]{3,2,1,0:T(8,128)(2,1)}, bf16[2,2,512,128]{3,2,...) custom-call(bf16[512,128]{1,0:T(8,128)(2,1)} %copy-done.31, ...), custom_call_target="tpu_custom_call" | custom-call | flops 40000000000 | bytes 1000 | tf_op jit(solution)/shard_map/layer/pallas_call | solution.py:558
  159.3 1.9 copy-done.11
  161.2 1.4 copy-done.14
  162.6 5.0 %weight_grad.5 = bf16[1536,768]{1,0:T(8,128)(2,1)} custom-call(bf16[1024,1536]{1,0:T(8,128)(2,1)S(1)} %bitcast.167, bf16[1024,768]{1,0:T(8,128)(2,1)S(1)} %bitcast.170), custom_call_target="tpu_custom_call" | custom-call | flops 4000000000 | bytes 1000 | tf_op jit(solution)/shard_map/weight_grad/pallas_call | solution.py:616
  167.5 4.8 %collective-permute-done.27.do2 = bf16[2,2,512,128]{3,2,1,0:T(8,128)(2,1)S(1)} collective-permute-done((bf16[2,2,512,128]{3,2,1,0:T(8,128)(2,1)}, bf16[2,2,512,128]{3,2,1,0:T(8,128)(2,1)S(1)}, u32[]{:S(2)}, u32[]{:S(2)}) %collective-permute-start.27) | collective-permute-done | bytes 524320 | tf_op jit(solution)/shard_map/ppermute | solution.py:34
  172.3 4.5 %weight_grad.6 = bf16[1536,768]{1,0:T(8,128)(2,1)} custom-call(bf16[1024,1536]{1,0:T(8,128)(2,1)S(1)} %bitcast.166, bf16[1024,768]{1,0:T(8,128)(2,1)S(1)} %bitcast.168), custom_call_target="tpu_custom_call" | custom-call | flops 4000000000 | bytes 1000 | tf_op jit(solution)/shard_map/weight_grad/pallas_call | solution.py:616
  178.4 1.4 copy-done.16
  179.8 1.4 copy-done.17
  181.2 1.9 weight_grad.7
  184.4 1.6 collective-permute-done.32.do2
  186.0 4.9 %weight_grad.8 = bf16[1536,768]{1,0:T(8,128)(2,1)S(1)} custom-call(bf16[1024,1536]{1,0:T(8,128)(2,1)S(1)} %bitcast.165, bf16[1024,768]{1,0:T(8,128)(2,1)S(1)} %bitcast.171, bf16[1536,768]{1,0:T(8,128)(2,1)} %collective-permute-done.31.refs_0_), custom_call_target="tpu_custom_call" | custom-call | flops 4000000000 | bytes 1000 | tf_op jit(solution)/shard_map/weight_grad/pallas_call | solution.py:616
  194.0 3.7 weight_grad.9
  201.1 16.9 %attend_back.3 = (bf16[256,768]{1,0:T(8,128)(2,1)S(1)}, bf16[4096,256]{1,0:T(8,128)(2,1)S(1)}) custom-call(s32[1,4096]{1,0:T(1,128)S(1)} %get-tuple-element.336.perm_ref, bf16[4096,128]{1,0:T(8,128)(2,1)S(1)} %copy-done.27, bf16[4096,128]{1,0:T(8,128)(2,1)S(1)} %copy-done.29, bf16[3,1,512,128]{3,2,1,0:T(8,128)(2,1)S(1)} %copy-done.30, ...), custom_call_target="tpu_custom_call" | custom-call | flops 22000001024 | bytes 1000 | tf_op jit(solution)/shard_map/attend_back/pallas_call | solution.py:353
  222.7 16.7 %attend_back.4 = (bf16[256,768]{1,0:T(8,128)(2,1)S(1)}, bf16[4096,256]{1,0:T(8,128)(2,1)S(1)}) custom-call(s32[1,4096]{1,0:T(1,128)S(1)} %get-tuple-element.151.perm_ref, bf16[4096,128]{1,0:T(8,128)(2,1)S(1)} %copy-done.23, bf16[4096,128]{1,0:T(8,128)(2,1)S(1)} %copy-done.25, bf16[3,1,512,128]{3,2,1,0:T(8,128)(2,1)S(1)} %copy-done.30, ...), custom_call_target="tpu_custom_call" | custom-call | flops 22000001024 | bytes 1000 | tf_op jit(solution)/shard_map/attend_back/pallas_call | solution.py:353
  239.5 6.2 %collective-permute-done.40 = bf16[384,768]{1,0:T(8,128)(2,1)S(1)} collective-permute-done((bf16[384,768]{1,0:T(8,128)(2,1)S(1)}, bf16[384,768]{1,0:T(8,128)(2,1)S(1)}, u32[]{:S(2)}, u32[]{:S(2)}) %collective-permute-start.40) | collective-permute-done | bytes 589856 | tf_op jit(solution)/shard_map/ppermute | solution.py:34
  245.6 3.2 collective-permute-done.41
  250.8 3.4 collective-permute-start.47
  254.2 3.0 collective-permute-start.46
  257.3 1.5 collective-permute-start.45
  258.9 2.0 collective-permute-start.44
  260.9 16.7 %attend_back.5 = (bf16[256,768]{1,0:T(8,128)(2,1)S(1)}, bf16[4096,256]{1,0:T(8,128)(2,1)S(1)}) custom-call(s32[1,4096]{1,0:T(1,128)S(1)} %get-tuple-element.160.perm_ref, bf16[4096,128]{1,0:T(8,128)(2,1)S(1)} %copy-done.19, bf16[4096,128]{1,0:T(8,128)(2,1)S(1)} %copy-done.21, bf16[3,1,512,128]{3,2,1,0:T(8,128)(2,1)S(1)} %copy-done.30, ...), custom_call_target="tpu_custom_call" | custom-call | flops 22000001024 | bytes 1000 | tf_op jit(solution)/shard_map/attend_back/pallas_call | solution.py:353
  279.6 8.0 %token_grad.1 = (bf16[2048,768]{1,0:T(8,128)(2,1)S(1)}, bf16[2048,768]{1,0:T(8,128)(2,1)}) custom-call(bf16[4096,256]{1,0:T(8,128)(2,1)S(1)} %get-tuple-element.212.d0, bf16[4096,256]{1,0:T(8,128)(2,1)S(1)} %get-tuple-element.213.d1, bf16[4096,256]{1,0:T(8,128)(2,1)S(1)} %get-tuple-element.214.d2, bf16[768,768]{1,0:T(8,128)(2,1)S(1)} %bitcast.155), custom_call_target="tpu_custom_call" | custom-call | flops 8000000000 | bytes 1000 | tf_op jit(solution)/shard_map/token_grad/pallas_call | solution.py:400
  289.3 1.4 fusion.1
  291.2 1.4 collective-permute-start.49
  292.5 2.6 collective-permute-start.50
  295.2 1.4 fusion.14
  296.7 2.0 fusion.6
  299.7 2.0 collective-permute-done.50
  304.7 2.7 add_convert_fusion
  307.5 1.5 copy-done.34
  309.5 2.3 collective-permute-done.54
  314.5 1.4 collective-permute-start.59
  315.9 7.2 %collective-permute-done.55 = bf16[1344,128]{1,0:T(8,128)(2,1)S(1)} collective-permute-done((bf16[1344,128]{1,0:T(8,128)(2,1)S(1)}, bf16[1344,128]{1,0:T(8,128)(2,1)S(1)}, u32[]{:S(2)}, u32[]{:S(2)}) %collective-permute-start.55) | collective-permute-done | bytes 344096 | tf_op jit(solution)/shard_map/ppermute | solution.py:34
  323.9 2.8 collective-permute-start.56
  326.7 2.3 collective-permute-start.58
  330.0 3.4 collective-permute-start.66
  333.4 2.0 collective-permute-done.58
  336.4 1.7 collective-permute-start.60
  338.5 2.4 collective-permute-start.62
  341.6 1.5 collective-permute-done.63
  343.1 1.4 collective-permute-start.65
  347.1 5.7 %collective-permute-done.65 = bf16[240,768]{1,0:T(8,128)(2,1)S(1)} collective-permute-done((bf16[240,768]{1,0:T(8,128)(2,1)S(1)}, bf16[240,768]{1,0:T(8,128)(2,1)S(1)}, u32[]{:S(2)}, u32[]{:S(2)}) %collective-permute-start.65) | collective-permute-done | bytes 368672 | tf_op jit(solution)/shard_map/ppermute | solution.py:34
  353.6 8.5 %schulz.1 = bf16[384,768]{1,0:T(8,128)(2,1)S(1)} custom-call(bf16[2688,128]{1,0:T(8,128)(2,1)S(1)} %pad_maximum_fusion.7.panels_ref, bf16[384,768]{1,0:T(8,128)(2,1)S(1)} %pad_maximum_fusion.11.matrix_ref), custom_call_target="tpu_custom_call" | custom-call | flops 8000000000 | bytes 1000 | tf_op jit(solution)/shard_map/schulz/pallas_call | solution.py:692
  362.8 1.3 collective-permute-start.68
  365.4 4.4 %bitcast_add_fusion = f32[1024,768]{1,0:T(8,128)} fusion(f32[2,512,768]{2,1,0:T(8,128)} %get-tuple-element.176, bf16[2048,768]{1,0:T(8,128)(2,1)S(1)} %copy-done.35, bf16[240,768]{1,0:T(8,128)(2,1)} %copy-done.46, bf16[336,768]{1,0:T(8,128)(2,1)} %copy-done.44, bf16[448,768]{1,0:T(8,128)(2,1)} %collective-permute-done.59), kind=kLoop, calls=%fused_computation.1 | loop fusion | flops 7077888 | bytes 9437184 | tf_op jit(solution)/shard_map/add | solution.py:979
  370.5 1.7 collective-permute-done.69
  (390 shorter events, 62.0 us)
Async XLA Ops:
  1.7 11.2 %collective-permute-start.3 = (bf16[72,768]{1,0:T(8,128)(2,1)S(1)}, bf16[72,768]{1,0:T(8,128)(2,1)S(1)}, u32[]{:S(2)}, u32[]{:S(2)}) collective-permute-start(bf16[72,768]{1,0:T(8,128)(2,1)S(1)} %bitcast.181), channel_id=1, source_target_pairs={{0,16},{4,20},{8,24},{12,28},{16,0},{20,4},{24,8},{28,12},{1,17},{... | collective-permute-start | bytes 331784 | tf_op jit(solution)/shard_map/ppermute | solution.py:34
  5.8 7.1 %collective-permute-start.4 = (bf16[72,768]{1,0:T(8,128)(2,1)S(1)}, bf16[72,768]{1,0:T(8,128)(2,1)S(1)}, u32[]{:S(2)}, u32[]{:S(2)}) collective-permute-start(bf16[72,768]{1,0:T(8,128)(2,1)S(1)} %bitcast.182), channel_id=1, source_target_pairs={{0,8},{4,12},{8,0},{12,4},{16,24},{20,28},{24,16},{28,20},{1,9},{5... | collective-permute-start | bytes 331784 | tf_op jit(solution)/shard_map/ppermute | solution.py:34
  7.3 7.4 %collective-permute-start.5 = (bf16[72,768]{1,0:T(8,128)(2,1)S(1)}, bf16[72,768]{1,0:T(8,128)(2,1)S(1)}, u32[]{:S(2)}, u32[]{:S(2)}) collective-permute-start(bf16[72,768]{1,0:T(8,128)(2,1)S(1)} %bitcast.183), channel_id=1, source_target_pairs={{0,24},{4,28},{8,16},{12,20},{16,8},{20,12},{24,0},{28,4},{1,25},{... | collective-permute-start | bytes 331784 | tf_op jit(solution)/shard_map/ppermute | solution.py:34
  7.3 36.4 %collective-permute-start.1 = (bf16[1024,768]{1,0:T(8,128)(2,1)}, bf16[1024,768]{1,0:T(8,128)(2,1)}, u32[]{:S(2)}, u32[]{:S(2)}) collective-permute-start(bf16[1024,768]{1,0:T(8,128)(2,1)} %x0.11), channel_id=1, source_target_pairs={{0,2},{1,3},{2,0},{3,1},{4,6},{5,7},{6,4},{7,5},{8,10},{9,11},{10,... | collective-permute-start | bytes 4718600 | tf_op jit(solution)/shard_map/ppermute | solution.py:34
  14.8 28.9 %collective-permute-start.9 = (bf16[288,768]{1,0:T(8,128)(2,1)S(1)}, bf16[288,768]{1,0:T(8,128)(2,1)S(1)}, u32[]{:S(2)}, u32[]{:S(2)}) collective-permute-start(bf16[288,768]{1,0:T(8,128)(2,1)S(1)} %pad_maximum_fusion.14), channel_id=1, source_target_pairs={{0,4},{4,0},{8,12},{12,8},{16,20},{20,16},{24,28},{28,24},{1,5},{5... | collective-permute-start | bytes 1327112 | tf_op jit(solution)/shard_map/ppermute | solution.py:34
  16.4 20.2 %collective-permute-start.6 = (bf16[216,768]{1,0:T(8,128)(2,1)S(1)}, bf16[216,768]{1,0:T(8,128)(2,1)S(1)}, u32[]{:S(2)}, u32[]{:S(2)}) collective-permute-start(bf16[216,768]{1,0:T(8,128)(2,1)S(1)} %constant_dynamic-update-slice_fusion), channel_id=1, source_target_pairs={{0,16},{4,20},{8,24},{12,28},{16,0},{20,4},{24,8},{28,12},{1,17},{... | collective-permute-start | bytes 995336 | tf_op jit(solution)/shard_map/ppermute | solution.py:34
  20.3 23.3 %collective-permute-start.7 = (bf16[216,768]{1,0:T(8,128)(2,1)S(1)}, bf16[216,768]{1,0:T(8,128)(2,1)S(1)}, u32[]{:S(2)}, u32[]{:S(2)}) collective-permute-start(bf16[216,768]{1,0:T(8,128)(2,1)S(1)} %constant_dynamic-update-slice_fusion), channel_id=1, source_target_pairs={{0,8},{4,12},{8,0},{12,4},{16,24},{20,28},{24,16},{28,20},{1,9},{5... | collective-permute-start | bytes 995336 | tf_op jit(solution)/shard_map/ppermute | solution.py:34
  20.3 23.3 %collective-permute-start.8 = (bf16[216,768]{1,0:T(8,128)(2,1)S(1)}, bf16[216,768]{1,0:T(8,128)(2,1)S(1)}, u32[]{:S(2)}, u32[]{:S(2)}) collective-permute-start(bf16[216,768]{1,0:T(8,128)(2,1)S(1)} %constant_dynamic-update-slice_fusion), channel_id=1, source_target_pairs={{0,24},{4,28},{8,16},{12,20},{16,8},{20,12},{24,0},{28,4},{1,25},{... | collective-permute-start | bytes 995336 | tf_op jit(solution)/shard_map/ppermute | solution.py:34
  36.6 10.3 %collective-permute-start = (bf16[1024,768]{1,0:T(8,128)(2,1)S(1)}, bf16[1024,768]{1,0:T(8,128)(2,1)S(1)}, u32[]{:S(2)}, u32[]{:S(2)}) collective-permute-start(bf16[1024,768]{1,0:T(8,128)(2,1)S(1)} %copy-done.2), channel_id=1, source_target_pairs={{0,1},{1,0},{2,3},{3,2},{4,5},{5,4},{6,7},{7,6},{8,9},{9,8},{10,11... | collective-permute-start | bytes 4718600 | tf_op jit(solution)/shard_map/ppermute | solution.py:34
  43.9 19.5 %collective-permute-start.11 = (bf16[480,768]{1,0:T(8,128)(2,1)S(1)}, bf16[480,768]{1,0:T(8,128)(2,1)S(1)}, u32[]{:S(2)}, u32[]{:S(2)}) collective-permute-start(bf16[480,768]{1,0:T(8,128)(2,1)S(1)} %constant_dynamic-update-slice_fusion.8), channel_id=1, source_target_pairs={{0,2},{1,3},{2,0},{3,1},{4,6},{5,7},{6,4},{7,5},{8,10},{9,11},{10,... | collective-permute-start | bytes 2211848 | tf_op jit(solution)/shard_map/ppermute | solution.py:34
  45.5 17.8 %collective-permute-start.10 = (bf16[384,768]{1,0:T(8,128)(2,1)S(1)}, bf16[384,768]{1,0:T(8,128)(2,1)S(1)}, u32[]{:S(2)}, u32[]{:S(2)}) collective-permute-start(bf16[384,768]{1,0:T(8,128)(2,1)S(1)} %pad_maximum_fusion.8), channel_id=1, source_target_pairs={{0,4},{4,0},{8,12},{12,8},{16,20},{20,16},{24,28},{28,24},{1,5},{5... | collective-permute-start | bytes 1769480 | tf_op jit(solution)/shard_map/ppermute | solution.py:34
  63.4 20.9 %collective-permute-start.12 = (bf16[384,768]{1,0:T(8,128)(2,1)S(1)}, bf16[384,768]{1,0:T(8,128)(2,1)S(1)}, u32[]{:S(2)}, u32[]{:S(2)}) collective-permute-start(bf16[384,768]{1,0:T(8,128)(2,1)S(1)} %pad_maximum_fusion.8), channel_id=1, source_target_pairs={{0,2},{1,3},{2,0},{3,1},{4,6},{5,7},{6,4},{7,5},{8,10},{9,11},{10,... | collective-permute-start | bytes 1769480 | tf_op jit(solution)/shard_map/ppermute | solution.py:34
  64.7 19.5 %collective-permute-start.15 = (bf16[768,768]{1,0:T(8,128)(2,1)S(1)}, bf16[768,768]{1,0:T(8,128)(2,1)S(1)}, u32[]{:S(2)}, u32[]{:S(2)}) collective-permute-start(bf16[768,768]{1,0:T(8,128)(2,1)S(1)} %constant_dynamic-update-slice_fusion.13.refs_16_), channel_id=1, source_target_pairs={{0,1},{1,0},{2,3},{3,2},{4,5},{5,4},{6,7},{7,6},{8,9},{9,8},{10,11... | collective-permute-start | bytes 3538952 | tf_op jit(solution)/shard_map/ppermute | solution.py:34
  64.8 19.4 %collective-permute-start.13 = (bf16[480,768]{1,0:T(8,128)(2,1)S(1)}, bf16[480,768]{1,0:T(8,128)(2,1)S(1)}, u32[]{:S(2)}, u32[]{:S(2)}) collective-permute-start(bf16[480,768]{1,0:T(8,128)(2,1)S(1)} %constant_dynamic-update-slice_fusion.8), channel_id=1, source_target_pairs={{0,4},{4,0},{8,12},{12,8},{16,20},{20,16},{24,28},{28,24},{1,5},{5... | collective-permute-start | bytes 2211848 | tf_op jit(solution)/shard_map/ppermute | solution.py:34
  65.8 18.4 %collective-permute-start.14 = (bf16[1024,128]{1,0:T(8,128)(2,1)S(1)}, bf16[1024,128]{1,0:T(8,128)(2,1)S(1)}, u32[]{:S(2)}, u32[]{:S(2)}) collective-permute-start(bf16[1024,128]{1,0:T(8,128)(2,1)S(1)} %get-tuple-element.150), channel_id=1, source_target_pairs={{0,2},{1,3},{2,0},{3,1},{4,6},{5,7},{6,4},{7,5},{8,10},{9,11},{10,... | collective-permute-start | bytes 786440 | tf_op jit(solution)/shard_map/ppermute | solution.py:34
  81.8 23.0 %collective-permute-start.18 = (bf16[1024,128]{1,0:T(8,128)(2,1)S(1)}, bf16[1024,128]{1,0:T(8,128)(2,1)S(1)}, u32[]{:S(2)}, u32[]{:S(2)}) collective-permute-start(bf16[1024,128]{1,0:T(8,128)(2,1)S(1)} %get-tuple-element.156), channel_id=1, source_target_pairs={{0,2},{1,3},{2,0},{3,1},{4,6},{5,7},{6,4},{7,5},{8,10},{9,11},{10,... | collective-permute-start | bytes 786440 | tf_op jit(solution)/shard_map/ppermute | solution.py:34
  85.3 19.6 %collective-permute-start.20 = (bf16[768,768]{1,0:T(8,128)(2,1)S(1)}, bf16[768,768]{1,0:T(8,128)(2,1)S(1)}, u32[]{:S(2)}, u32[]{:S(2)}) collective-permute-start(bf16[768,768]{1,0:T(8,128)(2,1)S(1)} %pad_maximum_fusion.refs_20_), channel_id=1, source_target_pairs={{0,1},{1,0},{2,3},{3,2},{4,5},{5,4},{6,7},{7,6},{8,9},{9,8},{10,11... | collective-permute-start | bytes 3538952 | tf_op jit(solution)/shard_map/ppermute | solution.py:34
  85.4 19.5 %collective-permute-start.19 = (bf16[1024,128]{1,0:T(8,128)(2,1)S(1)}, bf16[1024,128]{1,0:T(8,128)(2,1)S(1)}, u32[]{:S(2)}, u32[]{:S(2)}) collective-permute-start(bf16[1024,128]{1,0:T(8,128)(2,1)S(1)} %pad_maximum_fusion.21), channel_id=1, source_target_pairs={{0,1},{1,0},{2,3},{3,2},{4,5},{5,4},{6,7},{7,6},{8,9},{9,8},{10,11... | collective-permute-start | bytes 786440 | tf_op jit(solution)/shard_map/ppermute | solution.py:34
  86.0 18.9 %collective-permute-start.17 = (bf16[480,768]{1,0:T(8,128)(2,1)S(1)}, bf16[480,768]{1,0:T(8,128)(2,1)S(1)}, u32[]{:S(2)}, u32[]{:S(2)}) collective-permute-start(bf16[480,768]{1,0:T(8,128)(2,1)S(1)} %collective-permute-done.11), channel_id=1, source_target_pairs={{0,4},{4,0},{8,12},{12,8},{16,20},{20,16},{24,28},{28,24},{1,5},{5... | collective-permute-start | bytes 2211848 | tf_op jit(solution)/shard_map/ppermute | solution.py:34
  87.1 17.8 %collective-permute-start.16 = (bf16[384,768]{1,0:T(8,128)(2,1)S(1)}, bf16[384,768]{1,0:T(8,128)(2,1)S(1)}, u32[]{:S(2)}, u32[]{:S(2)}) collective-permute-start(bf16[384,768]{1,0:T(8,128)(2,1)S(1)} %collective-permute-done.10), channel_id=1, source_target_pairs={{0,2},{1,3},{2,0},{3,1},{4,6},{5,7},{6,4},{7,5},{8,10},{9,11},{10,... | collective-permute-start | bytes 1769480 | tf_op jit(solution)/shard_map/ppermute | solution.py:34
  106.0 11.0 %collective-permute-start.26 = (bf16[768,768]{1,0:T(8,128)(2,1)S(1)}, bf16[768,768]{1,0:T(8,128)(2,1)S(1)}, u32[]{:S(2)}, u32[]{:S(2)}) collective-permute-start(bf16[768,768]{1,0:T(8,128)(2,1)S(1)} %pad_maximum_fusion.1.refs_21_), channel_id=1, source_target_pairs={{0,1},{1,0},{2,3},{3,2},{4,5},{5,4},{6,7},{7,6},{8,9},{9,8},{10,11... | collective-permute-start | bytes 3538952 | tf_op jit(solution)/shard_map/ppermute | solution.py:34
  106.1 10.9 %collective-permute-start.25 = (bf16[768,768]{1,0:T(8,128)(2,1)S(1)}, bf16[768,768]{1,0:T(8,128)(2,1)S(1)}, u32[]{:S(2)}, u32[]{:S(2)}) collective-permute-start(bf16[768,768]{1,0:T(8,128)(2,1)S(1)} %constant_dynamic-update-slice_fusion.20.refs_17_), channel_id=1, source_target_pairs={{0,1},{1,0},{2,3},{3,2},{4,5},{5,4},{6,7},{7,6},{8,9},{9,8},{10,11... | collective-permute-start | bytes 3538952 | tf_op jit(solution)/shard_map/ppermute | solution.py:34
  106.7 8.3 %collective-permute-start.22 = (bf16[1024,128]{1,0:T(8,128)(2,1)S(1)}, bf16[1024,128]{1,0:T(8,128)(2,1)S(1)}, u32[]{:S(2)}, u32[]{:S(2)}) collective-permute-start(bf16[1024,128]{1,0:T(8,128)(2,1)S(1)} %get-tuple-element.169), channel_id=1, source_target_pairs={{0,2},{1,3},{2,0},{3,1},{4,6},{5,7},{6,4},{7,5},{8,10},{9,11},{10,... | collective-permute-start | bytes 786440 | tf_op jit(solution)/shard_map/ppermute | solution.py:34
  108.0 7.7 %collective-permute-start.24 = (bf16[384,768]{1,0:T(8,128)(2,1)S(1)}, bf16[384,768]{1,0:T(8,128)(2,1)S(1)}, u32[]{:S(2)}, u32[]{:S(2)}) collective-permute-start(bf16[384,768]{1,0:T(8,128)(2,1)S(1)} %pad_maximum_fusion.9), channel_id=1, source_target_pairs={{0,1},{1,0},{2,3},{3,2},{4,5},{5,4},{6,7},{7,6},{8,9},{9,8},{10,11... | collective-permute-start | bytes 1769480 | tf_op jit(solution)/shard_map/ppermute | solution.py:34
  158.0 14.3 %collective-permute-start.27 = (bf16[2,2,512,128]{3,2,1,0:T(8,128)(2,1)}, bf16[2,2,512,128]{3,2,1,0:T(8,128)(2,1)S(1)}, u32[]{:S(2)}, u32[]{:S(2)}) collective-permute-start(bf16[2,2,512,128]{3,2,1,0:T(8,128)(2,1)} %get-tuple-element.179), channel_id=1, source_target_pairs={{0,2},{1,3},{2,0},{3,1},{4,6},{5,7},{6,4},{7,5},{8,10},{9,11},{10,... | collective-permute-start | bytes 1572872 | tf_op jit(solution)/shard_map/ppermute | solution.py:34
  167.5 18.4 %collective-permute-start.31 = (bf16[1536,768]{1,0:T(8,128)(2,1)}, bf16[1536,768]{1,0:T(8,128)(2,1)}, u32[]{:S(2)}, u32[]{:S(2)}) collective-permute-start(bf16[1536,768]{1,0:T(8,128)(2,1)} %weight_grad.5), channel_id=1, source_target_pairs={{0,1},{1,0},{2,3},{3,2},{4,5},{5,4},{6,7},{7,6},{8,9},{9,8},{10,11... | collective-permute-start | bytes 7077896 | tf_op jit(solution)/shard_map/ppermute | solution.py:34
  176.8 16.9 %collective-permute-start.28 = (bf16[1536,768]{1,0:T(8,128)(2,1)}, bf16[1536,768]{1,0:T(8,128)(2,1)S(1)}, u32[]{:S(2)}, u32[]{:S(2)}) collective-permute-start(bf16[1536,768]{1,0:T(8,128)(2,1)} %weight_grad.6), channel_id=1, source_target_pairs={{0,1},{1,0},{2,3},{3,2},{4,5},{5,4},{6,7},{7,6},{8,9},{9,8},{10,11... | collective-permute-start | bytes 7077896 | tf_op jit(solution)/shard_map/ppermute | solution.py:34
  177.2 8.7 %collective-permute-start.32 = (bf16[1,2,512,128]{3,2,1,0:T(8,128)(2,1)S(1)}, bf16[1,2,512,128]{3,2,1,0:T(8,128)(2,1)S(1)}, u32[]{:S(2)}, u32[]{:S(2)}) collective-permute-start(bf16[1,2,512,128]{3,2,1,0:T(8,128)(2,1)S(1)} %copy-done.81), channel_id=1, source_target_pairs={{0,2},{1,3},{2,0},{3,1},{4,6},{5,7},{6,4},{7,5},{8,10},{9,11},{10,... | collective-permute-start | bytes 786440 | tf_op jit(solution)/shard_map/ppermute | solution.py:34
  183.3 10.4 %collective-permute-start.30 = (bf16[384,768]{1,0:T(8,128)(2,1)S(1)}, bf16[384,768]{1,0:T(8,128)(2,1)S(1)}, u32[]{:S(2)}, u32[]{:S(2)}) collective-permute-start(bf16[384,768]{1,0:T(8,128)(2,1)S(1)} %bitcast.189), channel_id=1, source_target_pairs={{0,1},{1,0},{2,3},{3,2},{4,5},{5,4},{6,7},{7,6},{8,9},{9,8},{10,11... | collective-permute-start | bytes 1769480 | tf_op jit(solution)/shard_map/ppermute | solution.py:34
  184.1 9.6 %collective-permute-start.29 = (bf16[2,2,512,128]{3,2,1,0:T(8,128)(2,1)S(1)}, bf16[2,2,512,128]{3,2,1,0:T(8,128)(2,1)S(1)}, u32[]{:S(2)}, u32[]{:S(2)}) collective-permute-start(bf16[2,2,512,128]{3,2,1,0:T(8,128)(2,1)S(1)} %pad_maximum_fusion.13), channel_id=1, source_target_pairs={{0,1},{1,0},{2,3},{3,2},{4,5},{5,4},{6,7},{7,6},{8,9},{9,8},{10,11... | collective-permute-start | bytes 1572872 | tf_op jit(solution)/shard_map/ppermute | solution.py:34
  191.9 29.8 %collective-permute-start.37 = (bf16[1,2,512,128]{3,2,1,0:T(8,128)(2,1)S(1)}, bf16[1,2,512,128]{3,2,1,0:T(8,128)(2,1)S(1)}, u32[]{:S(2)}, u32[]{:S(2)}) collective-permute-start(bf16[1,2,512,128]{3,2,1,0:T(8,128)(2,1)S(1)} %pad_maximum_fusion.24), channel_id=1, source_target_pairs={{0,1},{1,0},{2,3},{3,2},{4,5},{5,4},{6,7},{7,6},{8,9},{9,8},{10,11... | collective-permute-start | bytes 786440 | tf_op jit(solution)/shard_map/ppermute | solution.py:34
  192.5 25.6 %collective-permute-start.36 = (f32[5,768]{1,0:T(8,128)S(1)}, f32[5,768]{1,0:T(8,128)S(1)}, u32[]{:S(2)}, u32[]{:S(2)}) collective-permute-start(f32[5,768]{1,0:T(8,128)S(1)} %fusion.17), channel_id=1, source_target_pairs={{0,2},{1,3},{2,0},{3,1},{4,6},{5,7},{6,4},{7,5},{8,10},{9,11},{10,... | collective-permute-start | bytes 46088 | tf_op jit(solution)/shard_map/ppermute | solution.py:34
  197.9 21.3 %collective-permute-start.34 = (bf16[480,768]{1,0:T(8,128)(2,1)S(1)}, bf16[480,768]{1,0:T(8,128)(2,1)S(1)}, u32[]{:S(2)}, u32[]{:S(2)}) collective-permute-start(bf16[480,768]{1,0:T(8,128)(2,1)S(1)} %pad_maximum_fusion.6), channel_id=1, source_target_pairs={{0,4},{4,0},{8,12},{12,8},{16,20},{20,16},{24,28},{28,24},{1,5},{5... | collective-permute-start | bytes 2211848 | tf_op jit(solution)/shard_map/ppermute | solution.py:34
  199.1 20.0 %collective-permute-start.33 = (bf16[384,768]{1,0:T(8,128)(2,1)S(1)}, bf16[384,768]{1,0:T(8,128)(2,1)S(1)}, u32[]{:S(2)}, u32[]{:S(2)}) collective-permute-start(bf16[384,768]{1,0:T(8,128)(2,1)S(1)} %get-tuple-element.265), channel_id=1, source_target_pairs={{0,2},{1,3},{2,0},{3,1},{4,6},{5,7},{6,4},{7,5},{8,10},{9,11},{10,... | collective-permute-start | bytes 1769480 | tf_op jit(solution)/shard_map/ppermute | solution.py:34
  200.1 39.3 %collective-permute-start.39 = (bf16[480,768]{1,0:T(8,128)(2,1)S(1)}, bf16[480,768]{1,0:T(8,128)(2,1)S(1)}, u32[]{:S(2)}, u32[]{:S(2)}) collective-permute-start(bf16[480,768]{1,0:T(8,128)(2,1)S(1)} %pad_maximum_fusion.4), channel_id=1, source_target_pairs={{0,4},{4,0},{8,12},{12,8},{16,20},{20,16},{24,28},{28,24},{1,5},{5... | collective-permute-start | bytes 2211848 | tf_op jit(solution)/shard_map/ppermute | solution.py:34
  218.0 21.4 %collective-permute-start.38 = (bf16[384,768]{1,0:T(8,128)(2,1)S(1)}, bf16[384,768]{1,0:T(8,128)(2,1)S(1)}, u32[]{:S(2)}, u32[]{:S(2)}) collective-permute-start(bf16[384,768]{1,0:T(8,128)(2,1)S(1)} %get-tuple-element.266), channel_id=1, source_target_pairs={{0,2},{1,3},{2,0},{3,1},{4,6},{5,7},{6,4},{7,5},{8,10},{9,11},{10,... | collective-permute-start | bytes 1769480 | tf_op jit(solution)/shard_map/ppermute | solution.py:34
  219.1 20.3 %collective-permute-start.42 = (f32[5,768]{1,0:T(8,128)S(1)}, f32[5,768]{1,0:T(8,128)S(1)}, u32[]{:S(2)}, u32[]{:S(2)}) collective-permute-start(f32[5,768]{1,0:T(8,128)S(1)} %add.177), channel_id=1, source_target_pairs={{0,4},{4,0},{8,12},{12,8},{16,20},{20,16},{24,28},{28,24},{1,5},{5... | collective-permute-start | bytes 46088 | tf_op jit(solution)/shard_map/ppermute | solution.py:34
  220.5 28.3 %collective-permute-start.41 = (bf16[480,768]{1,0:T(8,128)(2,1)S(1)}, bf16[480,768]{1,0:T(8,128)(2,1)S(1)}, u32[]{:S(2)}, u32[]{:S(2)}) collective-permute-start(bf16[480,768]{1,0:T(8,128)(2,1)S(1)} %add_convert_fusion.2), channel_id=1, source_target_pairs={{0,2},{1,3},{2,0},{3,1},{4,6},{5,7},{6,4},{7,5},{8,10},{9,11},{10,... | collective-permute-start | bytes 2211848 | tf_op jit(solution)/shard_map/ppermute | solution.py:34
  221.7 23.9 %collective-permute-start.40 = (bf16[384,768]{1,0:T(8,128)(2,1)S(1)}, bf16[384,768]{1,0:T(8,128)(2,1)S(1)}, u32[]{:S(2)}, u32[]{:S(2)}) collective-permute-start(bf16[384,768]{1,0:T(8,128)(2,1)S(1)} %add_convert_fusion.4), channel_id=1, source_target_pairs={{0,4},{4,0},{8,12},{12,8},{16,20},{20,16},{24,28},{28,24},{1,5},{5... | collective-permute-start | bytes 1769480 | tf_op jit(solution)/shard_map/ppermute | solution.py:34
  250.8 36.8 %collective-permute-start.47 = (bf16[216,768]{1,0:T(8,128)(2,1)S(1)}, bf16[216,768]{1,0:T(8,128)(2,1)S(1)}, u32[]{:S(2)}, u32[]{:S(2)}) collective-permute-start(bf16[216,768]{1,0:T(8,128)(2,1)S(1)} %pad_maximum_fusion.18), channel_id=1, source_target_pairs={{0,24},{4,28},{8,16},{12,20},{16,8},{20,12},{24,0},{28,4},{1,25},{... | collective-permute-start | bytes 995336 | tf_op jit(solution)/shard_map/ppermute | solution.py:34
  254.2 33.4 %collective-permute-start.46 = (bf16[216,768]{1,0:T(8,128)(2,1)S(1)}, bf16[216,768]{1,0:T(8,128)(2,1)S(1)}, u32[]{:S(2)}, u32[]{:S(2)}) collective-permute-start(bf16[216,768]{1,0:T(8,128)(2,1)S(1)} %pad_maximum_fusion.17), channel_id=1, source_target_pairs={{0,8},{4,12},{8,0},{12,4},{16,24},{20,28},{24,16},{28,20},{1,9},{5... | collective-permute-start | bytes 995336 | tf_op jit(solution)/shard_map/ppermute | solution.py:34
  257.3 30.4 %collective-permute-start.45 = (bf16[216,768]{1,0:T(8,128)(2,1)S(1)}, bf16[216,768]{1,0:T(8,128)(2,1)S(1)}, u32[]{:S(2)}, u32[]{:S(2)}) collective-permute-start(bf16[216,768]{1,0:T(8,128)(2,1)S(1)} %pad_maximum_fusion.16), channel_id=1, source_target_pairs={{0,16},{4,20},{8,24},{12,28},{16,0},{20,4},{24,8},{28,12},{1,17},{... | collective-permute-start | bytes 995336 | tf_op jit(solution)/shard_map/ppermute | solution.py:34
  258.9 20.7 %collective-permute-start.44 = (f32[5,768]{1,0:T(8,128)S(1)}, f32[5,768]{1,0:T(8,128)S(1)}, u32[]{:S(2)}, u32[]{:S(2)}) collective-permute-start(f32[5,768]{1,0:T(8,128)S(1)} %add.178), channel_id=1, source_target_pairs={{0,8},{4,12},{8,0},{12,4},{16,24},{20,28},{24,16},{28,20},{1,9},{5... | collective-permute-start | bytes 46088 | tf_op jit(solution)/shard_map/ppermute | solution.py:34
  278.6 9.7 %collective-permute-start.43 = (bf16[288,768]{1,0:T(8,128)(2,1)S(1)}, bf16[288,768]{1,0:T(8,128)(2,1)S(1)}, u32[]{:S(2)}, u32[]{:S(2)}) collective-permute-start(bf16[288,768]{1,0:T(8,128)(2,1)S(1)} %bitcast.190), channel_id=1, source_target_pairs={{0,4},{4,0},{8,12},{12,8},{16,20},{20,16},{24,28},{28,24},{1,5},{5... | collective-permute-start | bytes 1327112 | tf_op jit(solution)/shard_map/ppermute | solution.py:34
  289.1 12.6 %collective-permute-start.51 = (bf16[2048,768]{1,0:T(8,128)(2,1)}, bf16[2048,768]{1,0:T(8,128)(2,1)}, u32[]{:S(2)}, u32[]{:S(2)}) collective-permute-start(bf16[2048,768]{1,0:T(8,128)(2,1)} %get-tuple-element.223), channel_id=1, source_target_pairs={{0,1},{1,0},{2,3},{3,2},{4,5},{5,4},{6,7},{7,6},{8,9},{9,8},{10,11... | collective-permute-start | bytes 9437192 | tf_op jit(solution)/shard_map/ppermute | solution.py:34
  290.7 9.0 %collective-permute-start.48 = (bf16[72,768]{1,0:T(8,128)(2,1)S(1)}, bf16[72,768]{1,0:T(8,128)(2,1)S(1)}, u32[]{:S(2)}, u32[]{:S(2)}) collective-permute-start(bf16[72,768]{1,0:T(8,128)(2,1)S(1)} %get-tuple-element.318), channel_id=1, source_target_pairs={{0,16},{4,20},{8,24},{12,28},{16,0},{20,4},{24,8},{28,12},{1,17},{... | collective-permute-start | bytes 331784 | tf_op jit(solution)/shard_map/ppermute | solution.py:34
  291.2 8.6 %collective-permute-start.49 = (bf16[72,768]{1,0:T(8,128)(2,1)S(1)}, bf16[72,768]{1,0:T(8,128)(2,1)S(1)}, u32[]{:S(2)}, u32[]{:S(2)}) collective-permute-start(bf16[72,768]{1,0:T(8,128)(2,1)S(1)} %get-tuple-element.317), channel_id=1, source_target_pairs={{0,8},{4,12},{8,0},{12,4},{16,24},{20,28},{24,16},{28,20},{1,9},{5... | collective-permute-start | bytes 331784 | tf_op jit(solution)/shard_map/ppermute | solution.py:34
  292.5 9.2 %collective-permute-start.50 = (bf16[72,768]{1,0:T(8,128)(2,1)S(1)}, bf16[72,768]{1,0:T(8,128)(2,1)S(1)}, u32[]{:S(2)}, u32[]{:S(2)}) collective-permute-start(bf16[72,768]{1,0:T(8,128)(2,1)S(1)} %get-tuple-element.316), channel_id=1, source_target_pairs={{0,24},{4,28},{8,16},{12,20},{16,8},{20,12},{24,0},{28,4},{1,25},{... | collective-permute-start | bytes 331784 | tf_op jit(solution)/shard_map/ppermute | solution.py:34
  302.8 6.7 %collective-permute-start.53 = (bf16[96,768]{1,0:T(8,128)(2,1)S(1)}, bf16[96,768]{1,0:T(8,128)(2,1)S(1)}, u32[]{:S(2)}, u32[]{:S(2)}) collective-permute-start(bf16[96,768]{1,0:T(8,128)(2,1)S(1)} %get-tuple-element.307), channel_id=1, source_target_pairs={{0,2},{1,3},{2,0},{3,1},{4,6},{5,7},{6,4},{7,5},{8,10},{9,11},{10,... | collective-permute-start | bytes 442376 | tf_op jit(solution)/shard_map/ppermute | solution.py:34
  303.5 8.3 %collective-permute-start.54 = (bf16[96,768]{1,0:T(8,128)(2,1)S(1)}, bf16[96,768]{1,0:T(8,128)(2,1)S(1)}, u32[]{:S(2)}, u32[]{:S(2)}) collective-permute-start(bf16[96,768]{1,0:T(8,128)(2,1)S(1)} %get-tuple-element.306), channel_id=1, source_target_pairs={{0,3},{1,2},{2,1},{3,0},{4,7},{5,6},{6,5},{7,4},{8,11},{9,10},{10,... | collective-permute-start | bytes 442376 | tf_op jit(solution)/shard_map/ppermute | solution.py:34
  312.8 10.3 %collective-permute-start.55 = (bf16[1344,128]{1,0:T(8,128)(2,1)S(1)}, bf16[1344,128]{1,0:T(8,128)(2,1)S(1)}, u32[]{:S(2)}, u32[]{:S(2)}) collective-permute-start(bf16[1344,128]{1,0:T(8,128)(2,1)S(1)} %dynamic-slice_bitcast_fusion), channel_id=1, source_target_pairs={{0,4},{4,0},{8,12},{12,8},{16,20},{20,16},{24,28},{28,24},{1,5},{5... | collective-permute-start | bytes 1032200 | tf_op jit(solution)/shard_map/ppermute | solution.py:34
  314.5 21.9 %collective-permute-start.59 = (bf16[448,768]{1,0:T(8,128)(2,1)}, bf16[448,768]{1,0:T(8,128)(2,1)}, u32[]{:S(2)}, u32[]{:S(2)}) collective-permute-start(bf16[448,768]{1,0:T(8,128)(2,1)} %slice.429), channel_id=1, source_target_pairs={{0,2},{1,3},{2,0},{3,1},{4,6},{5,7},{6,4},{7,5},{8,10},{9,11},{10,... | collective-permute-start | bytes 2064392 | tf_op jit(solution)/shard_map/ppermute | solution.py:34
  326.7 6.7 %collective-permute-start.57 = (bf16[336,128]{1,0:T(8,128)(2,1)S(1)}, bf16[336,128]{1,0:T(8,128)(2,1)}, u32[]{:S(2)}, u32[]{:S(2)}) collective-permute-start(bf16[336,128]{1,0:T(8,128)(2,1)S(1)} %get-tuple-element.325), channel_id=1, source_target_pairs={{0,8},{4,12},{8,0},{12,4},{16,24},{20,28},{24,16},{28,20},{1,9},{5... | collective-permute-start | bytes 258056 | tf_op jit(solution)/shard_map/ppermute | solution.py:34
  326.7 8.6 %collective-permute-start.58 = (bf16[336,128]{1,0:T(8,128)(2,1)S(1)}, bf16[336,128]{1,0:T(8,128)(2,1)}, u32[]{:S(2)}, u32[]{:S(2)}) collective-permute-start(bf16[336,128]{1,0:T(8,128)(2,1)S(1)} %get-tuple-element.324), channel_id=1, source_target_pairs={{0,24},{4,28},{8,16},{12,20},{16,8},{20,12},{24,0},{28,4},{1,25},{... | collective-permute-start | bytes 258056 | tf_op jit(solution)/shard_map/ppermute | solution.py:34
  329.1 14.0 %collective-permute-start.63 = (bf16[336,768]{1,0:T(8,128)(2,1)S(1)}, bf16[336,768]{1,0:T(8,128)(2,1)S(1)}, u32[]{:S(2)}, u32[]{:S(2)}) collective-permute-start(bf16[336,768]{1,0:T(8,128)(2,1)S(1)} %slice.430), channel_id=1, source_target_pairs={{0,2},{1,3},{2,0},{3,1},{4,6},{5,7},{6,4},{7,5},{8,10},{9,11},{10,... | collective-permute-start | bytes 1548296 | tf_op jit(solution)/shard_map/ppermute | solution.py:34
  330.0 17.1 %collective-permute-start.66 = (f32[5,768]{1,0:T(8,128)S(1)}, f32[5,768]{1,0:T(8,128)S(1)}, u32[]{:S(2)}, u32[]{:S(2)}) collective-permute-start(f32[5,768]{1,0:T(8,128)S(1)} %add.216), channel_id=1, source_target_pairs={{0,16},{4,20},{8,24},{12,28},{16,0},{20,4},{24,8},{28,12},{1,17},{... | collective-permute-start | bytes 46088 | tf_op jit(solution)/shard_map/ppermute | solution.py:34
  336.4 9.1 %collective-permute-start.60 = (bf16[336,128]{1,0:T(8,128)(2,1)S(1)}, bf16[336,128]{1,0:T(8,128)(2,1)S(1)}, u32[]{:S(2)}, u32[]{:S(2)}) collective-permute-start(bf16[336,128]{1,0:T(8,128)(2,1)S(1)} %fusion.10), channel_id=1, source_target_pairs={{0,16},{4,20},{8,24},{12,28},{16,0},{20,4},{24,8},{28,12},{1,17},{... | collective-permute-start | bytes 258056 | tf_op jit(solution)/shard_map/ppermute | solution.py:34
  338.1 7.4 %collective-permute-start.61 = (bf16[336,128]{1,0:T(8,128)(2,1)S(1)}, bf16[336,128]{1,0:T(8,128)(2,1)S(1)}, u32[]{:S(2)}, u32[]{:S(2)}) collective-permute-start(bf16[336,128]{1,0:T(8,128)(2,1)S(1)} %fusion.10), channel_id=1, source_target_pairs={{0,8},{4,12},{8,0},{12,4},{16,24},{20,28},{24,16},{28,20},{1,9},{5... | collective-permute-start | bytes 258056 | tf_op jit(solution)/shard_map/ppermute | solution.py:34
  338.5 7.0 %collective-permute-start.62 = (bf16[336,128]{1,0:T(8,128)(2,1)S(1)}, bf16[336,128]{1,0:T(8,128)(2,1)S(1)}, u32[]{:S(2)}, u32[]{:S(2)}) collective-permute-start(bf16[336,128]{1,0:T(8,128)(2,1)S(1)} %fusion.10), channel_id=1, source_target_pairs={{0,24},{4,28},{8,16},{12,20},{16,8},{20,12},{24,0},{28,4},{1,25},{... | collective-permute-start | bytes 258056 | tf_op jit(solution)/shard_map/ppermute | solution.py:34
  343.1 9.6 %collective-permute-start.65 = (bf16[240,768]{1,0:T(8,128)(2,1)S(1)}, bf16[240,768]{1,0:T(8,128)(2,1)S(1)}, u32[]{:S(2)}, u32[]{:S(2)}) collective-permute-start(bf16[240,768]{1,0:T(8,128)(2,1)S(1)} %slice.431), channel_id=1, source_target_pairs={{0,2},{1,3},{2,0},{3,1},{4,6},{5,7},{6,4},{7,5},{8,10},{9,11},{10,... | collective-permute-start | bytes 1105928 | tf_op jit(solution)/shard_map/ppermute | solution.py:34
  345.6 7.9 %collective-permute-start.64 = (bf16[1344,128]{1,0:T(8,128)(2,1)S(1)}, bf16[1344,128]{1,0:T(8,128)(2,1)S(1)}, u32[]{:S(2)}, u32[]{:S(2)}) collective-permute-start(bf16[1344,128]{1,0:T(8,128)(2,1)S(1)} %pad_maximum_fusion.15), channel_id=1, source_target_pairs={{0,4},{4,0},{8,12},{12,8},{16,20},{20,16},{24,28},{28,24},{1,5},{5... | collective-permute-start | bytes 1032200 | tf_op jit(solution)/shard_map/ppermute | solution.py:34
  362.8 7.7 %collective-permute-start.67 = (bf16[96,768]{1,0:T(8,128)(2,1)}, bf16[96,768]{1,0:T(8,128)(2,1)}, u32[]{:S(2)}, u32[]{:S(2)}) collective-permute-start(bf16[96,768]{1,0:T(8,128)(2,1)} %get-tuple-element.304), channel_id=1, source_target_pairs={{0,1},{1,0},{2,3},{3,2},{4,5},{5,4},{6,7},{7,6},{8,9},{9,8},{10,11... | collective-permute-start | bytes 442376 | tf_op jit(solution)/shard_map/ppermute | solution.py:34
  362.8 7.7 %collective-permute-start.68 = (bf16[96,768]{1,0:T(8,128)(2,1)}, bf16[96,768]{1,0:T(8,128)(2,1)}, u32[]{:S(2)}, u32[]{:S(2)}) collective-permute-start(bf16[96,768]{1,0:T(8,128)(2,1)} %get-tuple-element.303), channel_id=1, source_target_pairs={{0,2},{1,3},{2,0},{3,1},{4,6},{5,7},{6,4},{7,5},{8,10},{9,11},{10,... | collective-permute-start | bytes 442376 | tf_op jit(solution)/shard_map/ppermute | solution.py:34
  364.2 8.0 %collective-permute-start.69 = (bf16[96,768]{1,0:T(8,128)(2,1)S(1)}, bf16[96,768]{1,0:T(8,128)(2,1)}, u32[]{:S(2)}, u32[]{:S(2)}) collective-permute-start(bf16[96,768]{1,0:T(8,128)(2,1)S(1)} %get-tuple-element.302), channel_id=1, source_target_pairs={{0,3},{1,2},{2,1},{3,0},{4,7},{5,6},{6,5},{7,4},{8,11},{9,10},{10,... | collective-permute-start | bytes 442376 | tf_op jit(solution)/shard_map/ppermute | solution.py:34
  (90 other events, 457.0 us)

commit v5 on v4

--- a/solution.py
+++ b/solution.py
@@ -603,7 +603,7 @@
 
 def weight_grad(left, right, other=None):
     rows, width = left.shape
-    part = 384
+    part = 512 if width % 512 == 0 else 384
     args = [left, right]
     in_specs = [
         pl.BlockSpec((rows, part), lambda step: (0, step)),
@@ -977,7 +977,7 @@
     gx_other = jnp.concatenate(gx_got, axis=0)
     steps = schulz(panels, matrix).reshape(4, most, D)
     input_grad = dresidual + (gx_kept.astype(full) + gx_other.astype(full))
-    home = jnp.stack([steps[0]] + [swap(steps[turn], "ffn", turn) for turn in (1, 2, 3)])
+    home = [steps[0]] + [swap(steps[turn], "ffn", turn) for turn in (1, 2, 3)]
     step_rates = (
         0.5 * math.sqrt(3.0),
         0.5 * math.sqrt(CLUSTER / 3.0),
@@ -986,8 +986,11 @@
     )
     masters = []
     for member in range(4):
-        own = lax.dynamic_index_in_dim(home, jnp.bitwise_xor(ffn_here, member), keepdims=False)
-        own = own[: moments[member].shape[0]].astype(full)
+        rows = moments[member].shape[0]
+        own = home[member ^ 3][:rows]
+        for place in (2, 1, 0):
+            own = jnp.where(ffn_here == place, home[member ^ place][:rows], own)
+        own = own.astype(full)
         masters.append(weights[member] - step_rates[member] * own)
 
     grad_norm = small[:4]

time: 380 us -> 380 us (level)
    unnamed x187 -> x184, local copies, waits for them, and re-layouts: 17.2 us -> 14.7 us
  transfers between devices with their start and end apart: 70 -> 70, of which waited for: 25 -> 24; matrix products, arithmetic and copies ran while one was open for 7% -> 8% of each run, Pallas kernels for 33% -> 33%
where the time goes in v5:
time: 380 us; the launch traced here: 376 us
  Pallas kernels  170 us (45%)
  starting transfers between devices  77 us (20%)
  waiting for transfers between devices  76.4 us (20%)
  other arithmetic  26.8 us (7%)
  local copies, waits for them, and re-layouts  22.7 us (6%)
    ppermute x70, starting transfers between devices, swap(): lax.ppermute(value, axis, [(place, place ^ bit) for place in range(size)])  77 us
    ppermute x70, waiting for transfers between devices, swap(): lax.ppermute(value, axis, [(place, place ^ bit) for place in range(size)])  76.4 us
    pallas_call x3, Pallas kernels, attend_back(): pl.pallas_call(attend_back_kernel, grid=(1,), in_specs=[pl.BlockSpec(memo...  50.3 us
    pallas_call x3, Pallas kernels, attend(): pl.pallas_call(attend_kernel, in_specs=[pl.BlockSpec(memory_space=pltpu.S...  45.2 us
    pallas_call x1, Pallas kernels, layer(): pl.pallas_call(lambda *refs: layer_kernel(heads, *refs), grid=(LAYER_STEP...  38.9 us
    pallas_call x5, Pallas kernels, weight_grad(): pl.pallas_call(weight_grad_kernel, grid=(width // part,), in_specs=in_spe...  18.6 us
    unnamed x184, local copies, waits for them, and re-layouts  14.7 us
    pallas_call x1, Pallas kernels, schulz(): pl.pallas_call(schulz_kernel, in_specs=[in_vmem, in_vmem], out_specs=in_v...  8.47 us
  transfers between devices with their start and end apart: 70, of which 24 were waited for; matrix products, arithmetic and copies ran while one was open for 8% of the time, Pallas kernels for 33%

profile of v5, /device:TPU:0, one launch (start us, length us, event | category | flops | bytes accessed | tf_op | source)
XLA Modules:
  0.0 375.9 jit_solution(8092492234950906872)
XLA Ops:
  1.7 4.1 %collective-permute-start.3 = (bf16[72,768]{1,0:T(8,128)(2,1)S(1)}, bf16[72,768]{1,0:T(8,128)(2,1)S(1)}, u32[]{:S(2)}, u32[]{:S(2)}) collective-permute-start(bf16[72,768]{1,0:T(8,128)(2,1)S(1)} %get-tuple-element.337), channel_id=1, source_target_pairs={{0,16},{4,20},{8,24},{12,28},{16,0},{20,4},{24,8},{28,12},{1,17},{... | collective-permute-start | bytes 331784 | tf_op jit(solution)/shard_map/ppermute | solution.py:34
  5.8 1.6 collective-permute-start.4
  7.4 1.7 collective-permute-start.1
  12.9 1.9 collective-permute-done.5
  14.8 1.6 collective-permute-start.9
  16.4 3.9 %collective-permute-start.6 = (bf16[216,768]{1,0:T(8,128)(2,1)S(1)}, bf16[216,768]{1,0:T(8,128)(2,1)S(1)}, u32[]{:S(2)}, u32[]{:S(2)}) collective-permute-start(bf16[216,768]{1,0:T(8,128)(2,1)S(1)} %constant_dynamic-update-slice_fusion), channel_id=1, source_target_pairs={{0,16},{4,20},{8,24},{12,28},{16,0},{20,4},{24,8},{28,12},{1,17},{... | collective-permute-start | bytes 995336 | tf_op jit(solution)/shard_map/ppermute | solution.py:34
  20.3 1.5 collective-permute-start.8
  21.9 14.7 %collective-permute-done.6 = bf16[216,768]{1,0:T(8,128)(2,1)S(1)} collective-permute-done((bf16[216,768]{1,0:T(8,128)(2,1)S(1)}, bf16[216,768]{1,0:T(8,128)(2,1)S(1)}, u32[]{:S(2)}, u32[]{:S(2)}) %collective-permute-start.6) | collective-permute-done | bytes 331808 | tf_op jit(solution)/shard_map/ppermute | solution.py:34
  36.6 7.0 %collective-permute-done.7 = bf16[216,768]{1,0:T(8,128)(2,1)S(1)} collective-permute-done((bf16[216,768]{1,0:T(8,128)(2,1)S(1)}, bf16[216,768]{1,0:T(8,128)(2,1)S(1)}, u32[]{:S(2)}, u32[]{:S(2)}) %collective-permute-start.7) | collective-permute-done | bytes 331808 | tf_op jit(solution)/shard_map/ppermute | solution.py:34
  43.9 1.6 collective-permute-start.11
  47.9 15.4 %attend.3 = (bf16[512,128]{1,0:T(8,128)(2,1)S(1)}, bf16[512,128]{1,0:T(8,128)(2,1)S(1)}, bf16[1024,128]{1,0:T(8,128)(2,1)S(1)}, bf16[4096,128]{1,0:T(8,128)(2,1)S(1)}, bf16[4096,128]{1,0:T(8,128)(2,1)S(1)}) custom-call(s32[1,4096]{1,0:T(1,128)S(1)} %get-tuple-element.335.perm_ref, bf16[1024,768]{1,0:T(8,128)(2,1)S(1)} %copy-done, ...), custom_call_target="tpu_custom_call" | custom-call | flops 17999998976 | bytes 1000 | tf_op jit(solution)/shard_map/attend/pallas_call | solution.py:266
  63.4 1.3 collective-permute-start.12
  66.9 14.8 %attend.4 = (bf16[512,128]{1,0:T(8,128)(2,1)S(1)}, bf16[512,128]{1,0:T(8,128)(2,1)S(1)}, bf16[1024,128]{1,0:T(8,128)(2,1)S(1)}, bf16[4096,128]{1,0:T(8,128)(2,1)S(1)}, bf16[4096,128]{1,0:T(8,128)(2,1)S(1)}) custom-call(s32[1,4096]{1,0:T(1,128)S(1)} %get-tuple-element.151.perm_ref, bf16[1024,768]{1,0:T(8,128)(2,1)S(1)} %copy-done, ...), custom_call_target="tpu_custom_call" | custom-call | flops 17999998976 | bytes 1000 | tf_op jit(solution)/shard_map/attend/pallas_call | solution.py:266
  82.8 1.4 collective-permute-done.14.refs_2_
  87.1 1.4 collective-permute-start.16
  88.5 15.0 %attend.5 = (bf16[512,128]{1,0:T(8,128)(2,1)S(1)}, bf16[512,128]{1,0:T(8,128)(2,1)S(1)}, bf16[1024,128]{1,0:T(8,128)(2,1)S(1)}, bf16[4096,128]{1,0:T(8,128)(2,1)S(1)}, bf16[4096,128]{1,0:T(8,128)(2,1)S(1)}) custom-call(s32[1,4096]{1,0:T(1,128)S(1)} %get-tuple-element.160.perm_ref, bf16[1024,768]{1,0:T(8,128)(2,1)S(1)} %copy-done, ...), custom_call_target="tpu_custom_call" | custom-call | flops 17999998976 | bytes 1000 | tf_op jit(solution)/shard_map/attend/pallas_call | solution.py:266
  108.1 7.0 %collective-permute-done.22.refs_10_ = bf16[1024,128]{1,0:T(8,128)(2,1)S(1)} collective-permute-done((bf16[1024,128]{1,0:T(8,128)(2,1)S(1)}, bf16[1024,128]{1,0:T(8,128)(2,1)S(1)}, u32[]{:S(2)}, u32[]{:S(2)}) %collective-permute-start.22) | collective-permute-done | bytes 262176 | tf_op jit(solution)/shard_map/ppermute | solution.py:34
  119.2 38.9 %layer.1 = (bf16[3,1,512,128]{3,2,1,0:T(8,128)(2,1)}, bf16[2,1,512,128]{3,2,1,0:T(8,128)(2,1)}, bf16[1,1,512,128]{3,2,1,0:T(8,128)(2,1)}, bf16[2,2,512,128]{3,2,...) custom-call(bf16[512,128]{1,0:T(8,128)(2,1)} %copy-done.31, ...), custom_call_target="tpu_custom_call" | custom-call | flops 40000000000 | bytes 1000 | tf_op jit(solution)/shard_map/layer/pallas_call | solution.py:558
  159.3 1.9 copy-done.9
  161.2 1.4 copy-done.12
  162.6 4.7 %weight_grad.5 = bf16[1536,768]{1,0:T(8,128)(2,1)} custom-call(bf16[1024,1536]{1,0:T(8,128)(2,1)S(1)} %bitcast.168, bf16[1024,768]{1,0:T(8,128)(2,1)S(1)} %bitcast.171), custom_call_target="tpu_custom_call" | custom-call | flops 4000000000 | bytes 1000 | tf_op jit(solution)/shard_map/weight_grad/pallas_call | solution.py:616
  167.3 5.1 %collective-permute-done.27.do2 = bf16[2,2,512,128]{3,2,1,0:T(8,128)(2,1)S(1)} collective-permute-done((bf16[2,2,512,128]{3,2,1,0:T(8,128)(2,1)}, bf16[2,2,512,128]{3,2,1,0:T(8,128)(2,1)S(1)}, u32[]{:S(2)}, u32[]{:S(2)}) %collective-permute-start.27) | collective-permute-done | bytes 524320 | tf_op jit(solution)/shard_map/ppermute | solution.py:34
  172.4 4.2 %weight_grad.6 = bf16[1536,768]{1,0:T(8,128)(2,1)} custom-call(bf16[1024,1536]{1,0:T(8,128)(2,1)S(1)} %bitcast.167, bf16[1024,768]{1,0:T(8,128)(2,1)S(1)} %bitcast.169), custom_call_target="tpu_custom_call" | custom-call | flops 4000000000 | bytes 1000 | tf_op jit(solution)/shard_map/weight_grad/pallas_call | solution.py:616
  177.0 1.5 copy.42
  179.7 1.4 copy-done.15
  181.1 1.8 weight_grad.7
  184.3 3.0 collective-permute-done.32.do2
  187.4 4.5 %weight_grad.8 = bf16[1536,768]{1,0:T(8,128)(2,1)S(1)} custom-call(bf16[1024,1536]{1,0:T(8,128)(2,1)S(1)} %bitcast.166, bf16[1024,768]{1,0:T(8,128)(2,1)S(1)} %bitcast.172, bf16[1536,768]{1,0:T(8,128)(2,1)} %collective-permute-done.31.refs_0_), custom_call_target="tpu_custom_call" | custom-call | flops 4000000000 | bytes 1000 | tf_op jit(solution)/shard_map/weight_grad/pallas_call | solution.py:616
  194.8 3.4 weight_grad.9
  198.4 1.3 collective-permute-start.34
  201.7 16.9 %attend_back.3 = (bf16[256,768]{1,0:T(8,128)(2,1)S(1)}, bf16[4096,256]{1,0:T(8,128)(2,1)S(1)}) custom-call(s32[1,4096]{1,0:T(1,128)S(1)} %get-tuple-element.335.perm_ref, bf16[4096,128]{1,0:T(8,128)(2,1)S(1)} %copy-done.27, bf16[4096,128]{1,0:T(8,128)(2,1)S(1)} %copy-done.29, bf16[3,1,512,128]{3,2,1,0:T(8,128)(2,1)S(1)} %copy-done.30, ...), custom_call_target="tpu_custom_call" | custom-call | flops 22000001024 | bytes 1000 | tf_op jit(solution)/shard_map/attend_back/pallas_call | solution.py:353
  219.6 1.3 collective-permute-start.42
  223.2 16.7 %attend_back.4 = (bf16[256,768]{1,0:T(8,128)(2,1)S(1)}, bf16[4096,256]{1,0:T(8,128)(2,1)S(1)}) custom-call(s32[1,4096]{1,0:T(1,128)S(1)} %get-tuple-element.151.perm_ref, bf16[4096,128]{1,0:T(8,128)(2,1)S(1)} %copy-done.23, bf16[4096,128]{1,0:T(8,128)(2,1)S(1)} %copy-done.25, bf16[3,1,512,128]{3,2,1,0:T(8,128)(2,1)S(1)} %copy-done.30, ...), custom_call_target="tpu_custom_call" | custom-call | flops 22000001024 | bytes 1000 | tf_op jit(solution)/shard_map/attend_back/pallas_call | solution.py:353
  240.0 6.4 %collective-permute-done.40 = bf16[384,768]{1,0:T(8,128)(2,1)} collective-permute-done((bf16[384,768]{1,0:T(8,128)(2,1)S(1)}, bf16[384,768]{1,0:T(8,128)(2,1)}, u32[]{:S(2)}, u32[]{:S(2)}) %collective-permute-start.40) | collective-permute-done | bytes 589856 | tf_op jit(solution)/shard_map/ppermute | solution.py:34
  246.4 3.0 collective-permute-done.41
  249.6 1.5 add_convert_fusion.3
  252.0 3.4 collective-permute-start.47
  255.5 3.1 collective-permute-start.46
  258.6 1.5 collective-permute-start.45
  260.1 2.0 collective-permute-start.44
  262.2 16.7 %attend_back.5 = (bf16[256,768]{1,0:T(8,128)(2,1)S(1)}, bf16[4096,256]{1,0:T(8,128)(2,1)S(1)}) custom-call(s32[1,4096]{1,0:T(1,128)S(1)} %get-tuple-element.160.perm_ref, bf16[4096,128]{1,0:T(8,128)(2,1)S(1)} %copy-done.19, bf16[4096,128]{1,0:T(8,128)(2,1)S(1)} %copy-done.21, bf16[3,1,512,128]{3,2,1,0:T(8,128)(2,1)S(1)} %copy-done.30, ...), custom_call_target="tpu_custom_call" | custom-call | flops 22000001024 | bytes 1000 | tf_op jit(solution)/shard_map/attend_back/pallas_call | solution.py:353
  281.3 8.1 %token_grad.1 = (bf16[2048,768]{1,0:T(8,128)(2,1)S(1)}, bf16[2048,768]{1,0:T(8,128)(2,1)}) custom-call(bf16[4096,256]{1,0:T(8,128)(2,1)S(1)} %get-tuple-element.212.d0, bf16[4096,256]{1,0:T(8,128)(2,1)S(1)} %copy-done.17, bf16[4096,256]{1,0:T(8,128)(2,1)S(1)} %get-tuple-element.214.d2, bf16[768,768]{1,0:T(8,128)(2,1)S(1)} %bitcast.156), custom_call_target="tpu_custom_call" | custom-call | flops 8000000000 | bytes 1000 | tf_op jit(solution)/shard_map/token_grad/pallas_call | solution.py:400
  291.7 1.3 fusion.1
  293.3 1.4 collective-permute-start.49
  294.7 2.7 collective-permute-start.50
  297.4 1.4 fusion.16
  298.9 2.0 fusion.5
  301.9 2.0 collective-permute-done.50
  306.8 2.7 add_convert_fusion
  309.6 1.6 copy-done.34
  311.6 2.3 collective-permute-done.54
  316.8 1.3 collective-permute-start.59
  318.1 7.2 %collective-permute-done.55 = bf16[1344,128]{1,0:T(8,128)(2,1)S(1)} collective-permute-done((bf16[1344,128]{1,0:T(8,128)(2,1)S(1)}, bf16[1344,128]{1,0:T(8,128)(2,1)S(1)}, u32[]{:S(2)}, u32[]{:S(2)}) %collective-permute-start.55) | collective-permute-done | bytes 344096 | tf_op jit(solution)/shard_map/ppermute | solution.py:34
  326.0 2.8 collective-permute-start.56
  328.8 2.3 collective-permute-start.58
  332.4 3.2 collective-permute-start.66
  335.5 2.0 collective-permute-done.58
  338.5 1.7 collective-permute-start.60
  340.6 2.3 collective-permute-start.62
  343.7 1.6 collective-permute-done.63
  345.4 1.3 collective-permute-start.65
  349.4 5.7 %collective-permute-done.65 = bf16[240,768]{1,0:T(8,128)(2,1)S(1)} collective-permute-done((bf16[240,768]{1,0:T(8,128)(2,1)S(1)}, bf16[240,768]{1,0:T(8,128)(2,1)S(1)}, u32[]{:S(2)}, u32[]{:S(2)}) %collective-permute-start.65) | collective-permute-done | bytes 368672 | tf_op jit(solution)/shard_map/ppermute | solution.py:34
  355.8 8.5 %schulz.1 = bf16[384,768]{1,0:T(8,128)(2,1)S(1)} custom-call(bf16[2688,128]{1,0:T(8,128)(2,1)S(1)} %pad_maximum_fusion.6.panels_ref, bf16[384,768]{1,0:T(8,128)(2,1)S(1)} %pad_maximum_fusion.10.matrix_ref), custom_call_target="tpu_custom_call" | custom-call | flops 8000000000 | bytes 1000 | tf_op jit(solution)/shard_map/schulz/pallas_call | solution.py:692
  367.0 4.7 %bitcast_add_fusion = f32[1024,768]{1,0:T(8,128)} fusion(f32[2,512,768]{2,1,0:T(8,128)} %get-tuple-element.176, bf16[2048,768]{1,0:T(8,128)(2,1)} %copy-done.34, bf16[240,768]{1,0:T(8,128)(2,1)S(1)} %collective-permute-done.65, bf16[336,768]{1,0:T(8,128)(2,1)S(1)} %collective-permute-done.63, bf16[448,768]{1,0:T(8,128)(2,1)} %collective-permute-done.59), kind=kLoop, calls=%fused_computation.1 | loop fusion | flops 7077888 | bytes 9437184 | tf_op jit(solution)/shard_map/add | solution.py:979
  (388 shorter events, 61.9 us)
Async XLA Ops:
  1.7 11.2 %collective-permute-start.3 = (bf16[72,768]{1,0:T(8,128)(2,1)S(1)}, bf16[72,768]{1,0:T(8,128)(2,1)S(1)}, u32[]{:S(2)}, u32[]{:S(2)}) collective-permute-start(bf16[72,768]{1,0:T(8,128)(2,1)S(1)} %get-tuple-element.337), channel_id=1, source_target_pairs={{0,16},{4,20},{8,24},{12,28},{16,0},{20,4},{24,8},{28,12},{1,17},{... | collective-permute-start | bytes 331784 | tf_op jit(solution)/shard_map/ppermute | solution.py:34
  5.8 7.1 %collective-permute-start.4 = (bf16[72,768]{1,0:T(8,128)(2,1)S(1)}, bf16[72,768]{1,0:T(8,128)(2,1)S(1)}, u32[]{:S(2)}, u32[]{:S(2)}) collective-permute-start(bf16[72,768]{1,0:T(8,128)(2,1)S(1)} %get-tuple-element.337), channel_id=1, source_target_pairs={{0,8},{4,12},{8,0},{12,4},{16,24},{20,28},{24,16},{28,20},{1,9},{5... | collective-permute-start | bytes 331784 | tf_op jit(solution)/shard_map/ppermute | solution.py:34
  7.3 7.4 %collective-permute-start.5 = (bf16[72,768]{1,0:T(8,128)(2,1)S(1)}, bf16[72,768]{1,0:T(8,128)(2,1)S(1)}, u32[]{:S(2)}, u32[]{:S(2)}) collective-permute-start(bf16[72,768]{1,0:T(8,128)(2,1)S(1)} %get-tuple-element.337), channel_id=1, source_target_pairs={{0,24},{4,28},{8,16},{12,20},{16,8},{20,12},{24,0},{28,4},{1,25},{... | collective-permute-start | bytes 331784 | tf_op jit(solution)/shard_map/ppermute | solution.py:34
  7.4 36.4 %collective-permute-start.1 = (bf16[1024,768]{1,0:T(8,128)(2,1)}, bf16[1024,768]{1,0:T(8,128)(2,1)}, u32[]{:S(2)}, u32[]{:S(2)}) collective-permute-start(bf16[1024,768]{1,0:T(8,128)(2,1)} %x0.11), channel_id=1, source_target_pairs={{0,2},{1,3},{2,0},{3,1},{4,6},{5,7},{6,4},{7,5},{8,10},{9,11},{10,... | collective-permute-start | bytes 4718600 | tf_op jit(solution)/shard_map/ppermute | solution.py:34
  14.8 28.9 %collective-permute-start.9 = (bf16[288,768]{1,0:T(8,128)(2,1)S(1)}, bf16[288,768]{1,0:T(8,128)(2,1)S(1)}, u32[]{:S(2)}, u32[]{:S(2)}) collective-permute-start(bf16[288,768]{1,0:T(8,128)(2,1)S(1)} %pad_maximum_fusion.12), channel_id=1, source_target_pairs={{0,4},{4,0},{8,12},{12,8},{16,20},{20,16},{24,28},{28,24},{1,5},{5... | collective-permute-start | bytes 1327112 | tf_op jit(solution)/shard_map/ppermute | solution.py:34
  16.4 20.2 %collective-permute-start.6 = (bf16[216,768]{1,0:T(8,128)(2,1)S(1)}, bf16[216,768]{1,0:T(8,128)(2,1)S(1)}, u32[]{:S(2)}, u32[]{:S(2)}) collective-permute-start(bf16[216,768]{1,0:T(8,128)(2,1)S(1)} %constant_dynamic-update-slice_fusion), channel_id=1, source_target_pairs={{0,16},{4,20},{8,24},{12,28},{16,0},{20,4},{24,8},{28,12},{1,17},{... | collective-permute-start | bytes 995336 | tf_op jit(solution)/shard_map/ppermute | solution.py:34
  20.3 23.3 %collective-permute-start.7 = (bf16[216,768]{1,0:T(8,128)(2,1)S(1)}, bf16[216,768]{1,0:T(8,128)(2,1)S(1)}, u32[]{:S(2)}, u32[]{:S(2)}) collective-permute-start(bf16[216,768]{1,0:T(8,128)(2,1)S(1)} %constant_dynamic-update-slice_fusion), channel_id=1, source_target_pairs={{0,8},{4,12},{8,0},{12,4},{16,24},{20,28},{24,16},{28,20},{1,9},{5... | collective-permute-start | bytes 995336 | tf_op jit(solution)/shard_map/ppermute | solution.py:34
  20.3 23.3 %collective-permute-start.8 = (bf16[216,768]{1,0:T(8,128)(2,1)S(1)}, bf16[216,768]{1,0:T(8,128)(2,1)S(1)}, u32[]{:S(2)}, u32[]{:S(2)}) collective-permute-start(bf16[216,768]{1,0:T(8,128)(2,1)S(1)} %constant_dynamic-update-slice_fusion), channel_id=1, source_target_pairs={{0,24},{4,28},{8,16},{12,20},{16,8},{20,12},{24,0},{28,4},{1,25},{... | collective-permute-start | bytes 995336 | tf_op jit(solution)/shard_map/ppermute | solution.py:34
  36.6 10.3 %collective-permute-start = (bf16[1024,768]{1,0:T(8,128)(2,1)S(1)}, bf16[1024,768]{1,0:T(8,128)(2,1)S(1)}, u32[]{:S(2)}, u32[]{:S(2)}) collective-permute-start(bf16[1024,768]{1,0:T(8,128)(2,1)S(1)} %copy-done), channel_id=1, source_target_pairs={{0,1},{1,0},{2,3},{3,2},{4,5},{5,4},{6,7},{7,6},{8,9},{9,8},{10,11... | collective-permute-start | bytes 4718600 | tf_op jit(solution)/shard_map/ppermute | solution.py:34
  43.9 19.5 %collective-permute-start.11 = (bf16[480,768]{1,0:T(8,128)(2,1)S(1)}, bf16[480,768]{1,0:T(8,128)(2,1)S(1)}, u32[]{:S(2)}, u32[]{:S(2)}) collective-permute-start(bf16[480,768]{1,0:T(8,128)(2,1)S(1)} %constant_dynamic-update-slice_fusion.8), channel_id=1, source_target_pairs={{0,2},{1,3},{2,0},{3,1},{4,6},{5,7},{6,4},{7,5},{8,10},{9,11},{10,... | collective-permute-start | bytes 2211848 | tf_op jit(solution)/shard_map/ppermute | solution.py:34
  45.5 17.8 %collective-permute-start.10 = (bf16[384,768]{1,0:T(8,128)(2,1)S(1)}, bf16[384,768]{1,0:T(8,128)(2,1)S(1)}, u32[]{:S(2)}, u32[]{:S(2)}) collective-permute-start(bf16[384,768]{1,0:T(8,128)(2,1)S(1)} %pad_maximum_fusion.7), channel_id=1, source_target_pairs={{0,4},{4,0},{8,12},{12,8},{16,20},{20,16},{24,28},{28,24},{1,5},{5... | collective-permute-start | bytes 1769480 | tf_op jit(solution)/shard_map/ppermute | solution.py:34
  63.4 20.9 %collective-permute-start.12 = (bf16[384,768]{1,0:T(8,128)(2,1)S(1)}, bf16[384,768]{1,0:T(8,128)(2,1)S(1)}, u32[]{:S(2)}, u32[]{:S(2)}) collective-permute-start(bf16[384,768]{1,0:T(8,128)(2,1)S(1)} %pad_maximum_fusion.7), channel_id=1, source_target_pairs={{0,2},{1,3},{2,0},{3,1},{4,6},{5,7},{6,4},{7,5},{8,10},{9,11},{10,... | collective-permute-start | bytes 1769480 | tf_op jit(solution)/shard_map/ppermute | solution.py:34
  64.7 19.5 %collective-permute-start.15 = (bf16[768,768]{1,0:T(8,128)(2,1)S(1)}, bf16[768,768]{1,0:T(8,128)(2,1)S(1)}, u32[]{:S(2)}, u32[]{:S(2)}) collective-permute-start(bf16[768,768]{1,0:T(8,128)(2,1)S(1)} %constant_dynamic-update-slice_fusion.13.refs_16_), channel_id=1, source_target_pairs={{0,1},{1,0},{2,3},{3,2},{4,5},{5,4},{6,7},{7,6},{8,9},{9,8},{10,11... | collective-permute-start | bytes 3538952 | tf_op jit(solution)/shard_map/ppermute | solution.py:34
  64.8 19.4 %collective-permute-start.13 = (bf16[480,768]{1,0:T(8,128)(2,1)S(1)}, bf16[480,768]{1,0:T(8,128)(2,1)S(1)}, u32[]{:S(2)}, u32[]{:S(2)}) collective-permute-start(bf16[480,768]{1,0:T(8,128)(2,1)S(1)} %constant_dynamic-update-slice_fusion.8), channel_id=1, source_target_pairs={{0,4},{4,0},{8,12},{12,8},{16,20},{20,16},{24,28},{28,24},{1,5},{5... | collective-permute-start | bytes 2211848 | tf_op jit(solution)/shard_map/ppermute | solution.py:34
  65.8 18.4 %collective-permute-start.14 = (bf16[1024,128]{1,0:T(8,128)(2,1)S(1)}, bf16[1024,128]{1,0:T(8,128)(2,1)S(1)}, u32[]{:S(2)}, u32[]{:S(2)}) collective-permute-start(bf16[1024,128]{1,0:T(8,128)(2,1)S(1)} %get-tuple-element.150), channel_id=1, source_target_pairs={{0,2},{1,3},{2,0},{3,1},{4,6},{5,7},{6,4},{7,5},{8,10},{9,11},{10,... | collective-permute-start | bytes 786440 | tf_op jit(solution)/shard_map/ppermute | solution.py:34
  81.8 23.1 %collective-permute-start.18 = (bf16[1024,128]{1,0:T(8,128)(2,1)S(1)}, bf16[1024,128]{1,0:T(8,128)(2,1)S(1)}, u32[]{:S(2)}, u32[]{:S(2)}) collective-permute-start(bf16[1024,128]{1,0:T(8,128)(2,1)S(1)} %get-tuple-element.156), channel_id=1, source_target_pairs={{0,2},{1,3},{2,0},{3,1},{4,6},{5,7},{6,4},{7,5},{8,10},{9,11},{10,... | collective-permute-start | bytes 786440 | tf_op jit(solution)/shard_map/ppermute | solution.py:34
  85.3 19.7 %collective-permute-start.20 = (bf16[768,768]{1,0:T(8,128)(2,1)S(1)}, bf16[768,768]{1,0:T(8,128)(2,1)S(1)}, u32[]{:S(2)}, u32[]{:S(2)}) collective-permute-start(bf16[768,768]{1,0:T(8,128)(2,1)S(1)} %pad_maximum_fusion.refs_20_), channel_id=1, source_target_pairs={{0,1},{1,0},{2,3},{3,2},{4,5},{5,4},{6,7},{7,6},{8,9},{9,8},{10,11... | collective-permute-start | bytes 3538952 | tf_op jit(solution)/shard_map/ppermute | solution.py:34
  85.4 19.6 %collective-permute-start.19 = (bf16[1024,128]{1,0:T(8,128)(2,1)S(1)}, bf16[1024,128]{1,0:T(8,128)(2,1)S(1)}, u32[]{:S(2)}, u32[]{:S(2)}) collective-permute-start(bf16[1024,128]{1,0:T(8,128)(2,1)S(1)} %pad_maximum_fusion.19), channel_id=1, source_target_pairs={{0,1},{1,0},{2,3},{3,2},{4,5},{5,4},{6,7},{7,6},{8,9},{9,8},{10,11... | collective-permute-start | bytes 786440 | tf_op jit(solution)/shard_map/ppermute | solution.py:34
  86.0 19.0 %collective-permute-start.17 = (bf16[480,768]{1,0:T(8,128)(2,1)S(1)}, bf16[480,768]{1,0:T(8,128)(2,1)S(1)}, u32[]{:S(2)}, u32[]{:S(2)}) collective-permute-start(bf16[480,768]{1,0:T(8,128)(2,1)S(1)} %collective-permute-done.11), channel_id=1, source_target_pairs={{0,4},{4,0},{8,12},{12,8},{16,20},{20,16},{24,28},{28,24},{1,5},{5... | collective-permute-start | bytes 2211848 | tf_op jit(solution)/shard_map/ppermute | solution.py:34
  87.1 17.9 %collective-permute-start.16 = (bf16[384,768]{1,0:T(8,128)(2,1)S(1)}, bf16[384,768]{1,0:T(8,128)(2,1)S(1)}, u32[]{:S(2)}, u32[]{:S(2)}) collective-permute-start(bf16[384,768]{1,0:T(8,128)(2,1)S(1)} %collective-permute-done.10), channel_id=1, source_target_pairs={{0,2},{1,3},{2,0},{3,1},{4,6},{5,7},{6,4},{7,5},{8,10},{9,11},{10,... | collective-permute-start | bytes 1769480 | tf_op jit(solution)/shard_map/ppermute | solution.py:34
  106.1 11.0 %collective-permute-start.26 = (bf16[768,768]{1,0:T(8,128)(2,1)S(1)}, bf16[768,768]{1,0:T(8,128)(2,1)S(1)}, u32[]{:S(2)}, u32[]{:S(2)}) collective-permute-start(bf16[768,768]{1,0:T(8,128)(2,1)S(1)} %pad_maximum_fusion.1.refs_21_), channel_id=1, source_target_pairs={{0,1},{1,0},{2,3},{3,2},{4,5},{5,4},{6,7},{7,6},{8,9},{9,8},{10,11... | collective-permute-start | bytes 3538952 | tf_op jit(solution)/shard_map/ppermute | solution.py:34
  106.2 10.9 %collective-permute-start.25 = (bf16[768,768]{1,0:T(8,128)(2,1)S(1)}, bf16[768,768]{1,0:T(8,128)(2,1)S(1)}, u32[]{:S(2)}, u32[]{:S(2)}) collective-permute-start(bf16[768,768]{1,0:T(8,128)(2,1)S(1)} %constant_dynamic-update-slice_fusion.20.refs_17_), channel_id=1, source_target_pairs={{0,1},{1,0},{2,3},{3,2},{4,5},{5,4},{6,7},{7,6},{8,9},{9,8},{10,11... | collective-permute-start | bytes 3538952 | tf_op jit(solution)/shard_map/ppermute | solution.py:34
  106.8 8.3 %collective-permute-start.22 = (bf16[1024,128]{1,0:T(8,128)(2,1)S(1)}, bf16[1024,128]{1,0:T(8,128)(2,1)S(1)}, u32[]{:S(2)}, u32[]{:S(2)}) collective-permute-start(bf16[1024,128]{1,0:T(8,128)(2,1)S(1)} %get-tuple-element.169), channel_id=1, source_target_pairs={{0,2},{1,3},{2,0},{3,1},{4,6},{5,7},{6,4},{7,5},{8,10},{9,11},{10,... | collective-permute-start | bytes 786440 | tf_op jit(solution)/shard_map/ppermute | solution.py:34
  108.0 7.8 %collective-permute-start.24 = (bf16[384,768]{1,0:T(8,128)(2,1)S(1)}, bf16[384,768]{1,0:T(8,128)(2,1)S(1)}, u32[]{:S(2)}, u32[]{:S(2)}) collective-permute-start(bf16[384,768]{1,0:T(8,128)(2,1)S(1)} %pad_maximum_fusion.8), channel_id=1, source_target_pairs={{0,1},{1,0},{2,3},{3,2},{4,5},{5,4},{6,7},{7,6},{8,9},{9,8},{10,11... | collective-permute-start | bytes 1769480 | tf_op jit(solution)/shard_map/ppermute | solution.py:34
  158.1 14.3 %collective-permute-start.27 = (bf16[2,2,512,128]{3,2,1,0:T(8,128)(2,1)}, bf16[2,2,512,128]{3,2,1,0:T(8,128)(2,1)S(1)}, u32[]{:S(2)}, u32[]{:S(2)}) collective-permute-start(bf16[2,2,512,128]{3,2,1,0:T(8,128)(2,1)} %get-tuple-element.179), channel_id=1, source_target_pairs={{0,2},{1,3},{2,0},{3,1},{4,6},{5,7},{6,4},{7,5},{8,10},{9,11},{10,... | collective-permute-start | bytes 1572872 | tf_op jit(solution)/shard_map/ppermute | solution.py:34
  167.3 20.1 %collective-permute-start.31 = (bf16[1536,768]{1,0:T(8,128)(2,1)}, bf16[1536,768]{1,0:T(8,128)(2,1)}, u32[]{:S(2)}, u32[]{:S(2)}) collective-permute-start(bf16[1536,768]{1,0:T(8,128)(2,1)} %weight_grad.5), channel_id=1, source_target_pairs={{0,1},{1,0},{2,3},{3,2},{4,5},{5,4},{6,7},{7,6},{8,9},{9,8},{10,11... | collective-permute-start | bytes 7077896 | tf_op jit(solution)/shard_map/ppermute | solution.py:34
  176.6 17.9 %collective-permute-start.28 = (bf16[1536,768]{1,0:T(8,128)(2,1)}, bf16[1536,768]{1,0:T(8,128)(2,1)S(1)}, u32[]{:S(2)}, u32[]{:S(2)}) collective-permute-start(bf16[1536,768]{1,0:T(8,128)(2,1)} %weight_grad.6), channel_id=1, source_target_pairs={{0,1},{1,0},{2,3},{3,2},{4,5},{5,4},{6,7},{7,6},{8,9},{9,8},{10,11... | collective-permute-start | bytes 7077896 | tf_op jit(solution)/shard_map/ppermute | solution.py:34
  178.5 8.8 %collective-permute-start.32 = (bf16[1,2,512,128]{3,2,1,0:T(8,128)(2,1)S(1)}, bf16[1,2,512,128]{3,2,1,0:T(8,128)(2,1)S(1)}, u32[]{:S(2)}, u32[]{:S(2)}) collective-permute-start(bf16[1,2,512,128]{3,2,1,0:T(8,128)(2,1)S(1)} %copy-done.80), channel_id=1, source_target_pairs={{0,2},{1,3},{2,0},{3,1},{4,6},{5,7},{6,4},{7,5},{8,10},{9,11},{10,... | collective-permute-start | bytes 786440 | tf_op jit(solution)/shard_map/ppermute | solution.py:34
  183.2 11.4 %collective-permute-start.30 = (bf16[384,768]{1,0:T(8,128)(2,1)S(1)}, bf16[384,768]{1,0:T(8,128)(2,1)S(1)}, u32[]{:S(2)}, u32[]{:S(2)}) collective-permute-start(bf16[384,768]{1,0:T(8,128)(2,1)S(1)} %bitcast.184), channel_id=1, source_target_pairs={{0,1},{1,0},{2,3},{3,2},{4,5},{5,4},{6,7},{7,6},{8,9},{9,8},{10,11... | collective-permute-start | bytes 1769480 | tf_op jit(solution)/shard_map/ppermute | solution.py:34
  184.0 10.6 %collective-permute-start.29 = (bf16[2,2,512,128]{3,2,1,0:T(8,128)(2,1)S(1)}, bf16[2,2,512,128]{3,2,1,0:T(8,128)(2,1)S(1)}, u32[]{:S(2)}, u32[]{:S(2)}) collective-permute-start(bf16[2,2,512,128]{3,2,1,0:T(8,128)(2,1)S(1)} %pad_maximum_fusion.11), channel_id=1, source_target_pairs={{0,1},{1,0},{2,3},{3,2},{4,5},{5,4},{6,7},{7,6},{8,9},{9,8},{10,11... | collective-permute-start | bytes 1572872 | tf_op jit(solution)/shard_map/ppermute | solution.py:34
  192.8 29.5 %collective-permute-start.37 = (bf16[1,2,512,128]{3,2,1,0:T(8,128)(2,1)S(1)}, bf16[1,2,512,128]{3,2,1,0:T(8,128)(2,1)S(1)}, u32[]{:S(2)}, u32[]{:S(2)}) collective-permute-start(bf16[1,2,512,128]{3,2,1,0:T(8,128)(2,1)S(1)} %pad_maximum_fusion.22), channel_id=1, source_target_pairs={{0,1},{1,0},{2,3},{3,2},{4,5},{5,4},{6,7},{7,6},{8,9},{9,8},{10,11... | collective-permute-start | bytes 786440 | tf_op jit(solution)/shard_map/ppermute | solution.py:34
  193.4 25.2 %collective-permute-start.36 = (f32[5,768]{1,0:T(8,128)S(1)}, f32[5,768]{1,0:T(8,128)S(1)}, u32[]{:S(2)}, u32[]{:S(2)}) collective-permute-start(f32[5,768]{1,0:T(8,128)S(1)} %fusion.21), channel_id=1, source_target_pairs={{0,2},{1,3},{2,0},{3,1},{4,6},{5,7},{6,4},{7,5},{8,10},{9,11},{10,... | collective-permute-start | bytes 46088 | tf_op jit(solution)/shard_map/ppermute | solution.py:34
  198.4 21.2 %collective-permute-start.34 = (bf16[480,768]{1,0:T(8,128)(2,1)S(1)}, bf16[480,768]{1,0:T(8,128)(2,1)S(1)}, u32[]{:S(2)}, u32[]{:S(2)}) collective-permute-start(bf16[480,768]{1,0:T(8,128)(2,1)S(1)} %pad_maximum_fusion.5), channel_id=1, source_target_pairs={{0,4},{4,0},{8,12},{12,8},{16,20},{20,16},{24,28},{28,24},{1,5},{5... | collective-permute-start | bytes 2211848 | tf_op jit(solution)/shard_map/ppermute | solution.py:34
  199.7 20.0 %collective-permute-start.33 = (bf16[384,768]{1,0:T(8,128)(2,1)S(1)}, bf16[384,768]{1,0:T(8,128)(2,1)S(1)}, u32[]{:S(2)}, u32[]{:S(2)}) collective-permute-start(bf16[384,768]{1,0:T(8,128)(2,1)S(1)} %get-tuple-element.265), channel_id=1, source_target_pairs={{0,2},{1,3},{2,0},{3,1},{4,6},{5,7},{6,4},{7,5},{8,10},{9,11},{10,... | collective-permute-start | bytes 1769480 | tf_op jit(solution)/shard_map/ppermute | solution.py:34
  200.7 39.3 %collective-permute-start.39 = (bf16[480,768]{1,0:T(8,128)(2,1)S(1)}, bf16[480,768]{1,0:T(8,128)(2,1)S(1)}, u32[]{:S(2)}, u32[]{:S(2)}) collective-permute-start(bf16[480,768]{1,0:T(8,128)(2,1)S(1)} %pad_maximum_fusion.3), channel_id=1, source_target_pairs={{0,4},{4,0},{8,12},{12,8},{16,20},{20,16},{24,28},{28,24},{1,5},{5... | collective-permute-start | bytes 2211848 | tf_op jit(solution)/shard_map/ppermute | solution.py:34
  218.6 21.4 %collective-permute-start.38 = (bf16[384,768]{1,0:T(8,128)(2,1)S(1)}, bf16[384,768]{1,0:T(8,128)(2,1)S(1)}, u32[]{:S(2)}, u32[]{:S(2)}) collective-permute-start(bf16[384,768]{1,0:T(8,128)(2,1)S(1)} %get-tuple-element.266), channel_id=1, source_target_pairs={{0,2},{1,3},{2,0},{3,1},{4,6},{5,7},{6,4},{7,5},{8,10},{9,11},{10,... | collective-permute-start | bytes 1769480 | tf_op jit(solution)/shard_map/ppermute | solution.py:34
  219.6 20.4 %collective-permute-start.42 = (f32[5,768]{1,0:T(8,128)S(1)}, f32[5,768]{1,0:T(8,128)S(1)}, u32[]{:S(2)}, u32[]{:S(2)}) collective-permute-start(f32[5,768]{1,0:T(8,128)S(1)} %add.173), channel_id=1, source_target_pairs={{0,4},{4,0},{8,12},{12,8},{16,20},{20,16},{24,28},{28,24},{1,5},{5... | collective-permute-start | bytes 46088 | tf_op jit(solution)/shard_map/ppermute | solution.py:34
  221.1 28.2 %collective-permute-start.41 = (bf16[480,768]{1,0:T(8,128)(2,1)S(1)}, bf16[480,768]{1,0:T(8,128)(2,1)S(1)}, u32[]{:S(2)}, u32[]{:S(2)}) collective-permute-start(bf16[480,768]{1,0:T(8,128)(2,1)S(1)} %add_convert_fusion.2), channel_id=1, source_target_pairs={{0,2},{1,3},{2,0},{3,1},{4,6},{5,7},{6,4},{7,5},{8,10},{9,11},{10,... | collective-permute-start | bytes 2211848 | tf_op jit(solution)/shard_map/ppermute | solution.py:34
  222.3 24.1 %collective-permute-start.40 = (bf16[384,768]{1,0:T(8,128)(2,1)S(1)}, bf16[384,768]{1,0:T(8,128)(2,1)}, u32[]{:S(2)}, u32[]{:S(2)}) collective-permute-start(bf16[384,768]{1,0:T(8,128)(2,1)S(1)} %add_convert_fusion.4), channel_id=1, source_target_pairs={{0,4},{4,0},{8,12},{12,8},{16,20},{20,16},{24,28},{28,24},{1,5},{5... | collective-permute-start | bytes 1769480 | tf_op jit(solution)/shard_map/ppermute | solution.py:34
  252.0 37.4 %collective-permute-start.47 = (bf16[216,768]{1,0:T(8,128)(2,1)S(1)}, bf16[216,768]{1,0:T(8,128)(2,1)S(1)}, u32[]{:S(2)}, u32[]{:S(2)}) collective-permute-start(bf16[216,768]{1,0:T(8,128)(2,1)S(1)} %pad_maximum_fusion.16), channel_id=1, source_target_pairs={{0,24},{4,28},{8,16},{12,20},{16,8},{20,12},{24,0},{28,4},{1,25},{... | collective-permute-start | bytes 995336 | tf_op jit(solution)/shard_map/ppermute | solution.py:34
  255.5 33.9 %collective-permute-start.46 = (bf16[216,768]{1,0:T(8,128)(2,1)S(1)}, bf16[216,768]{1,0:T(8,128)(2,1)S(1)}, u32[]{:S(2)}, u32[]{:S(2)}) collective-permute-start(bf16[216,768]{1,0:T(8,128)(2,1)S(1)} %pad_maximum_fusion.15), channel_id=1, source_target_pairs={{0,8},{4,12},{8,0},{12,4},{16,24},{20,28},{24,16},{28,20},{1,9},{5... | collective-permute-start | bytes 995336 | tf_op jit(solution)/shard_map/ppermute | solution.py:34
  258.6 30.8 %collective-permute-start.45 = (bf16[216,768]{1,0:T(8,128)(2,1)S(1)}, bf16[216,768]{1,0:T(8,128)(2,1)S(1)}, u32[]{:S(2)}, u32[]{:S(2)}) collective-permute-start(bf16[216,768]{1,0:T(8,128)(2,1)S(1)} %pad_maximum_fusion.14), channel_id=1, source_target_pairs={{0,16},{4,20},{8,24},{12,28},{16,0},{20,4},{24,8},{28,12},{1,17},{... | collective-permute-start | bytes 995336 | tf_op jit(solution)/shard_map/ppermute | solution.py:34
  260.1 21.1 %collective-permute-start.44 = (f32[5,768]{1,0:T(8,128)S(1)}, f32[5,768]{1,0:T(8,128)S(1)}, u32[]{:S(2)}, u32[]{:S(2)}) collective-permute-start(f32[5,768]{1,0:T(8,128)S(1)} %add.174), channel_id=1, source_target_pairs={{0,8},{4,12},{8,0},{12,4},{16,24},{20,28},{24,16},{28,20},{1,9},{5... | collective-permute-start | bytes 46088 | tf_op jit(solution)/shard_map/ppermute | solution.py:34
  280.2 9.9 %collective-permute-start.43 = (bf16[288,768]{1,0:T(8,128)(2,1)S(1)}, bf16[288,768]{1,0:T(8,128)(2,1)}, u32[]{:S(2)}, u32[]{:S(2)}) collective-permute-start(bf16[288,768]{1,0:T(8,128)(2,1)S(1)} %bitcast.185), channel_id=1, source_target_pairs={{0,4},{4,0},{8,12},{12,8},{16,20},{20,16},{24,28},{28,24},{1,5},{5... | collective-permute-start | bytes 1327112 | tf_op jit(solution)/shard_map/ppermute | solution.py:34
  290.3 13.5 %collective-permute-start.51 = (bf16[2048,768]{1,0:T(8,128)(2,1)}, bf16[2048,768]{1,0:T(8,128)(2,1)}, u32[]{:S(2)}, u32[]{:S(2)}) collective-permute-start(bf16[2048,768]{1,0:T(8,128)(2,1)} %get-tuple-element.223), channel_id=1, source_target_pairs={{0,1},{1,0},{2,3},{3,2},{4,5},{5,4},{6,7},{7,6},{8,9},{9,8},{10,11... | collective-permute-start | bytes 9437192 | tf_op jit(solution)/shard_map/ppermute | solution.py:34
  293.0 8.9 %collective-permute-start.48 = (bf16[72,768]{1,0:T(8,128)(2,1)S(1)}, bf16[72,768]{1,0:T(8,128)(2,1)S(1)}, u32[]{:S(2)}, u32[]{:S(2)}) collective-permute-start(bf16[72,768]{1,0:T(8,128)(2,1)S(1)} %get-tuple-element.317), channel_id=1, source_target_pairs={{0,16},{4,20},{8,24},{12,28},{16,0},{20,4},{24,8},{28,12},{1,17},{... | collective-permute-start | bytes 331784 | tf_op jit(solution)/shard_map/ppermute | solution.py:34
  293.3 8.6 %collective-permute-start.49 = (bf16[72,768]{1,0:T(8,128)(2,1)S(1)}, bf16[72,768]{1,0:T(8,128)(2,1)S(1)}, u32[]{:S(2)}, u32[]{:S(2)}) collective-permute-start(bf16[72,768]{1,0:T(8,128)(2,1)S(1)} %get-tuple-element.316), channel_id=1, source_target_pairs={{0,8},{4,12},{8,0},{12,4},{16,24},{20,28},{24,16},{28,20},{1,9},{5... | collective-permute-start | bytes 331784 | tf_op jit(solution)/shard_map/ppermute | solution.py:34
  294.7 9.2 %collective-permute-start.50 = (bf16[72,768]{1,0:T(8,128)(2,1)S(1)}, bf16[72,768]{1,0:T(8,128)(2,1)S(1)}, u32[]{:S(2)}, u32[]{:S(2)}) collective-permute-start(bf16[72,768]{1,0:T(8,128)(2,1)S(1)} %get-tuple-element.315), channel_id=1, source_target_pairs={{0,24},{4,28},{8,16},{12,20},{16,8},{20,12},{24,0},{28,4},{1,25},{... | collective-permute-start | bytes 331784 | tf_op jit(solution)/shard_map/ppermute | solution.py:34
  304.9 6.7 %collective-permute-start.53 = (bf16[96,768]{1,0:T(8,128)(2,1)S(1)}, bf16[96,768]{1,0:T(8,128)(2,1)S(1)}, u32[]{:S(2)}, u32[]{:S(2)}) collective-permute-start(bf16[96,768]{1,0:T(8,128)(2,1)S(1)} %get-tuple-element.306), channel_id=1, source_target_pairs={{0,2},{1,3},{2,0},{3,1},{4,6},{5,7},{6,4},{7,5},{8,10},{9,11},{10,... | collective-permute-start | bytes 442376 | tf_op jit(solution)/shard_map/ppermute | solution.py:34
  306.0 7.9 %collective-permute-start.54 = (bf16[96,768]{1,0:T(8,128)(2,1)S(1)}, bf16[96,768]{1,0:T(8,128)(2,1)S(1)}, u32[]{:S(2)}, u32[]{:S(2)}) collective-permute-start(bf16[96,768]{1,0:T(8,128)(2,1)S(1)} %get-tuple-element.305), channel_id=1, source_target_pairs={{0,3},{1,2},{2,1},{3,0},{4,7},{5,6},{6,5},{7,4},{8,11},{9,10},{10,... | collective-permute-start | bytes 442376 | tf_op jit(solution)/shard_map/ppermute | solution.py:34
  314.9 10.3 %collective-permute-start.55 = (bf16[1344,128]{1,0:T(8,128)(2,1)S(1)}, bf16[1344,128]{1,0:T(8,128)(2,1)S(1)}, u32[]{:S(2)}, u32[]{:S(2)}) collective-permute-start(bf16[1344,128]{1,0:T(8,128)(2,1)S(1)} %dynamic-slice_bitcast_fusion), channel_id=1, source_target_pairs={{0,4},{4,0},{8,12},{12,8},{16,20},{20,16},{24,28},{28,24},{1,5},{5... | collective-permute-start | bytes 1032200 | tf_op jit(solution)/shard_map/ppermute | solution.py:34
  316.8 21.7 %collective-permute-start.59 = (bf16[448,768]{1,0:T(8,128)(2,1)}, bf16[448,768]{1,0:T(8,128)(2,1)}, u32[]{:S(2)}, u32[]{:S(2)}) collective-permute-start(bf16[448,768]{1,0:T(8,128)(2,1)} %slice.446), channel_id=1, source_target_pairs={{0,2},{1,3},{2,0},{3,1},{4,6},{5,7},{6,4},{7,5},{8,10},{9,11},{10,... | collective-permute-start | bytes 2064392 | tf_op jit(solution)/shard_map/ppermute | solution.py:34
  328.8 6.7 %collective-permute-start.57 = (bf16[336,128]{1,0:T(8,128)(2,1)S(1)}, bf16[336,128]{1,0:T(8,128)(2,1)}, u32[]{:S(2)}, u32[]{:S(2)}) collective-permute-start(bf16[336,128]{1,0:T(8,128)(2,1)S(1)} %get-tuple-element.324), channel_id=1, source_target_pairs={{0,8},{4,12},{8,0},{12,4},{16,24},{20,28},{24,16},{28,20},{1,9},{5... | collective-permute-start | bytes 258056 | tf_op jit(solution)/shard_map/ppermute | solution.py:34
  328.8 8.6 %collective-permute-start.58 = (bf16[336,128]{1,0:T(8,128)(2,1)S(1)}, bf16[336,128]{1,0:T(8,128)(2,1)}, u32[]{:S(2)}, u32[]{:S(2)}) collective-permute-start(bf16[336,128]{1,0:T(8,128)(2,1)S(1)} %get-tuple-element.323), channel_id=1, source_target_pairs={{0,24},{4,28},{8,16},{12,20},{16,8},{20,12},{24,0},{28,4},{1,25},{... | collective-permute-start | bytes 258056 | tf_op jit(solution)/shard_map/ppermute | solution.py:34
  331.2 14.2 %collective-permute-start.63 = (bf16[336,768]{1,0:T(8,128)(2,1)S(1)}, bf16[336,768]{1,0:T(8,128)(2,1)S(1)}, u32[]{:S(2)}, u32[]{:S(2)}) collective-permute-start(bf16[336,768]{1,0:T(8,128)(2,1)S(1)} %slice.447), channel_id=1, source_target_pairs={{0,2},{1,3},{2,0},{3,1},{4,6},{5,7},{6,4},{7,5},{8,10},{9,11},{10,... | collective-permute-start | bytes 1548296 | tf_op jit(solution)/shard_map/ppermute | solution.py:34
  332.4 17.0 %collective-permute-start.66 = (f32[5,768]{1,0:T(8,128)S(1)}, f32[5,768]{1,0:T(8,128)S(1)}, u32[]{:S(2)}, u32[]{:S(2)}) collective-permute-start(f32[5,768]{1,0:T(8,128)S(1)} %add.212), channel_id=1, source_target_pairs={{0,16},{4,20},{8,24},{12,28},{16,0},{20,4},{24,8},{28,12},{1,17},{... | collective-permute-start | bytes 46088 | tf_op jit(solution)/shard_map/ppermute | solution.py:34
  338.5 9.1 %collective-permute-start.60 = (bf16[336,128]{1,0:T(8,128)(2,1)S(1)}, bf16[336,128]{1,0:T(8,128)(2,1)S(1)}, u32[]{:S(2)}, u32[]{:S(2)}) collective-permute-start(bf16[336,128]{1,0:T(8,128)(2,1)S(1)} %fusion.9), channel_id=1, source_target_pairs={{0,16},{4,20},{8,24},{12,28},{16,0},{20,4},{24,8},{28,12},{1,17},{... | collective-permute-start | bytes 258056 | tf_op jit(solution)/shard_map/ppermute | solution.py:34
  340.2 7.4 %collective-permute-start.61 = (bf16[336,128]{1,0:T(8,128)(2,1)S(1)}, bf16[336,128]{1,0:T(8,128)(2,1)S(1)}, u32[]{:S(2)}, u32[]{:S(2)}) collective-permute-start(bf16[336,128]{1,0:T(8,128)(2,1)S(1)} %fusion.9), channel_id=1, source_target_pairs={{0,8},{4,12},{8,0},{12,4},{16,24},{20,28},{24,16},{28,20},{1,9},{5... | collective-permute-start | bytes 258056 | tf_op jit(solution)/shard_map/ppermute | solution.py:34
  340.6 7.0 %collective-permute-start.62 = (bf16[336,128]{1,0:T(8,128)(2,1)S(1)}, bf16[336,128]{1,0:T(8,128)(2,1)S(1)}, u32[]{:S(2)}, u32[]{:S(2)}) collective-permute-start(bf16[336,128]{1,0:T(8,128)(2,1)S(1)} %fusion.9), channel_id=1, source_target_pairs={{0,24},{4,28},{8,16},{12,20},{16,8},{20,12},{24,0},{28,4},{1,25},{... | collective-permute-start | bytes 258056 | tf_op jit(solution)/shard_map/ppermute | solution.py:34
  345.4 9.6 %collective-permute-start.65 = (bf16[240,768]{1,0:T(8,128)(2,1)S(1)}, bf16[240,768]{1,0:T(8,128)(2,1)S(1)}, u32[]{:S(2)}, u32[]{:S(2)}) collective-permute-start(bf16[240,768]{1,0:T(8,128)(2,1)S(1)} %slice.448), channel_id=1, source_target_pairs={{0,2},{1,3},{2,0},{3,1},{4,6},{5,7},{6,4},{7,5},{8,10},{9,11},{10,... | collective-permute-start | bytes 1105928 | tf_op jit(solution)/shard_map/ppermute | solution.py:34
  347.7 8.0 %collective-permute-start.64 = (bf16[1344,128]{1,0:T(8,128)(2,1)S(1)}, bf16[1344,128]{1,0:T(8,128)(2,1)S(1)}, u32[]{:S(2)}, u32[]{:S(2)}) collective-permute-start(bf16[1344,128]{1,0:T(8,128)(2,1)S(1)} %pad_maximum_fusion.13), channel_id=1, source_target_pairs={{0,4},{4,0},{8,12},{12,8},{16,20},{20,16},{24,28},{28,24},{1,5},{5... | collective-permute-start | bytes 1032200 | tf_op jit(solution)/shard_map/ppermute | solution.py:34
  364.3 8.0 %collective-permute-start.67 = (bf16[96,768]{1,0:T(8,128)(2,1)S(1)}, bf16[96,768]{1,0:T(8,128)(2,1)S(1)}, u32[]{:S(2)}, u32[]{:S(2)}) collective-permute-start(bf16[96,768]{1,0:T(8,128)(2,1)S(1)} %get-tuple-element.301), channel_id=1, source_target_pairs={{0,1},{1,0},{2,3},{3,2},{4,5},{5,4},{6,7},{7,6},{8,9},{9,8},{10,11... | collective-permute-start | bytes 442376 | tf_op jit(solution)/shard_map/ppermute | solution.py:34
  364.4 7.9 %collective-permute-start.68 = (bf16[96,768]{1,0:T(8,128)(2,1)S(1)}, bf16[96,768]{1,0:T(8,128)(2,1)S(1)}, u32[]{:S(2)}, u32[]{:S(2)}) collective-permute-start(bf16[96,768]{1,0:T(8,128)(2,1)S(1)} %get-tuple-element.303), channel_id=1, source_target_pairs={{0,2},{1,3},{2,0},{3,1},{4,6},{5,7},{6,4},{7,5},{8,10},{9,11},{10,... | collective-permute-start | bytes 442376 | tf_op jit(solution)/shard_map/ppermute | solution.py:34
  365.2 8.1 %collective-permute-start.69 = (bf16[96,768]{1,0:T(8,128)(2,1)S(1)}, bf16[96,768]{1,0:T(8,128)(2,1)S(1)}, u32[]{:S(2)}, u32[]{:S(2)}) collective-permute-start(bf16[96,768]{1,0:T(8,128)(2,1)S(1)} %get-tuple-element.302), channel_id=1, source_target_pairs={{0,3},{1,2},{2,1},{3,0},{4,7},{5,6},{6,5},{7,4},{8,11},{9,10},{10,... | collective-permute-start | bytes 442376 | tf_op jit(solution)/shard_map/ppermute | solution.py:34
  (89 other events, 475.3 us)
